TPU v7x, 256 devices: a whole 4x4x8 slice. The times are simulated.
256 devices in a mesh: region: 32 (over x_hi, z, core), panel: 8 (over x_lo, y).
Axes of the slice: x: 4 (x_hi: 2, x_lo: 2; x = x_hi * 2 + x_lo), y: 4, z: 8, core: 2. Of those that a mesh axis runs over, the one named last changes fastest.
Arguments:
- latents: bfloat16 [262144, 128], P(('region', 'panel')), may hold values from -6 to 6
- edge_feats: bfloat16 [786432, 128], P(('region', 'panel')), may hold values from -6 to 6
- weights: bfloat16 [9, 128, 128], replicated, may hold values from -0.5 to 0.5
- cotangent: bfloat16 [262144, 128], P(('region', 'panel')), may hold values from -6 to 6
- mesh_edges: int32 [2, 786432], P(None, ('region', 'panel')), may hold values from 0 to 1151, as said below
- boundary: int32 [65536], P(('region', 'panel')), may hold values from 0 to 1023, as said below
- contact_edges: int32 [2, 2097152], P(None, ('region', 'panel')), may hold values from 0 to 255, as said below
- contact_counts: int32 [256, 4], P(('region', 'panel')), may hold values from 256 to 2048, as said below
Outputs:
- new_latents: bfloat16 [262144, 128], P(('region', 'panel'))
- grad_latents: float32 [262144, 128], P(('region', 'panel'))
- grad_weights: float32 [9, 128, 128], replicated
Inputs may be any that keep to these rules, and one draw needn't show every extreme that they name: `mesh_edges`: within a block, row 1 is a receiver row of the block (0 to 1023) and row 0 a row of the block's extended matrix within 64 of the receiver's row + 64. A block's boundary rows are distinct, the k-th lies in 4k to 4k + 3. `contact_edges`: row 0 is a boundary slot of the block, row 1 a boundary slot of the round's partner; columns of a run at or after the round's count are padding with arbitrary slots. `contact_counts`: in every round some block has all 2048 slots live.
All inputs are finite; a program needn't handle non-finite values.
Results may differ from a plain program's by a relative error of at most 0.0079.
Values may be sent and summed in bfloat16 or wider, within the bound.
No kernel may reach another device: no remote copies, remote signals or barrier semaphores. Data moves between devices by JAX's collectives and lax.ppermute only.
A program may use at most 64 MiB of HBM per device.

v0:
```python
import math

import jax
import jax.numpy as jnp
from jax import lax
from jax.sharding import PartitionSpec as P

HB = 64


def swapped(block, axis, bit):
    count = lax.axis_size(axis)
    route = []
    for low in range(count):
        high = low | 1 << bit
        if high != low and high < count:
            route += [(low, high), (high, low)]
    return lax.ppermute(block, axis, route)


def extended_2(array, sides, width):
    for axis, dim in sides:
        size, length = (lax.axis_size(axis), array.shape[dim])
        up = [(i, (i + 1) % size) for i in range(size - 1)]
        down = [(j, i) for i, j in up]
        last = lax.slice_in_dim(array, length - width, length, axis=dim)
        first = lax.slice_in_dim(array, 0, width, axis=dim)
        before = lax.ppermute(last, axis, up)
        after = lax.ppermute(first, axis, down)
        array = jnp.concatenate([before, array, after], axis=dim)
    return array


def shifted(array, axis, by):
    length = lax.axis_size(axis)
    pairs = [(i, i + by) for i in range(length) if 0 <= i + by < length]
    return lax.ppermute(array, axis, pairs)


def swish_gradient(values):
    sigmoid = jax.nn.sigmoid(values)
    return sigmoid * (1.0 + values * (1.0 - sigmoid))


def product(left_side, right_side):
    return jnp.dot(left_side, right_side, preferred_element_type=jnp.float32)


def over_rows(left_side, right_side):
    return lax.dot_general(
        left_side, right_side, (((0,), (0,)), ((), ())), preferred_element_type=jnp.float32
    )


def times_transpose(left_side, right_side):
    return lax.dot_general(
        left_side, right_side, (((1,), (1,)), ((), ())), preferred_element_type=jnp.float32
    )


def exact_transpose(left_side, weight_matrix):
    return lax.dot_general(
        left_side,
        weight_matrix.astype(jnp.float32),
        (((1,), (1,)), ((), ())),
        precision=lax.Precision.HIGHEST,
        preferred_element_type=jnp.float32,
    )


def exact_over_rows(left_side, right_side):
    return lax.dot_general(
        left_side.astype(jnp.float32),
        right_side,
        (((0,), (0,)), ((), ())),
        precision=lax.Precision.HIGHEST,
        preferred_element_type=jnp.float32,
    )


def one_hot_rows(row_ids, count):
    return (row_ids[:, None] == jnp.arange(count, dtype=jnp.int32)[None, :]).astype(jnp.bfloat16)


def each_block(adder, totals, active_count, total_rows):
    return adder(totals, 0, total_rows, active_count)


def sliced_rows(self_index, remote_index, leading_row, count_of_rows, active_count, slot_count):
    active_flags = (leading_row + jnp.arange(count_of_rows, dtype=jnp.int32) < active_count).astype(
        jnp.float32
    )[:, None]
    return (
        one_hot_rows(self_index, slot_count),
        one_hot_rows(remote_index, slot_count),
        active_flags,
    )


def contact_rows_of(bound_lat, far_lat, weights, self_table, remote_table):
    self_rows = product(self_table, bound_lat).astype(jnp.bfloat16)
    remote_rows = product(remote_table, far_lat).astype(jnp.bfloat16)
    contact_preactivation = product(self_rows, weights[3]) + product(remote_rows, weights[4])
    return (self_rows, remote_rows, contact_preactivation)


def forward_adder(bound_lat, far_lat, weights, self_index, remote_index):
    slot_count = bound_lat.shape[0]

    def adder(totals, leading_row, count_of_rows, active_count):
        self_table, remote_table, active_flags = sliced_rows(
            self_index, remote_index, leading_row, count_of_rows, active_count, slot_count
        )
        self_rows, remote_rows, contact_preactivation = contact_rows_of(
            bound_lat, far_lat, weights, self_table, remote_table
        )
        message_value = (jax.nn.silu(contact_preactivation) * active_flags).astype(jnp.bfloat16)
        return totals + over_rows(self_table, message_value)

    return adder


def backward_adder(bound_lat, far_lat, boundary_gradient, weights, self_index, remote_index):
    slot_count = bound_lat.shape[0]

    def adder(totals, leading_row, count_of_rows, active_count):
        self_table, remote_table, active_flags = sliced_rows(
            self_index, remote_index, leading_row, count_of_rows, active_count, slot_count
        )
        self_rows, remote_rows, contact_preactivation = contact_rows_of(
            bound_lat, far_lat, weights, self_table, remote_table
        )
        local_gradient = product(self_table, boundary_gradient)
        contact_gradient = (
            local_gradient * swish_gradient(contact_preactivation) * active_flags
        ).astype(jnp.bfloat16)
        grad_three, grad_four, sum_own, sum_far = totals
        return (
            grad_three + over_rows(self_rows, contact_gradient),
            grad_four + over_rows(remote_rows, contact_gradient),
            sum_own + over_rows(self_table, contact_gradient),
            over_rows(remote_table, contact_gradient),
        )

    return adder


def shards(
    latents, edge_feats, weights, cotangent, mesh_edges, boundary, contact_edges, contact_counts
):
    rows_dev = latents.shape[0]
    width = latents.shape[1]
    bound_count = boundary.shape[0]
    rounds = contact_counts.shape[1]
    round_rows = contact_edges.shape[1] // rounds
    live_counts = contact_counts[0]
    contacts = contact_edges.reshape(2, rounds, round_rows)
    senders = mesh_edges[0]
    receivers = mesh_edges[1]
    region_size = lax.axis_size("region")
    bound_table = one_hot_rows(boundary, rows_dev)
    bound_lat = product(bound_table, latents).astype(jnp.bfloat16)
    partners = [swapped(bound_lat, "region", round_lookup) for round_lookup in range(rounds)]
    extended = extended_2(latents, (("panel", 0),), HB)
    send_table = one_hot_rows(senders, rows_dev + 2 * HB)
    recv_table = one_hot_rows(receivers, rows_dev)
    send_rows = product(send_table, extended).astype(jnp.bfloat16)
    recv_rows = product(recv_table, latents).astype(jnp.bfloat16)
    pre_mesh = (
        product(send_rows, weights[0])
        + product(recv_rows, weights[1])
        + product(edge_feats, weights[2])
    )
    msg_mesh = jax.nn.silu(pre_mesh).astype(jnp.bfloat16)
    agg_mesh = over_rows(recv_table, msg_mesh).astype(jnp.bfloat16)
    agg_bound = jnp.zeros((bound_count, width), jnp.float32)
    for round_lookup in range(rounds):
        adder = forward_adder(
            bound_lat,
            partners[round_lookup],
            weights,
            contacts[0, round_lookup],
            contacts[1, round_lookup],
        )
        agg_bound = each_block(adder, agg_bound, live_counts[round_lookup], round_rows)
    agg_contact = over_rows(bound_table, agg_bound.astype(jnp.bfloat16)).astype(jnp.bfloat16)
    pre_node = (
        product(latents, weights[5])
        + product(agg_mesh, weights[6])
        + product(agg_contact, weights[7])
    )
    hidden = jax.nn.silu(pre_node).astype(jnp.bfloat16)
    new_rows = (latents.astype(jnp.float32) + product(hidden, weights[8])).astype(jnp.bfloat16)
    d_node = (times_transpose(cotangent, weights[8]) * swish_gradient(pre_node)).astype(
        jnp.bfloat16
    )
    d_agg_mesh = times_transpose(d_node, weights[6]).astype(jnp.bfloat16)
    d_agg_contact = times_transpose(d_node, weights[7]).astype(jnp.bfloat16)
    d_mesh = (product(recv_table, d_agg_mesh) * swish_gradient(pre_mesh)).astype(jnp.bfloat16)
    d_extended = exact_transpose(over_rows(send_table, d_mesh), weights[0])
    from_prev = shifted(d_extended[HB + rows_dev :].astype(jnp.bfloat16), "panel", 1).astype(
        jnp.float32
    )
    from_next = shifted(d_extended[:HB].astype(jnp.bfloat16), "panel", -1).astype(jnp.float32)
    grad_rows = cotangent.astype(jnp.float32) + times_transpose(d_node, weights[5])
    grad_rows = grad_rows + exact_transpose(over_rows(recv_table, d_mesh), weights[1])
    grad_rows = grad_rows + d_extended[HB : HB + rows_dev]
    boundary_gradient = product(bound_table, d_agg_contact).astype(jnp.bfloat16)
    grad_three = jnp.zeros((width, width), jnp.float32)
    grad_four = jnp.zeros((width, width), jnp.float32)
    sum_own = jnp.zeros((bound_count, width), jnp.float32)
    far_grads = []
    for round_lookup in range(rounds):
        adder = backward_adder(
            bound_lat,
            partners[round_lookup],
            boundary_gradient,
            weights,
            contacts[0, round_lookup],
            contacts[1, round_lookup],
        )
        totals = (grad_three, grad_four, sum_own, jnp.zeros((bound_count, width), jnp.float32))
        grad_three, grad_four, sum_own, sum_far = each_block(
            adder, totals, live_counts[round_lookup], round_rows
        )
        far_grads.append(exact_transpose(sum_far, weights[4]))
    grad_own = exact_transpose(sum_own, weights[3])
    incoming = jnp.zeros((bound_count, width), jnp.float32)
    for round_lookup in range(rounds):
        incoming = incoming + swapped(
            far_grads[round_lookup].astype(jnp.bfloat16), "region", round_lookup
        ).astype(jnp.float32)
    grad_rows = grad_rows.at[:HB].add(from_prev)
    grad_rows = grad_rows.at[rows_dev - HB :].add(from_next)
    grad_rows = grad_rows + exact_over_rows(bound_table, grad_own + incoming)
    grads = jnp.stack(
        [
            over_rows(send_rows, d_mesh),
            over_rows(recv_rows, d_mesh),
            over_rows(edge_feats, d_mesh),
            grad_three,
            grad_four,
            over_rows(latents, d_node),
            over_rows(agg_mesh, d_node),
            over_rows(agg_contact, d_node),
            over_rows(hidden, cotangent),
        ]
    )
    summed = lax.psum(grads, ("region", "panel"))
    grad_scale = 1.0 / math.sqrt(rows_dev * region_size * lax.axis_size("panel"))
    return (new_rows, grad_rows, summed * grad_scale)


def solution(mesh):
    placed = (
        P(("region", "panel"), None),
        P(("region", "panel"), None),
        P(),
        P(("region", "panel"), None),
        P(None, ("region", "panel")),
        P(("region", "panel")),
        P(None, ("region", "panel")),
        P(("region", "panel"), None),
    )
    return jax.shard_map(
        shards,
        mesh=mesh,
        in_specs=placed,
        out_specs=(P(("region", "panel"), None), P(("region", "panel"), None), P()),
        check_vma=False,
    )
```

profile of v0, /device:TPU:1, one launch (start us, length us, event | category | flops | bytes accessed | tf_op | source)
XLA Modules:
  0.0 391.0 jit_solution(8464089230130186467)
XLA Ops:
  7.2 2.0 convolution_convert_fusion.11
  9.3 7.7 %collective-permute-start.5 = (bf16[256,128]{1,0:T(8,128)(2,1)}, bf16[256,128]{1,0:T(8,128)(2,1)}, u32[]{:S(2)}, u32[]{:S(2)}) collective-permute-start(bf16[256,128]{1,0:T(8,128)(2,1)} %convolution_convert_fusion.11), channel_id=1, source_target_pairs={{0,64},{64,0},{8,72},{72,8},{16,80},{80,16},{24,88},{88,24},{32,96... | collective-permute-start | bytes 196616 | tf_op jit(solution)/shard_map/ppermute | solution.py:18
  17.0 1.2 collective-permute-start.4
  18.2 0.7 collective-permute-start.3
  19.0 0.7 fusion.180
  19.7 3.2 collective-permute-start
  22.9 1.3 collective-permute-start.1
  24.2 0.9 reshape.97
  25.3 1.4 convolution_convert_fusion.1
  28.4 1.3 convolution_convert_fusion.3
  30.7 1.3 convolution_convert_fusion.5
  33.1 1.3 convolution_convert_fusion.7
  34.8 2.5 fusion.14
  38.0 1.9 collective-permute-start.2
  40.5 4.0 %fusion.15 = bf16[3072,128]{1,0:T(8,128)(2,1)S(1)} fusion(s32[3072]{0:T(1024)S(1)} %bitcast.201, bf16[64,128]{1,0:T(8,128)(2,1)} %copy-done.67, bf16[1024,128]{1,0:T(8,128)(2,1)S(1)} %copy-done.26, bf16[64,128]{1,0:T(8,128)(2,1)S(1)} %collective-permute-done), kind=kOutput, calls=%fused_computation.19 | convolution fusion | flops 910786560 | bytes 1093632 | tf_op jit(solution)/shard_map/dot_general | solution.py:46
  45.6 3.9 %fusion.39 = bf16[1024,128]{1,0:T(8,128)(2,1)S(1)} fusion(s32[3072]{0:T(1024)S(1)} %bitcast.198, f32[3072,128]{1,0:T(8,128)S(1)} %convolution_add_fusion), kind=kOutput, calls=%fused_computation.76 | convolution fusion | flops 810549248 | bytes 1847296 | tf_op jit(solution)/shard_map/dot_general | solution.py:50
  49.5 1.0 convolution_add_fusion.9
  50.5 1.3 convolution_convert_fusion
  52.2 2.0 fusion.26
  54.2 1.3 convolution_convert_fusion.2
  55.9 2.0 fusion.29
  57.9 1.3 convolution_convert_fusion.4
  59.6 2.0 fusion.32
  62.2 1.3 convolution_add_fusion.5
  63.4 16.7 %convolution_convert_fusion.10 = bf16[1024,128]{1,0:T(8,128)(2,1)} fusion(f32[256,128]{1,0:T(8,128)} %fusion.26, f32[256,128]{1,0:T(8,128)} %fusion.29, f32[256,128]{1,0:T(8,128)} %fusion.32, s32[2048]{0:T(1024)S(1)} %bitcast.204, s32[256]{0:T(256)S(1)} %copy-done.66, f32[2048,128]{1,0:T(8,128)} %convolution_add_fusion.5, f32[2048]{0:T(1024)S(1)} %fusion.160), kind=kOutput, calls=%fused_computation.79 | convolution fusion | flops 203948032 | bytes 1721344 | tf_op jit(solution)/shard_map/dot_general | solution.py:50
  80.2 1.3 convolution_add_fusion.8
  81.5 0.8 copy-done.38
  82.3 1.2 fusion.38
  83.6 1.3 fusion.48
  84.9 2.0 fusion.20
  87.0 1.6 fusion.21
  88.7 1.6 fusion.22
  91.0 4.2 %fusion.13 = bf16[3072,128]{1,0:T(8,128)(2,1)S(1)} fusion(s32[3072]{0:T(1024)S(1)} %bitcast.199, f32[3072,128]{1,0:T(8,128)} %copy-done.24, bf16[1024,128]{1,0:T(8,128)(2,1)S(1)} %fusion.38, bf16[9,128,128]{2,1,0:T(8,128)(2,1)} %param.14), kind=kOutput, calls=%fused_computation.17 | convolution fusion | flops 845676544 | bytes 2666496 | tf_op jit(solution)/shard_map/dot_general | solution.py:46
  95.2 2.1 fusion.23
  97.3 1.0 fusion.51
  98.4 5.2 %fusion = f32[1152,128]{1,0:T(8,128)} fusion(bf16[3072,128]{1,0:T(8,128)(2,1)S(1)} %fusion.13, s32[3072]{0:T(1024)S(1)} %bitcast.202), kind=kOutput, calls=%fused_computation.1 | convolution fusion | flops 909508608 | bytes 1388544 | tf_op jit(solution)/shard_map/dot_general | solution.py:50
  103.6 4.7 %fusion.2 = f32[1024,128]{1,0:T(8,128)} fusion(bf16[3072,128]{1,0:T(8,128)(2,1)S(1)} %fusion.13, s32[3072]{0:T(1024)S(1)} %bitcast.200), kind=kOutput, calls=%fused_computation.4 | convolution fusion | flops 808452096 | bytes 1323008 | tf_op jit(solution)/shard_map/dot_general | solution.py:50
  108.3 1.8 convolution_add_fusion.6
  110.1 1.7 fusion.28
  111.8 1.7 fusion.27
  113.5 1.7 fusion.25
  115.2 1.9 fusion.24
  117.1 1.7 fusion.33
  118.8 1.7 fusion.31
  120.6 1.7 fusion.30
  122.3 1.8 fusion.37
  125.9 1.0 fusion.50
  126.9 1.0 fusion.49
  127.9 1.0 fusion.55
  128.9 1.0 fusion.53
  129.9 0.9 fusion.59
  130.8 0.9 fusion.58
  131.7 0.9 fusion.57
  132.6 1.0 fusion.56
  133.7 1.0 fusion.46
  135.5 4.4 %collective-permute-start.6 = (bf16[64,128]{1,0:T(8,128)(2,1)S(1)}, bf16[64,128]{1,0:T(8,128)(2,1)S(1)}, u32[]{:S(2)}, u32[]{:S(2)}) collective-permute-start(bf16[64,128]{1,0:T(8,128)(2,1)S(1)} %get-tuple-element.28), channel_id=1, source_target_pairs={{0,1},{1,2},{2,3},{3,4},{4,5},{5,6},{6,7},{8,9},{9,10},{10,11},{11... | collective-permute-start | bytes 49160 | tf_op jit(solution)/shard_map/ppermute | solution.py:37
  139.9 1.3 collective-permute-start.7
  141.4 1.3 collective-permute-start.10
  144.6 0.8 collective-permute-start.9
  145.5 3.6 collective-permute-done.10
  149.1 2.4 collective-permute-done.11
  151.5 1.9 convolution_add_fusion.10
  153.4 228.5 %all-reduce.2.cloned.1.call-done = f32[9,128,128]{2,1,0:T(8,128)} async-done(((f32[9,128,128]{2,1,0:T(8,128)}), f32[9,128,128]{2,1,0:T(8,128)}) %all-reduce.2.cloned.1.call-update) | async-done | bytes 589840 | tf_op jit(solution)/shard_map/psum | solution.py:249
  381.8 1.9 broadcast_multiply_fusion
  (192 shorter events, 13.2 us)
Async XLA Ops:
  7.2 38.0 %copy-start = (bf16[3072,128]{1,0:T(8,128)(2,1)S(1)}, bf16[3072,128]{1,0:T(8,128)(2,1)}, u32[]{:S(2)}) copy-start(bf16[3072,128]{1,0:T(8,128)(2,1)} %param.13) | copy-start | bytes 2359300
  7.2 19.4 %copy-start.25 = (bf16[1024,128]{1,0:T(8,128)(2,1)S(1)}, bf16[1024,128]{1,0:T(8,128)(2,1)}, u32[]{:S(2)}) copy-start(bf16[1024,128]{1,0:T(8,128)(2,1)} %param.12) | copy-start | bytes 786436
  7.2 19.4 %copy-start.21 = (bf16[9,128,128]{2,1,0:T(8,128)(2,1)S(1)}, bf16[9,128,128]{2,1,0:T(8,128)(2,1)}, u32[]{:S(2)}) copy-start(bf16[9,128,128]{2,1,0:T(8,128)(2,1)} %param.14) | copy-start | bytes 884740
  7.2 374.6 %all-reduce.2.cloned.1.call-start = ((), (), s32[]{:S(2)}) async-start(), calls=%async_computation | async-start | bytes 1179648 | tf_op jit(solution)/shard_map/psum | solution.py:249
  9.3 41.2 %collective-permute-start.5 = (bf16[256,128]{1,0:T(8,128)(2,1)}, bf16[256,128]{1,0:T(8,128)(2,1)}, u32[]{:S(2)}, u32[]{:S(2)}) collective-permute-start(bf16[256,128]{1,0:T(8,128)(2,1)} %convolution_convert_fusion.11), channel_id=1, source_target_pairs={{0,64},{64,0},{8,72},{72,8},{16,80},{80,16},{24,88},{88,24},{32,96... | collective-permute-start | bytes 196616 | tf_op jit(solution)/shard_map/ppermute | solution.py:18
  17.0 37.2 %collective-permute-start.4 = (bf16[256,128]{1,0:T(8,128)(2,1)}, bf16[256,128]{1,0:T(8,128)(2,1)}, u32[]{:S(2)}, u32[]{:S(2)}) collective-permute-start(bf16[256,128]{1,0:T(8,128)(2,1)} %convolution_convert_fusion.11), channel_id=1, source_target_pairs={{0,32},{32,0},{8,40},{40,8},{16,48},{48,16},{24,56},{56,24},{64,96... | collective-permute-start | bytes 196616 | tf_op jit(solution)/shard_map/ppermute | solution.py:18
  18.2 39.7 %collective-permute-start.3 = (bf16[256,128]{1,0:T(8,128)(2,1)}, bf16[256,128]{1,0:T(8,128)(2,1)}, u32[]{:S(2)}, u32[]{:S(2)}) collective-permute-start(bf16[256,128]{1,0:T(8,128)(2,1)} %convolution_convert_fusion.11), channel_id=1, source_target_pairs={{0,16},{16,0},{8,24},{24,8},{32,48},{48,32},{40,56},{56,40},{64,80... | collective-permute-start | bytes 196616 | tf_op jit(solution)/shard_map/ppermute | solution.py:18
  19.7 18.3 %collective-permute-start = (bf16[64,128]{1,0:T(8,128)(2,1)S(1)}, bf16[64,128]{1,0:T(8,128)(2,1)S(1)}, u32[]{:S(2)}, u32[]{:S(2)}) collective-permute-start(bf16[64,128]{1,0:T(8,128)(2,1)S(1)} %get-tuple-element.29), channel_id=1, source_target_pairs={{0,1},{1,2},{2,3},{3,4},{4,5},{5,6},{6,7},{8,9},{9,10},{10,11},{11... | collective-permute-start | bytes 49160 | tf_op jit(solution)/shard_map/ppermute | solution.py:28
  22.9 17.0 %collective-permute-start.1 = (bf16[64,128]{1,0:T(8,128)(2,1)S(1)}, bf16[64,128]{1,0:T(8,128)(2,1)S(1)}, u32[]{:S(2)}, u32[]{:S(2)}) collective-permute-start(bf16[64,128]{1,0:T(8,128)(2,1)S(1)} %get-tuple-element.30), channel_id=1, source_target_pairs={{1,0},{2,1},{3,2},{4,3},{5,4},{6,5},{7,6},{9,8},{10,9},{11,10},{12... | collective-permute-start | bytes 49160 | tf_op jit(solution)/shard_map/ppermute | solution.py:29
  25.2 25.3 %copy-start.56 = (s32[1,1,2048]{2,1,0:T(1,128)}, s32[1,1,2048]{2,1,0:T(1,128)S(1)}, u32[]{:S(2)}) copy-start(s32[1,1,2048]{2,1,0:T(1,128)S(1)} %get-tuple-element.32) | copy-start | bytes 24580
  25.2 27.0 %copy-start.58 = (s32[1,1,2048]{2,1,0:T(1,128)}, s32[1,1,2048]{2,1,0:T(1,128)S(1)}, u32[]{:S(2)}) copy-start(s32[1,1,2048]{2,1,0:T(1,128)S(1)} %get-tuple-element.33) | copy-start | bytes 24580
  25.2 29.0 %copy-start.60 = (s32[1,1,2048]{2,1,0:T(1,128)}, s32[1,1,2048]{2,1,0:T(1,128)S(1)}, u32[]{:S(2)}) copy-start(s32[1,1,2048]{2,1,0:T(1,128)S(1)} %get-tuple-element.34) | copy-start | bytes 24580
  25.2 32.7 %copy-start.50 = (s32[1,1,2048]{2,1,0:T(1,128)}, s32[1,1,2048]{2,1,0:T(1,128)S(1)}, u32[]{:S(2)}) copy-start(s32[1,1,2048]{2,1,0:T(1,128)S(1)} %get-tuple-element.36) | copy-start | bytes 24580
  25.2 36.4 %copy-start.54 = (s32[1,1,2048]{2,1,0:T(1,128)}, s32[1,1,2048]{2,1,0:T(1,128)S(1)}, u32[]{:S(2)}) copy-start(s32[1,1,2048]{2,1,0:T(1,128)S(1)} %get-tuple-element.31) | copy-start | bytes 24580
  25.2 59.7 %copy-start.48 = (s32[1,1,2048]{2,1,0:T(1,128)}, s32[1,1,2048]{2,1,0:T(1,128)S(1)}, u32[]{:S(2)}) copy-start(s32[1,1,2048]{2,1,0:T(1,128)S(1)} %get-tuple-element.38) | copy-start | bytes 24580
  25.2 61.7 %copy-start.52 = (s32[1,1,2048]{2,1,0:T(1,128)}, s32[1,1,2048]{2,1,0:T(1,128)S(1)}, u32[]{:S(2)}) copy-start(s32[1,1,2048]{2,1,0:T(1,128)S(1)} %get-tuple-element.37) | copy-start | bytes 24580
  25.2 63.4 %copy-start.62 = (s32[1,1,2048]{2,1,0:T(1,128)}, s32[1,1,2048]{2,1,0:T(1,128)S(1)}, u32[]{:S(2)}) copy-start(s32[1,1,2048]{2,1,0:T(1,128)S(1)} %get-tuple-element.35) | copy-start | bytes 24580
  26.6 3.1 copy-start.1
  28.4 23.8 %copy-start.64 = (f32[2048]{0:T(1024)}, f32[2048]{0:T(1024)S(1)}, u32[]{:S(2)}) copy-start(f32[2048]{0:T(1024)S(1)} %fusion.163) | copy-start | bytes 24580
  29.8 2.6 copy-start.3
  32.1 2.6 copy-start.5
  32.4 2.3 copy-start.45
  34.7 5.7 %copy-start.46 = (s32[1,3072]{1,0:T(1,128)}, s32[1,3072]{1,0:T(1,128)S(1)}, u32[]{:S(2)}) copy-start(s32[1,3072]{1,0:T(1,128)S(1)} %get-tuple-element.39) | copy-start | bytes 36868
  34.8 5.7 %copy-start.26 = (bf16[1024,128]{1,0:T(8,128)(2,1)S(1)}, bf16[1024,128]{1,0:T(8,128)(2,1)}, u32[]{:S(2)}) copy-start(bf16[1024,128]{1,0:T(8,128)(2,1)} %param.12) | copy-start | bytes 786436
  38.0 23.6 %collective-permute-start.2 = (bf16[256,128]{1,0:T(8,128)(2,1)}, bf16[256,128]{1,0:T(8,128)(2,1)S(1)}, u32[]{:S(2)}, u32[]{:S(2)}) collective-permute-start(bf16[256,128]{1,0:T(8,128)(2,1)} %convolution_convert_fusion.11), channel_id=1, source_target_pairs={{0,8},{8,0},{16,24},{24,16},{32,40},{40,32},{48,56},{56,48},{64,72... | collective-permute-start | bytes 196616 | tf_op jit(solution)/shard_map/ppermute | solution.py:18
  40.5 4.0 %copy-start.22 = (bf16[9,128,128]{2,1,0:T(8,128)(2,1)S(1)}, bf16[9,128,128]{2,1,0:T(8,128)(2,1)}, u32[]{:S(2)}) copy-start(bf16[9,128,128]{2,1,0:T(8,128)(2,1)} %param.14) | copy-start | bytes 884740
  45.5 3.9 %copy-start.24 = (f32[3072,128]{1,0:T(8,128)}, f32[3072,128]{1,0:T(8,128)S(1)}, u32[]{:S(2)}) copy-start(f32[3072,128]{1,0:T(8,128)S(1)} %convolution_add_fusion) | copy-start | bytes 4718596
  49.5 2.7 copy-start.28
  51.9 2.3 copy-start.13
  55.6 2.3 copy-start.15
  59.3 2.3 copy-start.17
  62.2 18.0 %copy-start.19 = (bf16[2048,128]{1,0:T(8,128)(2,1)}, bf16[2048,128]{1,0:T(8,128)(2,1)S(1)}, u32[]{:S(2)}) copy-start(bf16[2048,128]{1,0:T(8,128)(2,1)S(1)} %convolution_convert_fusion.6) | copy-start | bytes 1572868
  84.9 3.7 copy-start.71
  84.9 2.1 copy-start.35
  87.0 3.6 copy-start.7
  103.6 4.7 %copy-start.40 = (bf16[1024,128]{1,0:T(8,128)(2,1)S(1)}, bf16[1024,128]{1,0:T(8,128)(2,1)}, u32[]{:S(2)}) copy-start(bf16[1024,128]{1,0:T(8,128)(2,1)} %param.15) | copy-start | bytes 786436
  103.6 6.5 %copy-start.10 = (bf16[2048,128]{1,0:T(8,128)(2,1)S(1)}, bf16[2048,128]{1,0:T(8,128)(2,1)}, u32[]{:S(2)}) copy-start(bf16[2048,128]{1,0:T(8,128)(2,1)} %fusion.22) | copy-start | bytes 1572868
  103.6 6.5 %copy-start.63 = (s32[1,1,2048]{2,1,0:T(1,128)S(1)}, s32[1,1,2048]{2,1,0:T(1,128)}, u32[]{:S(2)}) copy-start(s32[1,1,2048]{2,1,0:T(1,128)} %copy-done.62) | copy-start | bytes 24580
  108.3 3.5 copy-start.61
  108.3 5.2 %copy-start.59 = (s32[1,1,2048]{2,1,0:T(1,128)S(1)}, s32[1,1,2048]{2,1,0:T(1,128)}, u32[]{:S(2)}) copy-start(s32[1,1,2048]{2,1,0:T(1,128)} %copy-done.58) | copy-start | bytes 24580
  110.1 5.1 %copy-start.57 = (s32[1,1,2048]{2,1,0:T(1,128)S(1)}, s32[1,1,2048]{2,1,0:T(1,128)}, u32[]{:S(2)}) copy-start(s32[1,1,2048]{2,1,0:T(1,128)} %copy-done.56) | copy-start | bytes 24580
  111.8 5.3 %copy-start.8 = (bf16[2048,128]{1,0:T(8,128)(2,1)S(1)}, bf16[2048,128]{1,0:T(8,128)(2,1)}, u32[]{:S(2)}) copy-start(bf16[2048,128]{1,0:T(8,128)(2,1)} %copy-done.7) | copy-start | bytes 1572868
  111.8 5.3 %copy-start.55 = (s32[1,1,2048]{2,1,0:T(1,128)S(1)}, s32[1,1,2048]{2,1,0:T(1,128)}, u32[]{:S(2)}) copy-start(s32[1,1,2048]{2,1,0:T(1,128)} %copy-done.54) | copy-start | bytes 24580
  113.5 5.3 %copy-start.11 = (bf16[2048,128]{1,0:T(8,128)(2,1)S(1)}, bf16[2048,128]{1,0:T(8,128)(2,1)}, u32[]{:S(2)}) copy-start(bf16[2048,128]{1,0:T(8,128)(2,1)} %fusion.21) | copy-start | bytes 1572868
  113.5 5.3 %copy-start.53 = (s32[1,1,2048]{2,1,0:T(1,128)S(1)}, s32[1,1,2048]{2,1,0:T(1,128)}, u32[]{:S(2)}) copy-start(s32[1,1,2048]{2,1,0:T(1,128)} %copy-done.52) | copy-start | bytes 24580
  115.2 5.3 %copy-start.51 = (s32[1,1,2048]{2,1,0:T(1,128)S(1)}, s32[1,1,2048]{2,1,0:T(1,128)}, u32[]{:S(2)}) copy-start(s32[1,1,2048]{2,1,0:T(1,128)} %copy-done.50) | copy-start | bytes 24580
  117.1 5.1 %copy-start.27 = (bf16[1024,128]{1,0:T(8,128)(2,1)S(1)}, bf16[1024,128]{1,0:T(8,128)(2,1)}, u32[]{:S(2)}) copy-start(bf16[1024,128]{1,0:T(8,128)(2,1)} %param.12) | copy-start | bytes 786436
  117.1 5.1 %copy-start.39 = (f32[1024,128]{1,0:T(8,128)S(1)}, f32[1024,128]{1,0:T(8,128)}, u32[]{:S(2)}) copy-start(f32[1024,128]{1,0:T(8,128)} %copy-done.38) | copy-start | bytes 1572868
  122.3 2.2 copy-start.16
  125.8 2.1 copy-start.2
  127.9 2.8 copy-start.29
  127.9 3.7 copy-start.30
  133.7 7.5 %copy-start.44 = (f32[256,128]{1,0:T(8,128)S(1)}, f32[256,128]{1,0:T(8,128)}, u32[]{:S(2)}) copy-start(f32[256,128]{1,0:T(8,128)} %fusion.27) | copy-start | bytes 393220
  133.7 9.0 %copy-start.43 = (f32[256,128]{1,0:T(8,128)S(1)}, f32[256,128]{1,0:T(8,128)}, u32[]{:S(2)}) copy-start(f32[256,128]{1,0:T(8,128)} %fusion.24) | copy-start | bytes 393220
  133.7 9.3 %copy-start.42 = (f32[256,128]{1,0:T(8,128)S(1)}, f32[256,128]{1,0:T(8,128)}, u32[]{:S(2)}) copy-start(f32[256,128]{1,0:T(8,128)} %fusion.33) | copy-start | bytes 393220
  134.8 9.2 %copy-start.12 = (f32[1024,128]{1,0:T(8,128)S(1)}, f32[1024,128]{1,0:T(8,128)}, u32[]{:S(2)}) copy-start(f32[1024,128]{1,0:T(8,128)} %convolution_add_fusion.6) | copy-start | bytes 1572868
  134.8 9.2 %copy-start.37 = (f32[1024,128]{1,0:T(8,128)S(1)}, f32[1024,128]{1,0:T(8,128)}, u32[]{:S(2)}) copy-start(f32[1024,128]{1,0:T(8,128)} %fusion.2) | copy-start | bytes 1572868
  135.5 8.9 %copy-start.41 = (f32[256,128]{1,0:T(8,128)S(1)}, f32[256,128]{1,0:T(8,128)}, u32[]{:S(2)}) copy-start(f32[256,128]{1,0:T(8,128)} %fusion.30) | copy-start | bytes 393220
  135.5 9.1 %collective-permute-start.6 = (bf16[64,128]{1,0:T(8,128)(2,1)S(1)}, bf16[64,128]{1,0:T(8,128)(2,1)S(1)}, u32[]{:S(2)}, u32[]{:S(2)}) collective-permute-start(bf16[64,128]{1,0:T(8,128)(2,1)S(1)} %get-tuple-element.28), channel_id=1, source_target_pairs={{0,1},{1,2},{2,3},{3,4},{4,5},{5,6},{6,7},{8,9},{9,10},{10,11},{11... | collective-permute-start | bytes 49160 | tf_op jit(solution)/shard_map/ppermute | solution.py:37
  139.9 5.5 %collective-permute-start.7 = (bf16[64,128]{1,0:T(8,128)(2,1)S(1)}, bf16[64,128]{1,0:T(8,128)(2,1)S(1)}, u32[]{:S(2)}, u32[]{:S(2)}) collective-permute-start(bf16[64,128]{1,0:T(8,128)(2,1)S(1)} %get-tuple-element.27), channel_id=1, source_target_pairs={{1,0},{2,1},{3,2},{4,3},{5,4},{6,5},{7,6},{9,8},{10,9},{11,10},{12... | collective-permute-start | bytes 49160 | tf_op jit(solution)/shard_map/ppermute | solution.py:37
  141.4 7.6 %collective-permute-start.10 = (bf16[256,128]{1,0:T(8,128)(2,1)S(1)}, bf16[256,128]{1,0:T(8,128)(2,1)S(1)}, u32[]{:S(2)}, u32[]{:S(2)}) collective-permute-start(bf16[256,128]{1,0:T(8,128)(2,1)S(1)} %convolution_convert_fusion.13), channel_id=1, source_target_pairs={{0,32},{32,0},{8,40},{40,8},{16,48},{48,16},{24,56},{56,24},{64,96... | collective-permute-start | bytes 196616 | tf_op jit(solution)/shard_map/ppermute | solution.py:18
  142.9 8.5 %collective-permute-start.11 = (bf16[256,128]{1,0:T(8,128)(2,1)S(1)}, bf16[256,128]{1,0:T(8,128)(2,1)S(1)}, u32[]{:S(2)}, u32[]{:S(2)}) collective-permute-start(bf16[256,128]{1,0:T(8,128)(2,1)S(1)} %convolution_convert_fusion.12), channel_id=1, source_target_pairs={{0,64},{64,0},{8,72},{72,8},{16,80},{80,16},{24,88},{88,24},{32,96... | collective-permute-start | bytes 196616 | tf_op jit(solution)/shard_map/ppermute | solution.py:18
  143.3 8.2 %collective-permute-start.8 = (bf16[256,128]{1,0:T(8,128)(2,1)S(1)}, bf16[256,128]{1,0:T(8,128)(2,1)S(1)}, u32[]{:S(2)}, u32[]{:S(2)}) collective-permute-start(bf16[256,128]{1,0:T(8,128)(2,1)S(1)} %convolution_convert_fusion.15), channel_id=1, source_target_pairs={{0,8},{8,0},{16,24},{24,16},{32,40},{40,32},{48,56},{56,48},{64,72... | collective-permute-start | bytes 196616 | tf_op jit(solution)/shard_map/ppermute | solution.py:18
  144.6 6.8 %collective-permute-start.9 = (bf16[256,128]{1,0:T(8,128)(2,1)S(1)}, bf16[256,128]{1,0:T(8,128)(2,1)S(1)}, u32[]{:S(2)}, u32[]{:S(2)}) collective-permute-start(bf16[256,128]{1,0:T(8,128)(2,1)S(1)} %convolution_convert_fusion.14), channel_id=1, source_target_pairs={{0,16},{16,0},{8,24},{24,8},{32,48},{48,32},{40,56},{56,40},{64,80... | collective-permute-start | bytes 196616 | tf_op jit(solution)/shard_map/ppermute | solution.py:18
  (21 other events, 29.9 us)
Sparse Core Ops, SparseCore 0:
  133.7 248.0 all-reduce.1
where the time goes:
time: 398 us; the launch traced here: 391 us
  waiting for transfers between devices  235 us (59%)
  matrix products  107 us (27%)
  starting transfers between devices  24.6 us (6%)
  between operations  15.4 us (4%)
  other arithmetic  4.51 us (1%)
  local copies, waits for them, and re-layouts  4.5 us (1%)
    psum x1, waiting for transfers between devices, shards(): summed = lax.psum(grads, ('region', 'panel'))  228 us
    dot_general x30, matrix products, over_rows(): lax.dot_general(left_side, right_side, (((0,), (0,)), ((), ())), preferre...  60.5 us
    dot_general x32, matrix products, product(): return jnp.dot(left_side, right_side, preferred_element_type=jnp.float32)  40.1 us
    ppermute x8, starting transfers between devices, swapped(): return lax.ppermute(block, axis, route)  14.4 us
  transfers between devices with their start and end apart: 13, of which 3 were waited for; matrix products, arithmetic and copies ran while one was open for 10% of the time, Pallas kernels for 0%

commit v1 on v0

v1 whole, which is shorter than its diff:
```python
import functools
import math

import jax
import jax.numpy as jnp
from jax import lax
from jax.experimental import pallas as pl
from jax.experimental.pallas import tpu as pltpu
from jax.sharding import PartitionSpec as P

HB = 64
CHUNK = 512
BF = jnp.bfloat16
F32 = jnp.float32
VMEM_BYTES = 56 * 1024 * 1024


def nn(a, b):
    return lax.dot_general(a, b, (((1,), (0,)), ((), ())), preferred_element_type=F32)


def nt(a, b):
    return lax.dot_general(a, b, (((1,), (1,)), ((), ())), preferred_element_type=F32)


def tn(a, b):
    return lax.dot_general(a, b, (((0,), (0,)), ((), ())), preferred_element_type=F32)


def in_two(values):
    high = values.astype(BF)
    return high, (values - high.astype(F32)).astype(BF)


def wide_nt(a, b):
    high, low = in_two(a)
    return nt(high, b) + nt(low, b)


def wide_nn(a, b):
    high, low = in_two(b)
    return nn(a, high) + nn(a, low)


def identity():
    row = lax.broadcasted_iota(jnp.int32, (128, 128), 0)
    column = lax.broadcasted_iota(jnp.int32, (128, 128), 1)
    return (row == column).astype(BF)


def transposed(a):
    return nt(identity(), a).astype(BF)


def table(count, ids):
    rows = lax.broadcasted_iota(jnp.int32, (count, ids.shape[1]), 0)
    return (rows == ids).astype(BF)


def rim_table(rows_dev, ids):
    rows = lax.broadcasted_iota(jnp.int32, (2 * HB, ids.shape[1]), 0)
    rows = jnp.where(rows < HB, rows, rows + rows_dev)
    return (rows == ids).astype(BF)


def silu_parts(x):
    s = 0.5 * jnp.tanh(0.5 * x) + 0.5
    return x * s, s * (1.0 + x * (1.0 - s))


def columns(step):
    return pl.ds(pl.multiple_of(step * CHUNK, CHUNK), CHUNK)


def bound_kernel(lat_ref, bnd_ref, lat_t_ref, bound_t_ref):
    lat_t = transposed(lat_ref[...])
    lat_t_ref[...] = lat_t
    bound_t_ref[...] = nn(lat_t, table(lat_ref.shape[0], bnd_ref[...])).astype(BF)


def local_kernel(lat_t_ref, bound_t_ref, edges_ref, contacts_ref, rows_ref, own_ref):
    rows_dev = lat_t_ref.shape[1]

    @pl.loop(0, edges_ref.shape[1] // CHUNK)
    def _(step):
        at = columns(step)
        lat_t = lat_t_ref[...]
        rows_ref[:128, at] = nn(lat_t, table(rows_dev, edges_ref[0:1, at] - HB)).astype(BF)
        rows_ref[128:, at] = nn(lat_t, table(rows_dev, edges_ref[1:2, at])).astype(BF)

    @pl.loop(0, contacts_ref.shape[1] // CHUNK)
    def _(step):
        at = columns(step)
        bound_t = bound_t_ref[...]
        own_ref[:, at] = nn(bound_t, table(bound_t.shape[1], contacts_ref[0:1, at])).astype(BF)


def main_kernel(
    counts_ref,
    core_ref,
    lat_ref,
    lat_t_ref,
    rim_ref,
    far0_ref,
    far1_ref,
    far2_ref,
    far3_ref,
    rows_in_ref,
    own_ref,
    feats_ref,
    cot_ref,
    w_ref,
    edges_ref,
    contacts_ref,
    bnd_ref,
    new_ref,
    kept_ref,
    sent_ref,
    dm_ref,
    dc_ref,
    base_ref,
    agg_ref,
    aggb_ref,
    slope_m_ref,
    slope_c_ref,
    rows_ref,
    both_ref,
    gw_ref,
    wt_ref,
    aggc_ref,
    dagg_t_ref,
    daggc_t_ref,
    dbg_t_ref,
    *,
    scale,
):
    rows_dev = lat_ref.shape[0]
    bound_count = bnd_ref.shape[1]
    fars = (far0_ref, far1_ref, far2_ref, far3_ref)
    rounds = len(fars)
    round_rows = contacts_ref.shape[1] // rounds
    per_round = round_rows // CHUNK
    steps = edges_ref.shape[1] // CHUNK

    agg_ref[...] = jnp.zeros_like(agg_ref)
    aggb_ref[...] = jnp.zeros_like(aggb_ref)
    gw_ref[...] = jnp.zeros_like(gw_ref)
    wt_ref[0:128, 0:128] = transposed(w_ref[0])
    wt_ref[0:128, 128:256] = transposed(w_ref[1])
    wt_ref[128:256, 0:128] = transposed(w_ref[3])
    wt_ref[128:256, 128:256] = transposed(w_ref[4])
    w2_t = transposed(w_ref[2])
    rim_t = transposed(rim_ref[...])

    @pl.loop(0, steps)
    def _(step):
        at = columns(step)
        from_rim = nn(rim_t, rim_table(rows_dev, edges_ref[0:1, at]))
        rows_ref[:128, at] = (rows_in_ref[:128, at].astype(F32) + from_rim).astype(BF)
        rows_ref[128:, at] = rows_in_ref[128:, at]
        x = nn(wt_ref[0:128, :], rows_ref[:, at]) + nt(w2_t, feats_ref[at, :])
        message, slope = silu_parts(x)
        slope_m_ref[:, at] = slope
        agg_ref[...] += nt(table(rows_dev, edges_ref[1:2, at]), message.astype(BF))

    for r in range(rounds):
        far_ref = fars[r]
        count = counts_ref[0, r]

        @pl.loop(0, per_round)
        def _(part):
            @pl.when(part * CHUNK < count)
            def _():
                at = columns(r * per_round + part)
                place = lax.broadcasted_iota(jnp.int32, (1, CHUNK), 1) + part * CHUNK
                live = (place < count).astype(F32)
                both_ref[:128, at] = own_ref[:, at]
                both_ref[128:, at] = nn(
                    far_ref[...], table(bound_count, contacts_ref[1:2, at])
                ).astype(BF)
                x = nn(wt_ref[128:256, :], both_ref[:, at])
                message, slope = silu_parts(x)
                slope_c_ref[:, at] = slope * live
                aggb_ref[...] += nt(
                    table(bound_count, contacts_ref[0:1, at]), (message * live).astype(BF)
                )

    bound_table = table(rows_dev, bnd_ref[...])
    aggc_ref[...] = nn(bound_table, aggb_ref[...].astype(BF)).astype(BF)
    node = 256

    @pl.loop(0, rows_dev // node)
    def _(step):
        at = pl.ds(pl.multiple_of(step * node, node), node)
        lat = lat_ref[at, :]
        cot = cot_ref[at, :]
        agg = agg_ref[at, :].astype(BF)
        aggc = aggc_ref[at, :]
        x = nn(lat, w_ref[5]) + nn(agg, w_ref[6]) + nn(aggc, w_ref[7])
        message, slope = silu_parts(x)
        hidden = message.astype(BF)
        new_ref[at, :] = (lat.astype(F32) + nn(hidden, w_ref[8])).astype(BF)
        d_node = (nt(cot, w_ref[8]) * slope).astype(BF)
        base_ref[at, :] = cot.astype(F32) + nt(d_node, w_ref[5])
        dagg_t_ref[:, at] = nt(w_ref[6], d_node).astype(BF)
        daggc_t_ref[:, at] = nt(w_ref[7], d_node).astype(BF)
        gw_ref[640:768, :] += nn(lat_t_ref[:, at], d_node)
        gw_ref[768:896, :] += tn(agg, d_node)
        gw_ref[896:1024, :] += tn(aggc, d_node)
        gw_ref[1024:1152, :] += tn(hidden, cot)

    dbg_t_ref[...] = nn(daggc_t_ref[...], bound_table).astype(BF)

    @pl.loop(0, steps)
    def _(step):
        at = columns(step)
        gathered = nn(dagg_t_ref[...], table(rows_dev, edges_ref[1:2, at]))
        d = (gathered * slope_m_ref[:, at]).astype(BF)
        dm_ref[:, at] = d
        gw_ref[0:256, :] += nt(rows_ref[:, at], d)
        gw_ref[256:384, :] += nn(d, feats_ref[at, :])

    gw_ref[256:384, :] = gw_ref[256:384, :].T

    for r in range(rounds):
        count = counts_ref[0, r]

        @pl.loop(0, per_round)
        def _(part):
            @pl.when(part * CHUNK < count)
            def _():
                at = columns(r * per_round + part)
                gathered = nn(dbg_t_ref[...], table(bound_count, contacts_ref[0:1, at]))
                d = (gathered * slope_c_ref[:, at]).astype(BF)
                dc_ref[:, at] = d
                gw_ref[384:640, :] += nt(both_ref[:, at], d)

    half = gw_ref.shape[0] // 2
    core = core_ref[0]
    kept_ref[...] = gw_ref[pl.ds(pl.multiple_of(core * half, 64), half), :] * scale
    sent = gw_ref[pl.ds(pl.multiple_of((1 - core) * half, 64), half), :] * scale
    sent_ref[...] = sent.astype(BF)


def contact_back_kernel(
    counts_ref, w_ref, contacts_ref, dc_ref, far0_ref, far1_ref, far2_ref, far3_ref, own_ref, sum_ref
):
    outs = (far0_ref, far1_ref, far2_ref, far3_ref)
    bound_count = own_ref.shape[0]
    rounds = len(outs)
    per_round = contacts_ref.shape[1] // rounds // CHUNK
    own_ref[...] = jnp.zeros_like(own_ref)
    for r in range(rounds):
        count = counts_ref[0, r]
        sum_ref[...] = jnp.zeros_like(sum_ref)

        @pl.loop(0, per_round)
        def _(part):
            @pl.when(part * CHUNK < count)
            def _():
                at = columns(r * per_round + part)
                d = dc_ref[:, at]
                own_ref[...] += nt(table(bound_count, contacts_ref[0:1, at]), d)
                sum_ref[...] += nt(table(bound_count, contacts_ref[1:2, at]), d)

        outs[r][...] = wide_nt(sum_ref[...], w_ref[4]).astype(BF)
    own_ref[...] = wide_nt(own_ref[...], w_ref[3])


def mesh_back_kernel(
    w_ref, edges_ref, dm_ref, base_ref, grad_ref, low_ref, high_ref, send_ref, recv_ref
):
    rows_dev = base_ref.shape[0]
    send_ref[...] = jnp.zeros_like(send_ref)
    recv_ref[...] = jnp.zeros_like(recv_ref)

    @pl.loop(0, edges_ref.shape[1] // CHUNK)
    def _(step):
        at = columns(step)
        d = dm_ref[:, at]
        send_ref[...] += nt(table(rows_dev + 2 * HB, edges_ref[0:1, at]), d)
        recv_ref[...] += nt(table(rows_dev, edges_ref[1:2, at]), d)

    low_ref[...] = wide_nt(send_ref[:HB, :], w_ref[0]).astype(BF)
    high_ref[...] = wide_nt(send_ref[HB + rows_dev :, :], w_ref[0]).astype(BF)
    grad_ref[...] = (
        base_ref[...]
        + wide_nt(recv_ref[...], w_ref[1])
        + wide_nt(send_ref[HB : HB + rows_dev, :], w_ref[0])
    )


def last_kernel(
    part_ref, own_ref, in0_ref, in1_ref, in2_ref, in3_ref, prev_ref, next_ref, bnd_ref, out_ref
):
    rows_dev = part_ref.shape[0]
    total = own_ref[...]
    for ref in (in0_ref, in1_ref, in2_ref, in3_ref):
        total = total + ref[...].astype(F32)
    out_ref[...] = part_ref[...] + wide_nn(table(rows_dev, bnd_ref[...]), total)
    out_ref[:HB, :] += prev_ref[...].astype(F32)
    out_ref[rows_dev - HB :, :] += next_ref[...].astype(F32)


def call(kernel, outs, args, scratch=(), smem=0, flops=0):
    spec = pl.BlockSpec(memory_space=pltpu.VMEM)
    return pl.pallas_call(
        kernel,
        out_shape=[jax.ShapeDtypeStruct(shape, kind) for shape, kind in outs],
        in_specs=[pl.BlockSpec(memory_space=pltpu.SMEM)] * smem + [spec] * (len(args) - smem),
        out_specs=[spec] * len(outs),
        scratch_shapes=[pltpu.VMEM(shape, kind) for shape, kind in scratch],
        compiler_params=pltpu.CompilerParams(vmem_limit_bytes=VMEM_BYTES),
        cost_estimate=pl.CostEstimate(flops=flops, bytes_accessed=4000000, transcendentals=0),
    )(*args)


def exchanged(block, mask_x=0, mask_y=0, mask_z=0, mask_core=0):
    route = []
    for region in range(32):
        for panel in range(8):
            other_region = region ^ ((mask_x >> 1) << 4 | mask_z << 1 | mask_core)
            other_panel = panel ^ ((mask_x & 1) << 2 | mask_y)
            route.append((region * 8 + panel, other_region * 8 + other_panel))
    return lax.ppermute(block, ("region", "panel"), route)


def swapped(block, bit):
    size = lax.axis_size("region")
    return lax.ppermute(block, "region", [(i, i ^ (1 << bit)) for i in range(size)])


def shifted(array, by):
    length = lax.axis_size("panel")
    pairs = [(i, i + by) for i in range(length) if 0 <= i + by < length]
    return lax.ppermute(array, "panel", pairs)


def wide(block):
    return block.astype(F32)


def four_sum(block, name):
    one, two, three = [wide(exchanged(block, **{name: mask})) for mask in (1, 2, 3)]
    return ((wide(block) + one) + (two + three)).astype(BF)


def summed_everywhere(kept, sent, core, row_y):
    part = kept.shape[0] // 4
    block = (kept + wide(exchanged(sent, mask_core=1))).astype(BF)
    pieces = [
        lax.dynamic_slice_in_dim(block, (row_y ^ mask) * part, part, 0) for mask in range(4)
    ]
    one, two, three = [wide(exchanged(pieces[mask], mask_y=mask)) for mask in (1, 2, 3)]
    block = ((wide(pieces[0]) + one) + (two + three)).astype(BF)
    block = four_sum(block, "mask_x")
    block = four_sum(block, "mask_z")
    block = (wide(block) + wide(exchanged(block, mask_z=4))).astype(BF)
    found = [block] + [exchanged(block, mask_y=mask) for mask in (1, 2, 3)]
    odd, high = row_y % 2 == 1, row_y >= 2
    low_pair = [jnp.where(odd, found[1], found[0]), jnp.where(odd, found[0], found[1])]
    high_pair = [jnp.where(odd, found[3], found[2]), jnp.where(odd, found[2], found[3])]
    ordered = [jnp.where(high, b, a) for a, b in zip(low_pair, high_pair)]
    ordered += [jnp.where(high, a, b) for a, b in zip(low_pair, high_pair)]
    block = jnp.concatenate(ordered, axis=0)
    other = exchanged(block, mask_core=1)
    first = jnp.where(core == 1, other, block)
    second = jnp.where(core == 1, block, other)
    return wide(jnp.concatenate([first, second], axis=0))


def shards(
    latents, edge_feats, weights, cotangent, mesh_edges, boundary, contact_edges, contact_counts
):
    rows_dev, width = latents.shape
    bound_count = boundary.shape[0]
    rounds = contact_counts.shape[1]
    edge_count = mesh_edges.shape[1]
    contact_count = contact_edges.shape[1]
    bnd = boundary.reshape(1, bound_count)
    core = lax.axis_index("region") % 2
    row_y = lax.axis_index("panel") % 4
    scale = 1.0 / math.sqrt(rows_dev * lax.axis_size("region") * lax.axis_size("panel"))

    before = shifted(latents[rows_dev - HB :], 1)
    after = shifted(latents[:HB], -1)
    lat_t, bound_t = call(
        bound_kernel, [((width, rows_dev), BF), ((width, bound_count), BF)], [latents, bnd]
    )
    fars = [swapped(bound_t, r) for r in range(rounds)]
    rows, own_rows = call(
        local_kernel,
        [((2 * width, edge_count), BF), ((width, contact_count), BF)],
        [lat_t, bound_t, mesh_edges, contact_edges],
        flops=4 * 10**9,
    )
    rim = jnp.concatenate([before, after], axis=0)
    new_rows, kept, sent, d_mesh, d_contact, base = call(
        functools.partial(main_kernel, scale=scale),
        [
            ((rows_dev, width), BF),
            ((9 * width // 2, width), F32),
            ((9 * width // 2, width), BF),
            ((width, edge_count), BF),
            ((width, contact_count), BF),
            ((rows_dev, width), F32),
        ],
        [contact_counts, core.reshape(1), latents, lat_t, rim, *fars, rows, own_rows]
        + [edge_feats, cotangent, weights, mesh_edges, contact_edges, bnd],
        [
            ((rows_dev, width), F32),
            ((bound_count, width), F32),
            ((width, edge_count), F32),
            ((width, contact_count), F32),
            ((2 * width, edge_count), BF),
            ((2 * width, contact_count), BF),
            ((9 * width, width), F32),
            ((2 * width, 2 * width), BF),
            ((rows_dev, width), BF),
            ((width, rows_dev), BF),
            ((width, rows_dev), BF),
            ((width, bound_count), BF),
        ],
        smem=2,
        flops=8 * 10**9,
    )
    *far_grads, own_grad = call(
        contact_back_kernel,
        [((bound_count, width), BF)] * rounds + [((bound_count, width), F32)],
        [contact_counts, weights, contact_edges, d_contact],
        [((bound_count, width), F32)],
        smem=1,
        flops=10**9,
    )
    part, low, high = call(
        mesh_back_kernel,
        [((rows_dev, width), F32), ((HB, width), BF), ((HB, width), BF)],
        [weights, mesh_edges, d_mesh, base],
        [((rows_dev + 2 * HB, width), F32), ((rows_dev, width), F32)],
        flops=2 * 10**9,
    )
    incoming = [swapped(far_grads[r], r) for r in range(rounds)]
    from_prev = shifted(high, 1)
    from_next = shifted(low, -1)
    (grad_rows,) = call(
        last_kernel,
        [((rows_dev, width), F32)],
        [part, own_grad, *incoming, from_prev, from_next, bnd],
    )
    summed = summed_everywhere(kept, sent, core, row_y).reshape(9, width, width)
    return (new_rows, grad_rows, summed)


def solution(mesh):
    blocks = P(("region", "panel"), None)
    placed = (
        blocks,
        blocks,
        P(),
        blocks,
        P(None, ("region", "panel")),
        P(("region", "panel")),
        P(None, ("region", "panel")),
        blocks,
    )
    return jax.shard_map(
        shards, mesh=mesh, in_specs=placed, out_specs=(blocks, blocks, P()), check_vma=False
    )
```

time: 398 us -> 141 us (0.35)
  the two profiles are of different devices: /device:TPU:1 before, /device:TPU:6 now
where the time goes in v1:
time: 141 us
  starting transfers between devices  59.5 us (42%)
  Pallas kernels  52.3 us (37%)
  waiting for transfers between devices  23.4 us (17%)
  other arithmetic  2.67 us (2%)
  local copies, waits for them, and re-layouts  2 us (1%)
    pallas_call x6, Pallas kernels, call(): pl.pallas_call(kernel, out_shape=[jax.ShapeDtypeStruct(shape, kind) for s...  52.3 us
    ppermute x15, starting transfers between devices, exchanged(): return lax.ppermute(block, ('region', 'panel'), route)  26.6 us
    ppermute x8, starting transfers between devices, swapped(): lax.ppermute(block, 'region', [(i, i ^ 1 << bit) for i in range(size)])  17 us
    ppermute x4, starting transfers between devices, shifted(): return lax.ppermute(array, 'panel', pairs)  15.9 us
    ppermute x15, waiting for transfers between devices, exchanged(): return lax.ppermute(block, ('region', 'panel'), route)  13.5 us
    ppermute x8, waiting for transfers between devices, swapped(): lax.ppermute(block, 'region', [(i, i ^ 1 << bit) for i in range(size)])  9.87 us
  transfers between devices with their start and end apart: 27, of which 11 were waited for; matrix products, arithmetic and copies ran while one was open for 1% of the time, Pallas kernels for 17%

profile of v1, /device:TPU:6, one launch (start us, length us, event | category | flops | bytes accessed | tf_op | source)
XLA Modules:
  0.0 140.7 jit_solution(9796927429816543292)
XLA Ops:
  0.6 2.0 %shard_map.103 = (bf16[128,1024]{1,0:T(8,128)(2,1)}, bf16[128,256]{1,0:T(8,128)(2,1)}) custom-call(bf16[1024,128]{1,0:T(8,128)(2,1)} %lat_ref.3, s32[1,256]{1,0:T(1,128)} %bitcast.5), custom_call_target="tpu_custom_call" | custom-call | bytes 4000000 | tf_op jit(solution)/shard_map/pallas_call | solution.py:307
  2.6 0.0 collective-permute-start.2
  2.6 1.9 %collective-permute-start.3 = (bf16[128,256]{1,0:T(8,128)(2,1)}, bf16[128,256]{1,0:T(8,128)(2,1)S(1)}, u32[]{:S(2)}, u32[]{:S(2)}) collective-permute-start(bf16[128,256]{1,0:T(8,128)(2,1)} %get-tuple-element.22.bound_t_ref), channel_id=1, source_target_pairs={{0,16},{8,24},{16,0},{24,8},{32,48},{40,56},{48,32},{56,40},{64,80... | collective-permute-start | bytes 196616 | tf_op jit(solution)/shard_map/ppermute | solution.py:330
  4.5 3.3 %collective-permute-start.4 = (bf16[128,256]{1,0:T(8,128)(2,1)}, bf16[128,256]{1,0:T(8,128)(2,1)S(1)}, u32[]{:S(2)}, u32[]{:S(2)}) collective-permute-start(bf16[128,256]{1,0:T(8,128)(2,1)} %get-tuple-element.22.bound_t_ref), channel_id=1, source_target_pairs={{0,32},{8,40},{16,48},{24,56},{32,0},{40,8},{48,16},{56,24},{64,96... | collective-permute-start | bytes 196616 | tf_op jit(solution)/shard_map/ppermute | solution.py:330
  7.8 0.7 fusion
  8.5 3.5 %collective-permute-start = (bf16[64,128]{1,0:T(8,128)(2,1)S(1)}, bf16[64,128]{1,0:T(8,128)(2,1)S(1)}, u32[]{:S(2)}, u32[]{:S(2)}) collective-permute-start(bf16[64,128]{1,0:T(8,128)(2,1)S(1)} %get-tuple-element.41), channel_id=1, source_target_pairs={{0,1},{1,2},{2,3},{3,4},{4,5},{5,6},{6,7},{8,9},{9,10},{10,11},{11... | collective-permute-start | bytes 49160 | tf_op jit(solution)/shard_map/ppermute | solution.py:336
  12.0 4.5 %collective-permute-start.1 = (bf16[64,128]{1,0:T(8,128)(2,1)S(1)}, bf16[64,128]{1,0:T(8,128)(2,1)S(1)}, u32[]{:S(2)}, u32[]{:S(2)}) collective-permute-start(bf16[64,128]{1,0:T(8,128)(2,1)S(1)} %get-tuple-element.42), channel_id=1, source_target_pairs={{1,0},{2,1},{3,2},{4,3},{5,4},{6,5},{7,6},{9,8},{10,9},{11,10},{12... | collective-permute-start | bytes 49160 | tf_op jit(solution)/shard_map/ppermute | solution.py:336
  16.5 0.0 copy-start.9
  16.5 8.5 %shard_map.104 = (bf16[256,3072]{1,0:T(8,128)(2,1)}, bf16[128,8192]{1,0:T(8,128)(2,1)}) custom-call(bf16[128,1024]{1,0:T(8,128)(2,1)} %get-tuple-element.21.lat_t_ref, bf16[128,256]{1,0:T(8,128)(2,1)} %get-tuple-element.22.bound_t_ref, s32[2,3072]{1,0:T(2,128)} %edges_ref.5, s32[2,8192]{1,0:T(2,128)} %contacts_ref.5), custom_call_target="tpu_custom_call" | custom-call | flops 4000000000 | bytes 4000000 | tf_op jit(solution)/shard_map/pallas_call | solution.py:307
  25.0 0.0 collective-permute-done
  25.0 4.6 %collective-permute-start.5 = (bf16[128,256]{1,0:T(8,128)(2,1)S(1)}, bf16[128,256]{1,0:T(8,128)(2,1)S(1)}, u32[]{:S(2)}, u32[]{:S(2)}) collective-permute-start(bf16[128,256]{1,0:T(8,128)(2,1)S(1)} %copy-done.9), channel_id=1, source_target_pairs={{0,64},{8,72},{16,80},{24,88},{32,96},{40,104},{48,112},{56,120},{... | collective-permute-start | bytes 196616 | tf_op jit(solution)/shard_map/ppermute | solution.py:330
  29.6 0.0 collective-permute-done.1
  29.6 0.6 pad_maximum_fusion.2.rim_ref
  30.2 0.0 collective-permute-done.2.far0_ref
  30.2 0.0 collective-permute-done.3.far1_ref
  30.2 0.0 collective-permute-done.4.far2_ref
  30.2 3.0 %collective-permute-done.5.far3_ref = bf16[128,256]{1,0:T(8,128)(2,1)S(1)} collective-permute-done((bf16[128,256]{1,0:T(8,128)(2,1)S(1)}, bf16[128,256]{1,0:T(8,128)(2,1)S(1)}, u32[]{:S(2)}, u32[]{:S(2)}) %collective-permute-start.5) | collective-permute-done | bytes 65568 | tf_op jit(solution)/shard_map/ppermute | solution.py:330
  33.3 0.6 copy-done.10
  33.9 26.0 %shard_map.105 = (bf16[1024,128]{1,0:T(8,128)(2,1)}, f32[576,128]{1,0:T(8,128)}, bf16[576,128]{1,0:T(8,128)(2,1)}, bf16[128,3072]{1,0:T(8,128)(2,1)}, bf16[128,8192]{1,0:T(8,128)(2,1)}, /*index=5*/f32[1024,128]{1,0:T(8,128)}) custom-call(s32[1,4]{1,0:T(1,128)} %counts_ref.3, s32[1]{0:T(128)} %bitcast.core_ref, bf16[1024,128]{1,0:T(8,128)(2,1)} %lat_ref.3, ...), custom_call_target="tpu_custom_call" | custom-call | flops 8000000000 | bytes 4000000 | tf_op jit(solution)/shard_map/pallas_call | solution.py:307
  59.9 0.1 collective-permute-start.12
  60.0 1.5 %collective-permute-done.12 = bf16[576,128]{1,0:T(8,128)(2,1)S(1)} collective-permute-done((bf16[576,128]{1,0:T(8,128)(2,1)}, bf16[576,128]{1,0:T(8,128)(2,1)S(1)}, u32[]{:S(2)}, u32[]{:S(2)}) %collective-permute-start.12) | collective-permute-done | bytes 147488 | tf_op jit(solution)/shard_map/ppermute | solution.py:325
  61.6 1.0 add_convert_fusion
  62.6 0.1 collective-permute-start.13
  62.7 1.2 collective-permute-start.14
  63.9 3.5 %collective-permute-start.15 = (bf16[144,128]{1,0:T(8,128)(2,1)S(1)}, bf16[144,128]{1,0:T(8,128)(2,1)S(1)}, u32[]{:S(2)}, u32[]{:S(2)}) collective-permute-start(bf16[144,128]{1,0:T(8,128)(2,1)S(1)} %get-tuple-element.48), channel_id=1, source_target_pairs={{0,3},{1,2},{2,1},{3,0},{4,7},{5,6},{6,5},{7,4},{8,11},{9,10},{10,... | collective-permute-start | bytes 110600 | tf_op jit(solution)/shard_map/ppermute | solution.py:325
  67.4 0.0 collective-permute-done.13
  67.4 1.0 collective-permute-done.14
  68.4 1.0 collective-permute-done.15
  69.3 1.7 %collective-permute-start.16 = (bf16[144,128]{1,0:T(8,128)(2,1)S(1)}, bf16[144,128]{1,0:T(8,128)(2,1)S(1)}, u32[]{:S(2)}, u32[]{:S(2)}) collective-permute-start(bf16[144,128]{1,0:T(8,128)(2,1)S(1)} %add_convert_fusion.4), channel_id=1, source_target_pairs={{0,4},{1,5},{2,6},{3,7},{4,0},{5,1},{6,2},{7,3},{8,12},{9,13},{10,... | collective-permute-start | bytes 110600 | tf_op jit(solution)/shard_map/ppermute | solution.py:325
  71.1 5.8 %collective-permute-start.17 = (bf16[144,128]{1,0:T(8,128)(2,1)S(1)}, bf16[144,128]{1,0:T(8,128)(2,1)S(1)}, u32[]{:S(2)}, u32[]{:S(2)}) collective-permute-start(bf16[144,128]{1,0:T(8,128)(2,1)S(1)} %add_convert_fusion.4), channel_id=1, source_target_pairs={{0,128},{1,129},{2,130},{3,131},{4,132},{5,133},{6,134},{7,135},{8... | collective-permute-start | bytes 110600 | tf_op jit(solution)/shard_map/ppermute | solution.py:325
  76.9 0.5 collective-permute-start.18
  77.3 0.0 collective-permute-done.16
  77.3 1.8 %collective-permute-done.17 = bf16[144,128]{1,0:T(8,128)(2,1)S(1)} collective-permute-done((bf16[144,128]{1,0:T(8,128)(2,1)S(1)}, bf16[144,128]{1,0:T(8,128)(2,1)S(1)}, u32[]{:S(2)}, u32[]{:S(2)}) %collective-permute-start.17) | collective-permute-done | bytes 36896 | tf_op jit(solution)/shard_map/ppermute | solution.py:325
  79.1 2.9 %collective-permute-done.18 = bf16[144,128]{1,0:T(8,128)(2,1)S(1)} collective-permute-done((bf16[144,128]{1,0:T(8,128)(2,1)S(1)}, bf16[144,128]{1,0:T(8,128)(2,1)S(1)}, u32[]{:S(2)}, u32[]{:S(2)}) %collective-permute-start.18) | collective-permute-done | bytes 36896 | tf_op jit(solution)/shard_map/ppermute | solution.py:325
  82.1 0.1 collective-permute-start.19
  82.2 0.3 collective-permute-start.20
  82.5 4.1 %collective-permute-start.21 = (bf16[144,128]{1,0:T(8,128)(2,1)S(1)}, bf16[144,128]{1,0:T(8,128)(2,1)S(1)}, u32[]{:S(2)}, u32[]{:S(2)}) collective-permute-start(bf16[144,128]{1,0:T(8,128)(2,1)S(1)} %add_convert_fusion.3), channel_id=1, source_target_pairs={{0,48},{1,49},{2,50},{3,51},{4,52},{5,53},{6,54},{7,55},{8,56},{9,... | collective-permute-start | bytes 110600 | tf_op jit(solution)/shard_map/ppermute | solution.py:325
  86.5 0.0 collective-permute-done.19
  86.5 0.7 collective-permute-done.20
  87.3 1.6 %collective-permute-done.21 = bf16[144,128]{1,0:T(8,128)(2,1)S(1)} collective-permute-done((bf16[144,128]{1,0:T(8,128)(2,1)S(1)}, bf16[144,128]{1,0:T(8,128)(2,1)S(1)}, u32[]{:S(2)}, u32[]{:S(2)}) %collective-permute-start.21) | collective-permute-done | bytes 36896 | tf_op jit(solution)/shard_map/ppermute | solution.py:325
  88.9 5.0 %collective-permute-start.22 = (bf16[144,128]{1,0:T(8,128)(2,1)S(1)}, bf16[144,128]{1,0:T(8,128)(2,1)S(1)}, u32[]{:S(2)}, u32[]{:S(2)}) collective-permute-start(bf16[144,128]{1,0:T(8,128)(2,1)S(1)} %add_convert_fusion.2), channel_id=1, source_target_pairs={{0,64},{1,65},{2,66},{3,67},{4,68},{5,69},{6,70},{7,71},{8,72},{9,... | collective-permute-start | bytes 110600 | tf_op jit(solution)/shard_map/ppermute | solution.py:325
  93.9 3.0 %collective-permute-done.22 = bf16[144,128]{1,0:T(8,128)(2,1)S(1)} collective-permute-done((bf16[144,128]{1,0:T(8,128)(2,1)S(1)}, bf16[144,128]{1,0:T(8,128)(2,1)S(1)}, u32[]{:S(2)}, u32[]{:S(2)}) %collective-permute-start.22) | collective-permute-done | bytes 36896 | tf_op jit(solution)/shard_map/ppermute | solution.py:325
  96.9 0.1 collective-permute-start.23
  97.0 0.9 collective-permute-start.24
  97.8 3.2 %collective-permute-start.25 = (bf16[144,128]{1,0:T(8,128)(2,1)S(1)}, bf16[144,128]{1,0:T(8,128)(2,1)S(1)}, u32[]{:S(2)}, u32[]{:S(2)}) collective-permute-start(bf16[144,128]{1,0:T(8,128)(2,1)S(1)} %add_convert_fusion.1), channel_id=1, source_target_pairs={{0,1},{1,0},{2,3},{3,2},{4,5},{5,4},{6,7},{7,6},{8,9},{9,8},{10,11... | collective-permute-start | bytes 110600 | tf_op jit(solution)/shard_map/ppermute | solution.py:325
  101.1 7.3 %shard_map.106 = (f32[1024,128]{1,0:T(8,128)}, bf16[64,128]{1,0:T(8,128)(2,1)}, bf16[64,128]{1,0:T(8,128)(2,1)}) custom-call(bf16[9,128,128]{2,1,0:T(8,128)(2,1)} %w_ref.5, s32[2,3072]{1,0:T(2,128)} %edges_ref.5, bf16[128,3072]{1,0:T(8,128)(2,1)} %get-tuple-element.26.dm_ref, f32[1024,128]{1,0:T(8,128)} %get-tuple-element.27.base_ref), custom_call_target="tpu_custom_call" | custom-call | flops 2000000000 | bytes 4000000 | tf_op jit(solution)/shard_map/pallas_call | solution.py:307
  108.3 1.9 %collective-permute-start.10 = (bf16[64,128]{1,0:T(8,128)(2,1)}, bf16[64,128]{1,0:T(8,128)(2,1)S(1)}, u32[]{:S(2)}, u32[]{:S(2)}) collective-permute-start(bf16[64,128]{1,0:T(8,128)(2,1)} %get-tuple-element.35), channel_id=1, source_target_pairs={{0,1},{1,2},{2,3},{3,4},{4,5},{5,6},{6,7},{8,9},{9,10},{10,11},{11... | collective-permute-start | bytes 49160 | tf_op jit(solution)/shard_map/ppermute | solution.py:336
  110.2 6.0 %collective-permute-start.11 = (bf16[64,128]{1,0:T(8,128)(2,1)}, bf16[64,128]{1,0:T(8,128)(2,1)S(1)}, u32[]{:S(2)}, u32[]{:S(2)}) collective-permute-start(bf16[64,128]{1,0:T(8,128)(2,1)} %get-tuple-element.36), channel_id=1, source_target_pairs={{1,0},{2,1},{3,2},{4,3},{5,4},{6,5},{7,6},{9,8},{10,9},{11,10},{12... | collective-permute-start | bytes 49160 | tf_op jit(solution)/shard_map/ppermute | solution.py:336
  116.3 0.0 collective-permute-done.23
  116.3 0.0 collective-permute-done.24
  116.3 0.0 collective-permute-done.25
  116.4 0.1 collective-permute-start.26
  116.5 6.0 %shard_map.107 = (bf16[256,128]{1,0:T(8,128)(2,1)}, bf16[256,128]{1,0:T(8,128)(2,1)}, bf16[256,128]{1,0:T(8,128)(2,1)}, bf16[256,128]{1,0:T(8,128)(2,1)}, f32[256,128]{1,0:T(8,128)}) custom-call(s32[1,4]{1,0:T(1,128)} %counts_ref.3, bf16[9,128,128]{2,1,0:T(8,128)(2,1)} %w_ref.5, s32[2,8192]{1,0:T(2,128)} %contacts_ref.5, ...), custom_call_target="tpu_custom_call" | custom-call | flops 1000000000 | bytes 4000000 | tf_op jit(solution)/shard_map/pallas_call | solution.py:307
  122.5 0.8 collective-permute-start.6
  123.3 0.0 collective-permute-start.7
  123.3 0.0 collective-permute-done.10.prev_ref
  123.3 4.3 %collective-permute-start.8 = (bf16[256,128]{1,0:T(8,128)(2,1)}, bf16[256,128]{1,0:T(8,128)(2,1)S(1)}, u32[]{:S(2)}, u32[]{:S(2)}) collective-permute-start(bf16[256,128]{1,0:T(8,128)(2,1)} %get-tuple-element.33), channel_id=1, source_target_pairs={{0,32},{8,40},{16,48},{24,56},{32,0},{40,8},{48,16},{56,24},{64,96... | collective-permute-start | bytes 196616 | tf_op jit(solution)/shard_map/ppermute | solution.py:330
  127.6 2.2 %collective-permute-start.9 = (bf16[256,128]{1,0:T(8,128)(2,1)}, bf16[256,128]{1,0:T(8,128)(2,1)S(1)}, u32[]{:S(2)}, u32[]{:S(2)}) collective-permute-start(bf16[256,128]{1,0:T(8,128)(2,1)} %get-tuple-element.34), channel_id=1, source_target_pairs={{0,64},{8,72},{16,80},{24,88},{32,96},{40,104},{48,112},{56,120},{... | collective-permute-start | bytes 196616 | tf_op jit(solution)/shard_map/ppermute | solution.py:330
  129.8 1.5 %collective-permute-done.8.in2_ref = bf16[256,128]{1,0:T(8,128)(2,1)S(1)} collective-permute-done((bf16[256,128]{1,0:T(8,128)(2,1)}, bf16[256,128]{1,0:T(8,128)(2,1)S(1)}, u32[]{:S(2)}, u32[]{:S(2)}) %collective-permute-start.8) | collective-permute-done | bytes 65568 | tf_op jit(solution)/shard_map/ppermute | solution.py:330
  131.3 5.3 %collective-permute-done.9.in3_ref = bf16[256,128]{1,0:T(8,128)(2,1)S(1)} collective-permute-done((bf16[256,128]{1,0:T(8,128)(2,1)}, bf16[256,128]{1,0:T(8,128)(2,1)S(1)}, u32[]{:S(2)}, u32[]{:S(2)}) %collective-permute-start.9) | collective-permute-done | bytes 65568 | tf_op jit(solution)/shard_map/ppermute | solution.py:330
  136.6 0.6 copy-done.3
  137.2 2.5 %shard_map.108 = f32[1024,128]{1,0:T(8,128)} custom-call(f32[1024,128]{1,0:T(8,128)} %get-tuple-element.28.part_ref, f32[256,128]{1,0:T(8,128)} %get-tuple-element.30.own_ref, bf16[256,128]{1,0:T(8,128)(2,1)} %copy-done, bf16[256,128]{1,0:T(8,128)(2,1)} %copy-done.1, bf16[256,128]{1,0:T(8,128)(2,1)} %copy-done.2, bf16[256,128]{1,0:T(8,128)(2,1)} %copy-done.3, ...), custom_call_target="tpu_custom_call" | custom-call | bytes 4000000 | tf_op jit(solution)/shard_map/pallas_call | solution.py:307
  139.7 0.1 broadcast_select_fusion.1
  139.8 0.9 convert.1
  (31 shorter events, 0.2 us)
Async XLA Ops:
  2.6 27.6 %collective-permute-start.2 = (bf16[128,256]{1,0:T(8,128)(2,1)}, bf16[128,256]{1,0:T(8,128)(2,1)S(1)}, u32[]{:S(2)}, u32[]{:S(2)}) collective-permute-start(bf16[128,256]{1,0:T(8,128)(2,1)} %get-tuple-element.22.bound_t_ref), channel_id=1, source_target_pairs={{0,8},{8,0},{16,24},{24,16},{32,40},{40,32},{48,56},{56,48},{64,72... | collective-permute-start | bytes 196616 | tf_op jit(solution)/shard_map/ppermute | solution.py:330
  2.6 27.6 %collective-permute-start.3 = (bf16[128,256]{1,0:T(8,128)(2,1)}, bf16[128,256]{1,0:T(8,128)(2,1)S(1)}, u32[]{:S(2)}, u32[]{:S(2)}) collective-permute-start(bf16[128,256]{1,0:T(8,128)(2,1)} %get-tuple-element.22.bound_t_ref), channel_id=1, source_target_pairs={{0,16},{8,24},{16,0},{24,8},{32,48},{40,56},{48,32},{56,40},{64,80... | collective-permute-start | bytes 196616 | tf_op jit(solution)/shard_map/ppermute | solution.py:330
  4.5 25.7 %collective-permute-start.4 = (bf16[128,256]{1,0:T(8,128)(2,1)}, bf16[128,256]{1,0:T(8,128)(2,1)S(1)}, u32[]{:S(2)}, u32[]{:S(2)}) collective-permute-start(bf16[128,256]{1,0:T(8,128)(2,1)} %get-tuple-element.22.bound_t_ref), channel_id=1, source_target_pairs={{0,32},{8,40},{16,48},{24,56},{32,0},{40,8},{48,16},{56,24},{64,96... | collective-permute-start | bytes 196616 | tf_op jit(solution)/shard_map/ppermute | solution.py:330
  8.5 16.5 %collective-permute-start = (bf16[64,128]{1,0:T(8,128)(2,1)S(1)}, bf16[64,128]{1,0:T(8,128)(2,1)S(1)}, u32[]{:S(2)}, u32[]{:S(2)}) collective-permute-start(bf16[64,128]{1,0:T(8,128)(2,1)S(1)} %get-tuple-element.41), channel_id=1, source_target_pairs={{0,1},{1,2},{2,3},{3,4},{4,5},{5,6},{6,7},{8,9},{9,10},{10,11},{11... | collective-permute-start | bytes 49160 | tf_op jit(solution)/shard_map/ppermute | solution.py:336
  12.0 17.6 %collective-permute-start.1 = (bf16[64,128]{1,0:T(8,128)(2,1)S(1)}, bf16[64,128]{1,0:T(8,128)(2,1)S(1)}, u32[]{:S(2)}, u32[]{:S(2)}) collective-permute-start(bf16[64,128]{1,0:T(8,128)(2,1)S(1)} %get-tuple-element.42), channel_id=1, source_target_pairs={{1,0},{2,1},{3,2},{4,3},{5,4},{6,5},{7,6},{9,8},{10,9},{11,10},{12... | collective-permute-start | bytes 49160 | tf_op jit(solution)/shard_map/ppermute | solution.py:336
  16.5 8.5 %copy-start.9 = (bf16[128,256]{1,0:T(8,128)(2,1)S(1)}, bf16[128,256]{1,0:T(8,128)(2,1)}, u32[]{:S(2)}) copy-start(bf16[128,256]{1,0:T(8,128)(2,1)} %get-tuple-element.22.bound_t_ref) | copy-start | bytes 196612
  25.0 8.3 %collective-permute-start.5 = (bf16[128,256]{1,0:T(8,128)(2,1)S(1)}, bf16[128,256]{1,0:T(8,128)(2,1)S(1)}, u32[]{:S(2)}, u32[]{:S(2)}) collective-permute-start(bf16[128,256]{1,0:T(8,128)(2,1)S(1)} %copy-done.9), channel_id=1, source_target_pairs={{0,64},{8,72},{16,80},{24,88},{32,96},{40,104},{48,112},{56,120},{... | collective-permute-start | bytes 196616 | tf_op jit(solution)/shard_map/ppermute | solution.py:330
  30.2 3.1 %copy-start.6 = (bf16[128,256]{1,0:T(8,128)(2,1)}, bf16[128,256]{1,0:T(8,128)(2,1)S(1)}, u32[]{:S(2)}) copy-start(bf16[128,256]{1,0:T(8,128)(2,1)S(1)} %collective-permute-done.2.far0_ref) | copy-start | bytes 196612
  30.2 3.1 %copy-start.7 = (bf16[128,256]{1,0:T(8,128)(2,1)}, bf16[128,256]{1,0:T(8,128)(2,1)S(1)}, u32[]{:S(2)}) copy-start(bf16[128,256]{1,0:T(8,128)(2,1)S(1)} %collective-permute-done.3.far1_ref) | copy-start | bytes 196612
  30.2 3.1 %copy-start.8 = (bf16[128,256]{1,0:T(8,128)(2,1)}, bf16[128,256]{1,0:T(8,128)(2,1)S(1)}, u32[]{:S(2)}) copy-start(bf16[128,256]{1,0:T(8,128)(2,1)S(1)} %collective-permute-done.4.far2_ref) | copy-start | bytes 196612
  33.3 0.6 copy-start.10
  59.9 1.7 %collective-permute-start.12 = (bf16[576,128]{1,0:T(8,128)(2,1)}, bf16[576,128]{1,0:T(8,128)(2,1)S(1)}, u32[]{:S(2)}, u32[]{:S(2)}) collective-permute-start(bf16[576,128]{1,0:T(8,128)(2,1)} %get-tuple-element.38), channel_id=1, source_target_pairs={{0,8},{1,9},{2,10},{3,11},{4,12},{5,13},{6,14},{7,15},{8,0},{9,1},... | collective-permute-start | bytes 442376 | tf_op jit(solution)/shard_map/ppermute | solution.py:325
  62.6 4.8 %collective-permute-start.13 = (bf16[144,128]{1,0:T(8,128)(2,1)S(1)}, bf16[144,128]{1,0:T(8,128)(2,1)S(1)}, u32[]{:S(2)}, u32[]{:S(2)}) collective-permute-start(bf16[144,128]{1,0:T(8,128)(2,1)S(1)} %get-tuple-element.47), channel_id=1, source_target_pairs={{0,1},{1,0},{2,3},{3,2},{4,5},{5,4},{6,7},{7,6},{8,9},{9,8},{10,11... | collective-permute-start | bytes 110600 | tf_op jit(solution)/shard_map/ppermute | solution.py:325
  62.7 5.7 %collective-permute-start.14 = (bf16[144,128]{1,0:T(8,128)(2,1)S(1)}, bf16[144,128]{1,0:T(8,128)(2,1)S(1)}, u32[]{:S(2)}, u32[]{:S(2)}) collective-permute-start(bf16[144,128]{1,0:T(8,128)(2,1)S(1)} %get-tuple-element.49), channel_id=1, source_target_pairs={{0,2},{1,3},{2,0},{3,1},{4,6},{5,7},{6,4},{7,5},{8,10},{9,11},{10,... | collective-permute-start | bytes 110600 | tf_op jit(solution)/shard_map/ppermute | solution.py:325
  63.9 5.4 %collective-permute-start.15 = (bf16[144,128]{1,0:T(8,128)(2,1)S(1)}, bf16[144,128]{1,0:T(8,128)(2,1)S(1)}, u32[]{:S(2)}, u32[]{:S(2)}) collective-permute-start(bf16[144,128]{1,0:T(8,128)(2,1)S(1)} %get-tuple-element.48), channel_id=1, source_target_pairs={{0,3},{1,2},{2,1},{3,0},{4,7},{5,6},{6,5},{7,4},{8,11},{9,10},{10,... | collective-permute-start | bytes 110600 | tf_op jit(solution)/shard_map/ppermute | solution.py:325
  69.3 8.0 %collective-permute-start.16 = (bf16[144,128]{1,0:T(8,128)(2,1)S(1)}, bf16[144,128]{1,0:T(8,128)(2,1)S(1)}, u32[]{:S(2)}, u32[]{:S(2)}) collective-permute-start(bf16[144,128]{1,0:T(8,128)(2,1)S(1)} %add_convert_fusion.4), channel_id=1, source_target_pairs={{0,4},{1,5},{2,6},{3,7},{4,0},{5,1},{6,2},{7,3},{8,12},{9,13},{10,... | collective-permute-start | bytes 110600 | tf_op jit(solution)/shard_map/ppermute | solution.py:325
  71.1 8.0 %collective-permute-start.17 = (bf16[144,128]{1,0:T(8,128)(2,1)S(1)}, bf16[144,128]{1,0:T(8,128)(2,1)S(1)}, u32[]{:S(2)}, u32[]{:S(2)}) collective-permute-start(bf16[144,128]{1,0:T(8,128)(2,1)S(1)} %add_convert_fusion.4), channel_id=1, source_target_pairs={{0,128},{1,129},{2,130},{3,131},{4,132},{5,133},{6,134},{7,135},{8... | collective-permute-start | bytes 110600 | tf_op jit(solution)/shard_map/ppermute | solution.py:325
  76.9 5.2 %collective-permute-start.18 = (bf16[144,128]{1,0:T(8,128)(2,1)S(1)}, bf16[144,128]{1,0:T(8,128)(2,1)S(1)}, u32[]{:S(2)}, u32[]{:S(2)}) collective-permute-start(bf16[144,128]{1,0:T(8,128)(2,1)S(1)} %add_convert_fusion.4), channel_id=1, source_target_pairs={{0,132},{1,133},{2,134},{3,135},{4,128},{5,129},{6,130},{7,131},{8... | collective-permute-start | bytes 110600 | tf_op jit(solution)/shard_map/ppermute | solution.py:325
  82.1 4.5 %collective-permute-start.19 = (bf16[144,128]{1,0:T(8,128)(2,1)S(1)}, bf16[144,128]{1,0:T(8,128)(2,1)S(1)}, u32[]{:S(2)}, u32[]{:S(2)}) collective-permute-start(bf16[144,128]{1,0:T(8,128)(2,1)S(1)} %add_convert_fusion.3), channel_id=1, source_target_pairs={{0,16},{1,17},{2,18},{3,19},{4,20},{5,21},{6,22},{7,23},{8,24},{9,... | collective-permute-start | bytes 110600 | tf_op jit(solution)/shard_map/ppermute | solution.py:325
  82.2 5.1 %collective-permute-start.20 = (bf16[144,128]{1,0:T(8,128)(2,1)S(1)}, bf16[144,128]{1,0:T(8,128)(2,1)S(1)}, u32[]{:S(2)}, u32[]{:S(2)}) collective-permute-start(bf16[144,128]{1,0:T(8,128)(2,1)S(1)} %add_convert_fusion.3), channel_id=1, source_target_pairs={{0,32},{1,33},{2,34},{3,35},{4,36},{5,37},{6,38},{7,39},{8,40},{9,... | collective-permute-start | bytes 110600 | tf_op jit(solution)/shard_map/ppermute | solution.py:325
  82.5 6.4 %collective-permute-start.21 = (bf16[144,128]{1,0:T(8,128)(2,1)S(1)}, bf16[144,128]{1,0:T(8,128)(2,1)S(1)}, u32[]{:S(2)}, u32[]{:S(2)}) collective-permute-start(bf16[144,128]{1,0:T(8,128)(2,1)S(1)} %add_convert_fusion.3), channel_id=1, source_target_pairs={{0,48},{1,49},{2,50},{3,51},{4,52},{5,53},{6,54},{7,55},{8,56},{9,... | collective-permute-start | bytes 110600 | tf_op jit(solution)/shard_map/ppermute | solution.py:325
  88.9 8.0 %collective-permute-start.22 = (bf16[144,128]{1,0:T(8,128)(2,1)S(1)}, bf16[144,128]{1,0:T(8,128)(2,1)S(1)}, u32[]{:S(2)}, u32[]{:S(2)}) collective-permute-start(bf16[144,128]{1,0:T(8,128)(2,1)S(1)} %add_convert_fusion.2), channel_id=1, source_target_pairs={{0,64},{1,65},{2,66},{3,67},{4,68},{5,69},{6,70},{7,71},{8,72},{9,... | collective-permute-start | bytes 110600 | tf_op jit(solution)/shard_map/ppermute | solution.py:325
  96.9 19.4 %collective-permute-start.23 = (bf16[144,128]{1,0:T(8,128)(2,1)S(1)}, bf16[144,128]{1,0:T(8,128)(2,1)S(1)}, u32[]{:S(2)}, u32[]{:S(2)}) collective-permute-start(bf16[144,128]{1,0:T(8,128)(2,1)S(1)} %add_convert_fusion.1), channel_id=1, source_target_pairs={{0,3},{1,2},{2,1},{3,0},{4,7},{5,6},{6,5},{7,4},{8,11},{9,10},{10,... | collective-permute-start | bytes 110600 | tf_op jit(solution)/shard_map/ppermute | solution.py:325
  97.0 19.3 %collective-permute-start.24 = (bf16[144,128]{1,0:T(8,128)(2,1)S(1)}, bf16[144,128]{1,0:T(8,128)(2,1)S(1)}, u32[]{:S(2)}, u32[]{:S(2)}) collective-permute-start(bf16[144,128]{1,0:T(8,128)(2,1)S(1)} %add_convert_fusion.1), channel_id=1, source_target_pairs={{0,2},{1,3},{2,0},{3,1},{4,6},{5,7},{6,4},{7,5},{8,10},{9,11},{10,... | collective-permute-start | bytes 110600 | tf_op jit(solution)/shard_map/ppermute | solution.py:325
  97.8 18.5 %collective-permute-start.25 = (bf16[144,128]{1,0:T(8,128)(2,1)S(1)}, bf16[144,128]{1,0:T(8,128)(2,1)S(1)}, u32[]{:S(2)}, u32[]{:S(2)}) collective-permute-start(bf16[144,128]{1,0:T(8,128)(2,1)S(1)} %add_convert_fusion.1), channel_id=1, source_target_pairs={{0,1},{1,0},{2,3},{3,2},{4,5},{5,4},{6,7},{7,6},{8,9},{9,8},{10,11... | collective-permute-start | bytes 110600 | tf_op jit(solution)/shard_map/ppermute | solution.py:325
  108.3 15.0 %collective-permute-start.10 = (bf16[64,128]{1,0:T(8,128)(2,1)}, bf16[64,128]{1,0:T(8,128)(2,1)S(1)}, u32[]{:S(2)}, u32[]{:S(2)}) collective-permute-start(bf16[64,128]{1,0:T(8,128)(2,1)} %get-tuple-element.35), channel_id=1, source_target_pairs={{0,1},{1,2},{2,3},{3,4},{4,5},{5,6},{6,7},{8,9},{9,10},{10,11},{11... | collective-permute-start | bytes 49160 | tf_op jit(solution)/shard_map/ppermute | solution.py:336
  110.2 17.3 %collective-permute-start.11 = (bf16[64,128]{1,0:T(8,128)(2,1)}, bf16[64,128]{1,0:T(8,128)(2,1)S(1)}, u32[]{:S(2)}, u32[]{:S(2)}) collective-permute-start(bf16[64,128]{1,0:T(8,128)(2,1)} %get-tuple-element.36), channel_id=1, source_target_pairs={{1,0},{2,1},{3,2},{4,3},{5,4},{6,5},{7,6},{9,8},{10,9},{11,10},{12... | collective-permute-start | bytes 49160 | tf_op jit(solution)/shard_map/ppermute | solution.py:336
  116.4 23.3 %collective-permute-start.26 = (bf16[576,128]{1,0:T(8,128)(2,1)S(1)}, bf16[576,128]{1,0:T(8,128)(2,1)S(1)}, u32[]{:S(2)}, u32[]{:S(2)}) collective-permute-start(bf16[576,128]{1,0:T(8,128)(2,1)S(1)} %pad_maximum_fusion.1), channel_id=1, source_target_pairs={{0,8},{1,9},{2,10},{3,11},{4,12},{5,13},{6,14},{7,15},{8,0},{9,1},... | collective-permute-start | bytes 442376 | tf_op jit(solution)/shard_map/ppermute | solution.py:325
  122.5 7.2 %collective-permute-start.6 = (bf16[256,128]{1,0:T(8,128)(2,1)}, bf16[256,128]{1,0:T(8,128)(2,1)S(1)}, u32[]{:S(2)}, u32[]{:S(2)}) collective-permute-start(bf16[256,128]{1,0:T(8,128)(2,1)} %get-tuple-element.31), channel_id=1, source_target_pairs={{0,8},{8,0},{16,24},{24,16},{32,40},{40,32},{48,56},{56,48},{64,72... | collective-permute-start | bytes 196616 | tf_op jit(solution)/shard_map/ppermute | solution.py:330
  123.3 6.5 %collective-permute-start.7 = (bf16[256,128]{1,0:T(8,128)(2,1)}, bf16[256,128]{1,0:T(8,128)(2,1)S(1)}, u32[]{:S(2)}, u32[]{:S(2)}) collective-permute-start(bf16[256,128]{1,0:T(8,128)(2,1)} %get-tuple-element.32), channel_id=1, source_target_pairs={{0,16},{8,24},{16,0},{24,8},{32,48},{40,56},{48,32},{56,40},{64,80... | collective-permute-start | bytes 196616 | tf_op jit(solution)/shard_map/ppermute | solution.py:330
  123.3 13.3 %copy-start.4 = (bf16[64,128]{1,0:T(8,128)(2,1)}, bf16[64,128]{1,0:T(8,128)(2,1)S(1)}, u32[]{:S(2)}) copy-start(bf16[64,128]{1,0:T(8,128)(2,1)S(1)} %collective-permute-done.10.prev_ref) | copy-start | bytes 49156
  123.3 8.0 %collective-permute-start.8 = (bf16[256,128]{1,0:T(8,128)(2,1)}, bf16[256,128]{1,0:T(8,128)(2,1)S(1)}, u32[]{:S(2)}, u32[]{:S(2)}) collective-permute-start(bf16[256,128]{1,0:T(8,128)(2,1)} %get-tuple-element.33), channel_id=1, source_target_pairs={{0,32},{8,40},{16,48},{24,56},{32,0},{40,8},{48,16},{56,24},{64,96... | collective-permute-start | bytes 196616 | tf_op jit(solution)/shard_map/ppermute | solution.py:330
  127.6 9.0 %copy-start.5 = (bf16[64,128]{1,0:T(8,128)(2,1)}, bf16[64,128]{1,0:T(8,128)(2,1)S(1)}, u32[]{:S(2)}) copy-start(bf16[64,128]{1,0:T(8,128)(2,1)S(1)} %collective-permute-done.11.next_ref) | copy-start | bytes 49156
  127.6 9.0 %collective-permute-start.9 = (bf16[256,128]{1,0:T(8,128)(2,1)}, bf16[256,128]{1,0:T(8,128)(2,1)S(1)}, u32[]{:S(2)}, u32[]{:S(2)}) collective-permute-start(bf16[256,128]{1,0:T(8,128)(2,1)} %get-tuple-element.34), channel_id=1, source_target_pairs={{0,64},{8,72},{16,80},{24,88},{32,96},{40,104},{48,112},{56,120},{... | collective-permute-start | bytes 196616 | tf_op jit(solution)/shard_map/ppermute | solution.py:330
  129.7 6.9 %copy-start = (bf16[256,128]{1,0:T(8,128)(2,1)}, bf16[256,128]{1,0:T(8,128)(2,1)S(1)}, u32[]{:S(2)}) copy-start(bf16[256,128]{1,0:T(8,128)(2,1)S(1)} %collective-permute-done.6.in0_ref) | copy-start | bytes 196612
  129.7 6.9 %copy-start.1 = (bf16[256,128]{1,0:T(8,128)(2,1)}, bf16[256,128]{1,0:T(8,128)(2,1)S(1)}, u32[]{:S(2)}) copy-start(bf16[256,128]{1,0:T(8,128)(2,1)S(1)} %collective-permute-done.7.in1_ref) | copy-start | bytes 196612
  131.3 5.3 %copy-start.2 = (bf16[256,128]{1,0:T(8,128)(2,1)}, bf16[256,128]{1,0:T(8,128)(2,1)S(1)}, u32[]{:S(2)}) copy-start(bf16[256,128]{1,0:T(8,128)(2,1)S(1)} %collective-permute-done.8.in2_ref) | copy-start | bytes 196612
  136.6 0.6 copy-start.3

commit v2 on v1

v2 whole, which is shorter than its diff:
```python
import functools
import math

import jax
import jax.numpy as jnp
from jax import lax
from jax.experimental import pallas as pl
from jax.experimental.pallas import tpu as pltpu
from jax.sharding import PartitionSpec as P

HB = 64
BF = jnp.bfloat16
F32 = jnp.float32
MESH_SPAN = 1536
NODE_SPAN = 512
MIB = 1024 * 1024


def nn(a, b):
    return lax.dot_general(a, b, (((1,), (0,)), ((), ())), preferred_element_type=F32)


def nt(a, b):
    return lax.dot_general(a, b, (((1,), (1,)), ((), ())), preferred_element_type=F32)


def tn(a, b):
    return lax.dot_general(a, b, (((0,), (0,)), ((), ())), preferred_element_type=F32)


def in_two(values):
    high = values.astype(BF)
    return high, (values - high.astype(F32)).astype(BF)


def wide_nt(a, b):
    high, low = in_two(a)
    return nt(high, b) + nt(low, b)


def wide_nn(a, b):
    high, low = in_two(b)
    return nn(a, high) + nn(a, low)


def identity():
    row = lax.broadcasted_iota(jnp.int32, (128, 128), 0)
    column = lax.broadcasted_iota(jnp.int32, (128, 128), 1)
    return (row == column).astype(BF)


def transposed(a):
    return nt(identity(), a).astype(BF)


def table(count, ids):
    rows = lax.broadcasted_iota(jnp.int32, (count, ids.shape[1]), 0)
    return (rows == ids).astype(BF)


def silu_parts(x):
    s = 0.5 * jnp.tanh(0.5 * x) + 0.5
    return x * s, s * (1.0 + x * (1.0 - s))


def spans(total, size):
    return [slice(first, first + size) for first in range(0, total, size)]


def bound_kernel(lat_ref, bnd_ref, lat_t_ref, bound_t_ref):
    lat_t = transposed(lat_ref[...])
    lat_t_ref[...] = lat_t
    bound_t_ref[...] = nn(lat_t, table(lat_ref.shape[0], bnd_ref[...])).astype(BF)


def mesh_kernel(
    lat_t_ref, before_ref, after_ref, feats_ref, w_ref, edges_ref,
    rows_ref, slope_ref, agg_ref, ext_t_ref, sum_ref,
):
    rows_dev = lat_t_ref.shape[1]
    rim = transposed(jnp.concatenate([before_ref[...], after_ref[...]], axis=0))
    ext_t_ref[:, :rows_dev] = lat_t_ref[...]
    ext_t_ref[:, rows_dev:] = rim
    w_t = jnp.concatenate([transposed(w_ref[0]), transposed(w_ref[1])], axis=1)
    w2_t = transposed(w_ref[2])
    for at in spans(edges_ref.shape[1], MESH_SPAN):
        ids = edges_ref[0:1, at] - HB
        ids = jnp.where(ids < 0, ids + rows_dev + HB, jnp.where(ids < rows_dev, ids, ids + HB))
        rows_ref[:128, at] = nn(ext_t_ref[...], table(rows_dev + 2 * HB, ids)).astype(BF)
        hits = table(rows_dev, edges_ref[1:2, at])
        rows_ref[128:, at] = nn(lat_t_ref[...], hits).astype(BF)
        x = nn(w_t, rows_ref[:, at]) + nt(w2_t, feats_ref[at, :])
        message, slope = silu_parts(x)
        slope_ref[:, at] = slope
        part = nt(hits, message.astype(BF))
        if at.start:
            part = part + sum_ref[...]
        sum_ref[...] = part
    agg_ref[...] = sum_ref[...].astype(BF)


def main_kernel(
    counts_ref, core_ref, lat_ref, lat_t_ref, bound_t_ref, far0_ref, far1_ref, far2_ref,
    far3_ref, rows_ref, slope_m_ref, agg_ref, feats_ref, cot_ref, w_ref, edges_ref,
    contacts_ref, bnd_ref,
    new_ref, kept_ref, sent_ref, dm_ref, dc_ref, dn_ref,
    aggb_ref, slope_c_ref, both_ref, gw_ref, aggc_ref, dagg_t_ref, daggc_t_ref,
    *, scale,
):
    rows_dev = lat_ref.shape[0]
    bound_count = bnd_ref.shape[1]
    fars = (far0_ref, far1_ref, far2_ref, far3_ref)
    rounds = len(fars)
    round_rows = contacts_ref.shape[1] // rounds
    w_t = jnp.concatenate([transposed(w_ref[3]), transposed(w_ref[4])], axis=1)

    for r, at in enumerate(spans(contacts_ref.shape[1], round_rows)):
        place = lax.broadcasted_iota(jnp.int32, (1, round_rows), 1)
        live = (place < counts_ref[0, r]).astype(F32)
        hits = table(bound_count, contacts_ref[0:1, at])
        both_ref[:128, at] = nn(bound_t_ref[...], hits).astype(BF)
        both_ref[128:, at] = nn(
            fars[r][...], table(bound_count, contacts_ref[1:2, at])
        ).astype(BF)
        message, slope = silu_parts(nn(w_t, both_ref[:, at]))
        slope_c_ref[:, at] = slope * live
        part = nt(hits, (message * live).astype(BF))
        if r:
            part = part + aggb_ref[...]
        aggb_ref[...] = part

    bound_table = table(rows_dev, bnd_ref[...])
    aggc_ref[...] = nn(bound_table, aggb_ref[...].astype(BF)).astype(BF)
    for at in spans(rows_dev, NODE_SPAN):
        lat = lat_ref[at, :]
        cot = cot_ref[at, :]
        agg = agg_ref[at, :]
        aggc = aggc_ref[at, :]
        x = nn(lat, w_ref[5]) + nn(agg, w_ref[6]) + nn(aggc, w_ref[7])
        message, slope = silu_parts(x)
        hidden = message.astype(BF)
        new_ref[at, :] = (lat.astype(F32) + nn(hidden, w_ref[8])).astype(BF)
        d_node = (nt(cot, w_ref[8]) * slope).astype(BF)
        dn_ref[at, :] = d_node
        dagg_t_ref[:, at] = nt(w_ref[6], d_node).astype(BF)
        daggc_t_ref[:, at] = nt(w_ref[7], d_node).astype(BF)
        parts = [
            nn(lat_t_ref[:, at], d_node), tn(agg, d_node), tn(aggc, d_node), tn(hidden, cot)
        ]
        for k, part in enumerate(parts):
            where = slice(640 + 128 * k, 768 + 128 * k)
            gw_ref[where, :] = part + gw_ref[where, :] if at.start else part

    for at in spans(edges_ref.shape[1], MESH_SPAN):
        gathered = nn(dagg_t_ref[...], table(rows_dev, edges_ref[1:2, at]))
        d = (gathered * slope_m_ref[:, at]).astype(BF)
        dm_ref[:, at] = d
        pair = nt(rows_ref[:, at], d)
        own = nn(d, feats_ref[at, :])
        gw_ref[0:256, :] = pair + gw_ref[0:256, :] if at.start else pair
        gw_ref[256:384, :] = own + gw_ref[256:384, :] if at.start else own

    gw_ref[256:384, :] = gw_ref[256:384, :].T
    dbg_t = nn(daggc_t_ref[...], bound_table).astype(BF)
    for r, at in enumerate(spans(contacts_ref.shape[1], round_rows)):
        gathered = nn(dbg_t, table(bound_count, contacts_ref[0:1, at]))
        d = (gathered * slope_c_ref[:, at]).astype(BF)
        dc_ref[:, at] = d
        pair = nt(both_ref[:, at], d)
        gw_ref[384:640, :] = pair + gw_ref[384:640, :] if r else pair

    half = gw_ref.shape[0] // 2
    core = core_ref[0]
    kept_ref[...] = gw_ref[pl.ds(pl.multiple_of(core * half, 64), half), :] * scale
    sent = gw_ref[pl.ds(pl.multiple_of((1 - core) * half, 64), half), :] * scale
    sent_ref[...] = sent.astype(BF)


def contact_back_kernel(
    w_ref, contacts_ref, dc_ref, far0_ref, far1_ref, far2_ref, far3_ref, own_ref
):
    outs = (far0_ref, far1_ref, far2_ref, far3_ref)
    bound_count = own_ref.shape[0]
    for r, at in enumerate(spans(contacts_ref.shape[1], contacts_ref.shape[1] // len(outs))):
        d = dc_ref[:, at]
        part = nt(table(bound_count, contacts_ref[0:1, at]), d)
        own_ref[...] = part + own_ref[...] if r else part
        far = nt(table(bound_count, contacts_ref[1:2, at]), d)
        outs[r][...] = wide_nt(far, w_ref[4]).astype(BF)
    own_ref[...] = wide_nt(own_ref[...], w_ref[3])


def mesh_back_kernel(
    w_ref, edges_ref, dm_ref, dn_ref, cot_ref, grad_ref, low_ref, high_ref, send_ref, recv_ref
):
    rows_dev = cot_ref.shape[0]
    for at in spans(edges_ref.shape[1], MESH_SPAN):
        d = dm_ref[:, at]
        send = nt(table(rows_dev + 2 * HB, edges_ref[0:1, at]), d)
        recv = nt(table(rows_dev, edges_ref[1:2, at]), d)
        send_ref[...] = send + send_ref[...] if at.start else send
        recv_ref[...] = recv + recv_ref[...] if at.start else recv
    low_ref[...] = wide_nt(send_ref[:HB, :], w_ref[0]).astype(BF)
    high_ref[...] = wide_nt(send_ref[HB + rows_dev :, :], w_ref[0]).astype(BF)
    grad_ref[...] = (
        cot_ref[...].astype(F32)
        + nt(dn_ref[...], w_ref[5])
        + wide_nt(recv_ref[...], w_ref[1])
        + wide_nt(send_ref[HB : HB + rows_dev, :], w_ref[0])
    )


def last_kernel(
    part_ref, own_ref, in0_ref, in1_ref, in2_ref, in3_ref, prev_ref, next_ref, bnd_ref, out_ref
):
    rows_dev = part_ref.shape[0]
    total = own_ref[...]
    for ref in (in0_ref, in1_ref, in2_ref, in3_ref):
        total = total + ref[...].astype(F32)
    out_ref[...] = part_ref[...] + wide_nn(table(rows_dev, bnd_ref[...]), total)
    out_ref[:HB, :] += prev_ref[...].astype(F32)
    out_ref[rows_dev - HB :, :] += next_ref[...].astype(F32)


def call(kernel, outs, args, scratch=(), smem=0, flops=0, mib=32):
    spec = pl.BlockSpec(memory_space=pltpu.VMEM)
    return pl.pallas_call(
        kernel,
        out_shape=[jax.ShapeDtypeStruct(shape, kind) for shape, kind in outs],
        in_specs=[pl.BlockSpec(memory_space=pltpu.SMEM)] * smem + [spec] * (len(args) - smem),
        out_specs=[spec] * len(outs),
        scratch_shapes=[pltpu.VMEM(shape, kind) for shape, kind in scratch],
        compiler_params=pltpu.CompilerParams(vmem_limit_bytes=mib * MIB),
        cost_estimate=pl.CostEstimate(flops=flops, bytes_accessed=4000000, transcendentals=0),
    )(*args)


def exchanged(block, mask_x=0, mask_y=0, mask_z=0, mask_core=0):
    route = []
    for region in range(32):
        for panel in range(8):
            other_region = region ^ ((mask_x >> 1) << 4 | mask_z << 1 | mask_core)
            other_panel = panel ^ ((mask_x & 1) << 2 | mask_y)
            route.append((region * 8 + panel, other_region * 8 + other_panel))
    return lax.ppermute(block, ("region", "panel"), route)


def swapped(block, bit):
    size = lax.axis_size("region")
    return lax.ppermute(block, "region", [(i, i ^ (1 << bit)) for i in range(size)])


def shifted(array, by):
    length = lax.axis_size("panel")
    pairs = [(i, i + by) for i in range(length) if 0 <= i + by < length]
    return lax.ppermute(array, "panel", pairs)


def wide(block):
    return block.astype(F32)


def four_sum(block, name):
    one, two, three = [wide(exchanged(block, **{name: mask})) for mask in (1, 2, 3)]
    return ((wide(block) + one) + (two + three)).astype(BF)


def summed_over_y(kept, other, row_y):
    part = kept.shape[0] // 4
    block = (kept + wide(other)).astype(BF)
    pieces = [
        lax.dynamic_slice_in_dim(block, (row_y ^ mask) * part, part, 0) for mask in range(4)
    ]
    return pieces


def ordered_by_y(found, row_y):
    odd, high = row_y % 2 == 1, row_y >= 2
    low_pair = [jnp.where(odd, found[1], found[0]), jnp.where(odd, found[0], found[1])]
    high_pair = [jnp.where(odd, found[3], found[2]), jnp.where(odd, found[2], found[3])]
    ordered = [jnp.where(high, b, a) for a, b in zip(low_pair, high_pair)]
    ordered += [jnp.where(high, a, b) for a, b in zip(low_pair, high_pair)]
    return jnp.concatenate(ordered, axis=0)


def tie(*arrays):
    return lax.optimization_barrier(arrays)


def shards(
    latents, edge_feats, weights, cotangent, mesh_edges, boundary, contact_edges, contact_counts
):
    rows_dev, width = latents.shape
    bound_count = boundary.shape[0]
    rounds = contact_counts.shape[1]
    edge_count = mesh_edges.shape[1]
    contact_count = contact_edges.shape[1]
    bnd = boundary.reshape(1, bound_count)
    core = lax.axis_index("region") % 2
    row_y = lax.axis_index("panel") % 4
    scale = 1.0 / math.sqrt(rows_dev * lax.axis_size("region") * lax.axis_size("panel"))

    before = shifted(latents[rows_dev - HB :], 1)
    after = shifted(latents[:HB], -1)
    lat_t, bound_t = call(
        bound_kernel, [((width, rows_dev), BF), ((width, bound_count), BF)], [latents, bnd], mib=8
    )
    fars = [swapped(bound_t, r) for r in range(rounds)]
    rows, slope, agg = call(
        mesh_kernel,
        [((2 * width, edge_count), BF), ((width, edge_count), F32), ((rows_dev, width), BF)],
        [lat_t, before, after, edge_feats, weights, mesh_edges],
        [((width, rows_dev + 2 * HB), BF), ((rows_dev, width), F32)],
        flops=6 * 10**9,
    )
    new_rows, kept, sent, d_mesh, d_contact, d_node = call(
        functools.partial(main_kernel, scale=scale),
        [
            ((rows_dev, width), BF),
            ((9 * width // 2, width), F32),
            ((9 * width // 2, width), BF),
            ((width, edge_count), BF),
            ((width, contact_count), BF),
            ((rows_dev, width), BF),
        ],
        [contact_counts, core.reshape(1), latents, lat_t, bound_t, *fars, rows, slope, agg]
        + [edge_feats, cotangent, weights, mesh_edges, contact_edges, bnd],
        [
            ((bound_count, width), F32),
            ((width, contact_count), F32),
            ((2 * width, contact_count), BF),
            ((9 * width, width), F32),
            ((rows_dev, width), BF),
            ((width, rows_dev), BF),
            ((width, rows_dev), BF),
        ],
        smem=2,
        flops=8 * 10**9,
        mib=40,
    )
    other = exchanged(sent, mask_core=1)
    other, d_contact = tie(other, d_contact)
    pieces = summed_over_y(kept, other, row_y)
    *far_grads, own_grad = call(
        contact_back_kernel,
        [((bound_count, width), BF)] * rounds + [((bound_count, width), F32)],
        [weights, contact_edges, d_contact],
        flops=2 * 10**9,
    )
    one, two, three = [wide(exchanged(pieces[mask], mask_y=mask)) for mask in (1, 2, 3)]
    block = ((wide(pieces[0]) + one) + (two + three)).astype(BF)
    block, d_mesh, *far_grads = tie(block, d_mesh, *far_grads)
    part, low, high = call(
        mesh_back_kernel,
        [((rows_dev, width), F32), ((HB, width), BF), ((HB, width), BF)],
        [weights, mesh_edges, d_mesh, d_node, cotangent],
        [((rows_dev + 2 * HB, width), F32), ((rows_dev, width), F32)],
        flops=3 * 10**9,
    )
    block = four_sum(block, "mask_x")
    block, low, high, *far_grads = tie(block, low, high, *far_grads)
    incoming = [swapped(far_grads[r], r) for r in range(rounds)]
    block = four_sum(block, "mask_z")
    block, *incoming = tie(block, *incoming)
    from_prev = shifted(high, 1)
    from_next = shifted(low, -1)
    block = (wide(block) + wide(exchanged(block, mask_z=4))).astype(BF)
    block, from_prev, from_next = tie(block, from_prev, from_next)
    (grad_rows,) = call(
        last_kernel,
        [((rows_dev, width), F32)],
        [part, own_grad, *incoming, from_prev, from_next, bnd],
        flops=10**8,
        mib=8,
    )
    found = [block] + [exchanged(block, mask_y=mask) for mask in (1, 2, 3)]
    block = ordered_by_y(found, row_y)
    other = exchanged(block, mask_core=1)
    first = jnp.where(core == 1, other, block)
    second = jnp.where(core == 1, block, other)
    summed = wide(jnp.concatenate([first, second], axis=0)).reshape(9, width, width)
    return (new_rows, grad_rows, summed)


def solution(mesh):
    blocks = P(("region", "panel"), None)
    placed = (
        blocks,
        blocks,
        P(),
        blocks,
        P(None, ("region", "panel")),
        P(("region", "panel")),
        P(None, ("region", "panel")),
        blocks,
    )
    return jax.shard_map(
        shards, mesh=mesh, in_specs=placed, out_specs=(blocks, blocks, P()), check_vma=False
    )
```

time: 141 us -> 105 us (0.74)
  the two profiles are of different devices: /device:TPU:6 before, /device:TPU:1 now
where the time goes in v2:
time: 105 us; the launch traced here: 103 us
  starting transfers between devices  49.7 us (47%)
  Pallas kernels  27.9 us (27%)
  waiting for transfers between devices  15.2 us (14%)
  local copies, waits for them, and re-layouts  8.18 us (8%)
  other arithmetic  1.12 us (1%)
    pallas_call x6, Pallas kernels, call(): pl.pallas_call(kernel, out_shape=[jax.ShapeDtypeStruct(shape, kind) for s...  27.9 us
    ppermute x15, starting transfers between devices, exchanged(): return lax.ppermute(block, ('region', 'panel'), route)  27.2 us
    ppermute x8, starting transfers between devices, swapped(): lax.ppermute(block, 'region', [(i, i ^ 1 << bit) for i in range(size)])  14.6 us
    ppermute x4, starting transfers between devices, shifted(): return lax.ppermute(array, 'panel', pairs)  7.88 us
    ppermute x15, waiting for transfers between devices, exchanged(): return lax.ppermute(block, ('region', 'panel'), route)  7.71 us
    unnamed x30, local copies, waits for them, and re-layouts  7.42 us
    ppermute x8, waiting for transfers between devices, swapped(): lax.ppermute(block, 'region', [(i, i ^ 1 << bit) for i in range(size)])  7.26 us
  transfers between devices with their start and end apart: 27, of which 7 were waited for; matrix products, arithmetic and copies ran while one was open for 0% of the time, Pallas kernels for 16%

profile of v2, /device:TPU:1, one launch (start us, length us, event | category | flops | bytes accessed | tf_op | source)
XLA Modules:
  0.0 103.1 jit_solution(17985570682240110281)
XLA Ops:
  0.6 0.7 fusion
  1.4 4.0 %collective-permute-start.4 = (bf16[64,128]{1,0:T(8,128)(2,1)S(1)}, bf16[64,128]{1,0:T(8,128)(2,1)S(1)}, u32[]{:S(2)}, u32[]{:S(2)}) collective-permute-start(bf16[64,128]{1,0:T(8,128)(2,1)S(1)} %get-tuple-element.90), channel_id=1, source_target_pairs={{0,1},{1,2},{2,3},{3,4},{4,5},{5,6},{6,7},{8,9},{9,10},{10,11},{11... | collective-permute-start | bytes 49160 | tf_op jit(solution)/shard_map/ppermute | solution.py:256
  5.4 1.3 %collective-permute-start.5 = (bf16[64,128]{1,0:T(8,128)(2,1)S(1)}, bf16[64,128]{1,0:T(8,128)(2,1)S(1)}, u32[]{:S(2)}, u32[]{:S(2)}) collective-permute-start(bf16[64,128]{1,0:T(8,128)(2,1)S(1)} %get-tuple-element.89), channel_id=1, source_target_pairs={{1,0},{2,1},{3,2},{4,3},{5,4},{6,5},{7,6},{9,8},{10,9},{11,10},{12... | collective-permute-start | bytes 49160 | tf_op jit(solution)/shard_map/ppermute | solution.py:256
  6.7 0.0 copy-start
  6.7 0.9 copy-done
  7.7 0.7 copy-done.2
  8.3 0.4 shard_map.103
  8.7 1.0 %collective-permute-start = (bf16[128,256]{1,0:T(8,128)(2,1)S(1)}, bf16[128,256]{1,0:T(8,128)(2,1)S(1)}, u32[]{:S(2)}, u32[]{:S(2)}) collective-permute-start(bf16[128,256]{1,0:T(8,128)(2,1)S(1)} %get-tuple-element.46.bound_t_ref), channel_id=1, source_target_pairs={{0,8},{8,0},{16,24},{24,16},{32,40},{40,32},{48,56},{56,48},{64,72... | collective-permute-start | bytes 196616 | tf_op jit(solution)/shard_map/ppermute | solution.py:250
  9.8 1.7 %collective-permute-start.1 = (bf16[128,256]{1,0:T(8,128)(2,1)S(1)}, bf16[128,256]{1,0:T(8,128)(2,1)S(1)}, u32[]{:S(2)}, u32[]{:S(2)}) collective-permute-start(bf16[128,256]{1,0:T(8,128)(2,1)S(1)} %get-tuple-element.46.bound_t_ref), channel_id=1, source_target_pairs={{0,16},{8,24},{16,0},{24,8},{32,48},{40,56},{48,32},{56,40},{64,80... | collective-permute-start | bytes 196616 | tf_op jit(solution)/shard_map/ppermute | solution.py:250
  11.4 3.0 %collective-permute-start.2 = (bf16[128,256]{1,0:T(8,128)(2,1)S(1)}, bf16[128,256]{1,0:T(8,128)(2,1)S(1)}, u32[]{:S(2)}, u32[]{:S(2)}) collective-permute-start(bf16[128,256]{1,0:T(8,128)(2,1)S(1)} %get-tuple-element.46.bound_t_ref), channel_id=1, source_target_pairs={{0,32},{8,40},{16,48},{24,56},{32,0},{40,8},{48,16},{56,24},{64,96... | collective-permute-start | bytes 196616 | tf_op jit(solution)/shard_map/ppermute | solution.py:250
  14.4 0.0 collective-permute-done.4.before_ref
  14.4 4.2 %collective-permute-start.3 = (bf16[128,256]{1,0:T(8,128)(2,1)S(1)}, bf16[128,256]{1,0:T(8,128)(2,1)S(1)}, u32[]{:S(2)}, u32[]{:S(2)}) collective-permute-start(bf16[128,256]{1,0:T(8,128)(2,1)S(1)} %get-tuple-element.46.bound_t_ref), channel_id=1, source_target_pairs={{0,64},{8,72},{16,80},{24,88},{32,96},{40,104},{48,112},{56,120},{... | collective-permute-start | bytes 196616 | tf_op jit(solution)/shard_map/ppermute | solution.py:250
  18.6 1.1 %copy-done.4 = bf16[3072,128]{1,0:T(8,128)(2,1)S(1)} copy-done((bf16[3072,128]{1,0:T(8,128)(2,1)S(1)}, bf16[3072,128]{1,0:T(8,128)(2,1)}, u32[]{:S(2)}) %copy-start.4) | copy-done | bytes 786456
  19.8 1.0 copy-done.6
  20.7 0.7 copy-done.10
  21.5 0.0 copy-start.8
  21.5 0.0 copy-start.9
  21.5 0.0 copy-start.12
  21.5 6.7 %shard_map.104 = (bf16[256,3072]{1,0:T(8,128)(2,1)S(1)}, f32[128,3072]{1,0:T(8,128)S(1)}, bf16[1024,128]{1,0:T(8,128)(2,1)S(1)}) custom-call(bf16[128,1024]{1,0:T(8,128)(2,1)S(1)} %get-tuple-element.45.lat_t_ref, bf16[64,128]{1,0:T(8,128)(2,1)S(1)} %collective-permute-done.4.before_ref, bf16[64,128]{1,0:T(8,128)(2,1)S(1)} %collective-permute-done.5.after_ref, ...), custom_call_target="tpu_custom_call" | custom-call | flops 6000000000 | bytes 4000000 | tf_op jit(solution)/shard_map/pallas_call | solution.py:227
  28.2 0.0 collective-permute-done.1.far1_ref
  28.3 11.9 %shard_map.105 = (bf16[1024,128]{1,0:T(8,128)(2,1)}, f32[576,128]{1,0:T(8,128)S(1)}, bf16[576,128]{1,0:T(8,128)(2,1)S(1)}, bf16[128,3072]{1,0:T(8,128)(2,1)S(1)}...) custom-call(s32[1,4]{1,0:T(1,128)S(1)} %copy-done.12, s32[1]{0:T(128)} %bitcast.core_ref, ...), custom_call_target="tpu_custom_call" | custom-call | flops 8000000000 | bytes 4000000 | tf_op jit(solution)/shard_map/pallas_call | solution.py:227
  40.2 1.3 %copy-done.13 = bf16[128,8192]{1,0:T(8,128)(2,1)} copy-done((bf16[128,8192]{1,0:T(8,128)(2,1)}, bf16[128,8192]{1,0:T(8,128)(2,1)S(1)}, u32[]{:S(2)}) %copy-start.13) | copy-done | bytes 2097176
  41.6 0.9 collective-permute-start.6
  42.5 1.0 collective-permute-done.6
  43.5 2.5 %collective-permute-start.7 = (bf16[144,128]{1,0:T(8,128)(2,1)S(1)}, bf16[144,128]{1,0:T(8,128)(2,1)S(1)}, u32[]{:S(2)}, u32[]{:S(2)}) collective-permute-start(bf16[144,128]{1,0:T(8,128)(2,1)S(1)} %get-tuple-element.95), channel_id=1, source_target_pairs={{0,1},{1,0},{2,3},{3,2},{4,5},{5,4},{6,7},{7,6},{8,9},{9,8},{10,11... | collective-permute-start | bytes 110600 | tf_op jit(solution)/shard_map/ppermute | solution.py:245
  46.0 2.6 %collective-permute-start.8 = (bf16[144,128]{1,0:T(8,128)(2,1)S(1)}, bf16[144,128]{1,0:T(8,128)(2,1)S(1)}, u32[]{:S(2)}, u32[]{:S(2)}) collective-permute-start(bf16[144,128]{1,0:T(8,128)(2,1)S(1)} %get-tuple-element.97), channel_id=1, source_target_pairs={{0,2},{1,3},{2,0},{3,1},{4,6},{5,7},{6,4},{7,5},{8,10},{9,11},{10,... | collective-permute-start | bytes 110600 | tf_op jit(solution)/shard_map/ppermute | solution.py:245
  48.6 0.0 collective-permute-start.9
  48.6 1.6 %copy-done.14 = bf16[128,8192]{1,0:T(8,128)(2,1)S(1)} copy-done((bf16[128,8192]{1,0:T(8,128)(2,1)S(1)}, bf16[128,8192]{1,0:T(8,128)(2,1)}, u32[]{:S(2)}) %copy-start.14) | copy-done | bytes 2097176
  50.2 2.8 %shard_map.106 = (bf16[256,128]{1,0:T(8,128)(2,1)S(1)}, bf16[256,128]{1,0:T(8,128)(2,1)S(1)}, bf16[256,128]{1,0:T(8,128)(2,1)S(1)}, bf16[256,128]{1,0:T(8,128)(2,1)S(1)}, f32[256,128]{1,0:T(8,128)S(1)}) custom-call(bf16[9,128,128]{2,1,0:T(8,128)(2,1)S(1)} %copy-done.7, s32[2,8192]{1,0:T(2,128)S(1)} %copy-done.9, bf16[128,8192]{1,0:T(8,128)(2,1)S(1)} %copy-done.14), custom_call_target="tpu_custom_call" | custom-call | flops 2000000000 | bytes 4000000 | tf_op jit(solution)/shard_map/pallas_call | solution.py:227
  53.0 0.0 collective-permute-done.7
  53.0 0.0 collective-permute-done.9
  53.1 3.3 %collective-permute-start.10 = (bf16[144,128]{1,0:T(8,128)(2,1)S(1)}, bf16[144,128]{1,0:T(8,128)(2,1)S(1)}, u32[]{:S(2)}, u32[]{:S(2)}) collective-permute-start(bf16[144,128]{1,0:T(8,128)(2,1)S(1)} %add_convert_fusion.4), channel_id=1, source_target_pairs={{0,4},{1,5},{2,6},{3,7},{4,0},{5,1},{6,2},{7,3},{8,12},{9,13},{10,... | collective-permute-start | bytes 110600 | tf_op jit(solution)/shard_map/ppermute | solution.py:245
  56.4 2.5 %collective-permute-start.11 = (bf16[144,128]{1,0:T(8,128)(2,1)S(1)}, bf16[144,128]{1,0:T(8,128)(2,1)S(1)}, u32[]{:S(2)}, u32[]{:S(2)}) collective-permute-start(bf16[144,128]{1,0:T(8,128)(2,1)S(1)} %add_convert_fusion.4), channel_id=1, source_target_pairs={{0,128},{1,129},{2,130},{3,131},{4,132},{5,133},{6,134},{7,135},{8... | collective-permute-start | bytes 110600 | tf_op jit(solution)/shard_map/ppermute | solution.py:245
  58.9 0.0 collective-permute-start.12
  58.9 4.9 %shard_map.107 = (f32[1024,128]{1,0:T(8,128)S(1)}, bf16[64,128]{1,0:T(8,128)(2,1)S(1)}, bf16[64,128]{1,0:T(8,128)(2,1)S(1)}) custom-call(bf16[9,128,128]{2,1,0:T(8,128)(2,1)S(1)} %copy-done.7, s32[2,3072]{1,0:T(2,128)S(1)} %copy-done.11, bf16[128,3072]{1,0:T(8,128)(2,1)S(1)} %get-tuple-element.61.dm_ref, bf16[1024,128]{1,0:T(8,128)(2,1)S(1)} %get-tuple-element.62.dn_ref, ...), custom_call_target="tpu_custom_call" | custom-call | flops 3000000000 | bytes 4000000 | tf_op jit(solution)/shard_map/pallas_call | solution.py:227
  63.8 0.0 collective-permute-done.11
  63.8 0.0 collective-permute-done.12
  63.9 0.8 collective-permute-start.13
  64.7 1.2 %collective-permute-start.14 = (bf16[144,128]{1,0:T(8,128)(2,1)S(1)}, bf16[144,128]{1,0:T(8,128)(2,1)S(1)}, u32[]{:S(2)}, u32[]{:S(2)}) collective-permute-start(bf16[144,128]{1,0:T(8,128)(2,1)S(1)} %add_convert_fusion.3), channel_id=1, source_target_pairs={{0,32},{1,33},{2,34},{3,35},{4,36},{5,37},{6,38},{7,39},{8,40},{9,... | collective-permute-start | bytes 110600 | tf_op jit(solution)/shard_map/ppermute | solution.py:245
  65.9 1.6 %collective-permute-start.15 = (bf16[144,128]{1,0:T(8,128)(2,1)S(1)}, bf16[144,128]{1,0:T(8,128)(2,1)S(1)}, u32[]{:S(2)}, u32[]{:S(2)}) collective-permute-start(bf16[144,128]{1,0:T(8,128)(2,1)S(1)} %add_convert_fusion.3), channel_id=1, source_target_pairs={{0,48},{1,49},{2,50},{3,51},{4,52},{5,53},{6,54},{7,55},{8,56},{9,... | collective-permute-start | bytes 110600 | tf_op jit(solution)/shard_map/ppermute | solution.py:245
  67.5 2.8 %collective-permute-start.16 = (bf16[256,128]{1,0:T(8,128)(2,1)S(1)}, bf16[256,128]{1,0:T(8,128)(2,1)S(1)}, u32[]{:S(2)}, u32[]{:S(2)}) collective-permute-start(bf16[256,128]{1,0:T(8,128)(2,1)S(1)} %get-tuple-element.73), channel_id=1, source_target_pairs={{0,8},{8,0},{16,24},{24,16},{32,40},{40,32},{48,56},{56,48},{64,72... | collective-permute-start | bytes 196616 | tf_op jit(solution)/shard_map/ppermute | solution.py:250
  70.3 0.0 collective-permute-start.17
  70.3 1.9 %collective-permute-start.18 = (bf16[256,128]{1,0:T(8,128)(2,1)S(1)}, bf16[256,128]{1,0:T(8,128)(2,1)S(1)}, u32[]{:S(2)}, u32[]{:S(2)}) collective-permute-start(bf16[256,128]{1,0:T(8,128)(2,1)S(1)} %get-tuple-element.75), channel_id=1, source_target_pairs={{0,32},{8,40},{16,48},{24,56},{32,0},{40,8},{48,16},{56,24},{64,96... | collective-permute-start | bytes 196616 | tf_op jit(solution)/shard_map/ppermute | solution.py:250
  72.2 0.0 collective-permute-done.14
  72.2 0.0 collective-permute-start.19
  72.2 0.0 collective-permute-done.15
  72.3 0.0 collective-permute-done.16.in0_ref
  72.3 3.3 %collective-permute-done.17.in1_ref = bf16[256,128]{1,0:T(8,128)(2,1)S(1)} collective-permute-done((bf16[256,128]{1,0:T(8,128)(2,1)S(1)}, bf16[256,128]{1,0:T(8,128)(2,1)S(1)}, u32[]{:S(2)}, u32[]{:S(2)}) %collective-permute-start.17) | collective-permute-done | bytes 65568 | tf_op jit(solution)/shard_map/ppermute | solution.py:250
  75.6 3.9 %collective-permute-done.19.in3_ref = bf16[256,128]{1,0:T(8,128)(2,1)S(1)} collective-permute-done((bf16[256,128]{1,0:T(8,128)(2,1)S(1)}, bf16[256,128]{1,0:T(8,128)(2,1)S(1)}, u32[]{:S(2)}, u32[]{:S(2)}) %collective-permute-start.19) | collective-permute-done | bytes 65568 | tf_op jit(solution)/shard_map/ppermute | solution.py:250
  79.5 1.2 %collective-permute-start.20 = (bf16[144,128]{1,0:T(8,128)(2,1)S(1)}, bf16[144,128]{1,0:T(8,128)(2,1)S(1)}, u32[]{:S(2)}, u32[]{:S(2)}) collective-permute-start(bf16[144,128]{1,0:T(8,128)(2,1)S(1)} %add_convert_fusion.2), channel_id=1, source_target_pairs={{0,64},{1,65},{2,66},{3,67},{4,68},{5,69},{6,70},{7,71},{8,72},{9,... | collective-permute-start | bytes 110600 | tf_op jit(solution)/shard_map/ppermute | solution.py:245
  80.7 1.3 %collective-permute-start.21 = (bf16[64,128]{1,0:T(8,128)(2,1)S(1)}, bf16[64,128]{1,0:T(8,128)(2,1)S(1)}, u32[]{:S(2)}, u32[]{:S(2)}) collective-permute-start(bf16[64,128]{1,0:T(8,128)(2,1)S(1)} %get-tuple-element.82), channel_id=1, source_target_pairs={{0,1},{1,2},{2,3},{3,4},{4,5},{5,6},{6,7},{8,9},{9,10},{10,11},{11... | collective-permute-start | bytes 49160 | tf_op jit(solution)/shard_map/ppermute | solution.py:256
  82.0 1.3 %collective-permute-start.22 = (bf16[64,128]{1,0:T(8,128)(2,1)S(1)}, bf16[64,128]{1,0:T(8,128)(2,1)S(1)}, u32[]{:S(2)}, u32[]{:S(2)}) collective-permute-start(bf16[64,128]{1,0:T(8,128)(2,1)S(1)} %get-tuple-element.83), channel_id=1, source_target_pairs={{1,0},{2,1},{3,2},{4,3},{5,4},{6,5},{7,6},{9,8},{10,9},{11,10},{12... | collective-permute-start | bytes 49160 | tf_op jit(solution)/shard_map/ppermute | solution.py:256
  83.3 2.9 %collective-permute-done.20 = bf16[144,128]{1,0:T(8,128)(2,1)S(1)} collective-permute-done((bf16[144,128]{1,0:T(8,128)(2,1)S(1)}, bf16[144,128]{1,0:T(8,128)(2,1)S(1)}, u32[]{:S(2)}, u32[]{:S(2)}) %collective-permute-start.20) | collective-permute-done | bytes 36896 | tf_op jit(solution)/shard_map/ppermute | solution.py:245
  86.3 0.0 collective-permute-done.21.prev_ref
  86.3 0.2 collective-permute-done.22.next_ref
  86.5 5.4 %collective-permute-start.23 = (bf16[144,128]{1,0:T(8,128)(2,1)S(1)}, bf16[144,128]{1,0:T(8,128)(2,1)S(1)}, u32[]{:S(2)}, u32[]{:S(2)}) collective-permute-start(bf16[144,128]{1,0:T(8,128)(2,1)S(1)} %add_convert_fusion.1), channel_id=1, source_target_pairs={{0,3},{1,2},{2,1},{3,0},{4,7},{5,6},{6,5},{7,4},{8,11},{9,10},{10,... | collective-permute-start | bytes 110600 | tf_op jit(solution)/shard_map/ppermute | solution.py:245
  91.9 0.0 collective-permute-start.24
  91.9 0.6 collective-permute-start.25
  92.5 0.8 collective-permute-done.23
  93.2 3.0 %collective-permute-done.24 = bf16[144,128]{1,0:T(8,128)(2,1)S(1)} collective-permute-done((bf16[144,128]{1,0:T(8,128)(2,1)S(1)}, bf16[144,128]{1,0:T(8,128)(2,1)S(1)}, u32[]{:S(2)}, u32[]{:S(2)}) %collective-permute-start.24) | collective-permute-done | bytes 36896 | tf_op jit(solution)/shard_map/ppermute | solution.py:245
  96.2 4.6 %collective-permute-start.26 = (bf16[576,128]{1,0:T(8,128)(2,1)S(1)}, bf16[576,128]{1,0:T(8,128)(2,1)S(1)}, u32[]{:S(2)}, u32[]{:S(2)}) collective-permute-start(bf16[576,128]{1,0:T(8,128)(2,1)S(1)} %pad_maximum_fusion.1), channel_id=1, source_target_pairs={{0,8},{1,9},{2,10},{3,11},{4,12},{5,13},{6,14},{7,15},{8,0},{9,1},... | collective-permute-start | bytes 442376 | tf_op jit(solution)/shard_map/ppermute | solution.py:245
  100.9 1.2 %shard_map.108 = f32[1024,128]{1,0:T(8,128)} custom-call(f32[1024,128]{1,0:T(8,128)S(1)} %get-tuple-element.63.part_ref, f32[256,128]{1,0:T(8,128)S(1)} %get-tuple-element.64.own_ref, bf16[256,128]{1,0:T(8,128)(2,1)S(1)} %collective-permute-done.16.in0_ref, bf16[256,128]{1,0:T(8,128)(2,1)S(1)} %collective-permute-done.17.in1_ref, ...), custom_call_target="tpu_custom_call" | custom-call | flops 100000000 | bytes 4000000 | tf_op jit(solution)/shard_map/pallas_call | solution.py:227
  102.1 0.1 broadcast_select_fusion.1
  102.2 0.9 convert.1
  (38 shorter events, 0.3 us)
Async XLA Ops:
  1.4 13.1 %collective-permute-start.4 = (bf16[64,128]{1,0:T(8,128)(2,1)S(1)}, bf16[64,128]{1,0:T(8,128)(2,1)S(1)}, u32[]{:S(2)}, u32[]{:S(2)}) collective-permute-start(bf16[64,128]{1,0:T(8,128)(2,1)S(1)} %get-tuple-element.90), channel_id=1, source_target_pairs={{0,1},{1,2},{2,3},{3,4},{4,5},{5,6},{6,7},{8,9},{9,10},{10,11},{11... | collective-permute-start | bytes 49160 | tf_op jit(solution)/shard_map/ppermute | solution.py:256
  5.4 13.2 %collective-permute-start.5 = (bf16[64,128]{1,0:T(8,128)(2,1)S(1)}, bf16[64,128]{1,0:T(8,128)(2,1)S(1)}, u32[]{:S(2)}, u32[]{:S(2)}) collective-permute-start(bf16[64,128]{1,0:T(8,128)(2,1)S(1)} %get-tuple-element.89), channel_id=1, source_target_pairs={{1,0},{2,1},{3,2},{4,3},{5,4},{6,5},{7,6},{9,8},{10,9},{11,10},{12... | collective-permute-start | bytes 49160 | tf_op jit(solution)/shard_map/ppermute | solution.py:256
  6.7 1.0 copy-start
  7.7 0.7 copy-start.2
  8.7 19.5 %collective-permute-start = (bf16[128,256]{1,0:T(8,128)(2,1)S(1)}, bf16[128,256]{1,0:T(8,128)(2,1)S(1)}, u32[]{:S(2)}, u32[]{:S(2)}) collective-permute-start(bf16[128,256]{1,0:T(8,128)(2,1)S(1)} %get-tuple-element.46.bound_t_ref), channel_id=1, source_target_pairs={{0,8},{8,0},{16,24},{24,16},{32,40},{40,32},{48,56},{56,48},{64,72... | collective-permute-start | bytes 196616 | tf_op jit(solution)/shard_map/ppermute | solution.py:250
  9.8 18.5 %collective-permute-start.1 = (bf16[128,256]{1,0:T(8,128)(2,1)S(1)}, bf16[128,256]{1,0:T(8,128)(2,1)S(1)}, u32[]{:S(2)}, u32[]{:S(2)}) collective-permute-start(bf16[128,256]{1,0:T(8,128)(2,1)S(1)} %get-tuple-element.46.bound_t_ref), channel_id=1, source_target_pairs={{0,16},{8,24},{16,0},{24,8},{32,48},{40,56},{48,32},{56,40},{64,80... | collective-permute-start | bytes 196616 | tf_op jit(solution)/shard_map/ppermute | solution.py:250
  11.4 16.8 %collective-permute-start.2 = (bf16[128,256]{1,0:T(8,128)(2,1)S(1)}, bf16[128,256]{1,0:T(8,128)(2,1)S(1)}, u32[]{:S(2)}, u32[]{:S(2)}) collective-permute-start(bf16[128,256]{1,0:T(8,128)(2,1)S(1)} %get-tuple-element.46.bound_t_ref), channel_id=1, source_target_pairs={{0,32},{8,40},{16,48},{24,56},{32,0},{40,8},{48,16},{56,24},{64,96... | collective-permute-start | bytes 196616 | tf_op jit(solution)/shard_map/ppermute | solution.py:250
  14.4 13.8 %collective-permute-start.3 = (bf16[128,256]{1,0:T(8,128)(2,1)S(1)}, bf16[128,256]{1,0:T(8,128)(2,1)S(1)}, u32[]{:S(2)}, u32[]{:S(2)}) collective-permute-start(bf16[128,256]{1,0:T(8,128)(2,1)S(1)} %get-tuple-element.46.bound_t_ref), channel_id=1, source_target_pairs={{0,64},{8,72},{16,80},{24,88},{32,96},{40,104},{48,112},{56,120},{... | collective-permute-start | bytes 196616 | tf_op jit(solution)/shard_map/ppermute | solution.py:250
  18.6 1.1 %copy-start.4 = (bf16[3072,128]{1,0:T(8,128)(2,1)S(1)}, bf16[3072,128]{1,0:T(8,128)(2,1)}, u32[]{:S(2)}) copy-start(bf16[3072,128]{1,0:T(8,128)(2,1)} %feats_ref.3) | copy-start | bytes 2359300
  19.8 1.0 copy-start.6
  20.7 0.7 copy-start.10
  21.5 6.8 %copy-start.1 = (bf16[1024,128]{1,0:T(8,128)(2,1)S(1)}, bf16[1024,128]{1,0:T(8,128)(2,1)}, u32[]{:S(2)}) copy-start(bf16[1024,128]{1,0:T(8,128)(2,1)} %lat_ref.3) | copy-start | bytes 786436
  21.5 6.8 %copy-start.3 = (s32[256]{0:T(256)S(1)}, s32[256]{0:T(256)}, u32[]{:S(2)}) copy-start(s32[256]{0:T(256)} %param.13) | copy-start | bytes 3076
  21.5 6.8 %copy-start.5 = (bf16[3072,128]{1,0:T(8,128)(2,1)S(1)}, bf16[3072,128]{1,0:T(8,128)(2,1)}, u32[]{:S(2)}) copy-start(bf16[3072,128]{1,0:T(8,128)(2,1)} %feats_ref.3) | copy-start | bytes 2359300
  21.5 6.8 %copy-start.7 = (bf16[9,128,128]{2,1,0:T(8,128)(2,1)S(1)}, bf16[9,128,128]{2,1,0:T(8,128)(2,1)}, u32[]{:S(2)}) copy-start(bf16[9,128,128]{2,1,0:T(8,128)(2,1)} %w_ref.7) | copy-start | bytes 884740
  21.5 6.8 %copy-start.8 = (bf16[1024,128]{1,0:T(8,128)(2,1)S(1)}, bf16[1024,128]{1,0:T(8,128)(2,1)}, u32[]{:S(2)}) copy-start(bf16[1024,128]{1,0:T(8,128)(2,1)} %cot_ref.3) | copy-start | bytes 786436
  21.5 6.8 %copy-start.9 = (s32[2,8192]{1,0:T(2,128)S(1)}, s32[2,8192]{1,0:T(2,128)}, u32[]{:S(2)}) copy-start(s32[2,8192]{1,0:T(2,128)} %contacts_ref.3) | copy-start | bytes 196612
  21.5 6.8 %copy-start.11 = (s32[2,3072]{1,0:T(2,128)S(1)}, s32[2,3072]{1,0:T(2,128)}, u32[]{:S(2)}) copy-start(s32[2,3072]{1,0:T(2,128)} %edges_ref.5) | copy-start | bytes 73732
  21.5 6.8 %copy-start.12 = (s32[1,4]{1,0:T(1,128)S(1)}, s32[1,4]{1,0:T(1,128)}, u32[]{:S(2)}) copy-start(s32[1,4]{1,0:T(1,128)} %counts_ref.1) | copy-start | bytes 52
  40.2 1.3 %copy-start.13 = (bf16[128,8192]{1,0:T(8,128)(2,1)}, bf16[128,8192]{1,0:T(8,128)(2,1)S(1)}, u32[]{:S(2)}) copy-start(bf16[128,8192]{1,0:T(8,128)(2,1)S(1)} %get-tuple-element.56.dc_ref) | copy-start | bytes 6291460
  41.6 1.9 %collective-permute-start.6 = (bf16[576,128]{1,0:T(8,128)(2,1)S(1)}, bf16[576,128]{1,0:T(8,128)(2,1)S(1)}, u32[]{:S(2)}, u32[]{:S(2)}) collective-permute-start(bf16[576,128]{1,0:T(8,128)(2,1)S(1)} %get-tuple-element.52), channel_id=1, source_target_pairs={{0,8},{1,9},{2,10},{3,11},{4,12},{5,13},{6,14},{7,15},{8,0},{9,1},... | collective-permute-start | bytes 442376 | tf_op jit(solution)/shard_map/ppermute | solution.py:245
  43.5 9.5 %collective-permute-start.7 = (bf16[144,128]{1,0:T(8,128)(2,1)S(1)}, bf16[144,128]{1,0:T(8,128)(2,1)S(1)}, u32[]{:S(2)}, u32[]{:S(2)}) collective-permute-start(bf16[144,128]{1,0:T(8,128)(2,1)S(1)} %get-tuple-element.95), channel_id=1, source_target_pairs={{0,1},{1,0},{2,3},{3,2},{4,5},{5,4},{6,7},{7,6},{8,9},{9,8},{10,11... | collective-permute-start | bytes 110600 | tf_op jit(solution)/shard_map/ppermute | solution.py:245
  46.0 7.0 %collective-permute-start.8 = (bf16[144,128]{1,0:T(8,128)(2,1)S(1)}, bf16[144,128]{1,0:T(8,128)(2,1)S(1)}, u32[]{:S(2)}, u32[]{:S(2)}) collective-permute-start(bf16[144,128]{1,0:T(8,128)(2,1)S(1)} %get-tuple-element.97), channel_id=1, source_target_pairs={{0,2},{1,3},{2,0},{3,1},{4,6},{5,7},{6,4},{7,5},{8,10},{9,11},{10,... | collective-permute-start | bytes 110600 | tf_op jit(solution)/shard_map/ppermute | solution.py:245
  48.6 4.4 %collective-permute-start.9 = (bf16[144,128]{1,0:T(8,128)(2,1)S(1)}, bf16[144,128]{1,0:T(8,128)(2,1)S(1)}, u32[]{:S(2)}, u32[]{:S(2)}) collective-permute-start(bf16[144,128]{1,0:T(8,128)(2,1)S(1)} %get-tuple-element.96), channel_id=1, source_target_pairs={{0,3},{1,2},{2,1},{3,0},{4,7},{5,6},{6,5},{7,4},{8,11},{9,10},{10,... | collective-permute-start | bytes 110600 | tf_op jit(solution)/shard_map/ppermute | solution.py:245
  48.6 1.6 %copy-start.14 = (bf16[128,8192]{1,0:T(8,128)(2,1)S(1)}, bf16[128,8192]{1,0:T(8,128)(2,1)}, u32[]{:S(2)}) copy-start(bf16[128,8192]{1,0:T(8,128)(2,1)} %copy-done.13) | copy-start | bytes 6291460
  53.1 10.7 %collective-permute-start.10 = (bf16[144,128]{1,0:T(8,128)(2,1)S(1)}, bf16[144,128]{1,0:T(8,128)(2,1)S(1)}, u32[]{:S(2)}, u32[]{:S(2)}) collective-permute-start(bf16[144,128]{1,0:T(8,128)(2,1)S(1)} %add_convert_fusion.4), channel_id=1, source_target_pairs={{0,4},{1,5},{2,6},{3,7},{4,0},{5,1},{6,2},{7,3},{8,12},{9,13},{10,... | collective-permute-start | bytes 110600 | tf_op jit(solution)/shard_map/ppermute | solution.py:245
  56.4 7.4 %collective-permute-start.11 = (bf16[144,128]{1,0:T(8,128)(2,1)S(1)}, bf16[144,128]{1,0:T(8,128)(2,1)S(1)}, u32[]{:S(2)}, u32[]{:S(2)}) collective-permute-start(bf16[144,128]{1,0:T(8,128)(2,1)S(1)} %add_convert_fusion.4), channel_id=1, source_target_pairs={{0,128},{1,129},{2,130},{3,131},{4,132},{5,133},{6,134},{7,135},{8... | collective-permute-start | bytes 110600 | tf_op jit(solution)/shard_map/ppermute | solution.py:245
  58.9 5.0 %collective-permute-start.12 = (bf16[144,128]{1,0:T(8,128)(2,1)S(1)}, bf16[144,128]{1,0:T(8,128)(2,1)S(1)}, u32[]{:S(2)}, u32[]{:S(2)}) collective-permute-start(bf16[144,128]{1,0:T(8,128)(2,1)S(1)} %add_convert_fusion.4), channel_id=1, source_target_pairs={{0,132},{1,133},{2,134},{3,135},{4,128},{5,129},{6,130},{7,131},{8... | collective-permute-start | bytes 110600 | tf_op jit(solution)/shard_map/ppermute | solution.py:245
  63.9 6.4 %collective-permute-start.13 = (bf16[144,128]{1,0:T(8,128)(2,1)S(1)}, bf16[144,128]{1,0:T(8,128)(2,1)S(1)}, u32[]{:S(2)}, u32[]{:S(2)}) collective-permute-start(bf16[144,128]{1,0:T(8,128)(2,1)S(1)} %add_convert_fusion.3), channel_id=1, source_target_pairs={{0,16},{1,17},{2,18},{3,19},{4,20},{5,21},{6,22},{7,23},{8,24},{9,... | collective-permute-start | bytes 110600 | tf_op jit(solution)/shard_map/ppermute | solution.py:245
  64.7 7.5 %collective-permute-start.14 = (bf16[144,128]{1,0:T(8,128)(2,1)S(1)}, bf16[144,128]{1,0:T(8,128)(2,1)S(1)}, u32[]{:S(2)}, u32[]{:S(2)}) collective-permute-start(bf16[144,128]{1,0:T(8,128)(2,1)S(1)} %add_convert_fusion.3), channel_id=1, source_target_pairs={{0,32},{1,33},{2,34},{3,35},{4,36},{5,37},{6,38},{7,39},{8,40},{9,... | collective-permute-start | bytes 110600 | tf_op jit(solution)/shard_map/ppermute | solution.py:245
  65.9 6.4 %collective-permute-start.15 = (bf16[144,128]{1,0:T(8,128)(2,1)S(1)}, bf16[144,128]{1,0:T(8,128)(2,1)S(1)}, u32[]{:S(2)}, u32[]{:S(2)}) collective-permute-start(bf16[144,128]{1,0:T(8,128)(2,1)S(1)} %add_convert_fusion.3), channel_id=1, source_target_pairs={{0,48},{1,49},{2,50},{3,51},{4,52},{5,53},{6,54},{7,55},{8,56},{9,... | collective-permute-start | bytes 110600 | tf_op jit(solution)/shard_map/ppermute | solution.py:245
  67.5 4.8 %collective-permute-start.16 = (bf16[256,128]{1,0:T(8,128)(2,1)S(1)}, bf16[256,128]{1,0:T(8,128)(2,1)S(1)}, u32[]{:S(2)}, u32[]{:S(2)}) collective-permute-start(bf16[256,128]{1,0:T(8,128)(2,1)S(1)} %get-tuple-element.73), channel_id=1, source_target_pairs={{0,8},{8,0},{16,24},{24,16},{32,40},{40,32},{48,56},{56,48},{64,72... | collective-permute-start | bytes 196616 | tf_op jit(solution)/shard_map/ppermute | solution.py:250
  70.3 5.3 %collective-permute-start.17 = (bf16[256,128]{1,0:T(8,128)(2,1)S(1)}, bf16[256,128]{1,0:T(8,128)(2,1)S(1)}, u32[]{:S(2)}, u32[]{:S(2)}) collective-permute-start(bf16[256,128]{1,0:T(8,128)(2,1)S(1)} %get-tuple-element.74), channel_id=1, source_target_pairs={{0,16},{8,24},{16,0},{24,8},{32,48},{40,56},{48,32},{56,40},{64,80... | collective-permute-start | bytes 196616 | tf_op jit(solution)/shard_map/ppermute | solution.py:250
  70.3 5.3 %collective-permute-start.18 = (bf16[256,128]{1,0:T(8,128)(2,1)S(1)}, bf16[256,128]{1,0:T(8,128)(2,1)S(1)}, u32[]{:S(2)}, u32[]{:S(2)}) collective-permute-start(bf16[256,128]{1,0:T(8,128)(2,1)S(1)} %get-tuple-element.75), channel_id=1, source_target_pairs={{0,32},{8,40},{16,48},{24,56},{32,0},{40,8},{48,16},{56,24},{64,96... | collective-permute-start | bytes 196616 | tf_op jit(solution)/shard_map/ppermute | solution.py:250
  72.2 7.3 %collective-permute-start.19 = (bf16[256,128]{1,0:T(8,128)(2,1)S(1)}, bf16[256,128]{1,0:T(8,128)(2,1)S(1)}, u32[]{:S(2)}, u32[]{:S(2)}) collective-permute-start(bf16[256,128]{1,0:T(8,128)(2,1)S(1)} %get-tuple-element.76), channel_id=1, source_target_pairs={{0,64},{8,72},{16,80},{24,88},{32,96},{40,104},{48,112},{56,120},{... | collective-permute-start | bytes 196616 | tf_op jit(solution)/shard_map/ppermute | solution.py:250
  79.5 6.7 %collective-permute-start.20 = (bf16[144,128]{1,0:T(8,128)(2,1)S(1)}, bf16[144,128]{1,0:T(8,128)(2,1)S(1)}, u32[]{:S(2)}, u32[]{:S(2)}) collective-permute-start(bf16[144,128]{1,0:T(8,128)(2,1)S(1)} %add_convert_fusion.2), channel_id=1, source_target_pairs={{0,64},{1,65},{2,66},{3,67},{4,68},{5,69},{6,70},{7,71},{8,72},{9,... | collective-permute-start | bytes 110600 | tf_op jit(solution)/shard_map/ppermute | solution.py:245
  80.7 5.5 %collective-permute-start.21 = (bf16[64,128]{1,0:T(8,128)(2,1)S(1)}, bf16[64,128]{1,0:T(8,128)(2,1)S(1)}, u32[]{:S(2)}, u32[]{:S(2)}) collective-permute-start(bf16[64,128]{1,0:T(8,128)(2,1)S(1)} %get-tuple-element.82), channel_id=1, source_target_pairs={{0,1},{1,2},{2,3},{3,4},{4,5},{5,6},{6,7},{8,9},{9,10},{10,11},{11... | collective-permute-start | bytes 49160 | tf_op jit(solution)/shard_map/ppermute | solution.py:256
  82.0 4.5 %collective-permute-start.22 = (bf16[64,128]{1,0:T(8,128)(2,1)S(1)}, bf16[64,128]{1,0:T(8,128)(2,1)S(1)}, u32[]{:S(2)}, u32[]{:S(2)}) collective-permute-start(bf16[64,128]{1,0:T(8,128)(2,1)S(1)} %get-tuple-element.83), channel_id=1, source_target_pairs={{1,0},{2,1},{3,2},{4,3},{5,4},{6,5},{7,6},{9,8},{10,9},{11,10},{12... | collective-permute-start | bytes 49160 | tf_op jit(solution)/shard_map/ppermute | solution.py:256
  86.5 6.7 %collective-permute-start.23 = (bf16[144,128]{1,0:T(8,128)(2,1)S(1)}, bf16[144,128]{1,0:T(8,128)(2,1)S(1)}, u32[]{:S(2)}, u32[]{:S(2)}) collective-permute-start(bf16[144,128]{1,0:T(8,128)(2,1)S(1)} %add_convert_fusion.1), channel_id=1, source_target_pairs={{0,3},{1,2},{2,1},{3,0},{4,7},{5,6},{6,5},{7,4},{8,11},{9,10},{10,... | collective-permute-start | bytes 110600 | tf_op jit(solution)/shard_map/ppermute | solution.py:245
  91.9 4.3 %collective-permute-start.24 = (bf16[144,128]{1,0:T(8,128)(2,1)S(1)}, bf16[144,128]{1,0:T(8,128)(2,1)S(1)}, u32[]{:S(2)}, u32[]{:S(2)}) collective-permute-start(bf16[144,128]{1,0:T(8,128)(2,1)S(1)} %add_convert_fusion.1), channel_id=1, source_target_pairs={{0,2},{1,3},{2,0},{3,1},{4,6},{5,7},{6,4},{7,5},{8,10},{9,11},{10,... | collective-permute-start | bytes 110600 | tf_op jit(solution)/shard_map/ppermute | solution.py:245
  91.9 4.3 %collective-permute-start.25 = (bf16[144,128]{1,0:T(8,128)(2,1)S(1)}, bf16[144,128]{1,0:T(8,128)(2,1)S(1)}, u32[]{:S(2)}, u32[]{:S(2)}) collective-permute-start(bf16[144,128]{1,0:T(8,128)(2,1)S(1)} %add_convert_fusion.1), channel_id=1, source_target_pairs={{0,1},{1,0},{2,3},{3,2},{4,5},{5,4},{6,7},{7,6},{8,9},{9,8},{10,11... | collective-permute-start | bytes 110600 | tf_op jit(solution)/shard_map/ppermute | solution.py:245
  96.2 5.9 %collective-permute-start.26 = (bf16[576,128]{1,0:T(8,128)(2,1)S(1)}, bf16[576,128]{1,0:T(8,128)(2,1)S(1)}, u32[]{:S(2)}, u32[]{:S(2)}) collective-permute-start(bf16[576,128]{1,0:T(8,128)(2,1)S(1)} %pad_maximum_fusion.1), channel_id=1, source_target_pairs={{0,8},{1,9},{2,10},{3,11},{4,12},{5,13},{6,14},{7,15},{8,0},{9,1},... | collective-permute-start | bytes 442376 | tf_op jit(solution)/shard_map/ppermute | solution.py:245

commit v3 on v2

--- a/solution.py
+++ b/solution.py
@@ -67,29 +67,46 @@
     return [slice(first, first + size) for first in range(0, total, size)]
 
 
-def bound_kernel(lat_ref, bnd_ref, lat_t_ref, bound_t_ref):
-    lat_t = transposed(lat_ref[...])
+def fetched(pairs, sems):
+    copies = [pltpu.make_async_copy(a, b, sems.at[k]) for k, (a, b) in enumerate(pairs)]
+    for copy in copies:
+        copy.start()
+    return copies
+
+
+def bound_kernel(lat_hbm, bnd_hbm, low_ref, high_ref, lat_t_ref, bound_t_ref, lat, bnd, sems):
+    for copy in fetched([(lat_hbm, lat), (bnd_hbm, bnd)], sems):
+        copy.wait()
+    rows_dev = lat.shape[0]
+    low_ref[...] = lat[:HB, :]
+    high_ref[...] = lat[rows_dev - HB :, :]
+    lat_t = transposed(lat[...])
     lat_t_ref[...] = lat_t
-    bound_t_ref[...] = nn(lat_t, table(lat_ref.shape[0], bnd_ref[...])).astype(BF)
+    bound_t_ref[...] = nn(lat_t, table(rows_dev, bnd[...])).astype(BF)
 
 
 def mesh_kernel(
-    lat_t_ref, before_ref, after_ref, feats_ref, w_ref, edges_ref,
-    rows_ref, slope_ref, agg_ref, ext_t_ref, sum_ref,
+    lat_t_ref, before_ref, after_ref, edges_hbm, w_hbm, feats_hbm,
+    rows_ref, slope_ref, agg_ref, ext_t_ref, sum_ref, edges, w, feats, sems,
 ):
     rows_dev = lat_t_ref.shape[1]
+    copies = fetched([(edges_hbm, edges), (w_hbm.at[0:3], w), (feats_hbm, feats)], sems)
     rim = transposed(jnp.concatenate([before_ref[...], after_ref[...]], axis=0))
     ext_t_ref[:, :rows_dev] = lat_t_ref[...]
     ext_t_ref[:, rows_dev:] = rim
-    w_t = jnp.concatenate([transposed(w_ref[0]), transposed(w_ref[1])], axis=1)
-    w2_t = transposed(w_ref[2])
-    for at in spans(edges_ref.shape[1], MESH_SPAN):
-        ids = edges_ref[0:1, at] - HB
+    copies[0].wait()
+    for at in spans(edges.shape[1], MESH_SPAN):
+        ids = edges[0:1, at] - HB
         ids = jnp.where(ids < 0, ids + rows_dev + HB, jnp.where(ids < rows_dev, ids, ids + HB))
         rows_ref[:128, at] = nn(ext_t_ref[...], table(rows_dev + 2 * HB, ids)).astype(BF)
-        hits = table(rows_dev, edges_ref[1:2, at])
+        hits = table(rows_dev, edges[1:2, at])
         rows_ref[128:, at] = nn(lat_t_ref[...], hits).astype(BF)
-        x = nn(w_t, rows_ref[:, at]) + nt(w2_t, feats_ref[at, :])
+        if at.start == 0:
+            copies[1].wait()
+            copies[2].wait()
+            w_t = jnp.concatenate([transposed(w[0]), transposed(w[1])], axis=1)
+            w2_t = transposed(w[2])
+        x = nn(w_t, rows_ref[:, at]) + nt(w2_t, feats[at, :])
         message, slope = silu_parts(x)
         slope_ref[:, at] = slope
         part = nt(hits, message.astype(BF))
@@ -190,23 +207,26 @@
     own_ref[...] = wide_nt(own_ref[...], w_ref[3])
 
 
-def mesh_back_kernel(
-    w_ref, edges_ref, dm_ref, dn_ref, cot_ref, grad_ref, low_ref, high_ref, send_ref, recv_ref
-):
+def send_back_kernel(w_ref, edges_ref, dm_ref, part_ref, low_ref, high_ref, send_ref):
+    rows_dev = part_ref.shape[0]
+    for at in spans(edges_ref.shape[1], MESH_SPAN):
+        send = nt(table(rows_dev + 2 * HB, edges_ref[0:1, at]), dm_ref[:, at])
+        send_ref[...] = send + send_ref[...] if at.start else send
+    low_ref[...] = wide_nt(send_ref[:HB, :], w_ref[0]).astype(BF)
+    high_ref[...] = wide_nt(send_ref[HB + rows_dev :, :], w_ref[0]).astype(BF)
+    part_ref[...] = wide_nt(send_ref[HB : HB + rows_dev, :], w_ref[0])
+
+
+def recv_back_kernel(w_ref, edges_ref, dm_ref, dn_ref, cot_ref, part_ref, grad_ref, recv_ref):
     rows_dev = cot_ref.shape[0]
     for at in spans(edges_ref.shape[1], MESH_SPAN):
-        d = dm_ref[:, at]
-        send = nt(table(rows_dev + 2 * HB, edges_ref[0:1, at]), d)
-        recv = nt(table(rows_dev, edges_ref[1:2, at]), d)
-        send_ref[...] = send + send_ref[...] if at.start else send
+        recv = nt(table(rows_dev, edges_ref[1:2, at]), dm_ref[:, at])
         recv_ref[...] = recv + recv_ref[...] if at.start else recv
-    low_ref[...] = wide_nt(send_ref[:HB, :], w_ref[0]).astype(BF)
-    high_ref[...] = wide_nt(send_ref[HB + rows_dev :, :], w_ref[0]).astype(BF)
     grad_ref[...] = (
         cot_ref[...].astype(F32)
         + nt(dn_ref[...], w_ref[5])
         + wide_nt(recv_ref[...], w_ref[1])
-        + wide_nt(send_ref[HB : HB + rows_dev, :], w_ref[0])
+        + part_ref[...]
     )
 
 
@@ -222,14 +242,20 @@
     out_ref[rows_dev - HB :, :] += next_ref[...].astype(F32)
 
 
-def call(kernel, outs, args, scratch=(), smem=0, flops=0, mib=32):
+def call(kernel, outs, args, scratch=(), smem=0, hbm=0, flops=0, mib=32):
     spec = pl.BlockSpec(memory_space=pltpu.VMEM)
+    plain = len(args) - smem - hbm
+    in_specs = [pl.BlockSpec(memory_space=pltpu.SMEM)] * smem + [spec] * plain
+    in_specs += [pl.BlockSpec(memory_space=pltpu.HBM)] * hbm
+    scratch_shapes = [pltpu.VMEM(shape, kind) for shape, kind in scratch]
+    if hbm:
+        scratch_shapes.append(pltpu.SemaphoreType.DMA((hbm,)))
     return pl.pallas_call(
         kernel,
         out_shape=[jax.ShapeDtypeStruct(shape, kind) for shape, kind in outs],
-        in_specs=[pl.BlockSpec(memory_space=pltpu.SMEM)] * smem + [spec] * (len(args) - smem),
+        in_specs=in_specs,
         out_specs=[spec] * len(outs),
-        scratch_shapes=[pltpu.VMEM(shape, kind) for shape, kind in scratch],
+        scratch_shapes=scratch_shapes,
         compiler_params=pltpu.CompilerParams(vmem_limit_bytes=mib * MIB),
         cost_estimate=pl.CostEstimate(flops=flops, bytes_accessed=4000000, transcendentals=0),
     )(*args)
@@ -260,27 +286,15 @@
     return block.astype(F32)
 
 
-def four_sum(block, name):
-    one, two, three = [wide(exchanged(block, **{name: mask})) for mask in (1, 2, 3)]
-    return ((wide(block) + one) + (two + three)).astype(BF)
-
-
-def summed_over_y(kept, other, row_y):
-    part = kept.shape[0] // 4
-    block = (kept + wide(other)).astype(BF)
-    pieces = [
-        lax.dynamic_slice_in_dim(block, (row_y ^ mask) * part, part, 0) for mask in range(4)
-    ]
-    return pieces
-
-
-def ordered_by_y(found, row_y):
-    odd, high = row_y % 2 == 1, row_y >= 2
-    low_pair = [jnp.where(odd, found[1], found[0]), jnp.where(odd, found[0], found[1])]
-    high_pair = [jnp.where(odd, found[3], found[2]), jnp.where(odd, found[2], found[3])]
-    ordered = [jnp.where(high, b, a) for a, b in zip(low_pair, high_pair)]
-    ordered += [jnp.where(high, a, b) for a, b in zip(low_pair, high_pair)]
-    return jnp.concatenate(ordered, axis=0)
+def half_of(block, which):
+    size = block.shape[0] // 2
+    return lax.dynamic_slice_in_dim(block, which * size, size, 0)
+
+
+def joined(own, other, which):
+    first = jnp.where(which == 0, own, other)
+    second = jnp.where(which == 0, other, own)
+    return jnp.concatenate([first, second], axis=0)
 
 
 def tie(*arrays):
@@ -300,18 +314,31 @@
     row_y = lax.axis_index("panel") % 4
     scale = 1.0 / math.sqrt(rows_dev * lax.axis_size("region") * lax.axis_size("panel"))
 
-    before = shifted(latents[rows_dev - HB :], 1)
-    after = shifted(latents[:HB], -1)
-    lat_t, bound_t = call(
-        bound_kernel, [((width, rows_dev), BF), ((width, bound_count), BF)], [latents, bnd], mib=8
-    )
+    low_rows, high_rows, lat_t, bound_t = call(
+        bound_kernel,
+        [((HB, width), BF), ((HB, width), BF), ((width, rows_dev), BF), ((width, bound_count), BF)],
+        [latents, bnd],
+        [((rows_dev, width), BF), ((1, bound_count), jnp.int32)],
+        hbm=2,
+        mib=8,
+    )
+    before = shifted(high_rows, 1)
+    after = shifted(low_rows, -1)
     fars = [swapped(bound_t, r) for r in range(rounds)]
     rows, slope, agg = call(
         mesh_kernel,
         [((2 * width, edge_count), BF), ((width, edge_count), F32), ((rows_dev, width), BF)],
-        [lat_t, before, after, edge_feats, weights, mesh_edges],
-        [((width, rows_dev + 2 * HB), BF), ((rows_dev, width), F32)],
+        [lat_t, before, after, mesh_edges, weights, edge_feats],
+        [
+            ((width, rows_dev + 2 * HB), BF),
+            ((rows_dev, width), F32),
+            ((2, edge_count), jnp.int32),
+            ((3, width, width), BF),
+            ((edge_count, width), BF),
+        ],
+        hbm=3,
         flops=6 * 10**9,
+        mib=20,
     )
     new_rows, kept, sent, d_mesh, d_contact, d_node = call(
         functools.partial(main_kernel, scale=scale),
@@ -336,50 +363,85 @@
         ],
         smem=2,
         flops=8 * 10**9,
-        mib=40,
+        mib=26,
     )
     other = exchanged(sent, mask_core=1)
     other, d_contact = tie(other, d_contact)
-    pieces = summed_over_y(kept, other, row_y)
+    block = kept + wide(other)
+    half, quarter = (row_y ^ (row_y >> 1)) & 1, row_y >> 1
+    other = exchanged(half_of(block, 1 - half).astype(BF), mask_y=1)
     *far_grads, own_grad = call(
         contact_back_kernel,
         [((bound_count, width), BF)] * rounds + [((bound_count, width), F32)],
         [weights, contact_edges, d_contact],
         flops=2 * 10**9,
-    )
-    one, two, three = [wide(exchanged(pieces[mask], mask_y=mask)) for mask in (1, 2, 3)]
-    block = ((wide(pieces[0]) + one) + (two + three)).astype(BF)
-    block, d_mesh, *far_grads = tie(block, d_mesh, *far_grads)
+        mib=16,
+    )
+    other, *far_grads = tie(other, *far_grads)
+    block = half_of(block, half) + wide(other)
+    other = exchanged(half_of(block, 1 - quarter).astype(BF), mask_y=3)
+    in_zero = exchanged(far_grads[0], mask_core=1)
+    other, in_zero, d_mesh = tie(other, in_zero, d_mesh)
+    block = (half_of(block, quarter) + wide(other)).astype(BF)
+
+    size = block.shape[0]
+    other = exchanged(jnp.concatenate([block, far_grads[1]], axis=0), mask_z=1)
     part, low, high = call(
-        mesh_back_kernel,
+        send_back_kernel,
         [((rows_dev, width), F32), ((HB, width), BF), ((HB, width), BF)],
-        [weights, mesh_edges, d_mesh, d_node, cotangent],
-        [((rows_dev + 2 * HB, width), F32), ((rows_dev, width), F32)],
-        flops=3 * 10**9,
-    )
-    block = four_sum(block, "mask_x")
-    block, low, high, *far_grads = tie(block, low, high, *far_grads)
-    incoming = [swapped(far_grads[r], r) for r in range(rounds)]
-    block = four_sum(block, "mask_z")
-    block, *incoming = tie(block, *incoming)
-    from_prev = shifted(high, 1)
-    from_next = shifted(low, -1)
-    block = (wide(block) + wide(exchanged(block, mask_z=4))).astype(BF)
-    block, from_prev, from_next = tie(block, from_prev, from_next)
+        [weights, mesh_edges, d_mesh],
+        [((rows_dev + 2 * HB, width), F32)],
+        flops=2 * 10**9,
+        mib=16,
+    )
+    other, part, low, high = tie(other, part, low, high)
+    in_one = other[size:]
+    block = (wide(block) + wide(other[:size])).astype(BF)
+    other = exchanged(jnp.concatenate([block, far_grads[2], far_grads[3]], axis=0), mask_z=2)
+    (part,) = call(
+        recv_back_kernel,
+        [((rows_dev, width), F32)],
+        [weights, mesh_edges, d_mesh, d_node, cotangent, part],
+        [((rows_dev, width), F32)],
+        flops=2 * 10**9,
+        mib=16,
+    )
+    other, part = tie(other, part)
+    in_two = other[size : size + bound_count]
+    block = (wide(block) + wide(other[:size])).astype(BF)
+    other = exchanged(jnp.concatenate([block, other[size + bound_count :]], axis=0), mask_z=6)
+    in_three = other[size:]
+    block = wide(block) + wide(other[:size])
+
+    rim = wide(jnp.where(row_y == 0, low, high))
+    other = exchanged(jnp.concatenate([block, rim], axis=0), mask_x=1)
+    rim = other[size:].astype(BF)
+    block = block + other[:size]
+    block = (block + exchanged(block, mask_x=3)).astype(BF)
+    rim = jnp.where(row_y == 1, high, jnp.where(row_y == 2, low, rim))
+    other = exchanged(jnp.concatenate([block, rim], axis=0), mask_y=3)
+    rim_three = other[size:]
+    block = joined(block, other[:size], quarter)
+    rim = jnp.where(row_y % 2 == 0, high, low)
+    other = exchanged(jnp.concatenate([block, rim], axis=0), mask_y=1)
+    rim_one = other[2 * size :]
+    panel = lax.axis_index("panel")
+    nothing = jnp.zeros_like(rim)
+    from_prev = jnp.where(row_y % 2 == 0, rim_three, rim_one)
+    from_prev = jnp.where(panel == 0, nothing, from_prev)
+    from_next = jnp.where(row_y % 2 == 0, rim_one, rim_three)
+    from_next = jnp.where(panel == lax.axis_size("panel") - 1, nothing, from_next)
+    block = joined(block, other[: 2 * size], half)
+    other = exchanged(block, mask_core=1)
     (grad_rows,) = call(
         last_kernel,
         [((rows_dev, width), F32)],
-        [part, own_grad, *incoming, from_prev, from_next, bnd],
+        [part, own_grad, in_zero, in_one, in_two, in_three, from_prev, from_next, bnd],
         flops=10**8,
         mib=8,
     )
-    found = [block] + [exchanged(block, mask_y=mask) for mask in (1, 2, 3)]
-    block = ordered_by_y(found, row_y)
-    other = exchanged(block, mask_core=1)
-    first = jnp.where(core == 1, other, block)
-    second = jnp.where(core == 1, block, other)
-    summed = wide(jnp.concatenate([first, second], axis=0)).reshape(9, width, width)
-    return (new_rows, grad_rows, summed)
+    block = joined(block, other, core)
+    return (new_rows, grad_rows, wide(block).reshape(9, width, width))
 
 
 def solution(mesh):

time: 105 us -> 101 us (0.962); the launches traced: 103 us -> 101 us
  starting transfers between devices: 49.7 us -> 37.1 us
  waiting for transfers between devices: 15.2 us -> 25 us
    ppermute x15 -> x12, waiting for transfers between devices: 7.71 us -> 24.9 us  [exchanged(): return lax.ppermute(block, ('region', 'panel'), route)]
    ppermute x8 -> x4, waiting for transfers between devices: 7.26 us -> 0.01 us  [swapped(): lax.ppermute(block, 'region', [(i, i ^ 1 << bit) for i in range(size)])]
    ppermute x15 -> x12, starting transfers between devices: 27.2 us -> 21.9 us  [exchanged(): return lax.ppermute(block, ('region', 'panel'), route)]
    ppermute x8 -> x4, starting transfers between devices: 14.6 us -> 9.9 us  [swapped(): lax.ppermute(block, 'region', [(i, i ^ 1 << bit) for i in range(size)])]
    ppermute x4 -> x2, starting transfers between devices: 7.88 us -> 5.32 us  [shifted(): return lax.ppermute(array, 'panel', pairs)]
    pallas_call x6 -> x7, Pallas kernels: 27.9 us -> 28.7 us  [call(): pl.pallas_call(kernel, out_shape=[jax.ShapeDtypeStruct(shape, kind) for s...]
  transfers between devices with their start and end apart: 27 -> 18, of which waited for: 7 -> 9; matrix products, arithmetic and copies ran while one was open for 0% -> 0% of each run, Pallas kernels for 16% -> 16%
where the time goes in v3:
time: 101 us
  starting transfers between devices  37.1 us (37%)
  Pallas kernels  28.7 us (28%)
  waiting for transfers between devices  25 us (25%)
  local copies, waits for them, and re-layouts  7.49 us (7%)
  other arithmetic  1.22 us (1%)
  between operations  1.05 us (1%)
    pallas_call x7, Pallas kernels, call(): pl.pallas_call(kernel, out_shape=[jax.ShapeDtypeStruct(shape, kind) for s...  28.7 us
    ppermute x12, waiting for transfers between devices, exchanged(): return lax.ppermute(block, ('region', 'panel'), route)  24.9 us
    ppermute x12, starting transfers between devices, exchanged(): return lax.ppermute(block, ('region', 'panel'), route)  21.9 us
    ppermute x4, starting transfers between devices, swapped(): lax.ppermute(block, 'region', [(i, i ^ 1 << bit) for i in range(size)])  9.9 us
    unnamed x30, local copies, waits for them, and re-layouts  7.44 us
    ppermute x2, starting transfers between devices, shifted(): return lax.ppermute(array, 'panel', pairs)  5.32 us
  transfers between devices with their start and end apart: 18, of which 9 were waited for; matrix products, arithmetic and copies ran while one was open for 0% of the time, Pallas kernels for 16%

profile of v3, /device:TPU:1, one launch (start us, length us, event | category | flops | bytes accessed | tf_op | source)
XLA Modules:
  0.0 100.6 jit_solution(12087298292755191780)
XLA Ops:
  0.6 0.0 copy-start
  0.6 0.9 copy-done
  1.6 0.7 copy-done.2
  2.3 0.4 shard_map.103
  2.7 4.0 %collective-permute-start.4 = (bf16[64,128]{1,0:T(8,128)(2,1)S(1)}, bf16[64,128]{1,0:T(8,128)(2,1)S(1)}, u32[]{:S(2)}, u32[]{:S(2)}) collective-permute-start(bf16[64,128]{1,0:T(8,128)(2,1)S(1)} %get-tuple-element.42), channel_id=1, source_target_pairs={{0,1},{1,2},{2,3},{3,4},{4,5},{5,6},{6,7},{8,9},{9,10},{10,11},{11... | collective-permute-start | bytes 49160 | tf_op jit(solution)/shard_map/ppermute | solution.py:282
  6.8 1.3 %collective-permute-start.5 = (bf16[64,128]{1,0:T(8,128)(2,1)S(1)}, bf16[64,128]{1,0:T(8,128)(2,1)S(1)}, u32[]{:S(2)}, u32[]{:S(2)}) collective-permute-start(bf16[64,128]{1,0:T(8,128)(2,1)S(1)} %get-tuple-element.43), channel_id=1, source_target_pairs={{1,0},{2,1},{3,2},{4,3},{5,4},{6,5},{7,6},{9,8},{10,9},{11,10},{12... | collective-permute-start | bytes 49160 | tf_op jit(solution)/shard_map/ppermute | solution.py:282
  8.1 1.0 %collective-permute-start = (bf16[128,256]{1,0:T(8,128)(2,1)S(1)}, bf16[128,256]{1,0:T(8,128)(2,1)S(1)}, u32[]{:S(2)}, u32[]{:S(2)}) collective-permute-start(bf16[128,256]{1,0:T(8,128)(2,1)S(1)} %get-tuple-element.41.bound_t_ref), channel_id=1, source_target_pairs={{0,8},{8,0},{16,24},{24,16},{32,40},{40,32},{48,56},{56,48},{64,72... | collective-permute-start | bytes 196616 | tf_op jit(solution)/shard_map/ppermute | solution.py:276
  9.1 1.7 %collective-permute-start.1 = (bf16[128,256]{1,0:T(8,128)(2,1)S(1)}, bf16[128,256]{1,0:T(8,128)(2,1)S(1)}, u32[]{:S(2)}, u32[]{:S(2)}) collective-permute-start(bf16[128,256]{1,0:T(8,128)(2,1)S(1)} %get-tuple-element.41.bound_t_ref), channel_id=1, source_target_pairs={{0,16},{8,24},{16,0},{24,8},{32,48},{40,56},{48,32},{56,40},{64,80... | collective-permute-start | bytes 196616 | tf_op jit(solution)/shard_map/ppermute | solution.py:276
  10.8 3.0 %collective-permute-start.2 = (bf16[128,256]{1,0:T(8,128)(2,1)S(1)}, bf16[128,256]{1,0:T(8,128)(2,1)S(1)}, u32[]{:S(2)}, u32[]{:S(2)}) collective-permute-start(bf16[128,256]{1,0:T(8,128)(2,1)S(1)} %get-tuple-element.41.bound_t_ref), channel_id=1, source_target_pairs={{0,32},{8,40},{16,48},{24,56},{32,0},{40,8},{48,16},{56,24},{64,96... | collective-permute-start | bytes 196616 | tf_op jit(solution)/shard_map/ppermute | solution.py:276
  13.7 0.0 collective-permute-done.4.before_ref
  13.7 4.2 %collective-permute-start.3 = (bf16[128,256]{1,0:T(8,128)(2,1)S(1)}, bf16[128,256]{1,0:T(8,128)(2,1)S(1)}, u32[]{:S(2)}, u32[]{:S(2)}) collective-permute-start(bf16[128,256]{1,0:T(8,128)(2,1)S(1)} %get-tuple-element.41.bound_t_ref), channel_id=1, source_target_pairs={{0,64},{8,72},{16,80},{24,88},{32,96},{40,104},{48,112},{56,120},{... | collective-permute-start | bytes 196616 | tf_op jit(solution)/shard_map/ppermute | solution.py:276
  18.0 0.0 collective-permute-done.5.after_ref
  18.0 1.1 %copy-done.4 = bf16[3072,128]{1,0:T(8,128)(2,1)S(1)} copy-done((bf16[3072,128]{1,0:T(8,128)(2,1)S(1)}, bf16[3072,128]{1,0:T(8,128)(2,1)}, u32[]{:S(2)}) %copy-start.4) | copy-done | bytes 786456
  19.1 1.0 copy-done.6
  20.1 0.7 copy-done.10
  20.8 0.0 copy-start.8
  20.8 0.0 copy-start.9
  20.8 0.0 copy-start.12
  20.9 7.5 %shard_map.104 = (bf16[256,3072]{1,0:T(8,128)(2,1)S(1)}, f32[128,3072]{1,0:T(8,128)S(1)}, bf16[1024,128]{1,0:T(8,128)(2,1)S(1)}) custom-call(bf16[128,1024]{1,0:T(8,128)(2,1)S(1)} %get-tuple-element.40.lat_t_ref, bf16[64,128]{1,0:T(8,128)(2,1)S(1)} %collective-permute-done.4.before_ref, bf16[64,128]{1,0:T(8,128)(2,1)S(1)} %collective-permute-done.5.after_ref, ...), custom_call_target="tpu_custom_call" | custom-call | flops 6000000000 | bytes 4000000 | tf_op jit(solution)/shard_map/pallas_call | solution.py:253
  28.3 0.0 collective-permute-done.far0_ref
  28.3 0.0 collective-permute-done.1.far1_ref
  28.4 0.0 collective-permute-done.2.far2_ref
  28.4 0.0 collective-permute-done.3.far3_ref
  28.4 0.0 copy-done.1
  28.4 0.0 copy-done.3
  28.4 0.0 copy-done.5
  28.4 0.0 copy-done.7
  28.4 0.0 copy-done.8
  28.4 0.0 copy-done.9
  28.4 0.0 copy-done.11
  28.5 0.0 copy-done.12
  28.5 11.9 %shard_map.105 = (bf16[1024,128]{1,0:T(8,128)(2,1)}, f32[576,128]{1,0:T(8,128)S(1)}, bf16[576,128]{1,0:T(8,128)(2,1)S(1)}, bf16[128,3072]{1,0:T(8,128)(2,1)S(1)}...) custom-call(s32[1,4]{1,0:T(1,128)S(1)} %copy-done.12, s32[1]{0:T(128)} %bitcast.core_ref, ...), custom_call_target="tpu_custom_call" | custom-call | flops 8000000000 | bytes 4000000 | tf_op jit(solution)/shard_map/pallas_call | solution.py:253
  40.3 1.4 %copy-done.13 = bf16[128,8192]{1,0:T(8,128)(2,1)} copy-done((bf16[128,8192]{1,0:T(8,128)(2,1)}, bf16[128,8192]{1,0:T(8,128)(2,1)S(1)}, u32[]{:S(2)}) %copy-start.13) | copy-done | bytes 2097176
  41.7 0.9 collective-permute-start.6
  42.6 1.0 %collective-permute-done.6 = bf16[576,128]{1,0:T(8,128)(2,1)S(1)} collective-permute-done((bf16[576,128]{1,0:T(8,128)(2,1)S(1)}, bf16[576,128]{1,0:T(8,128)(2,1)S(1)}, u32[]{:S(2)}, u32[]{:S(2)}) %collective-permute-start.6) | collective-permute-done | bytes 147488 | tf_op jit(solution)/shard_map/ppermute | solution.py:271
  43.7 2.5 %collective-permute-start.7 = (bf16[288,128]{1,0:T(8,128)(2,1)S(1)}, bf16[288,128]{1,0:T(8,128)(2,1)S(1)}, u32[]{:S(2)}, u32[]{:S(2)}) collective-permute-start(bf16[288,128]{1,0:T(8,128)(2,1)S(1)} %dynamic-slice_convert_fusion), channel_id=1, source_target_pairs={{0,1},{1,0},{2,3},{3,2},{4,5},{5,4},{6,7},{7,6},{8,9},{9,8},{10,11... | collective-permute-start | bytes 221192 | tf_op jit(solution)/shard_map/ppermute | solution.py:271
  46.1 1.6 %copy-done.14 = bf16[128,8192]{1,0:T(8,128)(2,1)S(1)} copy-done((bf16[128,8192]{1,0:T(8,128)(2,1)S(1)}, bf16[128,8192]{1,0:T(8,128)(2,1)}, u32[]{:S(2)}) %copy-start.14) | copy-done | bytes 2097176
  47.7 2.8 %shard_map.106 = (bf16[256,128]{1,0:T(8,128)(2,1)S(1)}, bf16[256,128]{1,0:T(8,128)(2,1)S(1)}, bf16[256,128]{1,0:T(8,128)(2,1)S(1)}, bf16[256,128]{1,0:T(8,128)(2,1)S(1)}, f32[256,128]{1,0:T(8,128)S(1)}) custom-call(bf16[9,128,128]{2,1,0:T(8,128)(2,1)S(1)} %copy-done.7, s32[2,8192]{1,0:T(2,128)S(1)} %copy-done.9, bf16[128,8192]{1,0:T(8,128)(2,1)S(1)} %copy-done.14), custom_call_target="tpu_custom_call" | custom-call | flops 2000000000 | bytes 4000000 | tf_op jit(solution)/shard_map/pallas_call | solution.py:253
  50.5 0.0 collective-permute-done.7
  50.5 0.7 collective-permute-start.9
  51.3 2.0 %collective-permute-start.8 = (bf16[144,128]{1,0:T(8,128)(2,1)S(1)}, bf16[144,128]{1,0:T(8,128)(2,1)S(1)}, u32[]{:S(2)}, u32[]{:S(2)}) collective-permute-start(bf16[144,128]{1,0:T(8,128)(2,1)S(1)} %dynamic-slice_convert_fusion.1), channel_id=1, source_target_pairs={{0,3},{1,2},{2,1},{3,0},{4,7},{5,6},{6,5},{7,4},{8,11},{9,10},{10,... | collective-permute-start | bytes 110600 | tf_op jit(solution)/shard_map/ppermute | solution.py:271
  53.3 2.1 %collective-permute-done.8 = bf16[144,128]{1,0:T(8,128)(2,1)S(1)} collective-permute-done((bf16[144,128]{1,0:T(8,128)(2,1)S(1)}, bf16[144,128]{1,0:T(8,128)(2,1)S(1)}, u32[]{:S(2)}, u32[]{:S(2)}) %collective-permute-start.8) | collective-permute-done | bytes 36896 | tf_op jit(solution)/shard_map/ppermute | solution.py:271
  55.4 0.0 collective-permute-done.9.in0_ref
  55.5 0.8 collective-permute-start.10
  56.3 2.6 %shard_map.107 = (f32[1024,128]{1,0:T(8,128)S(1)}, bf16[64,128]{1,0:T(8,128)(2,1)S(1)}, bf16[64,128]{1,0:T(8,128)(2,1)S(1)}) custom-call(bf16[9,128,128]{2,1,0:T(8,128)(2,1)S(1)} %copy-done.7, s32[2,3072]{1,0:T(2,128)S(1)} %copy-done.11, bf16[128,3072]{1,0:T(8,128)(2,1)S(1)} %get-tuple-element.62.dm_ref), custom_call_target="tpu_custom_call" | custom-call | flops 2000000000 | bytes 4000000 | tf_op jit(solution)/shard_map/pallas_call | solution.py:253
  58.9 0.1 collective-permute-done.10
  59.1 1.5 %collective-permute-start.11 = (bf16[656,128]{1,0:T(8,128)(2,1)S(1)}, bf16[656,128]{1,0:T(8,128)(2,1)S(1)}, u32[]{:S(2)}, u32[]{:S(2)}) collective-permute-start(bf16[656,128]{1,0:T(8,128)(2,1)S(1)} %pad_maximum_fusion.1), channel_id=1, source_target_pairs={{0,32},{1,33},{2,34},{3,35},{4,36},{5,37},{6,38},{7,39},{8,40},{9,... | collective-permute-start | bytes 503816 | tf_op jit(solution)/shard_map/ppermute | solution.py:271
  60.6 2.3 %shard_map.108.part_ref = f32[1024,128]{1,0:T(8,128)S(1)} custom-call(bf16[9,128,128]{2,1,0:T(8,128)(2,1)S(1)} %copy-done.7, s32[2,3072]{1,0:T(2,128)S(1)} %copy-done.11, bf16[128,3072]{1,0:T(8,128)(2,1)S(1)} %get-tuple-element.62.dm_ref, bf16[1024,128]{1,0:T(8,128)(2,1)S(1)} %get-tuple-element.69.dn_ref, bf16[1024,128]{1,0:T(8,128)(2,1)S(1)} %copy-done.8, ...), custom_call_target="tpu_custom_call" | custom-call | flops 2000000000 | bytes 4000000 | tf_op jit(solution)/shard_map/pallas_call | solution.py:253
  62.9 6.3 %collective-permute-done.11 = bf16[656,128]{1,0:T(8,128)(2,1)S(1)} collective-permute-done((bf16[656,128]{1,0:T(8,128)(2,1)S(1)}, bf16[656,128]{1,0:T(8,128)(2,1)S(1)}, u32[]{:S(2)}, u32[]{:S(2)}) %collective-permute-start.11) | collective-permute-done | bytes 167968 | tf_op jit(solution)/shard_map/ppermute | solution.py:271
  69.3 0.1 collective-permute-start.12
  69.4 5.7 %collective-permute-done.12 = bf16[400,128]{1,0:T(8,128)(2,1)S(1)} collective-permute-done((bf16[400,128]{1,0:T(8,128)(2,1)S(1)}, bf16[400,128]{1,0:T(8,128)(2,1)S(1)}, u32[]{:S(2)}, u32[]{:S(2)}) %collective-permute-start.12) | collective-permute-done | bytes 102432 | tf_op jit(solution)/shard_map/ppermute | solution.py:271
  75.1 1.7 %collective-permute-start.13 = (f32[208,128]{1,0:T(8,128)S(1)}, f32[208,128]{1,0:T(8,128)S(1)}, u32[]{:S(2)}, u32[]{:S(2)}) collective-permute-start(f32[208,128]{1,0:T(8,128)S(1)} %pad_maximum_fusion.3), channel_id=1, source_target_pairs={{0,4},{1,5},{2,6},{3,7},{4,0},{5,1},{6,2},{7,3},{8,12},{9,13},{10,... | collective-permute-start | bytes 319496 | tf_op jit(solution)/shard_map/ppermute | solution.py:271
  76.8 2.1 %collective-permute-done.13 = f32[208,128]{1,0:T(8,128)S(1)} collective-permute-done((f32[208,128]{1,0:T(8,128)S(1)}, f32[208,128]{1,0:T(8,128)S(1)}, u32[]{:S(2)}, u32[]{:S(2)}) %collective-permute-start.13) | collective-permute-done | bytes 106528 | tf_op jit(solution)/shard_map/ppermute | solution.py:271
  78.9 2.8 %collective-permute-start.14 = (f32[144,128]{1,0:T(8,128)S(1)}, f32[144,128]{1,0:T(8,128)S(1)}, u32[]{:S(2)}, u32[]{:S(2)}) collective-permute-start(f32[144,128]{1,0:T(8,128)S(1)} %slice_add_fusion), channel_id=1, source_target_pairs={{0,132},{1,133},{2,134},{3,135},{4,128},{5,129},{6,130},{7,131},{8... | collective-permute-start | bytes 221192 | tf_op jit(solution)/shard_map/ppermute | solution.py:271
  81.7 1.7 %collective-permute-done.14 = f32[144,128]{1,0:T(8,128)S(1)} collective-permute-done((f32[144,128]{1,0:T(8,128)S(1)}, f32[144,128]{1,0:T(8,128)S(1)}, u32[]{:S(2)}, u32[]{:S(2)}) %collective-permute-start.14) | collective-permute-done | bytes 73760 | tf_op jit(solution)/shard_map/ppermute | solution.py:271
  83.5 1.8 %collective-permute-start.15 = (bf16[208,128]{1,0:T(8,128)(2,1)S(1)}, bf16[208,128]{1,0:T(8,128)(2,1)S(1)}, u32[]{:S(2)}, u32[]{:S(2)}) collective-permute-start(bf16[208,128]{1,0:T(8,128)(2,1)S(1)} %pad_maximum_fusion.8), channel_id=1, source_target_pairs={{0,3},{1,2},{2,1},{3,0},{4,7},{5,6},{6,5},{7,4},{8,11},{9,10},{10,... | collective-permute-start | bytes 159752 | tf_op jit(solution)/shard_map/ppermute | solution.py:271
  85.3 2.5 %collective-permute-done.15 = bf16[208,128]{1,0:T(8,128)(2,1)S(1)} collective-permute-done((bf16[208,128]{1,0:T(8,128)(2,1)S(1)}, bf16[208,128]{1,0:T(8,128)(2,1)S(1)}, u32[]{:S(2)}, u32[]{:S(2)}) %collective-permute-start.15) | collective-permute-done | bytes 53280 | tf_op jit(solution)/shard_map/ppermute | solution.py:271
  87.8 0.1 collective-permute-start.16
  88.0 3.3 %collective-permute-done.16 = bf16[352,128]{1,0:T(8,128)(2,1)S(1)} collective-permute-done((bf16[352,128]{1,0:T(8,128)(2,1)S(1)}, bf16[352,128]{1,0:T(8,128)(2,1)S(1)}, u32[]{:S(2)}, u32[]{:S(2)}) %collective-permute-start.16) | collective-permute-done | bytes 90144 | tf_op jit(solution)/shard_map/ppermute | solution.py:271
  91.3 7.0 %collective-permute-start.17 = (bf16[576,128]{1,0:T(8,128)(2,1)S(1)}, bf16[576,128]{1,0:T(8,128)(2,1)S(1)}, u32[]{:S(2)}, u32[]{:S(2)}) collective-permute-start(bf16[576,128]{1,0:T(8,128)(2,1)S(1)} %pad_maximum_fusion.2), channel_id=1, source_target_pairs={{0,8},{1,9},{2,10},{3,11},{4,12},{5,13},{6,14},{7,15},{8,0},{9,1},... | collective-permute-start | bytes 442376 | tf_op jit(solution)/shard_map/ppermute | solution.py:271
  98.4 1.3 %shard_map.109 = f32[1024,128]{1,0:T(8,128)} custom-call(f32[1024,128]{1,0:T(8,128)S(1)} %shard_map.108.part_ref, f32[256,128]{1,0:T(8,128)S(1)} %get-tuple-element.72.own_ref, bf16[256,128]{1,0:T(8,128)(2,1)S(1)} %collective-permute-done.9.in0_ref, bf16[256,128]{1,0:T(8,128)(2,1)S(1)} %slice.41.in1_ref, bf16[256,128]{1,0:T(8,128)(2,1)S(1)} %get-tuple-element.80.in2_ref, ...), custom_call_target="tpu_custom_call" | custom-call | flops 100000000 | bytes 4000000 | tf_op jit(solution)/shard_map/pallas_call | solution.py:253
  99.6 0.0 collective-permute-done.17
  99.6 0.1 broadcast_select_fusion.1
  99.7 0.9 convert.5
  (37 shorter events, 0.4 us)
Async XLA Ops:
  0.6 1.0 copy-start
  1.6 0.7 copy-start.2
  2.7 11.0 %collective-permute-start.4 = (bf16[64,128]{1,0:T(8,128)(2,1)S(1)}, bf16[64,128]{1,0:T(8,128)(2,1)S(1)}, u32[]{:S(2)}, u32[]{:S(2)}) collective-permute-start(bf16[64,128]{1,0:T(8,128)(2,1)S(1)} %get-tuple-element.42), channel_id=1, source_target_pairs={{0,1},{1,2},{2,3},{3,4},{4,5},{5,6},{6,7},{8,9},{9,10},{10,11},{11... | collective-permute-start | bytes 49160 | tf_op jit(solution)/shard_map/ppermute | solution.py:282
  6.8 11.2 %collective-permute-start.5 = (bf16[64,128]{1,0:T(8,128)(2,1)S(1)}, bf16[64,128]{1,0:T(8,128)(2,1)S(1)}, u32[]{:S(2)}, u32[]{:S(2)}) collective-permute-start(bf16[64,128]{1,0:T(8,128)(2,1)S(1)} %get-tuple-element.43), channel_id=1, source_target_pairs={{1,0},{2,1},{3,2},{4,3},{5,4},{6,5},{7,6},{9,8},{10,9},{11,10},{12... | collective-permute-start | bytes 49160 | tf_op jit(solution)/shard_map/ppermute | solution.py:282
  8.1 20.3 %collective-permute-start = (bf16[128,256]{1,0:T(8,128)(2,1)S(1)}, bf16[128,256]{1,0:T(8,128)(2,1)S(1)}, u32[]{:S(2)}, u32[]{:S(2)}) collective-permute-start(bf16[128,256]{1,0:T(8,128)(2,1)S(1)} %get-tuple-element.41.bound_t_ref), channel_id=1, source_target_pairs={{0,8},{8,0},{16,24},{24,16},{32,40},{40,32},{48,56},{56,48},{64,72... | collective-permute-start | bytes 196616 | tf_op jit(solution)/shard_map/ppermute | solution.py:276
  9.1 19.3 %collective-permute-start.1 = (bf16[128,256]{1,0:T(8,128)(2,1)S(1)}, bf16[128,256]{1,0:T(8,128)(2,1)S(1)}, u32[]{:S(2)}, u32[]{:S(2)}) collective-permute-start(bf16[128,256]{1,0:T(8,128)(2,1)S(1)} %get-tuple-element.41.bound_t_ref), channel_id=1, source_target_pairs={{0,16},{8,24},{16,0},{24,8},{32,48},{40,56},{48,32},{56,40},{64,80... | collective-permute-start | bytes 196616 | tf_op jit(solution)/shard_map/ppermute | solution.py:276
  10.8 17.6 %collective-permute-start.2 = (bf16[128,256]{1,0:T(8,128)(2,1)S(1)}, bf16[128,256]{1,0:T(8,128)(2,1)S(1)}, u32[]{:S(2)}, u32[]{:S(2)}) collective-permute-start(bf16[128,256]{1,0:T(8,128)(2,1)S(1)} %get-tuple-element.41.bound_t_ref), channel_id=1, source_target_pairs={{0,32},{8,40},{16,48},{24,56},{32,0},{40,8},{48,16},{56,24},{64,96... | collective-permute-start | bytes 196616 | tf_op jit(solution)/shard_map/ppermute | solution.py:276
  13.7 14.6 %collective-permute-start.3 = (bf16[128,256]{1,0:T(8,128)(2,1)S(1)}, bf16[128,256]{1,0:T(8,128)(2,1)S(1)}, u32[]{:S(2)}, u32[]{:S(2)}) collective-permute-start(bf16[128,256]{1,0:T(8,128)(2,1)S(1)} %get-tuple-element.41.bound_t_ref), channel_id=1, source_target_pairs={{0,64},{8,72},{16,80},{24,88},{32,96},{40,104},{48,112},{56,120},{... | collective-permute-start | bytes 196616 | tf_op jit(solution)/shard_map/ppermute | solution.py:276
  18.0 1.1 %copy-start.4 = (bf16[3072,128]{1,0:T(8,128)(2,1)S(1)}, bf16[3072,128]{1,0:T(8,128)(2,1)}, u32[]{:S(2)}) copy-start(bf16[3072,128]{1,0:T(8,128)(2,1)} %feats_ref.1) | copy-start | bytes 2359300
  19.1 1.0 copy-start.6
  20.1 0.7 copy-start.10
  20.8 7.6 %copy-start.1 = (bf16[1024,128]{1,0:T(8,128)(2,1)S(1)}, bf16[1024,128]{1,0:T(8,128)(2,1)}, u32[]{:S(2)}) copy-start(bf16[1024,128]{1,0:T(8,128)(2,1)} %lat_ref.1) | copy-start | bytes 786436
  20.8 7.6 %copy-start.3 = (s32[256]{0:T(256)S(1)}, s32[256]{0:T(256)}, u32[]{:S(2)}) copy-start(s32[256]{0:T(256)} %param.13) | copy-start | bytes 3076
  20.8 7.6 %copy-start.5 = (bf16[3072,128]{1,0:T(8,128)(2,1)S(1)}, bf16[3072,128]{1,0:T(8,128)(2,1)}, u32[]{:S(2)}) copy-start(bf16[3072,128]{1,0:T(8,128)(2,1)} %feats_ref.1) | copy-start | bytes 2359300
  20.8 7.6 %copy-start.7 = (bf16[9,128,128]{2,1,0:T(8,128)(2,1)S(1)}, bf16[9,128,128]{2,1,0:T(8,128)(2,1)}, u32[]{:S(2)}) copy-start(bf16[9,128,128]{2,1,0:T(8,128)(2,1)} %w_ref.7) | copy-start | bytes 884740
  20.8 7.6 %copy-start.8 = (bf16[1024,128]{1,0:T(8,128)(2,1)S(1)}, bf16[1024,128]{1,0:T(8,128)(2,1)}, u32[]{:S(2)}) copy-start(bf16[1024,128]{1,0:T(8,128)(2,1)} %cot_ref.3) | copy-start | bytes 786436
  20.8 7.6 %copy-start.9 = (s32[2,8192]{1,0:T(2,128)S(1)}, s32[2,8192]{1,0:T(2,128)}, u32[]{:S(2)}) copy-start(s32[2,8192]{1,0:T(2,128)} %contacts_ref.3) | copy-start | bytes 196612
  20.8 7.6 %copy-start.11 = (s32[2,3072]{1,0:T(2,128)S(1)}, s32[2,3072]{1,0:T(2,128)}, u32[]{:S(2)}) copy-start(s32[2,3072]{1,0:T(2,128)} %edges_ref.5) | copy-start | bytes 73732
  20.8 7.6 %copy-start.12 = (s32[1,4]{1,0:T(1,128)S(1)}, s32[1,4]{1,0:T(1,128)}, u32[]{:S(2)}) copy-start(s32[1,4]{1,0:T(1,128)} %counts_ref.1) | copy-start | bytes 52
  40.3 1.4 %copy-start.13 = (bf16[128,8192]{1,0:T(8,128)(2,1)}, bf16[128,8192]{1,0:T(8,128)(2,1)S(1)}, u32[]{:S(2)}) copy-start(bf16[128,8192]{1,0:T(8,128)(2,1)S(1)} %get-tuple-element.52.dc_ref) | copy-start | bytes 6291460
  41.7 1.9 %collective-permute-start.6 = (bf16[576,128]{1,0:T(8,128)(2,1)S(1)}, bf16[576,128]{1,0:T(8,128)(2,1)S(1)}, u32[]{:S(2)}, u32[]{:S(2)}) collective-permute-start(bf16[576,128]{1,0:T(8,128)(2,1)S(1)} %get-tuple-element.49), channel_id=1, source_target_pairs={{0,8},{1,9},{2,10},{3,11},{4,12},{5,13},{6,14},{7,15},{8,0},{9,1},... | collective-permute-start | bytes 442376 | tf_op jit(solution)/shard_map/ppermute | solution.py:271
  43.7 6.9 %collective-permute-start.7 = (bf16[288,128]{1,0:T(8,128)(2,1)S(1)}, bf16[288,128]{1,0:T(8,128)(2,1)S(1)}, u32[]{:S(2)}, u32[]{:S(2)}) collective-permute-start(bf16[288,128]{1,0:T(8,128)(2,1)S(1)} %dynamic-slice_convert_fusion), channel_id=1, source_target_pairs={{0,1},{1,0},{2,3},{3,2},{4,5},{5,4},{6,7},{7,6},{8,9},{9,8},{10,11... | collective-permute-start | bytes 221192 | tf_op jit(solution)/shard_map/ppermute | solution.py:271
  46.1 1.6 %copy-start.14 = (bf16[128,8192]{1,0:T(8,128)(2,1)S(1)}, bf16[128,8192]{1,0:T(8,128)(2,1)}, u32[]{:S(2)}) copy-start(bf16[128,8192]{1,0:T(8,128)(2,1)} %copy-done.13) | copy-start | bytes 6291460
  50.5 4.9 %collective-permute-start.9 = (bf16[256,128]{1,0:T(8,128)(2,1)S(1)}, bf16[256,128]{1,0:T(8,128)(2,1)S(1)}, u32[]{:S(2)}, u32[]{:S(2)}) collective-permute-start(bf16[256,128]{1,0:T(8,128)(2,1)S(1)} %get-tuple-element.58), channel_id=1, source_target_pairs={{0,8},{1,9},{2,10},{3,11},{4,12},{5,13},{6,14},{7,15},{8,0},{9,1},... | collective-permute-start | bytes 196616 | tf_op jit(solution)/shard_map/ppermute | solution.py:271
  51.3 4.1 %collective-permute-start.8 = (bf16[144,128]{1,0:T(8,128)(2,1)S(1)}, bf16[144,128]{1,0:T(8,128)(2,1)S(1)}, u32[]{:S(2)}, u32[]{:S(2)}) collective-permute-start(bf16[144,128]{1,0:T(8,128)(2,1)S(1)} %dynamic-slice_convert_fusion.1), channel_id=1, source_target_pairs={{0,3},{1,2},{2,1},{3,0},{4,7},{5,6},{6,5},{7,4},{8,11},{9,10},{10,... | collective-permute-start | bytes 110600 | tf_op jit(solution)/shard_map/ppermute | solution.py:271
  55.5 3.6 %collective-permute-start.10 = (bf16[400,128]{1,0:T(8,128)(2,1)S(1)}, bf16[400,128]{1,0:T(8,128)(2,1)S(1)}, u32[]{:S(2)}, u32[]{:S(2)}) collective-permute-start(bf16[400,128]{1,0:T(8,128)(2,1)S(1)} %pad_maximum_fusion.4), channel_id=1, source_target_pairs={{0,16},{1,17},{2,18},{3,19},{4,20},{5,21},{6,22},{7,23},{8,24},{9,... | collective-permute-start | bytes 307208 | tf_op jit(solution)/shard_map/ppermute | solution.py:271
  59.1 10.1 %collective-permute-start.11 = (bf16[656,128]{1,0:T(8,128)(2,1)S(1)}, bf16[656,128]{1,0:T(8,128)(2,1)S(1)}, u32[]{:S(2)}, u32[]{:S(2)}) collective-permute-start(bf16[656,128]{1,0:T(8,128)(2,1)S(1)} %pad_maximum_fusion.1), channel_id=1, source_target_pairs={{0,32},{1,33},{2,34},{3,35},{4,36},{5,37},{6,38},{7,39},{8,40},{9,... | collective-permute-start | bytes 503816 | tf_op jit(solution)/shard_map/ppermute | solution.py:271
  69.3 5.8 %collective-permute-start.12 = (bf16[400,128]{1,0:T(8,128)(2,1)S(1)}, bf16[400,128]{1,0:T(8,128)(2,1)S(1)}, u32[]{:S(2)}, u32[]{:S(2)}) collective-permute-start(bf16[400,128]{1,0:T(8,128)(2,1)S(1)} %pad_maximum_fusion.5), channel_id=1, source_target_pairs={{0,96},{1,97},{2,98},{3,99},{4,100},{5,101},{6,102},{7,103},{8,104... | collective-permute-start | bytes 307208 | tf_op jit(solution)/shard_map/ppermute | solution.py:271
  75.1 3.8 %collective-permute-start.13 = (f32[208,128]{1,0:T(8,128)S(1)}, f32[208,128]{1,0:T(8,128)S(1)}, u32[]{:S(2)}, u32[]{:S(2)}) collective-permute-start(f32[208,128]{1,0:T(8,128)S(1)} %pad_maximum_fusion.3), channel_id=1, source_target_pairs={{0,4},{1,5},{2,6},{3,7},{4,0},{5,1},{6,2},{7,3},{8,12},{9,13},{10,... | collective-permute-start | bytes 319496 | tf_op jit(solution)/shard_map/ppermute | solution.py:271
  78.9 4.6 %collective-permute-start.14 = (f32[144,128]{1,0:T(8,128)S(1)}, f32[144,128]{1,0:T(8,128)S(1)}, u32[]{:S(2)}, u32[]{:S(2)}) collective-permute-start(f32[144,128]{1,0:T(8,128)S(1)} %slice_add_fusion), channel_id=1, source_target_pairs={{0,132},{1,133},{2,134},{3,135},{4,128},{5,129},{6,130},{7,131},{8... | collective-permute-start | bytes 221192 | tf_op jit(solution)/shard_map/ppermute | solution.py:271
  83.5 4.3 %collective-permute-start.15 = (bf16[208,128]{1,0:T(8,128)(2,1)S(1)}, bf16[208,128]{1,0:T(8,128)(2,1)S(1)}, u32[]{:S(2)}, u32[]{:S(2)}) collective-permute-start(bf16[208,128]{1,0:T(8,128)(2,1)S(1)} %pad_maximum_fusion.8), channel_id=1, source_target_pairs={{0,3},{1,2},{2,1},{3,0},{4,7},{5,6},{6,5},{7,4},{8,11},{9,10},{10,... | collective-permute-start | bytes 159752 | tf_op jit(solution)/shard_map/ppermute | solution.py:271
  87.8 3.5 %collective-permute-start.16 = (bf16[352,128]{1,0:T(8,128)(2,1)S(1)}, bf16[352,128]{1,0:T(8,128)(2,1)S(1)}, u32[]{:S(2)}, u32[]{:S(2)}) collective-permute-start(bf16[352,128]{1,0:T(8,128)(2,1)S(1)} %pad_maximum_fusion.6), channel_id=1, source_target_pairs={{0,1},{1,0},{2,3},{3,2},{4,5},{5,4},{6,7},{7,6},{8,9},{9,8},{10,11... | collective-permute-start | bytes 270344 | tf_op jit(solution)/shard_map/ppermute | solution.py:271
  91.3 8.3 %collective-permute-start.17 = (bf16[576,128]{1,0:T(8,128)(2,1)S(1)}, bf16[576,128]{1,0:T(8,128)(2,1)S(1)}, u32[]{:S(2)}, u32[]{:S(2)}) collective-permute-start(bf16[576,128]{1,0:T(8,128)(2,1)S(1)} %pad_maximum_fusion.2), channel_id=1, source_target_pairs={{0,8},{1,9},{2,10},{3,11},{4,12},{5,13},{6,14},{7,15},{8,0},{9,1},... | collective-permute-start | bytes 442376 | tf_op jit(solution)/shard_map/ppermute | solution.py:271

commit v4 on v3

--- a/solution.py
+++ b/solution.py
@@ -286,9 +286,13 @@
     return block.astype(F32)
 
 
-def half_of(block, which):
-    size = block.shape[0] // 2
-    return lax.dynamic_slice_in_dim(block, which * size, size, 0)
+def ordered_by_y(found, row_y):
+    odd, high = row_y % 2 == 1, row_y >= 2
+    low_pair = [jnp.where(odd, found[1], found[0]), jnp.where(odd, found[0], found[1])]
+    high_pair = [jnp.where(odd, found[3], found[2]), jnp.where(odd, found[2], found[3])]
+    ordered = [jnp.where(high, b, a) for a, b in zip(low_pair, high_pair)]
+    ordered += [jnp.where(high, a, b) for a, b in zip(low_pair, high_pair)]
+    return jnp.concatenate(ordered, axis=0)
 
 
 def joined(own, other, which):
@@ -322,9 +326,14 @@
         hbm=2,
         mib=8,
     )
+    far_two = exchanged(bound_t, mask_z=2)
     before = shifted(high_rows, 1)
     after = shifted(low_rows, -1)
-    fars = [swapped(bound_t, r) for r in range(rounds)]
+    far_one = exchanged(bound_t, mask_z=1)
+    far_zero = exchanged(bound_t, mask_core=1)
+    far_two, before, after = tie(far_two, before, after)
+    far_three = exchanged(far_two, mask_z=6)
+    fars = [far_zero, far_one, far_two, far_three]
     rows, slope, agg = call(
         mesh_kernel,
         [((2 * width, edge_count), BF), ((width, edge_count), F32), ((rows_dev, width), BF)],
@@ -366,10 +375,6 @@
         mib=26,
     )
     other = exchanged(sent, mask_core=1)
-    other, d_contact = tie(other, d_contact)
-    block = kept + wide(other)
-    half, quarter = (row_y ^ (row_y >> 1)) & 1, row_y >> 1
-    other = exchanged(half_of(block, 1 - half).astype(BF), mask_y=1)
     *far_grads, own_grad = call(
         contact_back_kernel,
         [((bound_count, width), BF)] * rounds + [((bound_count, width), F32)],
@@ -378,14 +383,18 @@
         mib=16,
     )
     other, *far_grads = tie(other, *far_grads)
-    block = half_of(block, half) + wide(other)
-    other = exchanged(half_of(block, 1 - quarter).astype(BF), mask_y=3)
-    in_zero = exchanged(far_grads[0], mask_core=1)
-    other, in_zero, d_mesh = tie(other, in_zero, d_mesh)
-    block = (half_of(block, quarter) + wide(other)).astype(BF)
-
-    size = block.shape[0]
-    other = exchanged(jnp.concatenate([block, far_grads[1]], axis=0), mask_z=1)
+    block = kept + wide(other)
+    size = block.shape[0] // 4
+    pieces = [
+        lax.dynamic_slice_in_dim(block, (row_y ^ mask) * size, size, 0) for mask in range(4)
+    ]
+    one, two, three = [exchanged(pieces[mask].astype(BF), mask_y=mask) for mask in (1, 2, 3)]
+    in_one = exchanged(far_grads[1], mask_z=1)
+    pair = exchanged(jnp.concatenate(far_grads[2:], axis=0), mask_z=2)
+    one, two, three, d_mesh = tie(one, two, three, d_mesh)
+    block = ((pieces[0] + wide(one)) + (wide(two) + wide(three))).astype(BF)
+
+    one, two, three = [exchanged(block, mask_x=mask) for mask in (1, 2, 3)]
     part, low, high = call(
         send_back_kernel,
         [((rows_dev, width), F32), ((HB, width), BF), ((HB, width), BF)],
@@ -394,10 +403,17 @@
         flops=2 * 10**9,
         mib=16,
     )
-    other, part, low, high = tie(other, part, low, high)
-    in_one = other[size:]
-    block = (wide(block) + wide(other[:size])).astype(BF)
-    other = exchanged(jnp.concatenate([block, far_grads[2], far_grads[3]], axis=0), mask_z=2)
+    one, two, three, part, low, high, in_one, pair = tie(
+        one, two, three, part, low, high, in_one, pair
+    )
+    block = ((wide(block) + wide(one)) + (wide(two) + wide(three))).astype(BF)
+
+    other = exchanged(block, mask_z=1)
+    from_prev = shifted(high, 1)
+    from_next = shifted(low, -1)
+    other, part = tie(other, part)
+    block = (wide(block) + wide(other)).astype(BF)
+    other = exchanged(block, mask_z=2)
     (part,) = call(
         recv_back_kernel,
         [((rows_dev, width), F32)],
@@ -406,32 +422,18 @@
         flops=2 * 10**9,
         mib=16,
     )
-    other, part = tie(other, part)
-    in_two = other[size : size + bound_count]
-    block = (wide(block) + wide(other[:size])).astype(BF)
-    other = exchanged(jnp.concatenate([block, other[size + bound_count :]], axis=0), mask_z=6)
-    in_three = other[size:]
-    block = wide(block) + wide(other[:size])
-
-    rim = wide(jnp.where(row_y == 0, low, high))
-    other = exchanged(jnp.concatenate([block, rim], axis=0), mask_x=1)
-    rim = other[size:].astype(BF)
-    block = block + other[:size]
-    block = (block + exchanged(block, mask_x=3)).astype(BF)
-    rim = jnp.where(row_y == 1, high, jnp.where(row_y == 2, low, rim))
-    other = exchanged(jnp.concatenate([block, rim], axis=0), mask_y=3)
-    rim_three = other[size:]
-    block = joined(block, other[:size], quarter)
-    rim = jnp.where(row_y % 2 == 0, high, low)
-    other = exchanged(jnp.concatenate([block, rim], axis=0), mask_y=1)
-    rim_one = other[2 * size :]
-    panel = lax.axis_index("panel")
-    nothing = jnp.zeros_like(rim)
-    from_prev = jnp.where(row_y % 2 == 0, rim_three, rim_one)
-    from_prev = jnp.where(panel == 0, nothing, from_prev)
-    from_next = jnp.where(row_y % 2 == 0, rim_one, rim_three)
-    from_next = jnp.where(panel == lax.axis_size("panel") - 1, nothing, from_next)
-    block = joined(block, other[: 2 * size], half)
+    other, part, from_prev, from_next, pair = tie(other, part, from_prev, from_next, pair)
+    block = (wide(block) + wide(other)).astype(BF)
+    other = exchanged(block, mask_z=6)
+    in_zero = exchanged(far_grads[0], mask_core=1)
+    in_two = pair[:bound_count]
+    in_three = exchanged(pair[bound_count:], mask_z=6)
+    other, in_zero = tie(other, in_zero)
+    block = (wide(block) + wide(other)).astype(BF)
+
+    found = [exchanged(block, mask_y=mask) for mask in (1, 2, 3)]
+    *found, in_three = tie(*found, in_three)
+    block = ordered_by_y([block] + found, row_y)
     other = exchanged(block, mask_core=1)
     (grad_rows,) = call(
         last_kernel,

time: 101 us -> 95.3 us (0.944)
  waiting for transfers between devices: 25 us -> 8.23 us
  starting transfers between devices: 37.1 us -> 51.3 us
  local copies, waits for them, and re-layouts: 7.49 us -> 4.53 us
    ppermute x12 -> x22, starting transfers between devices: 21.9 us -> 44.2 us  [exchanged(): return lax.ppermute(block, ('region', 'panel'), route)]
    ppermute x12 -> x22, waiting for transfers between devices: 24.9 us -> 8.02 us  [exchanged(): return lax.ppermute(block, ('region', 'panel'), route)]
    ppermute x4 -> x0, starting transfers between devices: 9.9 us -> none  [swapped(): lax.ppermute(block, 'region', [(i, i ^ 1 << bit) for i in range(size)])]
    unnamed x30 -> x26, local copies, waits for them, and re-layouts: 7.44 us -> 4.49 us
    ppermute x2 -> x4, starting transfers between devices: 5.32 us -> 7.05 us  [shifted(): return lax.ppermute(array, 'panel', pairs)]
  transfers between devices with their start and end apart: 18 -> 26, of which waited for: 9 -> 8; matrix products, arithmetic and copies ran while one was open for 0% -> 0% of each run, Pallas kernels for 16% -> 17%
where the time goes in v4:
time: 95.3 us; the launch traced here: 94.9 us
  starting transfers between devices  51.3 us (54%)
  Pallas kernels  28.7 us (30%)
  waiting for transfers between devices  8.23 us (9%)
  local copies, waits for them, and re-layouts  4.53 us (5%)
  other arithmetic  1.13 us (1%)
  between operations  0.99 us (1%)
    ppermute x22, starting transfers between devices, exchanged(): return lax.ppermute(block, ('region', 'panel'), route)  44.2 us
    pallas_call x7, Pallas kernels, call(): pl.pallas_call(kernel, out_shape=[jax.ShapeDtypeStruct(shape, kind) for s...  28.7 us
    ppermute x22, waiting for transfers between devices, exchanged(): return lax.ppermute(block, ('region', 'panel'), route)  8.02 us
    ppermute x4, starting transfers between devices, shifted(): return lax.ppermute(array, 'panel', pairs)  7.05 us
    unnamed x26, local copies, waits for them, and re-layouts  4.49 us
  transfers between devices with their start and end apart: 26, of which 8 were waited for; matrix products, arithmetic and copies ran while one was open for 0% of the time, Pallas kernels for 17%

profile of v4, /device:TPU:1, one launch (start us, length us, event | category | flops | bytes accessed | tf_op | source)
XLA Modules:
  0.0 94.9 jit_solution(3263930055633985096)
XLA Ops:
  0.6 0.0 copy-start
  0.6 0.9 copy-done
  1.6 0.7 copy-done.2
  2.3 0.4 shard_map.103
  2.7 3.9 %collective-permute-start.2 = (bf16[128,256]{1,0:T(8,128)(2,1)S(1)}, bf16[128,256]{1,0:T(8,128)(2,1)S(1)}, u32[]{:S(2)}, u32[]{:S(2)}) collective-permute-start(bf16[128,256]{1,0:T(8,128)(2,1)S(1)} %get-tuple-element.58.bound_t_ref), channel_id=1, source_target_pairs={{0,32},{1,33},{2,34},{3,35},{4,36},{5,37},{6,38},{7,39},{8,40},{9,... | collective-permute-start | bytes 196616 | tf_op jit(solution)/shard_map/ppermute | solution.py:271
  6.6 3.2 %collective-permute-start.3 = (bf16[64,128]{1,0:T(8,128)(2,1)S(1)}, bf16[64,128]{1,0:T(8,128)(2,1)S(1)}, u32[]{:S(2)}, u32[]{:S(2)}) collective-permute-start(bf16[64,128]{1,0:T(8,128)(2,1)S(1)} %get-tuple-element.59), channel_id=1, source_target_pairs={{0,1},{1,2},{2,3},{3,4},{4,5},{5,6},{6,7},{8,9},{9,10},{10,11},{11... | collective-permute-start | bytes 49160 | tf_op jit(solution)/shard_map/ppermute | solution.py:282
  9.8 1.3 %collective-permute-start.4 = (bf16[64,128]{1,0:T(8,128)(2,1)S(1)}, bf16[64,128]{1,0:T(8,128)(2,1)S(1)}, u32[]{:S(2)}, u32[]{:S(2)}) collective-permute-start(bf16[64,128]{1,0:T(8,128)(2,1)S(1)} %get-tuple-element.60), channel_id=1, source_target_pairs={{1,0},{2,1},{3,2},{4,3},{5,4},{6,5},{7,6},{9,8},{10,9},{11,10},{12... | collective-permute-start | bytes 49160 | tf_op jit(solution)/shard_map/ppermute | solution.py:282
  11.1 1.3 %collective-permute-start = (bf16[128,256]{1,0:T(8,128)(2,1)S(1)}, bf16[128,256]{1,0:T(8,128)(2,1)S(1)}, u32[]{:S(2)}, u32[]{:S(2)}) collective-permute-start(bf16[128,256]{1,0:T(8,128)(2,1)S(1)} %get-tuple-element.58.bound_t_ref), channel_id=1, source_target_pairs={{0,8},{1,9},{2,10},{3,11},{4,12},{5,13},{6,14},{7,15},{8,0},{9,1},... | collective-permute-start | bytes 196616 | tf_op jit(solution)/shard_map/ppermute | solution.py:271
  12.4 1.7 %collective-permute-start.1 = (bf16[128,256]{1,0:T(8,128)(2,1)S(1)}, bf16[128,256]{1,0:T(8,128)(2,1)S(1)}, u32[]{:S(2)}, u32[]{:S(2)}) collective-permute-start(bf16[128,256]{1,0:T(8,128)(2,1)S(1)} %get-tuple-element.58.bound_t_ref), channel_id=1, source_target_pairs={{0,16},{1,17},{2,18},{3,19},{4,20},{5,21},{6,22},{7,23},{8,24},{9,... | collective-permute-start | bytes 196616 | tf_op jit(solution)/shard_map/ppermute | solution.py:271
  14.1 0.0 collective-permute-done.3.before_ref
  14.1 0.2 collective-permute-done.4.after_ref
  14.3 0.0 collective-permute-done.2.far2_ref
  14.3 4.2 %collective-permute-start.5 = (bf16[128,256]{1,0:T(8,128)(2,1)S(1)}, bf16[128,256]{1,0:T(8,128)(2,1)S(1)}, u32[]{:S(2)}, u32[]{:S(2)}) collective-permute-start(bf16[128,256]{1,0:T(8,128)(2,1)S(1)} %collective-permute-done.2.far2_ref), channel_id=1, source_target_pairs={{0,96},{1,97},{2,98},{3,99},{4,100},{5,101},{6,102},{7,103},{8,104... | collective-permute-start | bytes 196616 | tf_op jit(solution)/shard_map/ppermute | solution.py:271
  18.5 1.1 %copy-done.4 = bf16[3072,128]{1,0:T(8,128)(2,1)S(1)} copy-done((bf16[3072,128]{1,0:T(8,128)(2,1)S(1)}, bf16[3072,128]{1,0:T(8,128)(2,1)}, u32[]{:S(2)}) %copy-start.4) | copy-done | bytes 786456
  19.6 1.0 %copy-done.6 = bf16[9,128,128]{2,1,0:T(8,128)(2,1)S(1)} copy-done((bf16[9,128,128]{2,1,0:T(8,128)(2,1)S(1)}, bf16[9,128,128]{2,1,0:T(8,128)(2,1)}, u32[]{:S(2)}) %copy-start.6) | copy-done | bytes 294936
  20.6 0.7 copy-done.10
  21.4 0.0 copy-start.8
  21.4 0.0 copy-start.9
  21.4 0.0 copy-start.12
  21.4 7.5 %shard_map.104 = (bf16[256,3072]{1,0:T(8,128)(2,1)S(1)}, f32[128,3072]{1,0:T(8,128)S(1)}, bf16[1024,128]{1,0:T(8,128)(2,1)S(1)}) custom-call(bf16[128,1024]{1,0:T(8,128)(2,1)S(1)} %get-tuple-element.57.lat_t_ref, bf16[64,128]{1,0:T(8,128)(2,1)S(1)} %collective-permute-done.3.before_ref, bf16[64,128]{1,0:T(8,128)(2,1)S(1)} %collective-permute-done.4.after_ref, ...), custom_call_target="tpu_custom_call" | custom-call | flops 6000000000 | bytes 4000000 | tf_op jit(solution)/shard_map/pallas_call | solution.py:253
  28.9 0.0 collective-permute-done.far0_ref
  28.9 0.0 collective-permute-done.5.far3_ref
  29.0 11.9 %shard_map.105 = (bf16[1024,128]{1,0:T(8,128)(2,1)}, f32[576,128]{1,0:T(8,128)S(1)}, bf16[576,128]{1,0:T(8,128)(2,1)S(1)}, bf16[128,3072]{1,0:T(8,128)(2,1)S(1)}...) custom-call(s32[1,4]{1,0:T(1,128)S(1)} %copy-done.12, s32[1]{0:T(128)} %bitcast.core_ref, ...), custom_call_target="tpu_custom_call" | custom-call | flops 8000000000 | bytes 4000000 | tf_op jit(solution)/shard_map/pallas_call | solution.py:253
  40.9 2.7 %collective-permute-start.6 = (bf16[576,128]{1,0:T(8,128)(2,1)S(1)}, bf16[576,128]{1,0:T(8,128)(2,1)S(1)}, u32[]{:S(2)}, u32[]{:S(2)}) collective-permute-start(bf16[576,128]{1,0:T(8,128)(2,1)S(1)} %get-tuple-element.69), channel_id=1, source_target_pairs={{0,8},{1,9},{2,10},{3,11},{4,12},{5,13},{6,14},{7,15},{8,0},{9,1},... | collective-permute-start | bytes 442376 | tf_op jit(solution)/shard_map/ppermute | solution.py:271
  43.6 2.8 %shard_map.106 = (bf16[256,128]{1,0:T(8,128)(2,1)S(1)}, bf16[256,128]{1,0:T(8,128)(2,1)S(1)}, bf16[256,128]{1,0:T(8,128)(2,1)S(1)}, bf16[256,128]{1,0:T(8,128)(2,1)S(1)}, f32[256,128]{1,0:T(8,128)S(1)}) custom-call(bf16[9,128,128]{2,1,0:T(8,128)(2,1)S(1)} %copy-done.7, s32[2,8192]{1,0:T(2,128)S(1)} %copy-done.9, bf16[128,8192]{1,0:T(8,128)(2,1)S(1)} %get-tuple-element.70.dc_ref), custom_call_target="tpu_custom_call" | custom-call | flops 2000000000 | bytes 4000000 | tf_op jit(solution)/shard_map/pallas_call | solution.py:253
  46.4 0.0 collective-permute-done.6
  46.5 1.4 %collective-permute-start.7 = (bf16[144,128]{1,0:T(8,128)(2,1)S(1)}, bf16[144,128]{1,0:T(8,128)(2,1)S(1)}, u32[]{:S(2)}, u32[]{:S(2)}) collective-permute-start(bf16[144,128]{1,0:T(8,128)(2,1)S(1)} %get-tuple-element.115), channel_id=1, source_target_pairs={{0,1},{1,0},{2,3},{3,2},{4,5},{5,4},{6,7},{7,6},{8,9},{9,8},{10,11... | collective-permute-start | bytes 110600 | tf_op jit(solution)/shard_map/ppermute | solution.py:271
  47.9 4.3 %collective-permute-start.8 = (bf16[144,128]{1,0:T(8,128)(2,1)S(1)}, bf16[144,128]{1,0:T(8,128)(2,1)S(1)}, u32[]{:S(2)}, u32[]{:S(2)}) collective-permute-start(bf16[144,128]{1,0:T(8,128)(2,1)S(1)} %get-tuple-element.114), channel_id=1, source_target_pairs={{0,2},{1,3},{2,0},{3,1},{4,6},{5,7},{6,4},{7,5},{8,10},{9,11},{10,... | collective-permute-start | bytes 110600 | tf_op jit(solution)/shard_map/ppermute | solution.py:271
  52.2 0.0 collective-permute-start.9
  52.2 1.3 %collective-permute-start.14 = (bf16[512,128]{1,0:T(8,128)(2,1)S(1)}, bf16[512,128]{1,0:T(8,128)(2,1)S(1)}, u32[]{:S(2)}, u32[]{:S(2)}) collective-permute-start(bf16[512,128]{1,0:T(8,128)(2,1)S(1)} %pad_maximum_fusion.2), channel_id=1, source_target_pairs={{0,32},{1,33},{2,34},{3,35},{4,36},{5,37},{6,38},{7,39},{8,40},{9,... | collective-permute-start | bytes 393224 | tf_op jit(solution)/shard_map/ppermute | solution.py:271
  53.5 0.7 collective-permute-start.13
  54.2 0.1 collective-permute-done.8
  54.3 1.9 %collective-permute-done.9 = bf16[144,128]{1,0:T(8,128)(2,1)S(1)} collective-permute-done((bf16[144,128]{1,0:T(8,128)(2,1)S(1)}, bf16[144,128]{1,0:T(8,128)(2,1)S(1)}, u32[]{:S(2)}, u32[]{:S(2)}) %collective-permute-start.9) | collective-permute-done | bytes 36896 | tf_op jit(solution)/shard_map/ppermute | solution.py:271
  56.2 0.1 collective-permute-start.10
  56.3 2.5 %collective-permute-start.11 = (bf16[144,128]{1,0:T(8,128)(2,1)S(1)}, bf16[144,128]{1,0:T(8,128)(2,1)S(1)}, u32[]{:S(2)}, u32[]{:S(2)}) collective-permute-start(bf16[144,128]{1,0:T(8,128)(2,1)S(1)} %add_convert_fusion.4), channel_id=1, source_target_pairs={{0,128},{1,129},{2,130},{3,131},{4,132},{5,133},{6,134},{7,135},{8... | collective-permute-start | bytes 110600 | tf_op jit(solution)/shard_map/ppermute | solution.py:271
  58.9 1.3 %collective-permute-start.12 = (bf16[144,128]{1,0:T(8,128)(2,1)S(1)}, bf16[144,128]{1,0:T(8,128)(2,1)S(1)}, u32[]{:S(2)}, u32[]{:S(2)}) collective-permute-start(bf16[144,128]{1,0:T(8,128)(2,1)S(1)} %add_convert_fusion.4), channel_id=1, source_target_pairs={{0,132},{1,133},{2,134},{3,135},{4,128},{5,129},{6,130},{7,131},{8... | collective-permute-start | bytes 110600 | tf_op jit(solution)/shard_map/ppermute | solution.py:271
  60.2 2.6 %shard_map.107 = (f32[1024,128]{1,0:T(8,128)S(1)}, bf16[64,128]{1,0:T(8,128)(2,1)S(1)}, bf16[64,128]{1,0:T(8,128)(2,1)S(1)}) custom-call(bf16[9,128,128]{2,1,0:T(8,128)(2,1)S(1)} %copy-done.7, s32[2,3072]{1,0:T(2,128)S(1)} %copy-done.11, bf16[128,3072]{1,0:T(8,128)(2,1)S(1)} %get-tuple-element.80.dm_ref), custom_call_target="tpu_custom_call" | custom-call | flops 2000000000 | bytes 4000000 | tf_op jit(solution)/shard_map/pallas_call | solution.py:253
  62.9 0.0 collective-permute-done.10
  62.9 0.0 collective-permute-done.11
  62.9 0.4 collective-permute-done.12
  63.3 0.8 collective-permute-start.15
  64.2 3.0 %collective-permute-start.20 = (bf16[256,128]{1,0:T(8,128)(2,1)S(1)}, bf16[256,128]{1,0:T(8,128)(2,1)S(1)}, u32[]{:S(2)}, u32[]{:S(2)}) collective-permute-start(bf16[256,128]{1,0:T(8,128)(2,1)S(1)} %get-tuple-element.100), channel_id=1, source_target_pairs={{0,8},{1,9},{2,10},{3,11},{4,12},{5,13},{6,14},{7,15},{8,0},{9,1},... | collective-permute-start | bytes 196616 | tf_op jit(solution)/shard_map/ppermute | solution.py:271
  67.2 1.3 %collective-permute-start.17 = (bf16[64,128]{1,0:T(8,128)(2,1)S(1)}, bf16[64,128]{1,0:T(8,128)(2,1)S(1)}, u32[]{:S(2)}, u32[]{:S(2)}) collective-permute-start(bf16[64,128]{1,0:T(8,128)(2,1)S(1)} %get-tuple-element.94), channel_id=1, source_target_pairs={{0,1},{1,2},{2,3},{3,4},{4,5},{5,6},{6,7},{8,9},{9,10},{10,11},{11... | collective-permute-start | bytes 49160 | tf_op jit(solution)/shard_map/ppermute | solution.py:282
  68.5 1.3 %collective-permute-start.18 = (bf16[64,128]{1,0:T(8,128)(2,1)S(1)}, bf16[64,128]{1,0:T(8,128)(2,1)S(1)}, u32[]{:S(2)}, u32[]{:S(2)}) collective-permute-start(bf16[64,128]{1,0:T(8,128)(2,1)S(1)} %get-tuple-element.95), channel_id=1, source_target_pairs={{1,0},{2,1},{3,2},{4,3},{5,4},{6,5},{7,6},{9,8},{10,9},{11,10},{12... | collective-permute-start | bytes 49160 | tf_op jit(solution)/shard_map/ppermute | solution.py:282
  69.8 0.0 collective-permute-done.15
  69.8 1.3 %collective-permute-start.16 = (bf16[144,128]{1,0:T(8,128)(2,1)S(1)}, bf16[144,128]{1,0:T(8,128)(2,1)S(1)}, u32[]{:S(2)}, u32[]{:S(2)}) collective-permute-start(bf16[144,128]{1,0:T(8,128)(2,1)S(1)} %add_convert_fusion.2), channel_id=1, source_target_pairs={{0,32},{1,33},{2,34},{3,35},{4,36},{5,37},{6,38},{7,39},{8,40},{9,... | collective-permute-start | bytes 110600 | tf_op jit(solution)/shard_map/ppermute | solution.py:271
  71.1 2.3 %shard_map.108.part_ref = f32[1024,128]{1,0:T(8,128)S(1)} custom-call(bf16[9,128,128]{2,1,0:T(8,128)(2,1)S(1)} %copy-done.7, s32[2,3072]{1,0:T(2,128)S(1)} %copy-done.11, bf16[128,3072]{1,0:T(8,128)(2,1)S(1)} %get-tuple-element.80.dm_ref, bf16[1024,128]{1,0:T(8,128)(2,1)S(1)} %get-tuple-element.92.dn_ref, bf16[1024,128]{1,0:T(8,128)(2,1)S(1)} %copy-done.8, ...), custom_call_target="tpu_custom_call" | custom-call | flops 2000000000 | bytes 4000000 | tf_op jit(solution)/shard_map/pallas_call | solution.py:253
  73.4 0.0 collective-permute-done.17.prev_ref
  73.4 0.0 collective-permute-done.18.next_ref
  73.4 0.2 collective-permute-done.16
  73.6 0.4 collective-permute-start.19
  74.0 3.4 %collective-permute-start.24 = (bf16[256,128]{1,0:T(8,128)(2,1)S(1)}, bf16[256,128]{1,0:T(8,128)(2,1)S(1)}, u32[]{:S(2)}, u32[]{:S(2)}) collective-permute-start(bf16[256,128]{1,0:T(8,128)(2,1)S(1)} %get-tuple-element.120), channel_id=1, source_target_pairs={{0,96},{1,97},{2,98},{3,99},{4,100},{5,101},{6,102},{7,103},{8,104... | collective-permute-start | bytes 196616 | tf_op jit(solution)/shard_map/ppermute | solution.py:271
  77.4 0.0 collective-permute-done.20.in0_ref
  77.4 1.3 %collective-permute-done.19 = bf16[144,128]{1,0:T(8,128)(2,1)S(1)} collective-permute-done((bf16[144,128]{1,0:T(8,128)(2,1)S(1)}, bf16[144,128]{1,0:T(8,128)(2,1)S(1)}, u32[]{:S(2)}, u32[]{:S(2)}) %collective-permute-start.19) | collective-permute-done | bytes 36896 | tf_op jit(solution)/shard_map/ppermute | solution.py:271
  78.8 2.2 %collective-permute-start.21 = (bf16[144,128]{1,0:T(8,128)(2,1)S(1)}, bf16[144,128]{1,0:T(8,128)(2,1)S(1)}, u32[]{:S(2)}, u32[]{:S(2)}) collective-permute-start(bf16[144,128]{1,0:T(8,128)(2,1)S(1)} %add_convert_fusion), channel_id=1, source_target_pairs={{0,1},{1,0},{2,3},{3,2},{4,5},{5,4},{6,7},{7,6},{8,9},{9,8},{10,11... | collective-permute-start | bytes 110600 | tf_op jit(solution)/shard_map/ppermute | solution.py:271
  80.9 3.4 %collective-permute-start.22 = (bf16[144,128]{1,0:T(8,128)(2,1)S(1)}, bf16[144,128]{1,0:T(8,128)(2,1)S(1)}, u32[]{:S(2)}, u32[]{:S(2)}) collective-permute-start(bf16[144,128]{1,0:T(8,128)(2,1)S(1)} %add_convert_fusion), channel_id=1, source_target_pairs={{0,2},{1,3},{2,0},{3,1},{4,6},{5,7},{6,4},{7,5},{8,10},{9,11},{10,... | collective-permute-start | bytes 110600 | tf_op jit(solution)/shard_map/ppermute | solution.py:271
  84.3 0.0 collective-permute-start.23
  84.3 1.7 %collective-permute-done.22 = bf16[144,128]{1,0:T(8,128)(2,1)S(1)} collective-permute-done((bf16[144,128]{1,0:T(8,128)(2,1)S(1)}, bf16[144,128]{1,0:T(8,128)(2,1)S(1)}, u32[]{:S(2)}, u32[]{:S(2)}) %collective-permute-start.22) | collective-permute-done | bytes 36896 | tf_op jit(solution)/shard_map/ppermute | solution.py:271
  86.1 2.3 %collective-permute-done.23 = bf16[144,128]{1,0:T(8,128)(2,1)S(1)} collective-permute-done((bf16[144,128]{1,0:T(8,128)(2,1)S(1)}, bf16[144,128]{1,0:T(8,128)(2,1)S(1)}, u32[]{:S(2)}, u32[]{:S(2)}) %collective-permute-start.23) | collective-permute-done | bytes 36896 | tf_op jit(solution)/shard_map/ppermute | solution.py:271
  88.4 4.3 %collective-permute-start.25 = (bf16[576,128]{1,0:T(8,128)(2,1)S(1)}, bf16[576,128]{1,0:T(8,128)(2,1)S(1)}, u32[]{:S(2)}, u32[]{:S(2)}) collective-permute-start(bf16[576,128]{1,0:T(8,128)(2,1)S(1)} %pad_maximum_fusion.1), channel_id=1, source_target_pairs={{0,8},{1,9},{2,10},{3,11},{4,12},{5,13},{6,14},{7,15},{8,0},{9,1},... | collective-permute-start | bytes 442376 | tf_op jit(solution)/shard_map/ppermute | solution.py:271
  92.7 1.2 %shard_map.109 = f32[1024,128]{1,0:T(8,128)} custom-call(f32[1024,128]{1,0:T(8,128)S(1)} %shard_map.108.part_ref, f32[256,128]{1,0:T(8,128)S(1)} %get-tuple-element.98.own_ref, bf16[256,128]{1,0:T(8,128)(2,1)S(1)} %collective-permute-done.20.in0_ref, bf16[256,128]{1,0:T(8,128)(2,1)S(1)} %collective-permute-done.13.in1_ref, ...), custom_call_target="tpu_custom_call" | custom-call | flops 100000000 | bytes 4000000 | tf_op jit(solution)/shard_map/pallas_call | solution.py:253
  93.9 0.0 collective-permute-done.25
  93.9 0.1 broadcast_select_fusion.1
  94.0 0.9 convert.1
  (35 shorter events, 0.3 us)
Async XLA Ops:
  0.6 1.0 %copy-start = (bf16[1024,128]{1,0:T(8,128)(2,1)S(1)}, bf16[1024,128]{1,0:T(8,128)(2,1)}, u32[]{:S(2)}) copy-start(bf16[1024,128]{1,0:T(8,128)(2,1)} %lat_ref.1) | copy-start | bytes 786436
  1.6 0.7 copy-start.2
  2.7 11.6 %collective-permute-start.2 = (bf16[128,256]{1,0:T(8,128)(2,1)S(1)}, bf16[128,256]{1,0:T(8,128)(2,1)S(1)}, u32[]{:S(2)}, u32[]{:S(2)}) collective-permute-start(bf16[128,256]{1,0:T(8,128)(2,1)S(1)} %get-tuple-element.58.bound_t_ref), channel_id=1, source_target_pairs={{0,32},{1,33},{2,34},{3,35},{4,36},{5,37},{6,38},{7,39},{8,40},{9,... | collective-permute-start | bytes 196616 | tf_op jit(solution)/shard_map/ppermute | solution.py:271
  6.6 7.5 %collective-permute-start.3 = (bf16[64,128]{1,0:T(8,128)(2,1)S(1)}, bf16[64,128]{1,0:T(8,128)(2,1)S(1)}, u32[]{:S(2)}, u32[]{:S(2)}) collective-permute-start(bf16[64,128]{1,0:T(8,128)(2,1)S(1)} %get-tuple-element.59), channel_id=1, source_target_pairs={{0,1},{1,2},{2,3},{3,4},{4,5},{5,6},{6,7},{8,9},{9,10},{10,11},{11... | collective-permute-start | bytes 49160 | tf_op jit(solution)/shard_map/ppermute | solution.py:282
  9.8 4.5 %collective-permute-start.4 = (bf16[64,128]{1,0:T(8,128)(2,1)S(1)}, bf16[64,128]{1,0:T(8,128)(2,1)S(1)}, u32[]{:S(2)}, u32[]{:S(2)}) collective-permute-start(bf16[64,128]{1,0:T(8,128)(2,1)S(1)} %get-tuple-element.60), channel_id=1, source_target_pairs={{1,0},{2,1},{3,2},{4,3},{5,4},{6,5},{7,6},{9,8},{10,9},{11,10},{12... | collective-permute-start | bytes 49160 | tf_op jit(solution)/shard_map/ppermute | solution.py:282
  11.1 17.8 %collective-permute-start = (bf16[128,256]{1,0:T(8,128)(2,1)S(1)}, bf16[128,256]{1,0:T(8,128)(2,1)S(1)}, u32[]{:S(2)}, u32[]{:S(2)}) collective-permute-start(bf16[128,256]{1,0:T(8,128)(2,1)S(1)} %get-tuple-element.58.bound_t_ref), channel_id=1, source_target_pairs={{0,8},{1,9},{2,10},{3,11},{4,12},{5,13},{6,14},{7,15},{8,0},{9,1},... | collective-permute-start | bytes 196616 | tf_op jit(solution)/shard_map/ppermute | solution.py:271
  12.4 16.5 %collective-permute-start.1 = (bf16[128,256]{1,0:T(8,128)(2,1)S(1)}, bf16[128,256]{1,0:T(8,128)(2,1)S(1)}, u32[]{:S(2)}, u32[]{:S(2)}) collective-permute-start(bf16[128,256]{1,0:T(8,128)(2,1)S(1)} %get-tuple-element.58.bound_t_ref), channel_id=1, source_target_pairs={{0,16},{1,17},{2,18},{3,19},{4,20},{5,21},{6,22},{7,23},{8,24},{9,... | collective-permute-start | bytes 196616 | tf_op jit(solution)/shard_map/ppermute | solution.py:271
  14.3 14.6 %collective-permute-start.5 = (bf16[128,256]{1,0:T(8,128)(2,1)S(1)}, bf16[128,256]{1,0:T(8,128)(2,1)S(1)}, u32[]{:S(2)}, u32[]{:S(2)}) collective-permute-start(bf16[128,256]{1,0:T(8,128)(2,1)S(1)} %collective-permute-done.2.far2_ref), channel_id=1, source_target_pairs={{0,96},{1,97},{2,98},{3,99},{4,100},{5,101},{6,102},{7,103},{8,104... | collective-permute-start | bytes 196616 | tf_op jit(solution)/shard_map/ppermute | solution.py:271
  18.5 1.1 %copy-start.4 = (bf16[3072,128]{1,0:T(8,128)(2,1)S(1)}, bf16[3072,128]{1,0:T(8,128)(2,1)}, u32[]{:S(2)}) copy-start(bf16[3072,128]{1,0:T(8,128)(2,1)} %feats_ref.1) | copy-start | bytes 2359300
  19.6 1.0 %copy-start.6 = (bf16[9,128,128]{2,1,0:T(8,128)(2,1)S(1)}, bf16[9,128,128]{2,1,0:T(8,128)(2,1)}, u32[]{:S(2)}) copy-start(bf16[9,128,128]{2,1,0:T(8,128)(2,1)} %w_ref.7) | copy-start | bytes 884740
  20.6 0.7 copy-start.10
  21.3 7.6 %copy-start.1 = (bf16[1024,128]{1,0:T(8,128)(2,1)S(1)}, bf16[1024,128]{1,0:T(8,128)(2,1)}, u32[]{:S(2)}) copy-start(bf16[1024,128]{1,0:T(8,128)(2,1)} %lat_ref.1) | copy-start | bytes 786436
  21.3 7.6 %copy-start.3 = (s32[256]{0:T(256)S(1)}, s32[256]{0:T(256)}, u32[]{:S(2)}) copy-start(s32[256]{0:T(256)} %param.13) | copy-start | bytes 3076
  21.3 7.6 %copy-start.5 = (bf16[3072,128]{1,0:T(8,128)(2,1)S(1)}, bf16[3072,128]{1,0:T(8,128)(2,1)}, u32[]{:S(2)}) copy-start(bf16[3072,128]{1,0:T(8,128)(2,1)} %feats_ref.1) | copy-start | bytes 2359300
  21.3 7.6 %copy-start.7 = (bf16[9,128,128]{2,1,0:T(8,128)(2,1)S(1)}, bf16[9,128,128]{2,1,0:T(8,128)(2,1)}, u32[]{:S(2)}) copy-start(bf16[9,128,128]{2,1,0:T(8,128)(2,1)} %w_ref.7) | copy-start | bytes 884740
  21.4 7.6 %copy-start.8 = (bf16[1024,128]{1,0:T(8,128)(2,1)S(1)}, bf16[1024,128]{1,0:T(8,128)(2,1)}, u32[]{:S(2)}) copy-start(bf16[1024,128]{1,0:T(8,128)(2,1)} %cot_ref.3) | copy-start | bytes 786436
  21.4 7.6 %copy-start.9 = (s32[2,8192]{1,0:T(2,128)S(1)}, s32[2,8192]{1,0:T(2,128)}, u32[]{:S(2)}) copy-start(s32[2,8192]{1,0:T(2,128)} %contacts_ref.3) | copy-start | bytes 196612
  21.4 7.6 %copy-start.11 = (s32[2,3072]{1,0:T(2,128)S(1)}, s32[2,3072]{1,0:T(2,128)}, u32[]{:S(2)}) copy-start(s32[2,3072]{1,0:T(2,128)} %edges_ref.5) | copy-start | bytes 73732
  21.4 7.6 %copy-start.12 = (s32[1,4]{1,0:T(1,128)S(1)}, s32[1,4]{1,0:T(1,128)}, u32[]{:S(2)}) copy-start(s32[1,4]{1,0:T(1,128)} %counts_ref.1) | copy-start | bytes 52
  40.9 5.6 %collective-permute-start.6 = (bf16[576,128]{1,0:T(8,128)(2,1)S(1)}, bf16[576,128]{1,0:T(8,128)(2,1)S(1)}, u32[]{:S(2)}, u32[]{:S(2)}) collective-permute-start(bf16[576,128]{1,0:T(8,128)(2,1)S(1)} %get-tuple-element.69), channel_id=1, source_target_pairs={{0,8},{1,9},{2,10},{3,11},{4,12},{5,13},{6,14},{7,15},{8,0},{9,1},... | collective-permute-start | bytes 442376 | tf_op jit(solution)/shard_map/ppermute | solution.py:271
  46.5 7.7 %collective-permute-start.7 = (bf16[144,128]{1,0:T(8,128)(2,1)S(1)}, bf16[144,128]{1,0:T(8,128)(2,1)S(1)}, u32[]{:S(2)}, u32[]{:S(2)}) collective-permute-start(bf16[144,128]{1,0:T(8,128)(2,1)S(1)} %get-tuple-element.115), channel_id=1, source_target_pairs={{0,1},{1,0},{2,3},{3,2},{4,5},{5,4},{6,7},{7,6},{8,9},{9,8},{10,11... | collective-permute-start | bytes 110600 | tf_op jit(solution)/shard_map/ppermute | solution.py:271
  47.9 6.4 %collective-permute-start.8 = (bf16[144,128]{1,0:T(8,128)(2,1)S(1)}, bf16[144,128]{1,0:T(8,128)(2,1)S(1)}, u32[]{:S(2)}, u32[]{:S(2)}) collective-permute-start(bf16[144,128]{1,0:T(8,128)(2,1)S(1)} %get-tuple-element.114), channel_id=1, source_target_pairs={{0,2},{1,3},{2,0},{3,1},{4,6},{5,7},{6,4},{7,5},{8,10},{9,11},{10,... | collective-permute-start | bytes 110600 | tf_op jit(solution)/shard_map/ppermute | solution.py:271
  52.2 4.0 %collective-permute-start.9 = (bf16[144,128]{1,0:T(8,128)(2,1)S(1)}, bf16[144,128]{1,0:T(8,128)(2,1)S(1)}, u32[]{:S(2)}, u32[]{:S(2)}) collective-permute-start(bf16[144,128]{1,0:T(8,128)(2,1)S(1)} %get-tuple-element.113), channel_id=1, source_target_pairs={{0,3},{1,2},{2,1},{3,0},{4,7},{5,6},{6,5},{7,4},{8,11},{9,10},{10,... | collective-permute-start | bytes 110600 | tf_op jit(solution)/shard_map/ppermute | solution.py:271
  52.2 11.1 %collective-permute-start.14 = (bf16[512,128]{1,0:T(8,128)(2,1)S(1)}, bf16[512,128]{1,0:T(8,128)(2,1)S(1)}, u32[]{:S(2)}, u32[]{:S(2)}) collective-permute-start(bf16[512,128]{1,0:T(8,128)(2,1)S(1)} %pad_maximum_fusion.2), channel_id=1, source_target_pairs={{0,32},{1,33},{2,34},{3,35},{4,36},{5,37},{6,38},{7,39},{8,40},{9,... | collective-permute-start | bytes 393224 | tf_op jit(solution)/shard_map/ppermute | solution.py:271
  53.5 9.4 %collective-permute-start.13 = (bf16[256,128]{1,0:T(8,128)(2,1)S(1)}, bf16[256,128]{1,0:T(8,128)(2,1)S(1)}, u32[]{:S(2)}, u32[]{:S(2)}) collective-permute-start(bf16[256,128]{1,0:T(8,128)(2,1)S(1)} %get-tuple-element.84), channel_id=1, source_target_pairs={{0,16},{1,17},{2,18},{3,19},{4,20},{5,21},{6,22},{7,23},{8,24},{9,... | collective-permute-start | bytes 196616 | tf_op jit(solution)/shard_map/ppermute | solution.py:271
  56.2 6.6 %collective-permute-start.10 = (bf16[144,128]{1,0:T(8,128)(2,1)S(1)}, bf16[144,128]{1,0:T(8,128)(2,1)S(1)}, u32[]{:S(2)}, u32[]{:S(2)}) collective-permute-start(bf16[144,128]{1,0:T(8,128)(2,1)S(1)} %add_convert_fusion.4), channel_id=1, source_target_pairs={{0,4},{1,5},{2,6},{3,7},{4,0},{5,1},{6,2},{7,3},{8,12},{9,13},{10,... | collective-permute-start | bytes 110600 | tf_op jit(solution)/shard_map/ppermute | solution.py:271
  56.3 6.5 %collective-permute-start.11 = (bf16[144,128]{1,0:T(8,128)(2,1)S(1)}, bf16[144,128]{1,0:T(8,128)(2,1)S(1)}, u32[]{:S(2)}, u32[]{:S(2)}) collective-permute-start(bf16[144,128]{1,0:T(8,128)(2,1)S(1)} %add_convert_fusion.4), channel_id=1, source_target_pairs={{0,128},{1,129},{2,130},{3,131},{4,132},{5,133},{6,134},{7,135},{8... | collective-permute-start | bytes 110600 | tf_op jit(solution)/shard_map/ppermute | solution.py:271
  58.9 4.4 %collective-permute-start.12 = (bf16[144,128]{1,0:T(8,128)(2,1)S(1)}, bf16[144,128]{1,0:T(8,128)(2,1)S(1)}, u32[]{:S(2)}, u32[]{:S(2)}) collective-permute-start(bf16[144,128]{1,0:T(8,128)(2,1)S(1)} %add_convert_fusion.4), channel_id=1, source_target_pairs={{0,132},{1,133},{2,134},{3,135},{4,128},{5,129},{6,130},{7,131},{8... | collective-permute-start | bytes 110600 | tf_op jit(solution)/shard_map/ppermute | solution.py:271
  63.3 6.5 %collective-permute-start.15 = (bf16[144,128]{1,0:T(8,128)(2,1)S(1)}, bf16[144,128]{1,0:T(8,128)(2,1)S(1)}, u32[]{:S(2)}, u32[]{:S(2)}) collective-permute-start(bf16[144,128]{1,0:T(8,128)(2,1)S(1)} %add_convert_fusion.3), channel_id=1, source_target_pairs={{0,16},{1,17},{2,18},{3,19},{4,20},{5,21},{6,22},{7,23},{8,24},{9,... | collective-permute-start | bytes 110600 | tf_op jit(solution)/shard_map/ppermute | solution.py:271
  64.2 13.2 %collective-permute-start.20 = (bf16[256,128]{1,0:T(8,128)(2,1)S(1)}, bf16[256,128]{1,0:T(8,128)(2,1)S(1)}, u32[]{:S(2)}, u32[]{:S(2)}) collective-permute-start(bf16[256,128]{1,0:T(8,128)(2,1)S(1)} %get-tuple-element.100), channel_id=1, source_target_pairs={{0,8},{1,9},{2,10},{3,11},{4,12},{5,13},{6,14},{7,15},{8,0},{9,1},... | collective-permute-start | bytes 196616 | tf_op jit(solution)/shard_map/ppermute | solution.py:271
  67.2 6.2 %collective-permute-start.17 = (bf16[64,128]{1,0:T(8,128)(2,1)S(1)}, bf16[64,128]{1,0:T(8,128)(2,1)S(1)}, u32[]{:S(2)}, u32[]{:S(2)}) collective-permute-start(bf16[64,128]{1,0:T(8,128)(2,1)S(1)} %get-tuple-element.94), channel_id=1, source_target_pairs={{0,1},{1,2},{2,3},{3,4},{4,5},{5,6},{6,7},{8,9},{9,10},{10,11},{11... | collective-permute-start | bytes 49160 | tf_op jit(solution)/shard_map/ppermute | solution.py:282
  68.5 4.9 %collective-permute-start.18 = (bf16[64,128]{1,0:T(8,128)(2,1)S(1)}, bf16[64,128]{1,0:T(8,128)(2,1)S(1)}, u32[]{:S(2)}, u32[]{:S(2)}) collective-permute-start(bf16[64,128]{1,0:T(8,128)(2,1)S(1)} %get-tuple-element.95), channel_id=1, source_target_pairs={{1,0},{2,1},{3,2},{4,3},{5,4},{6,5},{7,6},{9,8},{10,9},{11,10},{12... | collective-permute-start | bytes 49160 | tf_op jit(solution)/shard_map/ppermute | solution.py:282
  69.8 3.8 %collective-permute-start.16 = (bf16[144,128]{1,0:T(8,128)(2,1)S(1)}, bf16[144,128]{1,0:T(8,128)(2,1)S(1)}, u32[]{:S(2)}, u32[]{:S(2)}) collective-permute-start(bf16[144,128]{1,0:T(8,128)(2,1)S(1)} %add_convert_fusion.2), channel_id=1, source_target_pairs={{0,32},{1,33},{2,34},{3,35},{4,36},{5,37},{6,38},{7,39},{8,40},{9,... | collective-permute-start | bytes 110600 | tf_op jit(solution)/shard_map/ppermute | solution.py:271
  73.6 5.1 %collective-permute-start.19 = (bf16[144,128]{1,0:T(8,128)(2,1)S(1)}, bf16[144,128]{1,0:T(8,128)(2,1)S(1)}, u32[]{:S(2)}, u32[]{:S(2)}) collective-permute-start(bf16[144,128]{1,0:T(8,128)(2,1)S(1)} %add_convert_fusion.1), channel_id=1, source_target_pairs={{0,96},{1,97},{2,98},{3,99},{4,100},{5,101},{6,102},{7,103},{8,104... | collective-permute-start | bytes 110600 | tf_op jit(solution)/shard_map/ppermute | solution.py:271
  74.0 10.3 %collective-permute-start.24 = (bf16[256,128]{1,0:T(8,128)(2,1)S(1)}, bf16[256,128]{1,0:T(8,128)(2,1)S(1)}, u32[]{:S(2)}, u32[]{:S(2)}) collective-permute-start(bf16[256,128]{1,0:T(8,128)(2,1)S(1)} %get-tuple-element.120), channel_id=1, source_target_pairs={{0,96},{1,97},{2,98},{3,99},{4,100},{5,101},{6,102},{7,103},{8,104... | collective-permute-start | bytes 196616 | tf_op jit(solution)/shard_map/ppermute | solution.py:271
  78.8 5.6 %collective-permute-start.21 = (bf16[144,128]{1,0:T(8,128)(2,1)S(1)}, bf16[144,128]{1,0:T(8,128)(2,1)S(1)}, u32[]{:S(2)}, u32[]{:S(2)}) collective-permute-start(bf16[144,128]{1,0:T(8,128)(2,1)S(1)} %add_convert_fusion), channel_id=1, source_target_pairs={{0,1},{1,0},{2,3},{3,2},{4,5},{5,4},{6,7},{7,6},{8,9},{9,8},{10,11... | collective-permute-start | bytes 110600 | tf_op jit(solution)/shard_map/ppermute | solution.py:271
  80.9 5.1 %collective-permute-start.22 = (bf16[144,128]{1,0:T(8,128)(2,1)S(1)}, bf16[144,128]{1,0:T(8,128)(2,1)S(1)}, u32[]{:S(2)}, u32[]{:S(2)}) collective-permute-start(bf16[144,128]{1,0:T(8,128)(2,1)S(1)} %add_convert_fusion), channel_id=1, source_target_pairs={{0,2},{1,3},{2,0},{3,1},{4,6},{5,7},{6,4},{7,5},{8,10},{9,11},{10,... | collective-permute-start | bytes 110600 | tf_op jit(solution)/shard_map/ppermute | solution.py:271
  84.3 4.0 %collective-permute-start.23 = (bf16[144,128]{1,0:T(8,128)(2,1)S(1)}, bf16[144,128]{1,0:T(8,128)(2,1)S(1)}, u32[]{:S(2)}, u32[]{:S(2)}) collective-permute-start(bf16[144,128]{1,0:T(8,128)(2,1)S(1)} %add_convert_fusion), channel_id=1, source_target_pairs={{0,3},{1,2},{2,1},{3,0},{4,7},{5,6},{6,5},{7,4},{8,11},{9,10},{10,... | collective-permute-start | bytes 110600 | tf_op jit(solution)/shard_map/ppermute | solution.py:271
  88.4 5.5 %collective-permute-start.25 = (bf16[576,128]{1,0:T(8,128)(2,1)S(1)}, bf16[576,128]{1,0:T(8,128)(2,1)S(1)}, u32[]{:S(2)}, u32[]{:S(2)}) collective-permute-start(bf16[576,128]{1,0:T(8,128)(2,1)S(1)} %pad_maximum_fusion.1), channel_id=1, source_target_pairs={{0,8},{1,9},{2,10},{3,11},{4,12},{5,13},{6,14},{7,15},{8,0},{9,1},... | collective-permute-start | bytes 442376 | tf_op jit(solution)/shard_map/ppermute | solution.py:271

commit v5 on v4

--- a/solution.py
+++ b/solution.py
@@ -85,31 +85,29 @@
     bound_t_ref[...] = nn(lat_t, table(rows_dev, bnd[...])).astype(BF)
 
 
+def gather_kernel(lat_t_ref, edges_ref, send_ref, recv_ref):
+    rows_dev = lat_t_ref.shape[1]
+    for at in spans(edges_ref.shape[1], MESH_SPAN):
+        send_ref[:, at] = nn(lat_t_ref[...], table(rows_dev, edges_ref[0:1, at] - HB)).astype(BF)
+        recv_ref[:, at] = nn(lat_t_ref[...], table(rows_dev, edges_ref[1:2, at])).astype(BF)
+
+
 def mesh_kernel(
-    lat_t_ref, before_ref, after_ref, edges_hbm, w_hbm, feats_hbm,
-    rows_ref, slope_ref, agg_ref, ext_t_ref, sum_ref, edges, w, feats, sems,
+    before_ref, after_ref, own_ref, recv_ref, edges_ref, w_ref, feats_ref,
+    send_ref, slope_ref, agg_ref, sum_ref,
 ):
-    rows_dev = lat_t_ref.shape[1]
-    copies = fetched([(edges_hbm, edges), (w_hbm.at[0:3], w), (feats_hbm, feats)], sems)
-    rim = transposed(jnp.concatenate([before_ref[...], after_ref[...]], axis=0))
-    ext_t_ref[:, :rows_dev] = lat_t_ref[...]
-    ext_t_ref[:, rows_dev:] = rim
-    copies[0].wait()
-    for at in spans(edges.shape[1], MESH_SPAN):
-        ids = edges[0:1, at] - HB
-        ids = jnp.where(ids < 0, ids + rows_dev + HB, jnp.where(ids < rows_dev, ids, ids + HB))
-        rows_ref[:128, at] = nn(ext_t_ref[...], table(rows_dev + 2 * HB, ids)).astype(BF)
-        hits = table(rows_dev, edges[1:2, at])
-        rows_ref[128:, at] = nn(lat_t_ref[...], hits).astype(BF)
-        if at.start == 0:
-            copies[1].wait()
-            copies[2].wait()
-            w_t = jnp.concatenate([transposed(w[0]), transposed(w[1])], axis=1)
-            w2_t = transposed(w[2])
-        x = nn(w_t, rows_ref[:, at]) + nt(w2_t, feats[at, :])
+    rows_dev = agg_ref.shape[0]
+    rim_t = transposed(jnp.concatenate([before_ref[...], after_ref[...]], axis=0))
+    w0_t, w1_t, w2_t = transposed(w_ref[0]), transposed(w_ref[1]), transposed(w_ref[2])
+    for at in spans(edges_ref.shape[1], MESH_SPAN):
+        ids = edges_ref[0:1, at]
+        ids = jnp.where(ids < HB, ids, jnp.where(ids < HB + rows_dev, -1, ids - rows_dev))
+        rim_rows = nn(rim_t, table(2 * HB, ids))
+        send_ref[:, at] = (own_ref[:, at].astype(F32) + rim_rows).astype(BF)
+        x = nn(w0_t, send_ref[:, at]) + nn(w1_t, recv_ref[:, at]) + nt(w2_t, feats_ref[at, :])
         message, slope = silu_parts(x)
         slope_ref[:, at] = slope
-        part = nt(hits, message.astype(BF))
+        part = nt(table(rows_dev, edges_ref[1:2, at]), message.astype(BF))
         if at.start:
             part = part + sum_ref[...]
         sum_ref[...] = part
@@ -118,7 +116,7 @@
 
 def main_kernel(
     counts_ref, core_ref, lat_ref, lat_t_ref, bound_t_ref, far0_ref, far1_ref, far2_ref,
-    far3_ref, rows_ref, slope_m_ref, agg_ref, feats_ref, cot_ref, w_ref, edges_ref,
+    far3_ref, send_ref, recv_ref, slope_m_ref, agg_ref, feats_ref, cot_ref, w_ref, edges_ref,
     contacts_ref, bnd_ref,
     new_ref, kept_ref, sent_ref, dm_ref, dc_ref, dn_ref,
     aggb_ref, slope_c_ref, both_ref, gw_ref, aggc_ref, dagg_t_ref, daggc_t_ref,
@@ -172,10 +170,10 @@
         gathered = nn(dagg_t_ref[...], table(rows_dev, edges_ref[1:2, at]))
         d = (gathered * slope_m_ref[:, at]).astype(BF)
         dm_ref[:, at] = d
-        pair = nt(rows_ref[:, at], d)
-        own = nn(d, feats_ref[at, :])
-        gw_ref[0:256, :] = pair + gw_ref[0:256, :] if at.start else pair
-        gw_ref[256:384, :] = own + gw_ref[256:384, :] if at.start else own
+        parts = [nt(send_ref[:, at], d), nt(recv_ref[:, at], d), nn(d, feats_ref[at, :])]
+        for k, part in enumerate(parts):
+            where = slice(128 * k, 128 * k + 128)
+            gw_ref[where, :] = part + gw_ref[where, :] if at.start else part
 
     gw_ref[256:384, :] = gw_ref[256:384, :].T
     dbg_t = nn(daggc_t_ref[...], bound_table).astype(BF)
@@ -324,30 +322,28 @@
         [latents, bnd],
         [((rows_dev, width), BF), ((1, bound_count), jnp.int32)],
         hbm=2,
+        flops=10**10,
         mib=8,
     )
-    far_two = exchanged(bound_t, mask_z=2)
     before = shifted(high_rows, 1)
     after = shifted(low_rows, -1)
-    far_one = exchanged(bound_t, mask_z=1)
-    far_zero = exchanged(bound_t, mask_core=1)
-    far_two, before, after = tie(far_two, before, after)
-    far_three = exchanged(far_two, mask_z=6)
-    fars = [far_zero, far_one, far_two, far_three]
-    rows, slope, agg = call(
+    fars = [exchanged(bound_t, mask_core=1)]
+    fars += [exchanged(bound_t, mask_z=mask) for mask in (1, 2, 4)]
+    own_rows, recv_rows = call(
+        gather_kernel,
+        [((width, edge_count), BF), ((width, edge_count), BF)],
+        [lat_t, mesh_edges],
+        flops=4 * 10**9,
+        mib=16,
+    )
+    before, after, own_rows = tie(before, after, own_rows)
+    send_rows, slope, agg = call(
         mesh_kernel,
-        [((2 * width, edge_count), BF), ((width, edge_count), F32), ((rows_dev, width), BF)],
-        [lat_t, before, after, mesh_edges, weights, edge_feats],
-        [
-            ((width, rows_dev + 2 * HB), BF),
-            ((rows_dev, width), F32),
-            ((2, edge_count), jnp.int32),
-            ((3, width, width), BF),
-            ((edge_count, width), BF),
-        ],
-        hbm=3,
-        flops=6 * 10**9,
-        mib=20,
+        [((width, edge_count), BF), ((width, edge_count), F32), ((rows_dev, width), BF)],
+        [before, after, own_rows, recv_rows, mesh_edges, weights, edge_feats],
+        [((rows_dev, width), F32)],
+        flops=3 * 10**9,
+        mib=16,
     )
     new_rows, kept, sent, d_mesh, d_contact, d_node = call(
         functools.partial(main_kernel, scale=scale),
@@ -359,7 +355,7 @@
             ((width, contact_count), BF),
             ((rows_dev, width), BF),
         ],
-        [contact_counts, core.reshape(1), latents, lat_t, bound_t, *fars, rows, slope, agg]
+        [contact_counts, core.reshape(1), latents, lat_t, bound_t, *fars, send_rows, recv_rows, slope, agg]
         + [edge_feats, cotangent, weights, mesh_edges, contact_edges, bnd],
         [
             ((bound_count, width), F32),
@@ -409,9 +405,8 @@
     block = ((wide(block) + wide(one)) + (wide(two) + wide(three))).astype(BF)
 
     other = exchanged(block, mask_z=1)
-    from_prev = shifted(high, 1)
-    from_next = shifted(low, -1)
-    other, part = tie(other, part)
+    in_zero = exchanged(far_grads[0], mask_core=1)
+    other, in_zero, part = tie(other, in_zero, part)
     block = (wide(block) + wide(other)).astype(BF)
     other = exchanged(block, mask_z=2)
     (part,) = call(
@@ -422,18 +417,19 @@
         flops=2 * 10**9,
         mib=16,
     )
-    other, part, from_prev, from_next, pair = tie(other, part, from_prev, from_next, pair)
+    other, part, pair, low, high = tie(other, part, pair, low, high)
     block = (wide(block) + wide(other)).astype(BF)
-    other = exchanged(block, mask_z=6)
-    in_zero = exchanged(far_grads[0], mask_core=1)
     in_two = pair[:bound_count]
-    in_three = exchanged(pair[bound_count:], mask_z=6)
-    other, in_zero = tie(other, in_zero)
-    block = (wide(block) + wide(other)).astype(BF)
+    other = exchanged(jnp.concatenate([block, pair[bound_count:]], axis=0), mask_z=6)
+    from_prev = shifted(high, 1)
+    from_next = shifted(low, -1)
+    other, from_prev, from_next = tie(other, from_prev, from_next)
+    in_three = other[size:]
+    block = (wide(block) + wide(other[:size])).astype(BF)
 
     found = [exchanged(block, mask_y=mask) for mask in (1, 2, 3)]
-    *found, in_three = tie(*found, in_three)
-    block = ordered_by_y([block] + found, row_y)
+    found = tie(*found)
+    block = ordered_by_y([block, *found], row_y)
     other = exchanged(block, mask_core=1)
     (grad_rows,) = call(
         last_kernel,

time: 95.3 us -> 95.9 us (level)
  waiting for transfers between devices: 8.23 us -> 11.9 us
  local copies, waits for them, and re-layouts: 4.53 us -> 1.71 us
    ppermute x4, waiting for transfers between devices: 0.21 us -> 3.48 us  [shifted(): return lax.ppermute(array, 'panel', pairs)]
    unnamed x26 -> x20, local copies, waits for them, and re-layouts: 4.49 us -> 1.67 us
    pallas_call x7 -> x8, Pallas kernels: 28.7 us -> 27.9 us  [call(): pl.pallas_call(kernel, out_shape=[jax.ShapeDtypeStruct(shape, kind) for s...]
    ppermute x22 -> x21, starting transfers between devices: 44.2 us -> 44.9 us  [exchanged(): return lax.ppermute(block, ('region', 'panel'), route)]
    ppermute x22 -> x21, waiting for transfers between devices: 8.02 us -> 8.42 us  [exchanged(): return lax.ppermute(block, ('region', 'panel'), route)]
  transfers between devices with their start and end apart: 26 -> 25, of which waited for: 8 -> 7; matrix products, arithmetic and copies ran while one was open for 0% -> 0% of each run, Pallas kernels for 17% -> 16%
where the time goes in v5:
time: 95.9 us; the launch traced here: 95.6 us
  starting transfers between devices  52 us (54%)
  Pallas kernels  27.9 us (29%)
  waiting for transfers between devices  11.9 us (12%)
  local copies, waits for them, and re-layouts  1.71 us (2%)
  other arithmetic  1.14 us (1%)
  between operations  1.04 us (1%)
    ppermute x21, starting transfers between devices, exchanged(): return lax.ppermute(block, ('region', 'panel'), route)  44.9 us
    pallas_call x8, Pallas kernels, call(): pl.pallas_call(kernel, out_shape=[jax.ShapeDtypeStruct(shape, kind) for s...  27.9 us
    ppermute x21, waiting for transfers between devices, exchanged(): return lax.ppermute(block, ('region', 'panel'), route)  8.42 us
    ppermute x4, starting transfers between devices, shifted(): return lax.ppermute(array, 'panel', pairs)  7.05 us
    ppermute x4, waiting for transfers between devices, shifted(): return lax.ppermute(array, 'panel', pairs)  3.48 us
  transfers between devices with their start and end apart: 25, of which 7 were waited for; matrix products, arithmetic and copies ran while one was open for 0% of the time, Pallas kernels for 16%

profile of v5, /device:TPU:1, one launch (start us, length us, event | category | flops | bytes accessed | tf_op | source)
XLA Modules:
  0.0 95.6 jit_solution(4700428761425679996)
XLA Ops:
  0.6 0.0 copy-start
  0.6 0.7 copy-done
  1.3 0.9 copy-done.4
  2.3 0.4 shard_map.103
  2.7 3.3 %collective-permute-start = (bf16[128,256]{1,0:T(8,128)(2,1)S(1)}, bf16[128,256]{1,0:T(8,128)(2,1)S(1)}, u32[]{:S(2)}, u32[]{:S(2)}) collective-permute-start(bf16[128,256]{1,0:T(8,128)(2,1)S(1)} %get-tuple-element.61.bound_t_ref), channel_id=1, source_target_pairs={{0,8},{1,9},{2,10},{3,11},{4,12},{5,13},{6,14},{7,15},{8,0},{9,1},... | collective-permute-start | bytes 196616 | tf_op jit(solution)/shard_map/ppermute | solution.py:269
  6.0 0.0 collective-permute-start.1
  6.0 2.9 %collective-permute-start.2 = (bf16[128,256]{1,0:T(8,128)(2,1)S(1)}, bf16[128,256]{1,0:T(8,128)(2,1)S(1)}, u32[]{:S(2)}, u32[]{:S(2)}) collective-permute-start(bf16[128,256]{1,0:T(8,128)(2,1)S(1)} %get-tuple-element.61.bound_t_ref), channel_id=1, source_target_pairs={{0,32},{1,33},{2,34},{3,35},{4,36},{5,37},{6,38},{7,39},{8,40},{9,... | collective-permute-start | bytes 196616 | tf_op jit(solution)/shard_map/ppermute | solution.py:269
  9.0 3.2 %collective-permute-start.4 = (bf16[64,128]{1,0:T(8,128)(2,1)S(1)}, bf16[64,128]{1,0:T(8,128)(2,1)S(1)}, u32[]{:S(2)}, u32[]{:S(2)}) collective-permute-start(bf16[64,128]{1,0:T(8,128)(2,1)S(1)} %get-tuple-element.62), channel_id=1, source_target_pairs={{0,1},{1,2},{2,3},{3,4},{4,5},{5,6},{6,7},{8,9},{9,10},{10,11},{11... | collective-permute-start | bytes 49160 | tf_op jit(solution)/shard_map/ppermute | solution.py:280
  12.2 1.3 %collective-permute-start.5 = (bf16[64,128]{1,0:T(8,128)(2,1)S(1)}, bf16[64,128]{1,0:T(8,128)(2,1)S(1)}, u32[]{:S(2)}, u32[]{:S(2)}) collective-permute-start(bf16[64,128]{1,0:T(8,128)(2,1)S(1)} %get-tuple-element.63), channel_id=1, source_target_pairs={{1,0},{2,1},{3,2},{4,3},{5,4},{6,5},{7,6},{9,8},{10,9},{11,10},{12... | collective-permute-start | bytes 49160 | tf_op jit(solution)/shard_map/ppermute | solution.py:280
  13.5 0.0 copy-start.2
  13.5 0.0 copy-start.3
  13.5 1.9 %shard_map.104 = (bf16[128,3072]{1,0:T(8,128)(2,1)S(1)}, bf16[128,3072]{1,0:T(8,128)(2,1)S(1)}) custom-call(bf16[128,1024]{1,0:T(8,128)(2,1)S(1)} %get-tuple-element.60.lat_t_ref, s32[2,3072]{1,0:T(2,128)S(1)} %copy-done.8), custom_call_target="tpu_custom_call" | custom-call | flops 4000000000 | bytes 4000000 | tf_op jit(solution)/shard_map/pallas_call | solution.py:251
  15.4 0.0 collective-permute-done.4.before_ref
  15.4 4.5 %collective-permute-start.3 = (bf16[128,256]{1,0:T(8,128)(2,1)S(1)}, bf16[128,256]{1,0:T(8,128)(2,1)S(1)}, u32[]{:S(2)}, u32[]{:S(2)}) collective-permute-start(bf16[128,256]{1,0:T(8,128)(2,1)S(1)} %get-tuple-element.61.bound_t_ref), channel_id=1, source_target_pairs={{0,64},{1,65},{2,66},{3,67},{4,68},{5,69},{6,70},{7,71},{8,72},{9,... | collective-permute-start | bytes 196616 | tf_op jit(solution)/shard_map/ppermute | solution.py:269
  19.9 0.0 collective-permute-done.5.after_ref
  19.9 0.0 copy-start.1
  19.9 0.0 copy-start.5
  20.0 0.0 copy-start.6
  20.0 0.0 copy-start.7
  20.0 0.0 copy-start.9
  20.0 4.5 %shard_map.105 = (bf16[128,3072]{1,0:T(8,128)(2,1)S(1)}, f32[128,3072]{1,0:T(8,128)S(1)}, bf16[1024,128]{1,0:T(8,128)(2,1)S(1)}) custom-call(bf16[64,128]{1,0:T(8,128)(2,1)S(1)} %collective-permute-done.4.before_ref, bf16[64,128]{1,0:T(8,128)(2,1)S(1)} %collective-permute-done.5.after_ref, bf16[128,3072]{1,0:T(8,128)(2,1)S(1)} %get-tuple-element.67.own_ref, ...), custom_call_target="tpu_custom_call" | custom-call | flops 3000000000 | bytes 4000000 | tf_op jit(solution)/shard_map/pallas_call | solution.py:251
  24.5 0.0 collective-permute-done.far0_ref
  24.5 0.0 collective-permute-done.1.far1_ref
  24.5 0.0 collective-permute-done.2.far2_ref
  24.6 12.1 %shard_map.106 = (bf16[1024,128]{1,0:T(8,128)(2,1)}, f32[576,128]{1,0:T(8,128)S(1)}, bf16[576,128]{1,0:T(8,128)(2,1)S(1)}, bf16[128,3072]{1,0:T(8,128)(2,1)S(1)}...) custom-call(s32[1,4]{1,0:T(1,128)S(1)} %copy-done.9, s32[1]{0:T(128)} %bitcast.core_ref, ...), custom_call_target="tpu_custom_call" | custom-call | flops 8000000000 | bytes 4000000 | tf_op jit(solution)/shard_map/pallas_call | solution.py:251
  36.7 1.3 %collective-permute-start.6 = (bf16[576,128]{1,0:T(8,128)(2,1)S(1)}, bf16[576,128]{1,0:T(8,128)(2,1)S(1)}, u32[]{:S(2)}, u32[]{:S(2)}) collective-permute-start(bf16[576,128]{1,0:T(8,128)(2,1)S(1)} %get-tuple-element.74), channel_id=1, source_target_pairs={{0,8},{1,9},{2,10},{3,11},{4,12},{5,13},{6,14},{7,15},{8,0},{9,1},... | collective-permute-start | bytes 442376 | tf_op jit(solution)/shard_map/ppermute | solution.py:269
  38.0 2.8 %shard_map.107 = (bf16[256,128]{1,0:T(8,128)(2,1)S(1)}, bf16[256,128]{1,0:T(8,128)(2,1)S(1)}, bf16[256,128]{1,0:T(8,128)(2,1)S(1)}, bf16[256,128]{1,0:T(8,128)(2,1)S(1)}, f32[256,128]{1,0:T(8,128)S(1)}) custom-call(bf16[9,128,128]{2,1,0:T(8,128)(2,1)S(1)} %copy-done.3, s32[2,8192]{1,0:T(2,128)S(1)} %copy-done.7, bf16[128,8192]{1,0:T(8,128)(2,1)S(1)} %get-tuple-element.75.dc_ref), custom_call_target="tpu_custom_call" | custom-call | flops 2000000000 | bytes 4000000 | tf_op jit(solution)/shard_map/pallas_call | solution.py:251
  40.8 0.0 collective-permute-done.6
  40.9 2.5 %collective-permute-start.7 = (bf16[144,128]{1,0:T(8,128)(2,1)S(1)}, bf16[144,128]{1,0:T(8,128)(2,1)S(1)}, u32[]{:S(2)}, u32[]{:S(2)}) collective-permute-start(bf16[144,128]{1,0:T(8,128)(2,1)S(1)} %get-tuple-element.121), channel_id=1, source_target_pairs={{0,1},{1,0},{2,3},{3,2},{4,5},{5,4},{6,7},{7,6},{8,9},{9,8},{10,11... | collective-permute-start | bytes 110600 | tf_op jit(solution)/shard_map/ppermute | solution.py:269
  43.3 2.6 %collective-permute-start.8 = (bf16[144,128]{1,0:T(8,128)(2,1)S(1)}, bf16[144,128]{1,0:T(8,128)(2,1)S(1)}, u32[]{:S(2)}, u32[]{:S(2)}) collective-permute-start(bf16[144,128]{1,0:T(8,128)(2,1)S(1)} %get-tuple-element.120), channel_id=1, source_target_pairs={{0,2},{1,3},{2,0},{3,1},{4,6},{5,7},{6,4},{7,5},{8,10},{9,11},{10,... | collective-permute-start | bytes 110600 | tf_op jit(solution)/shard_map/ppermute | solution.py:269
  45.9 0.0 collective-permute-start.9
  46.0 1.3 %collective-permute-start.14 = (bf16[512,128]{1,0:T(8,128)(2,1)S(1)}, bf16[512,128]{1,0:T(8,128)(2,1)S(1)}, u32[]{:S(2)}, u32[]{:S(2)}) collective-permute-start(bf16[512,128]{1,0:T(8,128)(2,1)S(1)} %pad_maximum_fusion.2), channel_id=1, source_target_pairs={{0,32},{1,33},{2,34},{3,35},{4,36},{5,37},{6,38},{7,39},{8,40},{9,... | collective-permute-start | bytes 393224 | tf_op jit(solution)/shard_map/ppermute | solution.py:269
  47.2 0.7 collective-permute-start.13
  48.0 0.0 collective-permute-done.7
  48.0 0.1 collective-permute-done.8
  48.1 1.9 %collective-permute-done.9 = bf16[144,128]{1,0:T(8,128)(2,1)S(1)} collective-permute-done((bf16[144,128]{1,0:T(8,128)(2,1)S(1)}, bf16[144,128]{1,0:T(8,128)(2,1)S(1)}, u32[]{:S(2)}, u32[]{:S(2)}) %collective-permute-start.9) | collective-permute-done | bytes 36896 | tf_op jit(solution)/shard_map/ppermute | solution.py:269
  50.0 1.3 %collective-permute-start.10 = (bf16[144,128]{1,0:T(8,128)(2,1)S(1)}, bf16[144,128]{1,0:T(8,128)(2,1)S(1)}, u32[]{:S(2)}, u32[]{:S(2)}) collective-permute-start(bf16[144,128]{1,0:T(8,128)(2,1)S(1)} %add_convert_fusion.4), channel_id=1, source_target_pairs={{0,4},{1,5},{2,6},{3,7},{4,0},{5,1},{6,2},{7,3},{8,12},{9,13},{10,... | collective-permute-start | bytes 110600 | tf_op jit(solution)/shard_map/ppermute | solution.py:269
  51.3 2.5 %collective-permute-start.11 = (bf16[144,128]{1,0:T(8,128)(2,1)S(1)}, bf16[144,128]{1,0:T(8,128)(2,1)S(1)}, u32[]{:S(2)}, u32[]{:S(2)}) collective-permute-start(bf16[144,128]{1,0:T(8,128)(2,1)S(1)} %add_convert_fusion.4), channel_id=1, source_target_pairs={{0,128},{1,129},{2,130},{3,131},{4,132},{5,133},{6,134},{7,135},{8... | collective-permute-start | bytes 110600 | tf_op jit(solution)/shard_map/ppermute | solution.py:269
  53.8 0.1 collective-permute-start.12
  53.9 2.6 %shard_map.108 = (f32[1024,128]{1,0:T(8,128)S(1)}, bf16[64,128]{1,0:T(8,128)(2,1)S(1)}, bf16[64,128]{1,0:T(8,128)(2,1)S(1)}) custom-call(bf16[9,128,128]{2,1,0:T(8,128)(2,1)S(1)} %copy-done.3, s32[2,3072]{1,0:T(2,128)S(1)} %copy-done.8, bf16[128,3072]{1,0:T(8,128)(2,1)S(1)} %get-tuple-element.85.dm_ref), custom_call_target="tpu_custom_call" | custom-call | flops 2000000000 | bytes 4000000 | tf_op jit(solution)/shard_map/pallas_call | solution.py:251
  56.6 2.7 %collective-permute-start.16 = (bf16[256,128]{1,0:T(8,128)(2,1)S(1)}, bf16[256,128]{1,0:T(8,128)(2,1)S(1)}, u32[]{:S(2)}, u32[]{:S(2)}) collective-permute-start(bf16[256,128]{1,0:T(8,128)(2,1)S(1)} %get-tuple-element.95), channel_id=1, source_target_pairs={{0,8},{1,9},{2,10},{3,11},{4,12},{5,13},{6,14},{7,15},{8,0},{9,1},... | collective-permute-start | bytes 196616 | tf_op jit(solution)/shard_map/ppermute | solution.py:269
  59.3 0.0 collective-permute-done.14
  59.3 0.8 collective-permute-start.15
  60.1 0.0 collective-permute-done.16.in0_ref
  60.2 2.0 %collective-permute-done.15 = bf16[144,128]{1,0:T(8,128)(2,1)S(1)} collective-permute-done((bf16[144,128]{1,0:T(8,128)(2,1)S(1)}, bf16[144,128]{1,0:T(8,128)(2,1)S(1)}, u32[]{:S(2)}, u32[]{:S(2)}) %collective-permute-start.15) | collective-permute-done | bytes 36896 | tf_op jit(solution)/shard_map/ppermute | solution.py:269
  62.2 1.5 %collective-permute-start.17 = (bf16[144,128]{1,0:T(8,128)(2,1)S(1)}, bf16[144,128]{1,0:T(8,128)(2,1)S(1)}, u32[]{:S(2)}, u32[]{:S(2)}) collective-permute-start(bf16[144,128]{1,0:T(8,128)(2,1)S(1)} %add_convert_fusion.2), channel_id=1, source_target_pairs={{0,32},{1,33},{2,34},{3,35},{4,36},{5,37},{6,38},{7,39},{8,40},{9,... | collective-permute-start | bytes 110600 | tf_op jit(solution)/shard_map/ppermute | solution.py:269
  63.7 2.3 %shard_map.109.part_ref = f32[1024,128]{1,0:T(8,128)S(1)} custom-call(bf16[9,128,128]{2,1,0:T(8,128)(2,1)S(1)} %copy-done.3, s32[2,3072]{1,0:T(2,128)S(1)} %copy-done.8, bf16[128,3072]{1,0:T(8,128)(2,1)S(1)} %get-tuple-element.85.dm_ref, bf16[1024,128]{1,0:T(8,128)(2,1)S(1)} %get-tuple-element.98.dn_ref, bf16[1024,128]{1,0:T(8,128)(2,1)S(1)} %copy-done.6, ...), custom_call_target="tpu_custom_call" | custom-call | flops 2000000000 | bytes 4000000 | tf_op jit(solution)/shard_map/pallas_call | solution.py:251
  66.0 0.3 collective-permute-done.17
  66.3 3.5 %collective-permute-start.18 = (bf16[400,128]{1,0:T(8,128)(2,1)S(1)}, bf16[400,128]{1,0:T(8,128)(2,1)S(1)}, u32[]{:S(2)}, u32[]{:S(2)}) collective-permute-start(bf16[400,128]{1,0:T(8,128)(2,1)S(1)} %pad_maximum_fusion.3), channel_id=1, source_target_pairs={{0,96},{1,97},{2,98},{3,99},{4,100},{5,101},{6,102},{7,103},{8,104... | collective-permute-start | bytes 307208 | tf_op jit(solution)/shard_map/ppermute | solution.py:269
  69.9 1.3 %collective-permute-start.19 = (bf16[64,128]{1,0:T(8,128)(2,1)S(1)}, bf16[64,128]{1,0:T(8,128)(2,1)S(1)}, u32[]{:S(2)}, u32[]{:S(2)}) collective-permute-start(bf16[64,128]{1,0:T(8,128)(2,1)S(1)} %get-tuple-element.109), channel_id=1, source_target_pairs={{0,1},{1,2},{2,3},{3,4},{4,5},{5,6},{6,7},{8,9},{9,10},{10,11},{11... | collective-permute-start | bytes 49160 | tf_op jit(solution)/shard_map/ppermute | solution.py:280
  71.2 1.3 %collective-permute-start.20 = (bf16[64,128]{1,0:T(8,128)(2,1)S(1)}, bf16[64,128]{1,0:T(8,128)(2,1)S(1)}, u32[]{:S(2)}, u32[]{:S(2)}) collective-permute-start(bf16[64,128]{1,0:T(8,128)(2,1)S(1)} %get-tuple-element.110), channel_id=1, source_target_pairs={{1,0},{2,1},{3,2},{4,3},{5,4},{6,5},{7,6},{9,8},{10,9},{11,10},{12... | collective-permute-start | bytes 49160 | tf_op jit(solution)/shard_map/ppermute | solution.py:280
  72.5 0.0 collective-permute-done.19.prev_ref
  72.5 3.5 %collective-permute-done.20.next_ref = bf16[64,128]{1,0:T(8,128)(2,1)S(1)} collective-permute-done((bf16[64,128]{1,0:T(8,128)(2,1)S(1)}, bf16[64,128]{1,0:T(8,128)(2,1)S(1)}, u32[]{:S(2)}, u32[]{:S(2)}) %collective-permute-start.20) | collective-permute-done | bytes 16416 | tf_op jit(solution)/shard_map/ppermute | solution.py:280
  76.0 0.0 collective-permute-done.18
  76.0 1.4 %collective-permute-start.21 = (bf16[144,128]{1,0:T(8,128)(2,1)S(1)}, bf16[144,128]{1,0:T(8,128)(2,1)S(1)}, u32[]{:S(2)}, u32[]{:S(2)}) collective-permute-start(bf16[144,128]{1,0:T(8,128)(2,1)S(1)} %add_convert_fusion), channel_id=1, source_target_pairs={{0,1},{1,0},{2,3},{3,2},{4,5},{5,4},{6,7},{7,6},{8,9},{9,8},{10,11... | collective-permute-start | bytes 110600 | tf_op jit(solution)/shard_map/ppermute | solution.py:269
  77.4 4.7 %collective-permute-start.22 = (bf16[144,128]{1,0:T(8,128)(2,1)S(1)}, bf16[144,128]{1,0:T(8,128)(2,1)S(1)}, u32[]{:S(2)}, u32[]{:S(2)}) collective-permute-start(bf16[144,128]{1,0:T(8,128)(2,1)S(1)} %add_convert_fusion), channel_id=1, source_target_pairs={{0,2},{1,3},{2,0},{3,1},{4,6},{5,7},{6,4},{7,5},{8,10},{9,11},{10,... | collective-permute-start | bytes 110600 | tf_op jit(solution)/shard_map/ppermute | solution.py:269
  82.1 0.0 collective-permute-start.23
  82.1 0.0 collective-permute-done.21
  82.1 1.7 %collective-permute-done.22 = bf16[144,128]{1,0:T(8,128)(2,1)S(1)} collective-permute-done((bf16[144,128]{1,0:T(8,128)(2,1)S(1)}, bf16[144,128]{1,0:T(8,128)(2,1)S(1)}, u32[]{:S(2)}, u32[]{:S(2)}) %collective-permute-start.22) | collective-permute-done | bytes 36896 | tf_op jit(solution)/shard_map/ppermute | solution.py:269
  83.8 2.3 %collective-permute-done.23 = bf16[144,128]{1,0:T(8,128)(2,1)S(1)} collective-permute-done((bf16[144,128]{1,0:T(8,128)(2,1)S(1)}, bf16[144,128]{1,0:T(8,128)(2,1)S(1)}, u32[]{:S(2)}, u32[]{:S(2)}) %collective-permute-start.23) | collective-permute-done | bytes 36896 | tf_op jit(solution)/shard_map/ppermute | solution.py:269
  86.1 7.3 %collective-permute-start.24 = (bf16[576,128]{1,0:T(8,128)(2,1)S(1)}, bf16[576,128]{1,0:T(8,128)(2,1)S(1)}, u32[]{:S(2)}, u32[]{:S(2)}) collective-permute-start(bf16[576,128]{1,0:T(8,128)(2,1)S(1)} %pad_maximum_fusion.1), channel_id=1, source_target_pairs={{0,8},{1,9},{2,10},{3,11},{4,12},{5,13},{6,14},{7,15},{8,0},{9,1},... | collective-permute-start | bytes 442376 | tf_op jit(solution)/shard_map/ppermute | solution.py:269
  93.4 1.3 %shard_map.110 = f32[1024,128]{1,0:T(8,128)} custom-call(f32[1024,128]{1,0:T(8,128)S(1)} %shard_map.109.part_ref, f32[256,128]{1,0:T(8,128)S(1)} %get-tuple-element.104.own_ref, bf16[256,128]{1,0:T(8,128)(2,1)S(1)} %collective-permute-done.16.in0_ref, bf16[256,128]{1,0:T(8,128)(2,1)S(1)} %collective-permute-done.13.in1_ref, ...), custom_call_target="tpu_custom_call" | custom-call | flops 100000000 | bytes 4000000 | tf_op jit(solution)/shard_map/pallas_call | solution.py:251
  94.7 0.1 broadcast_select_fusion.1
  94.8 0.9 convert.1
  (30 shorter events, 0.3 us)
Async XLA Ops:
  0.6 0.7 copy-start
  1.3 0.9 copy-start.4
  2.3 11.2 %copy-start.8 = (s32[2,3072]{1,0:T(2,128)S(1)}, s32[2,3072]{1,0:T(2,128)}, u32[]{:S(2)}) copy-start(s32[2,3072]{1,0:T(2,128)} %edges_ref.9) | copy-start | bytes 73732
  2.7 21.8 %collective-permute-start = (bf16[128,256]{1,0:T(8,128)(2,1)S(1)}, bf16[128,256]{1,0:T(8,128)(2,1)S(1)}, u32[]{:S(2)}, u32[]{:S(2)}) collective-permute-start(bf16[128,256]{1,0:T(8,128)(2,1)S(1)} %get-tuple-element.61.bound_t_ref), channel_id=1, source_target_pairs={{0,8},{1,9},{2,10},{3,11},{4,12},{5,13},{6,14},{7,15},{8,0},{9,1},... | collective-permute-start | bytes 196616 | tf_op jit(solution)/shard_map/ppermute | solution.py:269
  6.0 18.5 %collective-permute-start.1 = (bf16[128,256]{1,0:T(8,128)(2,1)S(1)}, bf16[128,256]{1,0:T(8,128)(2,1)S(1)}, u32[]{:S(2)}, u32[]{:S(2)}) collective-permute-start(bf16[128,256]{1,0:T(8,128)(2,1)S(1)} %get-tuple-element.61.bound_t_ref), channel_id=1, source_target_pairs={{0,16},{1,17},{2,18},{3,19},{4,20},{5,21},{6,22},{7,23},{8,24},{9,... | collective-permute-start | bytes 196616 | tf_op jit(solution)/shard_map/ppermute | solution.py:269
  6.0 18.5 %collective-permute-start.2 = (bf16[128,256]{1,0:T(8,128)(2,1)S(1)}, bf16[128,256]{1,0:T(8,128)(2,1)S(1)}, u32[]{:S(2)}, u32[]{:S(2)}) collective-permute-start(bf16[128,256]{1,0:T(8,128)(2,1)S(1)} %get-tuple-element.61.bound_t_ref), channel_id=1, source_target_pairs={{0,32},{1,33},{2,34},{3,35},{4,36},{5,37},{6,38},{7,39},{8,40},{9,... | collective-permute-start | bytes 196616 | tf_op jit(solution)/shard_map/ppermute | solution.py:269
  9.0 6.5 %collective-permute-start.4 = (bf16[64,128]{1,0:T(8,128)(2,1)S(1)}, bf16[64,128]{1,0:T(8,128)(2,1)S(1)}, u32[]{:S(2)}, u32[]{:S(2)}) collective-permute-start(bf16[64,128]{1,0:T(8,128)(2,1)S(1)} %get-tuple-element.62), channel_id=1, source_target_pairs={{0,1},{1,2},{2,3},{3,4},{4,5},{5,6},{6,7},{8,9},{9,10},{10,11},{11... | collective-permute-start | bytes 49160 | tf_op jit(solution)/shard_map/ppermute | solution.py:280
  12.2 7.8 %collective-permute-start.5 = (bf16[64,128]{1,0:T(8,128)(2,1)S(1)}, bf16[64,128]{1,0:T(8,128)(2,1)S(1)}, u32[]{:S(2)}, u32[]{:S(2)}) collective-permute-start(bf16[64,128]{1,0:T(8,128)(2,1)S(1)} %get-tuple-element.63), channel_id=1, source_target_pairs={{1,0},{2,1},{3,2},{4,3},{5,4},{6,5},{7,6},{9,8},{10,9},{11,10},{12... | collective-permute-start | bytes 49160 | tf_op jit(solution)/shard_map/ppermute | solution.py:280
  13.5 6.5 %copy-start.2 = (bf16[3072,128]{1,0:T(8,128)(2,1)S(1)}, bf16[3072,128]{1,0:T(8,128)(2,1)}, u32[]{:S(2)}) copy-start(bf16[3072,128]{1,0:T(8,128)(2,1)} %feats_ref.3) | copy-start | bytes 2359300
  13.5 6.5 %copy-start.3 = (bf16[9,128,128]{2,1,0:T(8,128)(2,1)S(1)}, bf16[9,128,128]{2,1,0:T(8,128)(2,1)}, u32[]{:S(2)}) copy-start(bf16[9,128,128]{2,1,0:T(8,128)(2,1)} %w_ref.9) | copy-start | bytes 884740
  15.4 9.1 %collective-permute-start.3 = (bf16[128,256]{1,0:T(8,128)(2,1)S(1)}, bf16[128,256]{1,0:T(8,128)(2,1)S(1)}, u32[]{:S(2)}, u32[]{:S(2)}) collective-permute-start(bf16[128,256]{1,0:T(8,128)(2,1)S(1)} %get-tuple-element.61.bound_t_ref), channel_id=1, source_target_pairs={{0,64},{1,65},{2,66},{3,67},{4,68},{5,69},{6,70},{7,71},{8,72},{9,... | collective-permute-start | bytes 196616 | tf_op jit(solution)/shard_map/ppermute | solution.py:269
  19.9 4.6 %copy-start.1 = (s32[256]{0:T(256)S(1)}, s32[256]{0:T(256)}, u32[]{:S(2)}) copy-start(s32[256]{0:T(256)} %param.13) | copy-start | bytes 3076
  19.9 4.6 %copy-start.5 = (bf16[1024,128]{1,0:T(8,128)(2,1)S(1)}, bf16[1024,128]{1,0:T(8,128)(2,1)}, u32[]{:S(2)}) copy-start(bf16[1024,128]{1,0:T(8,128)(2,1)} %lat_ref.1) | copy-start | bytes 786436
  20.0 4.6 %copy-start.6 = (bf16[1024,128]{1,0:T(8,128)(2,1)S(1)}, bf16[1024,128]{1,0:T(8,128)(2,1)}, u32[]{:S(2)}) copy-start(bf16[1024,128]{1,0:T(8,128)(2,1)} %cot_ref.3) | copy-start | bytes 786436
  20.0 4.6 %copy-start.7 = (s32[2,8192]{1,0:T(2,128)S(1)}, s32[2,8192]{1,0:T(2,128)}, u32[]{:S(2)}) copy-start(s32[2,8192]{1,0:T(2,128)} %contacts_ref.3) | copy-start | bytes 196612
  20.0 4.6 %copy-start.9 = (s32[1,4]{1,0:T(1,128)S(1)}, s32[1,4]{1,0:T(1,128)}, u32[]{:S(2)}) copy-start(s32[1,4]{1,0:T(1,128)} %counts_ref.1) | copy-start | bytes 52
  36.7 4.1 %collective-permute-start.6 = (bf16[576,128]{1,0:T(8,128)(2,1)S(1)}, bf16[576,128]{1,0:T(8,128)(2,1)S(1)}, u32[]{:S(2)}, u32[]{:S(2)}) collective-permute-start(bf16[576,128]{1,0:T(8,128)(2,1)S(1)} %get-tuple-element.74), channel_id=1, source_target_pairs={{0,8},{1,9},{2,10},{3,11},{4,12},{5,13},{6,14},{7,15},{8,0},{9,1},... | collective-permute-start | bytes 442376 | tf_op jit(solution)/shard_map/ppermute | solution.py:269
  40.9 7.1 %collective-permute-start.7 = (bf16[144,128]{1,0:T(8,128)(2,1)S(1)}, bf16[144,128]{1,0:T(8,128)(2,1)S(1)}, u32[]{:S(2)}, u32[]{:S(2)}) collective-permute-start(bf16[144,128]{1,0:T(8,128)(2,1)S(1)} %get-tuple-element.121), channel_id=1, source_target_pairs={{0,1},{1,0},{2,3},{3,2},{4,5},{5,4},{6,7},{7,6},{8,9},{9,8},{10,11... | collective-permute-start | bytes 110600 | tf_op jit(solution)/shard_map/ppermute | solution.py:269
  43.3 4.8 %collective-permute-start.8 = (bf16[144,128]{1,0:T(8,128)(2,1)S(1)}, bf16[144,128]{1,0:T(8,128)(2,1)S(1)}, u32[]{:S(2)}, u32[]{:S(2)}) collective-permute-start(bf16[144,128]{1,0:T(8,128)(2,1)S(1)} %get-tuple-element.120), channel_id=1, source_target_pairs={{0,2},{1,3},{2,0},{3,1},{4,6},{5,7},{6,4},{7,5},{8,10},{9,11},{10,... | collective-permute-start | bytes 110600 | tf_op jit(solution)/shard_map/ppermute | solution.py:269
  45.9 4.0 %collective-permute-start.9 = (bf16[144,128]{1,0:T(8,128)(2,1)S(1)}, bf16[144,128]{1,0:T(8,128)(2,1)S(1)}, u32[]{:S(2)}, u32[]{:S(2)}) collective-permute-start(bf16[144,128]{1,0:T(8,128)(2,1)S(1)} %get-tuple-element.119), channel_id=1, source_target_pairs={{0,3},{1,2},{2,1},{3,0},{4,7},{5,6},{6,5},{7,4},{8,11},{9,10},{10,... | collective-permute-start | bytes 110600 | tf_op jit(solution)/shard_map/ppermute | solution.py:269
  46.0 13.3 %collective-permute-start.14 = (bf16[512,128]{1,0:T(8,128)(2,1)S(1)}, bf16[512,128]{1,0:T(8,128)(2,1)S(1)}, u32[]{:S(2)}, u32[]{:S(2)}) collective-permute-start(bf16[512,128]{1,0:T(8,128)(2,1)S(1)} %pad_maximum_fusion.2), channel_id=1, source_target_pairs={{0,32},{1,33},{2,34},{3,35},{4,36},{5,37},{6,38},{7,39},{8,40},{9,... | collective-permute-start | bytes 393224 | tf_op jit(solution)/shard_map/ppermute | solution.py:269
  47.2 9.4 %collective-permute-start.13 = (bf16[256,128]{1,0:T(8,128)(2,1)S(1)}, bf16[256,128]{1,0:T(8,128)(2,1)S(1)}, u32[]{:S(2)}, u32[]{:S(2)}) collective-permute-start(bf16[256,128]{1,0:T(8,128)(2,1)S(1)} %get-tuple-element.89), channel_id=1, source_target_pairs={{0,16},{1,17},{2,18},{3,19},{4,20},{5,21},{6,22},{7,23},{8,24},{9,... | collective-permute-start | bytes 196616 | tf_op jit(solution)/shard_map/ppermute | solution.py:269
  50.0 9.3 %collective-permute-start.10 = (bf16[144,128]{1,0:T(8,128)(2,1)S(1)}, bf16[144,128]{1,0:T(8,128)(2,1)S(1)}, u32[]{:S(2)}, u32[]{:S(2)}) collective-permute-start(bf16[144,128]{1,0:T(8,128)(2,1)S(1)} %add_convert_fusion.4), channel_id=1, source_target_pairs={{0,4},{1,5},{2,6},{3,7},{4,0},{5,1},{6,2},{7,3},{8,12},{9,13},{10,... | collective-permute-start | bytes 110600 | tf_op jit(solution)/shard_map/ppermute | solution.py:269
  51.3 7.9 %collective-permute-start.11 = (bf16[144,128]{1,0:T(8,128)(2,1)S(1)}, bf16[144,128]{1,0:T(8,128)(2,1)S(1)}, u32[]{:S(2)}, u32[]{:S(2)}) collective-permute-start(bf16[144,128]{1,0:T(8,128)(2,1)S(1)} %add_convert_fusion.4), channel_id=1, source_target_pairs={{0,128},{1,129},{2,130},{3,131},{4,132},{5,133},{6,134},{7,135},{8... | collective-permute-start | bytes 110600 | tf_op jit(solution)/shard_map/ppermute | solution.py:269
  53.8 5.5 %collective-permute-start.12 = (bf16[144,128]{1,0:T(8,128)(2,1)S(1)}, bf16[144,128]{1,0:T(8,128)(2,1)S(1)}, u32[]{:S(2)}, u32[]{:S(2)}) collective-permute-start(bf16[144,128]{1,0:T(8,128)(2,1)S(1)} %add_convert_fusion.4), channel_id=1, source_target_pairs={{0,132},{1,133},{2,134},{3,135},{4,128},{5,129},{6,130},{7,131},{8... | collective-permute-start | bytes 110600 | tf_op jit(solution)/shard_map/ppermute | solution.py:269
  56.6 3.6 %collective-permute-start.16 = (bf16[256,128]{1,0:T(8,128)(2,1)S(1)}, bf16[256,128]{1,0:T(8,128)(2,1)S(1)}, u32[]{:S(2)}, u32[]{:S(2)}) collective-permute-start(bf16[256,128]{1,0:T(8,128)(2,1)S(1)} %get-tuple-element.95), channel_id=1, source_target_pairs={{0,8},{1,9},{2,10},{3,11},{4,12},{5,13},{6,14},{7,15},{8,0},{9,1},... | collective-permute-start | bytes 196616 | tf_op jit(solution)/shard_map/ppermute | solution.py:269
  59.3 2.9 %collective-permute-start.15 = (bf16[144,128]{1,0:T(8,128)(2,1)S(1)}, bf16[144,128]{1,0:T(8,128)(2,1)S(1)}, u32[]{:S(2)}, u32[]{:S(2)}) collective-permute-start(bf16[144,128]{1,0:T(8,128)(2,1)S(1)} %add_convert_fusion.3), channel_id=1, source_target_pairs={{0,16},{1,17},{2,18},{3,19},{4,20},{5,21},{6,22},{7,23},{8,24},{9,... | collective-permute-start | bytes 110600 | tf_op jit(solution)/shard_map/ppermute | solution.py:269
  62.2 4.1 %collective-permute-start.17 = (bf16[144,128]{1,0:T(8,128)(2,1)S(1)}, bf16[144,128]{1,0:T(8,128)(2,1)S(1)}, u32[]{:S(2)}, u32[]{:S(2)}) collective-permute-start(bf16[144,128]{1,0:T(8,128)(2,1)S(1)} %add_convert_fusion.2), channel_id=1, source_target_pairs={{0,32},{1,33},{2,34},{3,35},{4,36},{5,37},{6,38},{7,39},{8,40},{9,... | collective-permute-start | bytes 110600 | tf_op jit(solution)/shard_map/ppermute | solution.py:269
  66.3 9.6 %collective-permute-start.18 = (bf16[400,128]{1,0:T(8,128)(2,1)S(1)}, bf16[400,128]{1,0:T(8,128)(2,1)S(1)}, u32[]{:S(2)}, u32[]{:S(2)}) collective-permute-start(bf16[400,128]{1,0:T(8,128)(2,1)S(1)} %pad_maximum_fusion.3), channel_id=1, source_target_pairs={{0,96},{1,97},{2,98},{3,99},{4,100},{5,101},{6,102},{7,103},{8,104... | collective-permute-start | bytes 307208 | tf_op jit(solution)/shard_map/ppermute | solution.py:269
  69.9 2.6 %collective-permute-start.19 = (bf16[64,128]{1,0:T(8,128)(2,1)S(1)}, bf16[64,128]{1,0:T(8,128)(2,1)S(1)}, u32[]{:S(2)}, u32[]{:S(2)}) collective-permute-start(bf16[64,128]{1,0:T(8,128)(2,1)S(1)} %get-tuple-element.109), channel_id=1, source_target_pairs={{0,1},{1,2},{2,3},{3,4},{4,5},{5,6},{6,7},{8,9},{9,10},{10,11},{11... | collective-permute-start | bytes 49160 | tf_op jit(solution)/shard_map/ppermute | solution.py:280
  71.2 4.8 %collective-permute-start.20 = (bf16[64,128]{1,0:T(8,128)(2,1)S(1)}, bf16[64,128]{1,0:T(8,128)(2,1)S(1)}, u32[]{:S(2)}, u32[]{:S(2)}) collective-permute-start(bf16[64,128]{1,0:T(8,128)(2,1)S(1)} %get-tuple-element.110), channel_id=1, source_target_pairs={{1,0},{2,1},{3,2},{4,3},{5,4},{6,5},{7,6},{9,8},{10,9},{11,10},{12... | collective-permute-start | bytes 49160 | tf_op jit(solution)/shard_map/ppermute | solution.py:280
  76.0 6.1 %collective-permute-start.21 = (bf16[144,128]{1,0:T(8,128)(2,1)S(1)}, bf16[144,128]{1,0:T(8,128)(2,1)S(1)}, u32[]{:S(2)}, u32[]{:S(2)}) collective-permute-start(bf16[144,128]{1,0:T(8,128)(2,1)S(1)} %add_convert_fusion), channel_id=1, source_target_pairs={{0,1},{1,0},{2,3},{3,2},{4,5},{5,4},{6,7},{7,6},{8,9},{9,8},{10,11... | collective-permute-start | bytes 110600 | tf_op jit(solution)/shard_map/ppermute | solution.py:269
  77.4 6.4 %collective-permute-start.22 = (bf16[144,128]{1,0:T(8,128)(2,1)S(1)}, bf16[144,128]{1,0:T(8,128)(2,1)S(1)}, u32[]{:S(2)}, u32[]{:S(2)}) collective-permute-start(bf16[144,128]{1,0:T(8,128)(2,1)S(1)} %add_convert_fusion), channel_id=1, source_target_pairs={{0,2},{1,3},{2,0},{3,1},{4,6},{5,7},{6,4},{7,5},{8,10},{9,11},{10,... | collective-permute-start | bytes 110600 | tf_op jit(solution)/shard_map/ppermute | solution.py:269
  82.1 4.0 %collective-permute-start.23 = (bf16[144,128]{1,0:T(8,128)(2,1)S(1)}, bf16[144,128]{1,0:T(8,128)(2,1)S(1)}, u32[]{:S(2)}, u32[]{:S(2)}) collective-permute-start(bf16[144,128]{1,0:T(8,128)(2,1)S(1)} %add_convert_fusion), channel_id=1, source_target_pairs={{0,3},{1,2},{2,1},{3,0},{4,7},{5,6},{6,5},{7,4},{8,11},{9,10},{10,... | collective-permute-start | bytes 110600 | tf_op jit(solution)/shard_map/ppermute | solution.py:269
  86.1 8.5 %collective-permute-start.24 = (bf16[576,128]{1,0:T(8,128)(2,1)S(1)}, bf16[576,128]{1,0:T(8,128)(2,1)S(1)}, u32[]{:S(2)}, u32[]{:S(2)}) collective-permute-start(bf16[576,128]{1,0:T(8,128)(2,1)S(1)} %pad_maximum_fusion.1), channel_id=1, source_target_pairs={{0,8},{1,9},{2,10},{3,11},{4,12},{5,13},{6,14},{7,15},{8,0},{9,1},... | collective-permute-start | bytes 442376 | tf_op jit(solution)/shard_map/ppermute | solution.py:269

commit v6 on v5

--- a/solution.py
+++ b/solution.py
@@ -371,26 +371,6 @@
         mib=26,
     )
     other = exchanged(sent, mask_core=1)
-    *far_grads, own_grad = call(
-        contact_back_kernel,
-        [((bound_count, width), BF)] * rounds + [((bound_count, width), F32)],
-        [weights, contact_edges, d_contact],
-        flops=2 * 10**9,
-        mib=16,
-    )
-    other, *far_grads = tie(other, *far_grads)
-    block = kept + wide(other)
-    size = block.shape[0] // 4
-    pieces = [
-        lax.dynamic_slice_in_dim(block, (row_y ^ mask) * size, size, 0) for mask in range(4)
-    ]
-    one, two, three = [exchanged(pieces[mask].astype(BF), mask_y=mask) for mask in (1, 2, 3)]
-    in_one = exchanged(far_grads[1], mask_z=1)
-    pair = exchanged(jnp.concatenate(far_grads[2:], axis=0), mask_z=2)
-    one, two, three, d_mesh = tie(one, two, three, d_mesh)
-    block = ((pieces[0] + wide(one)) + (wide(two) + wide(three))).astype(BF)
-
-    one, two, three = [exchanged(block, mask_x=mask) for mask in (1, 2, 3)]
     part, low, high = call(
         send_back_kernel,
         [((rows_dev, width), F32), ((HB, width), BF), ((HB, width), BF)],
@@ -399,16 +379,33 @@
         flops=2 * 10**9,
         mib=16,
     )
-    one, two, three, part, low, high, in_one, pair = tie(
-        one, two, three, part, low, high, in_one, pair
-    )
-    block = ((wide(block) + wide(one)) + (wide(two) + wide(three))).astype(BF)
+    other, part, low, high, d_contact = tie(other, part, low, high, d_contact)
+    block = kept + wide(other)
+    size = block.shape[0] // 4
+    pieces = [
+        lax.dynamic_slice_in_dim(block, (row_y ^ mask) * size, size, 0) for mask in range(4)
+    ]
+    found = [exchanged(pieces[mask].astype(BF), mask_y=mask) for mask in (1, 2, 3)]
+    *far_grads, own_grad = call(
+        contact_back_kernel,
+        [((bound_count, width), BF)] * rounds + [((bound_count, width), F32)],
+        [weights, contact_edges, d_contact],
+        flops=2 * 10**9,
+        mib=16,
+    )
+    one, two, three, *far_grads = tie(*found, *far_grads)
+    block = ((pieces[0] + wide(one)) + (wide(two) + wide(three))).astype(BF)
+
+    rim = jnp.where(row_y == 0, low, high)
+    one = exchanged(jnp.concatenate([block, rim], axis=0), mask_x=1)
+    two, three = [exchanged(block, mask_x=mask) for mask in (2, 3)]
+    in_one = exchanged(far_grads[1], mask_z=1)
+    pair = exchanged(jnp.concatenate(far_grads[2:], axis=0), mask_z=2)
+    one, two, three, part = tie(one, two, three, part)
+    rim = one[size:]
+    block = ((wide(block) + wide(one[:size])) + (wide(two) + wide(three))).astype(BF)
 
     other = exchanged(block, mask_z=1)
-    in_zero = exchanged(far_grads[0], mask_core=1)
-    other, in_zero, part = tie(other, in_zero, part)
-    block = (wide(block) + wide(other)).astype(BF)
-    other = exchanged(block, mask_z=2)
     (part,) = call(
         recv_back_kernel,
         [((rows_dev, width), F32)],
@@ -417,19 +414,30 @@
         flops=2 * 10**9,
         mib=16,
     )
-    other, part, pair, low, high = tie(other, part, pair, low, high)
+    other, part, in_one = tie(other, part, in_one)
+    block = (wide(block) + wide(other)).astype(BF)
+    other = exchanged(block, mask_z=2)
+    in_zero = exchanged(far_grads[0], mask_core=1)
+    other, in_zero, pair = tie(other, in_zero, pair)
     block = (wide(block) + wide(other)).astype(BF)
     in_two = pair[:bound_count]
     other = exchanged(jnp.concatenate([block, pair[bound_count:]], axis=0), mask_z=6)
-    from_prev = shifted(high, 1)
-    from_next = shifted(low, -1)
-    other, from_prev, from_next = tie(other, from_prev, from_next)
     in_three = other[size:]
     block = (wide(block) + wide(other[:size])).astype(BF)
 
-    found = [exchanged(block, mask_y=mask) for mask in (1, 2, 3)]
-    found = tie(*found)
-    block = ordered_by_y([block, *found], row_y)
+    rim = jnp.where(row_y == 1, high, jnp.where(row_y == 2, low, rim))
+    three = exchanged(jnp.concatenate([block, rim], axis=0), mask_y=3)
+    rim = jnp.where(row_y % 2 == 0, high, low)
+    one = exchanged(jnp.concatenate([block, rim], axis=0), mask_y=1)
+    two = exchanged(block, mask_y=2)
+    one, two, three = tie(one, two, three)
+    panel = lax.axis_index("panel")
+    nothing = jnp.zeros_like(rim)
+    from_prev = jnp.where(row_y % 2 == 0, three[size:], one[size:])
+    from_prev = jnp.where(panel == 0, nothing, from_prev)
+    from_next = jnp.where(row_y % 2 == 0, one[size:], three[size:])
+    from_next = jnp.where(panel == lax.axis_size("panel") - 1, nothing, from_next)
+    block = ordered_by_y([block, one[:size], two, three[:size]], row_y)
     other = exchanged(block, mask_core=1)
     (grad_rows,) = call(
         last_kernel,

time: 95.9 us -> 86.8 us (0.905)
  starting transfers between devices: 52 us -> 45.7 us
  waiting for transfers between devices: 11.9 us -> 9.08 us
    ppermute x21, starting transfers between devices: 44.9 us -> 41.3 us  [exchanged(): return lax.ppermute(block, ('region', 'panel'), route)]
    ppermute x4 -> x2, waiting for transfers between devices: 3.48 us -> 0.01 us  [shifted(): return lax.ppermute(array, 'panel', pairs)]
    ppermute x4 -> x2, starting transfers between devices: 7.05 us -> 4.48 us  [shifted(): return lax.ppermute(array, 'panel', pairs)]
  transfers between devices with their start and end apart: 25 -> 23, of which waited for: 7 -> 5; matrix products, arithmetic and copies ran while one was open for 0% -> 0% of each run, Pallas kernels for 16% -> 18%
where the time goes in v6:
time: 86.8 us; the launch traced here: 86.7 us
  starting transfers between devices  45.7 us (53%)
  Pallas kernels  27.9 us (32%)
  waiting for transfers between devices  9.08 us (10%)
  local copies, waits for them, and re-layouts  1.72 us (2%)
  other arithmetic  1.16 us (1%)
  between operations  1.05 us (1%)
    ppermute x21, starting transfers between devices, exchanged(): return lax.ppermute(block, ('region', 'panel'), route)  41.3 us
    pallas_call x8, Pallas kernels, call(): pl.pallas_call(kernel, out_shape=[jax.ShapeDtypeStruct(shape, kind) for s...  27.9 us
    ppermute x21, waiting for transfers between devices, exchanged(): return lax.ppermute(block, ('region', 'panel'), route)  9.08 us
    ppermute x2, starting transfers between devices, shifted(): return lax.ppermute(array, 'panel', pairs)  4.48 us
  transfers between devices with their start and end apart: 23, of which 5 were waited for; matrix products, arithmetic and copies ran while one was open for 0% of the time, Pallas kernels for 18%

profile of v6, /device:TPU:1, one launch (start us, length us, event | category | flops | bytes accessed | tf_op | source)
XLA Modules:
  0.0 86.7 jit_solution(15316333119219290122)
XLA Ops:
  0.6 0.0 copy-start
  0.6 0.7 copy-done
  1.3 0.9 %copy-done.4 = bf16[1024,128]{1,0:T(8,128)(2,1)S(1)} copy-done((bf16[1024,128]{1,0:T(8,128)(2,1)S(1)}, bf16[1024,128]{1,0:T(8,128)(2,1)}, u32[]{:S(2)}) %copy-start.4) | copy-done | bytes 262168
  2.3 0.4 shard_map.103
  2.7 3.3 %collective-permute-start = (bf16[128,256]{1,0:T(8,128)(2,1)S(1)}, bf16[128,256]{1,0:T(8,128)(2,1)S(1)}, u32[]{:S(2)}, u32[]{:S(2)}) collective-permute-start(bf16[128,256]{1,0:T(8,128)(2,1)S(1)} %get-tuple-element.55.bound_t_ref), channel_id=1, source_target_pairs={{0,8},{1,9},{2,10},{3,11},{4,12},{5,13},{6,14},{7,15},{8,0},{9,1},... | collective-permute-start | bytes 196616 | tf_op jit(solution)/shard_map/ppermute | solution.py:269
  6.0 0.0 collective-permute-start.1
  6.0 2.9 %collective-permute-start.2 = (bf16[128,256]{1,0:T(8,128)(2,1)S(1)}, bf16[128,256]{1,0:T(8,128)(2,1)S(1)}, u32[]{:S(2)}, u32[]{:S(2)}) collective-permute-start(bf16[128,256]{1,0:T(8,128)(2,1)S(1)} %get-tuple-element.55.bound_t_ref), channel_id=1, source_target_pairs={{0,32},{1,33},{2,34},{3,35},{4,36},{5,37},{6,38},{7,39},{8,40},{9,... | collective-permute-start | bytes 196616 | tf_op jit(solution)/shard_map/ppermute | solution.py:269
  9.0 3.2 %collective-permute-start.4 = (bf16[64,128]{1,0:T(8,128)(2,1)S(1)}, bf16[64,128]{1,0:T(8,128)(2,1)S(1)}, u32[]{:S(2)}, u32[]{:S(2)}) collective-permute-start(bf16[64,128]{1,0:T(8,128)(2,1)S(1)} %get-tuple-element.56), channel_id=1, source_target_pairs={{0,1},{1,2},{2,3},{3,4},{4,5},{5,6},{6,7},{8,9},{9,10},{10,11},{11... | collective-permute-start | bytes 49160 | tf_op jit(solution)/shard_map/ppermute | solution.py:280
  12.2 1.3 %collective-permute-start.5 = (bf16[64,128]{1,0:T(8,128)(2,1)S(1)}, bf16[64,128]{1,0:T(8,128)(2,1)S(1)}, u32[]{:S(2)}, u32[]{:S(2)}) collective-permute-start(bf16[64,128]{1,0:T(8,128)(2,1)S(1)} %get-tuple-element.57), channel_id=1, source_target_pairs={{1,0},{2,1},{3,2},{4,3},{5,4},{6,5},{7,6},{9,8},{10,9},{11,10},{12... | collective-permute-start | bytes 49160 | tf_op jit(solution)/shard_map/ppermute | solution.py:280
  13.5 0.0 copy-start.2
  13.5 0.0 copy-start.3
  13.5 1.9 %shard_map.104 = (bf16[128,3072]{1,0:T(8,128)(2,1)S(1)}, bf16[128,3072]{1,0:T(8,128)(2,1)S(1)}) custom-call(bf16[128,1024]{1,0:T(8,128)(2,1)S(1)} %get-tuple-element.54.lat_t_ref, s32[2,3072]{1,0:T(2,128)S(1)} %copy-done.8), custom_call_target="tpu_custom_call" | custom-call | flops 4000000000 | bytes 4000000 | tf_op jit(solution)/shard_map/pallas_call | solution.py:251
  15.4 0.0 collective-permute-done.4.before_ref
  15.4 4.5 %collective-permute-start.3 = (bf16[128,256]{1,0:T(8,128)(2,1)S(1)}, bf16[128,256]{1,0:T(8,128)(2,1)S(1)}, u32[]{:S(2)}, u32[]{:S(2)}) collective-permute-start(bf16[128,256]{1,0:T(8,128)(2,1)S(1)} %get-tuple-element.55.bound_t_ref), channel_id=1, source_target_pairs={{0,64},{1,65},{2,66},{3,67},{4,68},{5,69},{6,70},{7,71},{8,72},{9,... | collective-permute-start | bytes 196616 | tf_op jit(solution)/shard_map/ppermute | solution.py:269
  19.9 0.0 collective-permute-done.5.after_ref
  19.9 0.0 copy-start.1
  19.9 0.0 copy-start.5
  20.0 0.0 copy-start.6
  20.0 0.0 copy-start.7
  20.0 0.0 copy-start.9
  20.0 4.5 %shard_map.105 = (bf16[128,3072]{1,0:T(8,128)(2,1)S(1)}, f32[128,3072]{1,0:T(8,128)S(1)}, bf16[1024,128]{1,0:T(8,128)(2,1)S(1)}) custom-call(bf16[64,128]{1,0:T(8,128)(2,1)S(1)} %collective-permute-done.4.before_ref, bf16[64,128]{1,0:T(8,128)(2,1)S(1)} %collective-permute-done.5.after_ref, bf16[128,3072]{1,0:T(8,128)(2,1)S(1)} %get-tuple-element.61.own_ref, ...), custom_call_target="tpu_custom_call" | custom-call | flops 3000000000 | bytes 4000000 | tf_op jit(solution)/shard_map/pallas_call | solution.py:251
  24.5 0.0 collective-permute-done.far0_ref
  24.5 0.0 collective-permute-done.1.far1_ref
  24.5 0.0 collective-permute-done.2.far2_ref
  24.5 0.0 collective-permute-done.3.far3_ref
  24.6 12.1 %shard_map.106 = (bf16[1024,128]{1,0:T(8,128)(2,1)}, f32[576,128]{1,0:T(8,128)S(1)}, bf16[576,128]{1,0:T(8,128)(2,1)S(1)}, bf16[128,3072]{1,0:T(8,128)(2,1)S(1)}...) custom-call(s32[1,4]{1,0:T(1,128)S(1)} %copy-done.9, s32[1]{0:T(128)} %bitcast.core_ref, ...), custom_call_target="tpu_custom_call" | custom-call | flops 8000000000 | bytes 4000000 | tf_op jit(solution)/shard_map/pallas_call | solution.py:251
  36.7 1.3 %collective-permute-start.6 = (bf16[576,128]{1,0:T(8,128)(2,1)S(1)}, bf16[576,128]{1,0:T(8,128)(2,1)S(1)}, u32[]{:S(2)}, u32[]{:S(2)}) collective-permute-start(bf16[576,128]{1,0:T(8,128)(2,1)S(1)} %get-tuple-element.68), channel_id=1, source_target_pairs={{0,8},{1,9},{2,10},{3,11},{4,12},{5,13},{6,14},{7,15},{8,0},{9,1},... | collective-permute-start | bytes 442376 | tf_op jit(solution)/shard_map/ppermute | solution.py:269
  38.0 2.6 %shard_map.107 = (f32[1024,128]{1,0:T(8,128)S(1)}, bf16[64,128]{1,0:T(8,128)(2,1)S(1)}, bf16[64,128]{1,0:T(8,128)(2,1)S(1)}) custom-call(bf16[9,128,128]{2,1,0:T(8,128)(2,1)S(1)} %copy-done.3, s32[2,3072]{1,0:T(2,128)S(1)} %copy-done.8, bf16[128,3072]{1,0:T(8,128)(2,1)S(1)} %get-tuple-element.69.dm_ref), custom_call_target="tpu_custom_call" | custom-call | flops 2000000000 | bytes 4000000 | tf_op jit(solution)/shard_map/pallas_call | solution.py:251
  40.7 0.0 collective-permute-done.6
  40.7 2.4 %collective-permute-start.7 = (bf16[144,128]{1,0:T(8,128)(2,1)S(1)}, bf16[144,128]{1,0:T(8,128)(2,1)S(1)}, u32[]{:S(2)}, u32[]{:S(2)}) collective-permute-start(bf16[144,128]{1,0:T(8,128)(2,1)S(1)} %get-tuple-element.109), channel_id=1, source_target_pairs={{0,1},{1,0},{2,3},{3,2},{4,5},{5,4},{6,7},{7,6},{8,9},{9,8},{10,11... | collective-permute-start | bytes 110600 | tf_op jit(solution)/shard_map/ppermute | solution.py:269
  43.2 2.6 %collective-permute-start.8 = (bf16[144,128]{1,0:T(8,128)(2,1)S(1)}, bf16[144,128]{1,0:T(8,128)(2,1)S(1)}, u32[]{:S(2)}, u32[]{:S(2)}) collective-permute-start(bf16[144,128]{1,0:T(8,128)(2,1)S(1)} %get-tuple-element.108), channel_id=1, source_target_pairs={{0,2},{1,3},{2,0},{3,1},{4,6},{5,7},{6,4},{7,5},{8,10},{9,11},{10,... | collective-permute-start | bytes 110600 | tf_op jit(solution)/shard_map/ppermute | solution.py:269
  45.8 0.0 collective-permute-start.9
  45.8 2.8 %shard_map.108 = (bf16[256,128]{1,0:T(8,128)(2,1)S(1)}, bf16[256,128]{1,0:T(8,128)(2,1)S(1)}, bf16[256,128]{1,0:T(8,128)(2,1)S(1)}, bf16[256,128]{1,0:T(8,128)(2,1)S(1)}, f32[256,128]{1,0:T(8,128)S(1)}) custom-call(bf16[9,128,128]{2,1,0:T(8,128)(2,1)S(1)} %copy-done.3, s32[2,8192]{1,0:T(2,128)S(1)} %copy-done.7, bf16[128,8192]{1,0:T(8,128)(2,1)S(1)} %get-tuple-element.75.dc_ref), custom_call_target="tpu_custom_call" | custom-call | flops 2000000000 | bytes 4000000 | tf_op jit(solution)/shard_map/pallas_call | solution.py:251
  48.6 0.0 collective-permute-done.7
  48.6 0.0 collective-permute-done.8
  48.7 1.2 %collective-permute-done.9 = bf16[144,128]{1,0:T(8,128)(2,1)S(1)} collective-permute-done((bf16[144,128]{1,0:T(8,128)(2,1)S(1)}, bf16[144,128]{1,0:T(8,128)(2,1)S(1)}, u32[]{:S(2)}, u32[]{:S(2)}) %collective-permute-start.9) | collective-permute-done | bytes 36896 | tf_op jit(solution)/shard_map/ppermute | solution.py:269
  49.9 2.8 %collective-permute-start.11 = (bf16[144,128]{1,0:T(8,128)(2,1)S(1)}, bf16[144,128]{1,0:T(8,128)(2,1)S(1)}, u32[]{:S(2)}, u32[]{:S(2)}) collective-permute-start(bf16[144,128]{1,0:T(8,128)(2,1)S(1)} %add_convert_fusion.4), channel_id=1, source_target_pairs={{0,128},{1,129},{2,130},{3,131},{4,132},{5,133},{6,134},{7,135},{8... | collective-permute-start | bytes 110600 | tf_op jit(solution)/shard_map/ppermute | solution.py:269
  52.7 1.7 %collective-permute-start.12 = (bf16[144,128]{1,0:T(8,128)(2,1)S(1)}, bf16[144,128]{1,0:T(8,128)(2,1)S(1)}, u32[]{:S(2)}, u32[]{:S(2)}) collective-permute-start(bf16[144,128]{1,0:T(8,128)(2,1)S(1)} %add_convert_fusion.4), channel_id=1, source_target_pairs={{0,132},{1,133},{2,134},{3,135},{4,128},{5,129},{6,130},{7,131},{8... | collective-permute-start | bytes 110600 | tf_op jit(solution)/shard_map/ppermute | solution.py:269
  54.5 1.3 %collective-permute-start.17 = (bf16[512,128]{1,0:T(8,128)(2,1)S(1)}, bf16[512,128]{1,0:T(8,128)(2,1)S(1)}, u32[]{:S(2)}, u32[]{:S(2)}) collective-permute-start(bf16[512,128]{1,0:T(8,128)(2,1)S(1)} %pad_maximum_fusion.2), channel_id=1, source_target_pairs={{0,32},{1,33},{2,34},{3,35},{4,36},{5,37},{6,38},{7,39},{8,40},{9,... | collective-permute-start | bytes 393224 | tf_op jit(solution)/shard_map/ppermute | solution.py:269
  55.7 0.7 collective-permute-start.14
  56.4 0.0 collective-permute-done.11
  56.4 2.0 %collective-permute-start.16 = (bf16[256,128]{1,0:T(8,128)(2,1)S(1)}, bf16[256,128]{1,0:T(8,128)(2,1)S(1)}, u32[]{:S(2)}, u32[]{:S(2)}) collective-permute-start(bf16[256,128]{1,0:T(8,128)(2,1)S(1)} %get-tuple-element.95), channel_id=1, source_target_pairs={{0,8},{1,9},{2,10},{3,11},{4,12},{5,13},{6,14},{7,15},{8,0},{9,1},... | collective-permute-start | bytes 196616 | tf_op jit(solution)/shard_map/ppermute | solution.py:269
  58.4 0.0 collective-permute-done.12
  58.4 0.0 collective-permute-done.10
  58.4 1.1 %collective-permute-start.13 = (bf16[144,128]{1,0:T(8,128)(2,1)S(1)}, bf16[144,128]{1,0:T(8,128)(2,1)S(1)}, u32[]{:S(2)}, u32[]{:S(2)}) collective-permute-start(bf16[144,128]{1,0:T(8,128)(2,1)S(1)} %add_convert_fusion.3), channel_id=1, source_target_pairs={{0,16},{1,17},{2,18},{3,19},{4,20},{5,21},{6,22},{7,23},{8,24},{9,... | collective-permute-start | bytes 110600 | tf_op jit(solution)/shard_map/ppermute | solution.py:269
  59.5 2.3 %shard_map.109.part_ref = f32[1024,128]{1,0:T(8,128)S(1)} custom-call(bf16[9,128,128]{2,1,0:T(8,128)(2,1)S(1)} %copy-done.3, s32[2,3072]{1,0:T(2,128)S(1)} %copy-done.8, bf16[128,3072]{1,0:T(8,128)(2,1)S(1)} %get-tuple-element.69.dm_ref, bf16[1024,128]{1,0:T(8,128)(2,1)S(1)} %get-tuple-element.89.dn_ref, bf16[1024,128]{1,0:T(8,128)(2,1)S(1)} %copy-done.6, ...), custom_call_target="tpu_custom_call" | custom-call | flops 2000000000 | bytes 4000000 | tf_op jit(solution)/shard_map/pallas_call | solution.py:251
  61.8 0.0 collective-permute-done.14.in1_ref
  61.8 0.1 collective-permute-done.13
  61.9 1.7 %collective-permute-start.15 = (bf16[144,128]{1,0:T(8,128)(2,1)S(1)}, bf16[144,128]{1,0:T(8,128)(2,1)S(1)}, u32[]{:S(2)}, u32[]{:S(2)}) collective-permute-start(bf16[144,128]{1,0:T(8,128)(2,1)S(1)} %add_convert_fusion.2), channel_id=1, source_target_pairs={{0,32},{1,33},{2,34},{3,35},{4,36},{5,37},{6,38},{7,39},{8,40},{9,... | collective-permute-start | bytes 110600 | tf_op jit(solution)/shard_map/ppermute | solution.py:269
  63.6 0.0 collective-permute-done.16.in0_ref
  63.6 2.1 %collective-permute-done.15 = bf16[144,128]{1,0:T(8,128)(2,1)S(1)} collective-permute-done((bf16[144,128]{1,0:T(8,128)(2,1)S(1)}, bf16[144,128]{1,0:T(8,128)(2,1)S(1)}, u32[]{:S(2)}, u32[]{:S(2)}) %collective-permute-start.15) | collective-permute-done | bytes 36896 | tf_op jit(solution)/shard_map/ppermute | solution.py:269
  65.7 0.0 collective-permute-done.17
  65.8 3.6 %collective-permute-start.18 = (bf16[400,128]{1,0:T(8,128)(2,1)S(1)}, bf16[400,128]{1,0:T(8,128)(2,1)S(1)}, u32[]{:S(2)}, u32[]{:S(2)}) collective-permute-start(bf16[400,128]{1,0:T(8,128)(2,1)S(1)} %pad_maximum_fusion.3), channel_id=1, source_target_pairs={{0,96},{1,97},{2,98},{3,99},{4,100},{5,101},{6,102},{7,103},{8,104... | collective-permute-start | bytes 307208 | tf_op jit(solution)/shard_map/ppermute | solution.py:269
  69.4 2.5 %collective-permute-done.18 = bf16[400,128]{1,0:T(8,128)(2,1)S(1)} collective-permute-done((bf16[400,128]{1,0:T(8,128)(2,1)S(1)}, bf16[400,128]{1,0:T(8,128)(2,1)S(1)}, u32[]{:S(2)}, u32[]{:S(2)}) %collective-permute-start.18) | collective-permute-done | bytes 102432 | tf_op jit(solution)/shard_map/ppermute | solution.py:269
  71.9 0.1 collective-permute-start.19
  72.0 2.1 %collective-permute-start.21 = (bf16[208,128]{1,0:T(8,128)(2,1)S(1)}, bf16[208,128]{1,0:T(8,128)(2,1)S(1)}, u32[]{:S(2)}, u32[]{:S(2)}) collective-permute-start(bf16[208,128]{1,0:T(8,128)(2,1)S(1)} %get-tuple-element.118), channel_id=1, source_target_pairs={{0,3},{1,2},{2,1},{3,0},{4,7},{5,6},{6,5},{7,4},{8,11},{9,10},{10,... | collective-permute-start | bytes 159752 | tf_op jit(solution)/shard_map/ppermute | solution.py:269
  74.1 1.1 %collective-permute-start.20 = (bf16[144,128]{1,0:T(8,128)(2,1)S(1)}, bf16[144,128]{1,0:T(8,128)(2,1)S(1)}, u32[]{:S(2)}, u32[]{:S(2)}) collective-permute-start(bf16[144,128]{1,0:T(8,128)(2,1)S(1)} %add_convert_fusion), channel_id=1, source_target_pairs={{0,2},{1,3},{2,0},{3,1},{4,6},{5,7},{6,4},{7,5},{8,10},{9,11},{10,... | collective-permute-start | bytes 110600 | tf_op jit(solution)/shard_map/ppermute | solution.py:269
  75.3 3.2 %collective-permute-done.20 = bf16[144,128]{1,0:T(8,128)(2,1)S(1)} collective-permute-done((bf16[144,128]{1,0:T(8,128)(2,1)S(1)}, bf16[144,128]{1,0:T(8,128)(2,1)S(1)}, u32[]{:S(2)}, u32[]{:S(2)}) %collective-permute-start.20) | collective-permute-done | bytes 36896 | tf_op jit(solution)/shard_map/ppermute | solution.py:269
  78.4 0.0 collective-permute-done.19
  78.4 0.0 collective-permute-done.21
  78.5 5.9 %collective-permute-start.22 = (bf16[576,128]{1,0:T(8,128)(2,1)S(1)}, bf16[576,128]{1,0:T(8,128)(2,1)S(1)}, u32[]{:S(2)}, u32[]{:S(2)}) collective-permute-start(bf16[576,128]{1,0:T(8,128)(2,1)S(1)} %pad_maximum_fusion.1), channel_id=1, source_target_pairs={{0,8},{1,9},{2,10},{3,11},{4,12},{5,13},{6,14},{7,15},{8,0},{9,1},... | collective-permute-start | bytes 442376 | tf_op jit(solution)/shard_map/ppermute | solution.py:269
  84.4 1.3 %shard_map.110 = f32[1024,128]{1,0:T(8,128)} custom-call(f32[1024,128]{1,0:T(8,128)S(1)} %shard_map.109.part_ref, f32[256,128]{1,0:T(8,128)S(1)} %get-tuple-element.93.own_ref, bf16[256,128]{1,0:T(8,128)(2,1)S(1)} %collective-permute-done.16.in0_ref, bf16[256,128]{1,0:T(8,128)(2,1)S(1)} %collective-permute-done.14.in1_ref, ...), custom_call_target="tpu_custom_call" | custom-call | flops 100000000 | bytes 4000000 | tf_op jit(solution)/shard_map/pallas_call | solution.py:251
  85.7 0.1 broadcast_select_fusion.1
  85.8 0.9 convert.1
  (31 shorter events, 0.3 us)
Async XLA Ops:
  0.6 0.7 copy-start
  1.3 0.9 %copy-start.4 = (bf16[1024,128]{1,0:T(8,128)(2,1)S(1)}, bf16[1024,128]{1,0:T(8,128)(2,1)}, u32[]{:S(2)}) copy-start(bf16[1024,128]{1,0:T(8,128)(2,1)} %lat_ref.1) | copy-start | bytes 786436
  2.3 11.2 %copy-start.8 = (s32[2,3072]{1,0:T(2,128)S(1)}, s32[2,3072]{1,0:T(2,128)}, u32[]{:S(2)}) copy-start(s32[2,3072]{1,0:T(2,128)} %edges_ref.9) | copy-start | bytes 73732
  2.7 21.8 %collective-permute-start = (bf16[128,256]{1,0:T(8,128)(2,1)S(1)}, bf16[128,256]{1,0:T(8,128)(2,1)S(1)}, u32[]{:S(2)}, u32[]{:S(2)}) collective-permute-start(bf16[128,256]{1,0:T(8,128)(2,1)S(1)} %get-tuple-element.55.bound_t_ref), channel_id=1, source_target_pairs={{0,8},{1,9},{2,10},{3,11},{4,12},{5,13},{6,14},{7,15},{8,0},{9,1},... | collective-permute-start | bytes 196616 | tf_op jit(solution)/shard_map/ppermute | solution.py:269
  6.0 18.5 %collective-permute-start.1 = (bf16[128,256]{1,0:T(8,128)(2,1)S(1)}, bf16[128,256]{1,0:T(8,128)(2,1)S(1)}, u32[]{:S(2)}, u32[]{:S(2)}) collective-permute-start(bf16[128,256]{1,0:T(8,128)(2,1)S(1)} %get-tuple-element.55.bound_t_ref), channel_id=1, source_target_pairs={{0,16},{1,17},{2,18},{3,19},{4,20},{5,21},{6,22},{7,23},{8,24},{9,... | collective-permute-start | bytes 196616 | tf_op jit(solution)/shard_map/ppermute | solution.py:269
  6.0 18.5 %collective-permute-start.2 = (bf16[128,256]{1,0:T(8,128)(2,1)S(1)}, bf16[128,256]{1,0:T(8,128)(2,1)S(1)}, u32[]{:S(2)}, u32[]{:S(2)}) collective-permute-start(bf16[128,256]{1,0:T(8,128)(2,1)S(1)} %get-tuple-element.55.bound_t_ref), channel_id=1, source_target_pairs={{0,32},{1,33},{2,34},{3,35},{4,36},{5,37},{6,38},{7,39},{8,40},{9,... | collective-permute-start | bytes 196616 | tf_op jit(solution)/shard_map/ppermute | solution.py:269
  9.0 6.5 %collective-permute-start.4 = (bf16[64,128]{1,0:T(8,128)(2,1)S(1)}, bf16[64,128]{1,0:T(8,128)(2,1)S(1)}, u32[]{:S(2)}, u32[]{:S(2)}) collective-permute-start(bf16[64,128]{1,0:T(8,128)(2,1)S(1)} %get-tuple-element.56), channel_id=1, source_target_pairs={{0,1},{1,2},{2,3},{3,4},{4,5},{5,6},{6,7},{8,9},{9,10},{10,11},{11... | collective-permute-start | bytes 49160 | tf_op jit(solution)/shard_map/ppermute | solution.py:280
  12.2 7.8 %collective-permute-start.5 = (bf16[64,128]{1,0:T(8,128)(2,1)S(1)}, bf16[64,128]{1,0:T(8,128)(2,1)S(1)}, u32[]{:S(2)}, u32[]{:S(2)}) collective-permute-start(bf16[64,128]{1,0:T(8,128)(2,1)S(1)} %get-tuple-element.57), channel_id=1, source_target_pairs={{1,0},{2,1},{3,2},{4,3},{5,4},{6,5},{7,6},{9,8},{10,9},{11,10},{12... | collective-permute-start | bytes 49160 | tf_op jit(solution)/shard_map/ppermute | solution.py:280
  13.5 6.5 %copy-start.2 = (bf16[3072,128]{1,0:T(8,128)(2,1)S(1)}, bf16[3072,128]{1,0:T(8,128)(2,1)}, u32[]{:S(2)}) copy-start(bf16[3072,128]{1,0:T(8,128)(2,1)} %feats_ref.3) | copy-start | bytes 2359300
  13.5 6.5 %copy-start.3 = (bf16[9,128,128]{2,1,0:T(8,128)(2,1)S(1)}, bf16[9,128,128]{2,1,0:T(8,128)(2,1)}, u32[]{:S(2)}) copy-start(bf16[9,128,128]{2,1,0:T(8,128)(2,1)} %w_ref.9) | copy-start | bytes 884740
  15.4 9.1 %collective-permute-start.3 = (bf16[128,256]{1,0:T(8,128)(2,1)S(1)}, bf16[128,256]{1,0:T(8,128)(2,1)S(1)}, u32[]{:S(2)}, u32[]{:S(2)}) collective-permute-start(bf16[128,256]{1,0:T(8,128)(2,1)S(1)} %get-tuple-element.55.bound_t_ref), channel_id=1, source_target_pairs={{0,64},{1,65},{2,66},{3,67},{4,68},{5,69},{6,70},{7,71},{8,72},{9,... | collective-permute-start | bytes 196616 | tf_op jit(solution)/shard_map/ppermute | solution.py:269
  19.9 4.6 %copy-start.1 = (s32[256]{0:T(256)S(1)}, s32[256]{0:T(256)}, u32[]{:S(2)}) copy-start(s32[256]{0:T(256)} %param.13) | copy-start | bytes 3076
  19.9 4.6 %copy-start.5 = (bf16[1024,128]{1,0:T(8,128)(2,1)S(1)}, bf16[1024,128]{1,0:T(8,128)(2,1)}, u32[]{:S(2)}) copy-start(bf16[1024,128]{1,0:T(8,128)(2,1)} %lat_ref.1) | copy-start | bytes 786436
  20.0 4.6 %copy-start.6 = (bf16[1024,128]{1,0:T(8,128)(2,1)S(1)}, bf16[1024,128]{1,0:T(8,128)(2,1)}, u32[]{:S(2)}) copy-start(bf16[1024,128]{1,0:T(8,128)(2,1)} %cot_ref.3) | copy-start | bytes 786436
  20.0 4.6 %copy-start.7 = (s32[2,8192]{1,0:T(2,128)S(1)}, s32[2,8192]{1,0:T(2,128)}, u32[]{:S(2)}) copy-start(s32[2,8192]{1,0:T(2,128)} %contacts_ref.3) | copy-start | bytes 196612
  20.0 4.6 %copy-start.9 = (s32[1,4]{1,0:T(1,128)S(1)}, s32[1,4]{1,0:T(1,128)}, u32[]{:S(2)}) copy-start(s32[1,4]{1,0:T(1,128)} %counts_ref.1) | copy-start | bytes 52
  36.7 3.9 %collective-permute-start.6 = (bf16[576,128]{1,0:T(8,128)(2,1)S(1)}, bf16[576,128]{1,0:T(8,128)(2,1)S(1)}, u32[]{:S(2)}, u32[]{:S(2)}) collective-permute-start(bf16[576,128]{1,0:T(8,128)(2,1)S(1)} %get-tuple-element.68), channel_id=1, source_target_pairs={{0,8},{1,9},{2,10},{3,11},{4,12},{5,13},{6,14},{7,15},{8,0},{9,1},... | collective-permute-start | bytes 442376 | tf_op jit(solution)/shard_map/ppermute | solution.py:269
  40.7 7.9 %collective-permute-start.7 = (bf16[144,128]{1,0:T(8,128)(2,1)S(1)}, bf16[144,128]{1,0:T(8,128)(2,1)S(1)}, u32[]{:S(2)}, u32[]{:S(2)}) collective-permute-start(bf16[144,128]{1,0:T(8,128)(2,1)S(1)} %get-tuple-element.109), channel_id=1, source_target_pairs={{0,1},{1,0},{2,3},{3,2},{4,5},{5,4},{6,7},{7,6},{8,9},{9,8},{10,11... | collective-permute-start | bytes 110600 | tf_op jit(solution)/shard_map/ppermute | solution.py:269
  43.2 5.5 %collective-permute-start.8 = (bf16[144,128]{1,0:T(8,128)(2,1)S(1)}, bf16[144,128]{1,0:T(8,128)(2,1)S(1)}, u32[]{:S(2)}, u32[]{:S(2)}) collective-permute-start(bf16[144,128]{1,0:T(8,128)(2,1)S(1)} %get-tuple-element.108), channel_id=1, source_target_pairs={{0,2},{1,3},{2,0},{3,1},{4,6},{5,7},{6,4},{7,5},{8,10},{9,11},{10,... | collective-permute-start | bytes 110600 | tf_op jit(solution)/shard_map/ppermute | solution.py:269
  45.8 4.0 %collective-permute-start.9 = (bf16[144,128]{1,0:T(8,128)(2,1)S(1)}, bf16[144,128]{1,0:T(8,128)(2,1)S(1)}, u32[]{:S(2)}, u32[]{:S(2)}) collective-permute-start(bf16[144,128]{1,0:T(8,128)(2,1)S(1)} %get-tuple-element.107), channel_id=1, source_target_pairs={{0,3},{1,2},{2,1},{3,0},{4,7},{5,6},{6,5},{7,4},{8,11},{9,10},{10,... | collective-permute-start | bytes 110600 | tf_op jit(solution)/shard_map/ppermute | solution.py:269
  49.9 6.6 %collective-permute-start.11 = (bf16[144,128]{1,0:T(8,128)(2,1)S(1)}, bf16[144,128]{1,0:T(8,128)(2,1)S(1)}, u32[]{:S(2)}, u32[]{:S(2)}) collective-permute-start(bf16[144,128]{1,0:T(8,128)(2,1)S(1)} %add_convert_fusion.4), channel_id=1, source_target_pairs={{0,128},{1,129},{2,130},{3,131},{4,132},{5,133},{6,134},{7,135},{8... | collective-permute-start | bytes 110600 | tf_op jit(solution)/shard_map/ppermute | solution.py:269
  52.7 5.7 %collective-permute-start.12 = (bf16[144,128]{1,0:T(8,128)(2,1)S(1)}, bf16[144,128]{1,0:T(8,128)(2,1)S(1)}, u32[]{:S(2)}, u32[]{:S(2)}) collective-permute-start(bf16[144,128]{1,0:T(8,128)(2,1)S(1)} %add_convert_fusion.4), channel_id=1, source_target_pairs={{0,132},{1,133},{2,134},{3,135},{4,128},{5,129},{6,130},{7,131},{8... | collective-permute-start | bytes 110600 | tf_op jit(solution)/shard_map/ppermute | solution.py:269
  54.4 4.0 %collective-permute-start.10 = (bf16[208,128]{1,0:T(8,128)(2,1)S(1)}, bf16[208,128]{1,0:T(8,128)(2,1)S(1)}, u32[]{:S(2)}, u32[]{:S(2)}) collective-permute-start(bf16[208,128]{1,0:T(8,128)(2,1)S(1)} %pad_maximum_fusion.6), channel_id=1, source_target_pairs={{0,4},{1,5},{2,6},{3,7},{4,0},{5,1},{6,2},{7,3},{8,12},{9,13},{10,... | collective-permute-start | bytes 159752 | tf_op jit(solution)/shard_map/ppermute | solution.py:269
  54.5 11.3 %collective-permute-start.17 = (bf16[512,128]{1,0:T(8,128)(2,1)S(1)}, bf16[512,128]{1,0:T(8,128)(2,1)S(1)}, u32[]{:S(2)}, u32[]{:S(2)}) collective-permute-start(bf16[512,128]{1,0:T(8,128)(2,1)S(1)} %pad_maximum_fusion.2), channel_id=1, source_target_pairs={{0,32},{1,33},{2,34},{3,35},{4,36},{5,37},{6,38},{7,39},{8,40},{9,... | collective-permute-start | bytes 393224 | tf_op jit(solution)/shard_map/ppermute | solution.py:269
  55.7 6.1 %collective-permute-start.14 = (bf16[256,128]{1,0:T(8,128)(2,1)S(1)}, bf16[256,128]{1,0:T(8,128)(2,1)S(1)}, u32[]{:S(2)}, u32[]{:S(2)}) collective-permute-start(bf16[256,128]{1,0:T(8,128)(2,1)S(1)} %get-tuple-element.91), channel_id=1, source_target_pairs={{0,16},{1,17},{2,18},{3,19},{4,20},{5,21},{6,22},{7,23},{8,24},{9,... | collective-permute-start | bytes 196616 | tf_op jit(solution)/shard_map/ppermute | solution.py:269
  56.4 7.2 %collective-permute-start.16 = (bf16[256,128]{1,0:T(8,128)(2,1)S(1)}, bf16[256,128]{1,0:T(8,128)(2,1)S(1)}, u32[]{:S(2)}, u32[]{:S(2)}) collective-permute-start(bf16[256,128]{1,0:T(8,128)(2,1)S(1)} %get-tuple-element.95), channel_id=1, source_target_pairs={{0,8},{1,9},{2,10},{3,11},{4,12},{5,13},{6,14},{7,15},{8,0},{9,1},... | collective-permute-start | bytes 196616 | tf_op jit(solution)/shard_map/ppermute | solution.py:269
  58.4 3.5 %collective-permute-start.13 = (bf16[144,128]{1,0:T(8,128)(2,1)S(1)}, bf16[144,128]{1,0:T(8,128)(2,1)S(1)}, u32[]{:S(2)}, u32[]{:S(2)}) collective-permute-start(bf16[144,128]{1,0:T(8,128)(2,1)S(1)} %add_convert_fusion.3), channel_id=1, source_target_pairs={{0,16},{1,17},{2,18},{3,19},{4,20},{5,21},{6,22},{7,23},{8,24},{9,... | collective-permute-start | bytes 110600 | tf_op jit(solution)/shard_map/ppermute | solution.py:269
  61.9 3.8 %collective-permute-start.15 = (bf16[144,128]{1,0:T(8,128)(2,1)S(1)}, bf16[144,128]{1,0:T(8,128)(2,1)S(1)}, u32[]{:S(2)}, u32[]{:S(2)}) collective-permute-start(bf16[144,128]{1,0:T(8,128)(2,1)S(1)} %add_convert_fusion.2), channel_id=1, source_target_pairs={{0,32},{1,33},{2,34},{3,35},{4,36},{5,37},{6,38},{7,39},{8,40},{9,... | collective-permute-start | bytes 110600 | tf_op jit(solution)/shard_map/ppermute | solution.py:269
  65.8 6.1 %collective-permute-start.18 = (bf16[400,128]{1,0:T(8,128)(2,1)S(1)}, bf16[400,128]{1,0:T(8,128)(2,1)S(1)}, u32[]{:S(2)}, u32[]{:S(2)}) collective-permute-start(bf16[400,128]{1,0:T(8,128)(2,1)S(1)} %pad_maximum_fusion.3), channel_id=1, source_target_pairs={{0,96},{1,97},{2,98},{3,99},{4,100},{5,101},{6,102},{7,103},{8,104... | collective-permute-start | bytes 307208 | tf_op jit(solution)/shard_map/ppermute | solution.py:269
  71.9 6.5 %collective-permute-start.19 = (bf16[208,128]{1,0:T(8,128)(2,1)S(1)}, bf16[208,128]{1,0:T(8,128)(2,1)S(1)}, u32[]{:S(2)}, u32[]{:S(2)}) collective-permute-start(bf16[208,128]{1,0:T(8,128)(2,1)S(1)} %get-tuple-element.119), channel_id=1, source_target_pairs={{0,1},{1,0},{2,3},{3,2},{4,5},{5,4},{6,7},{7,6},{8,9},{9,8},{10,11... | collective-permute-start | bytes 159752 | tf_op jit(solution)/shard_map/ppermute | solution.py:269
  72.0 6.4 %collective-permute-start.21 = (bf16[208,128]{1,0:T(8,128)(2,1)S(1)}, bf16[208,128]{1,0:T(8,128)(2,1)S(1)}, u32[]{:S(2)}, u32[]{:S(2)}) collective-permute-start(bf16[208,128]{1,0:T(8,128)(2,1)S(1)} %get-tuple-element.118), channel_id=1, source_target_pairs={{0,3},{1,2},{2,1},{3,0},{4,7},{5,6},{6,5},{7,4},{8,11},{9,10},{10,... | collective-permute-start | bytes 159752 | tf_op jit(solution)/shard_map/ppermute | solution.py:269
  74.1 4.3 %collective-permute-start.20 = (bf16[144,128]{1,0:T(8,128)(2,1)S(1)}, bf16[144,128]{1,0:T(8,128)(2,1)S(1)}, u32[]{:S(2)}, u32[]{:S(2)}) collective-permute-start(bf16[144,128]{1,0:T(8,128)(2,1)S(1)} %add_convert_fusion), channel_id=1, source_target_pairs={{0,2},{1,3},{2,0},{3,1},{4,6},{5,7},{6,4},{7,5},{8,10},{9,11},{10,... | collective-permute-start | bytes 110600 | tf_op jit(solution)/shard_map/ppermute | solution.py:269
  78.5 7.2 %collective-permute-start.22 = (bf16[576,128]{1,0:T(8,128)(2,1)S(1)}, bf16[576,128]{1,0:T(8,128)(2,1)S(1)}, u32[]{:S(2)}, u32[]{:S(2)}) collective-permute-start(bf16[576,128]{1,0:T(8,128)(2,1)S(1)} %pad_maximum_fusion.1), channel_id=1, source_target_pairs={{0,8},{1,9},{2,10},{3,11},{4,12},{5,13},{6,14},{7,15},{8,0},{9,1},... | collective-permute-start | bytes 442376 | tf_op jit(solution)/shard_map/ppermute | solution.py:269

commit v7 on v6

--- a/solution.py
+++ b/solution.py
@@ -114,38 +114,54 @@
     agg_ref[...] = sum_ref[...].astype(BF)
 
 
+def contact_round(count, bound_t, far_t, w_t, self_ids, far_ids, both_ref, slope_ref, at):
+    slots = bound_t.shape[1]
+    place = lax.broadcasted_iota(jnp.int32, self_ids.shape, 1)
+    live = (place < count).astype(F32)
+    hits = table(slots, self_ids)
+    both_ref[:128, at] = nn(bound_t, hits).astype(BF)
+    both_ref[128:, at] = nn(far_t, table(slots, far_ids)).astype(BF)
+    message, slope = silu_parts(nn(w_t, both_ref[:, at]))
+    slope_ref[:, at] = slope * live
+    return nt(hits, (message * live).astype(BF))
+
+
+def contact_kernel(
+    counts_ref, bound_t_ref, far0_ref, far1_ref, far2_ref, w_ref, contacts_ref,
+    both_ref, slope_ref, sum_ref,
+):
+    fars = (far0_ref, far1_ref, far2_ref)
+    w_t = jnp.concatenate([transposed(w_ref[3]), transposed(w_ref[4])], axis=1)
+    round_rows = both_ref.shape[1] // len(fars)
+    for r, at in enumerate(spans(both_ref.shape[1], round_rows)):
+        part = contact_round(
+            counts_ref[0, r], bound_t_ref[...], fars[r][...], w_t,
+            contacts_ref[0:1, at], contacts_ref[1:2, at], both_ref, slope_ref, at,
+        )
+        sum_ref[...] = part + sum_ref[...] if r else part
+
+
 def main_kernel(
-    counts_ref, core_ref, lat_ref, lat_t_ref, bound_t_ref, far0_ref, far1_ref, far2_ref,
-    far3_ref, send_ref, recv_ref, slope_m_ref, agg_ref, feats_ref, cot_ref, w_ref, edges_ref,
+    counts_ref, core_ref, lat_ref, lat_t_ref, bound_t_ref, far3_ref, both_ref, slope_c_ref,
+    aggb_ref, send_ref, recv_ref, slope_m_ref, agg_ref, feats_ref, cot_ref, w_ref, edges_ref,
     contacts_ref, bnd_ref,
     new_ref, kept_ref, sent_ref, dm_ref, dc_ref, dn_ref,
-    aggb_ref, slope_c_ref, both_ref, gw_ref, aggc_ref, dagg_t_ref, daggc_t_ref,
+    slope_l_ref, both_l_ref, gw_ref, aggc_ref, dagg_t_ref, daggc_t_ref,
     *, scale,
 ):
     rows_dev = lat_ref.shape[0]
     bound_count = bnd_ref.shape[1]
-    fars = (far0_ref, far1_ref, far2_ref, far3_ref)
-    rounds = len(fars)
-    round_rows = contacts_ref.shape[1] // rounds
+    round_rows = both_l_ref.shape[1]
+    last = contacts_ref.shape[1] // round_rows - 1
     w_t = jnp.concatenate([transposed(w_ref[3]), transposed(w_ref[4])], axis=1)
-
-    for r, at in enumerate(spans(contacts_ref.shape[1], round_rows)):
-        place = lax.broadcasted_iota(jnp.int32, (1, round_rows), 1)
-        live = (place < counts_ref[0, r]).astype(F32)
-        hits = table(bound_count, contacts_ref[0:1, at])
-        both_ref[:128, at] = nn(bound_t_ref[...], hits).astype(BF)
-        both_ref[128:, at] = nn(
-            fars[r][...], table(bound_count, contacts_ref[1:2, at])
-        ).astype(BF)
-        message, slope = silu_parts(nn(w_t, both_ref[:, at]))
-        slope_c_ref[:, at] = slope * live
-        part = nt(hits, (message * live).astype(BF))
-        if r:
-            part = part + aggb_ref[...]
-        aggb_ref[...] = part
+    at = slice(last * round_rows, (last + 1) * round_rows)
+    aggb = aggb_ref[...] + contact_round(
+        counts_ref[0, last], bound_t_ref[...], far3_ref[...], w_t,
+        contacts_ref[0:1, at], contacts_ref[1:2, at], both_l_ref, slope_l_ref, slice(None),
+    )
 
     bound_table = table(rows_dev, bnd_ref[...])
-    aggc_ref[...] = nn(bound_table, aggb_ref[...].astype(BF)).astype(BF)
+    aggc_ref[...] = nn(bound_table, aggb.astype(BF)).astype(BF)
     for at in spans(rows_dev, NODE_SPAN):
         lat = lat_ref[at, :]
         cot = cot_ref[at, :]
@@ -179,9 +195,11 @@
     dbg_t = nn(daggc_t_ref[...], bound_table).astype(BF)
     for r, at in enumerate(spans(contacts_ref.shape[1], round_rows)):
         gathered = nn(dbg_t, table(bound_count, contacts_ref[0:1, at]))
-        d = (gathered * slope_c_ref[:, at]).astype(BF)
+        slope = slope_l_ref[...] if r == last else slope_c_ref[:, at]
+        both = both_l_ref[...] if r == last else both_ref[:, at]
+        d = (gathered * slope).astype(BF)
         dc_ref[:, at] = d
-        pair = nt(both_ref[:, at], d)
+        pair = nt(both, d)
         gw_ref[384:640, :] = pair + gw_ref[384:640, :] if r else pair
 
     half = gw_ref.shape[0] // 2
@@ -345,6 +363,16 @@
         flops=3 * 10**9,
         mib=16,
     )
+    first = (rounds - 1) * contact_count // rounds
+    both, slope_c, aggb = call(
+        contact_kernel,
+        [((2 * width, first), BF), ((width, first), F32), ((bound_count, width), F32)],
+        [contact_counts, bound_t, *fars[:3], weights, contact_edges],
+        smem=1,
+        flops=3 * 10**9,
+        mib=16,
+    )
+    fars[3], both = tie(fars[3], both)
     new_rows, kept, sent, d_mesh, d_contact, d_node = call(
         functools.partial(main_kernel, scale=scale),
         [
@@ -355,20 +383,20 @@
             ((width, contact_count), BF),
             ((rows_dev, width), BF),
         ],
-        [contact_counts, core.reshape(1), latents, lat_t, bound_t, *fars, send_rows, recv_rows, slope, agg]
+        [contact_counts, core.reshape(1), latents, lat_t, bound_t, fars[3], both, slope_c, aggb]
+        + [send_rows, recv_rows, slope, agg]
         + [edge_feats, cotangent, weights, mesh_edges, contact_edges, bnd],
         [
-            ((bound_count, width), F32),
-            ((width, contact_count), F32),
-            ((2 * width, contact_count), BF),
+            ((width, contact_count // rounds), F32),
+            ((2 * width, contact_count // rounds), BF),
             ((9 * width, width), F32),
             ((rows_dev, width), BF),
             ((width, rows_dev), BF),
             ((width, rows_dev), BF),
         ],
         smem=2,
-        flops=8 * 10**9,
-        mib=26,
+        flops=6 * 10**9,
+        mib=20,
     )
     other = exchanged(sent, mask_core=1)
     part, low, high = call(
@@ -446,8 +474,8 @@
         flops=10**8,
         mib=8,
     )
-    block = joined(block, other, core)
-    return (new_rows, grad_rows, wide(block).reshape(9, width, width))
+    block = joined(wide(block), wide(other), core)
+    return (new_rows, grad_rows, block.reshape(9, width, width))
 
 
 def solution(mesh):

time: 86.8 us -> 87.4 us (level)
  waiting for transfers between devices: 9.08 us -> 11.6 us
  starting transfers between devices: 45.7 us -> 43.3 us
    ppermute x21, waiting for transfers between devices: 9.08 us -> 11.6 us  [exchanged(): return lax.ppermute(block, ('region', 'panel'), route)]
    ppermute x21, starting transfers between devices: 41.3 us -> 38.8 us  [exchanged(): return lax.ppermute(block, ('region', 'panel'), route)]
    pallas_call x8 -> x9, Pallas kernels: 27.9 us -> 28.6 us  [call(): pl.pallas_call(kernel, out_shape=[jax.ShapeDtypeStruct(shape, kind) for s...]
  transfers between devices with their start and end apart: 23 -> 23, of which waited for: 5 -> 5; matrix products, arithmetic and copies ran while one was open for 0% -> 0% of each run, Pallas kernels for 18% -> 23%
where the time goes in v7:
time: 87.4 us; the launch traced here: 87.3 us
  starting transfers between devices  43.3 us (50%)
  Pallas kernels  28.6 us (33%)
  waiting for transfers between devices  11.6 us (13%)
  local copies, waits for them, and re-layouts  1.72 us (2%)
  other arithmetic  1.11 us (1%)
  between operations  1.05 us (1%)
    ppermute x21, starting transfers between devices, exchanged(): return lax.ppermute(block, ('region', 'panel'), route)  38.8 us
    pallas_call x9, Pallas kernels, call(): pl.pallas_call(kernel, out_shape=[jax.ShapeDtypeStruct(shape, kind) for s...  28.6 us
    ppermute x21, waiting for transfers between devices, exchanged(): return lax.ppermute(block, ('region', 'panel'), route)  11.6 us
    ppermute x2, starting transfers between devices, shifted(): return lax.ppermute(array, 'panel', pairs)  4.48 us
  transfers between devices with their start and end apart: 23, of which 5 were waited for; matrix products, arithmetic and copies ran while one was open for 0% of the time, Pallas kernels for 23%

profile of v7, /device:TPU:1, one launch (start us, length us, event | category | flops | bytes accessed | tf_op | source)
XLA Modules:
  0.0 87.3 jit_solution(11305059568382383124)
XLA Ops:
  0.6 0.0 copy-start
  0.6 0.7 copy-done
  1.3 0.9 %copy-done.4 = bf16[1024,128]{1,0:T(8,128)(2,1)S(1)} copy-done((bf16[1024,128]{1,0:T(8,128)(2,1)S(1)}, bf16[1024,128]{1,0:T(8,128)(2,1)}, u32[]{:S(2)}) %copy-start.4) | copy-done | bytes 262168
  2.3 0.4 shard_map.103
  2.7 3.3 %collective-permute-start.1 = (bf16[128,256]{1,0:T(8,128)(2,1)S(1)}, bf16[128,256]{1,0:T(8,128)(2,1)S(1)}, u32[]{:S(2)}, u32[]{:S(2)}) collective-permute-start(bf16[128,256]{1,0:T(8,128)(2,1)S(1)} %get-tuple-element.60.bound_t_ref), channel_id=1, source_target_pairs={{0,8},{1,9},{2,10},{3,11},{4,12},{5,13},{6,14},{7,15},{8,0},{9,1},... | collective-permute-start | bytes 196616 | tf_op jit(solution)/shard_map/ppermute | solution.py:287
  6.0 0.0 collective-permute-start.2
  6.0 2.9 %collective-permute-start.3 = (bf16[128,256]{1,0:T(8,128)(2,1)S(1)}, bf16[128,256]{1,0:T(8,128)(2,1)S(1)}, u32[]{:S(2)}, u32[]{:S(2)}) collective-permute-start(bf16[128,256]{1,0:T(8,128)(2,1)S(1)} %get-tuple-element.60.bound_t_ref), channel_id=1, source_target_pairs={{0,32},{1,33},{2,34},{3,35},{4,36},{5,37},{6,38},{7,39},{8,40},{9,... | collective-permute-start | bytes 196616 | tf_op jit(solution)/shard_map/ppermute | solution.py:287
  9.0 3.2 %collective-permute-start.4 = (bf16[64,128]{1,0:T(8,128)(2,1)S(1)}, bf16[64,128]{1,0:T(8,128)(2,1)S(1)}, u32[]{:S(2)}, u32[]{:S(2)}) collective-permute-start(bf16[64,128]{1,0:T(8,128)(2,1)S(1)} %get-tuple-element.66), channel_id=1, source_target_pairs={{0,1},{1,2},{2,3},{3,4},{4,5},{5,6},{6,7},{8,9},{9,10},{10,11},{11... | collective-permute-start | bytes 49160 | tf_op jit(solution)/shard_map/ppermute | solution.py:298
  12.2 1.3 %collective-permute-start.5 = (bf16[64,128]{1,0:T(8,128)(2,1)S(1)}, bf16[64,128]{1,0:T(8,128)(2,1)S(1)}, u32[]{:S(2)}, u32[]{:S(2)}) collective-permute-start(bf16[64,128]{1,0:T(8,128)(2,1)S(1)} %get-tuple-element.67), channel_id=1, source_target_pairs={{1,0},{2,1},{3,2},{4,3},{5,4},{6,5},{7,6},{9,8},{10,9},{11,10},{12... | collective-permute-start | bytes 49160 | tf_op jit(solution)/shard_map/ppermute | solution.py:298
  13.5 0.0 copy-start.2
  13.5 0.0 copy-start.3
  13.5 1.9 %shard_map.105 = (bf16[128,3072]{1,0:T(8,128)(2,1)S(1)}, bf16[128,3072]{1,0:T(8,128)(2,1)S(1)}) custom-call(bf16[128,1024]{1,0:T(8,128)(2,1)S(1)} %get-tuple-element.59.lat_t_ref, s32[2,3072]{1,0:T(2,128)S(1)} %copy-done.8), custom_call_target="tpu_custom_call" | custom-call | flops 4000000000 | bytes 4000000 | tf_op jit(solution)/shard_map/pallas_call | solution.py:269
  15.4 0.0 collective-permute-done.4.before_ref
  15.4 4.5 %collective-permute-start = (bf16[128,256]{1,0:T(8,128)(2,1)S(1)}, bf16[128,256]{1,0:T(8,128)(2,1)S(1)}, u32[]{:S(2)}, u32[]{:S(2)}) collective-permute-start(bf16[128,256]{1,0:T(8,128)(2,1)S(1)} %get-tuple-element.60.bound_t_ref), channel_id=1, source_target_pairs={{0,64},{1,65},{2,66},{3,67},{4,68},{5,69},{6,70},{7,71},{8,72},{9,... | collective-permute-start | bytes 196616 | tf_op jit(solution)/shard_map/ppermute | solution.py:287
  19.9 0.0 collective-permute-done.5.after_ref
  19.9 0.0 copy-start.7
  19.9 0.0 copy-start.9
  20.0 4.5 %shard_map.106 = (bf16[128,3072]{1,0:T(8,128)(2,1)S(1)}, f32[128,3072]{1,0:T(8,128)S(1)}, bf16[1024,128]{1,0:T(8,128)(2,1)S(1)}) custom-call(bf16[64,128]{1,0:T(8,128)(2,1)S(1)} %collective-permute-done.4.before_ref, bf16[64,128]{1,0:T(8,128)(2,1)S(1)} %collective-permute-done.5.after_ref, bf16[128,3072]{1,0:T(8,128)(2,1)S(1)} %get-tuple-element.71.own_ref, ...), custom_call_target="tpu_custom_call" | custom-call | flops 3000000000 | bytes 4000000 | tf_op jit(solution)/shard_map/pallas_call | solution.py:269
  24.5 0.0 copy-start.1
  24.5 0.0 copy-start.5
  24.5 0.0 copy-start.6
  24.5 0.0 collective-permute-done.1.far0_ref
  24.5 0.0 collective-permute-done.2.far1_ref
  24.5 0.0 collective-permute-done.3.far2_ref
  24.5 4.4 %shard_map.104 = (bf16[256,6144]{1,0:T(8,128)(2,1)S(1)}, f32[128,6144]{1,0:T(8,128)S(1)}, f32[256,128]{1,0:T(8,128)S(1)}) custom-call(s32[1,4]{1,0:T(1,128)S(1)} %copy-done.9, bf16[128,256]{1,0:T(8,128)(2,1)S(1)} %get-tuple-element.60.bound_t_ref, bf16[128,256]{1,0:T(8,128)(2,1)S(1)} %collective-permute-done.1.far0_ref, ...), custom_call_target="tpu_custom_call" | custom-call | flops 3000000000 | bytes 4000000 | tf_op jit(solution)/shard_map/pallas_call | solution.py:269
  28.9 0.0 collective-permute-done.far3_ref
  29.0 8.4 %shard_map.107 = (bf16[1024,128]{1,0:T(8,128)(2,1)}, f32[576,128]{1,0:T(8,128)S(1)}, bf16[576,128]{1,0:T(8,128)(2,1)S(1)}, bf16[128,3072]{1,0:T(8,128)(2,1)S(1)}...) custom-call(s32[1,4]{1,0:T(1,128)S(1)} %copy-done.9, s32[1]{0:T(128)} %bitcast.core_ref, ...), custom_call_target="tpu_custom_call" | custom-call | flops 6000000000 | bytes 4000000 | tf_op jit(solution)/shard_map/pallas_call | solution.py:269
  37.4 1.3 %collective-permute-start.6 = (bf16[576,128]{1,0:T(8,128)(2,1)S(1)}, bf16[576,128]{1,0:T(8,128)(2,1)S(1)}, u32[]{:S(2)}, u32[]{:S(2)}) collective-permute-start(bf16[576,128]{1,0:T(8,128)(2,1)S(1)} %get-tuple-element.78), channel_id=1, source_target_pairs={{0,8},{1,9},{2,10},{3,11},{4,12},{5,13},{6,14},{7,15},{8,0},{9,1},... | collective-permute-start | bytes 442376 | tf_op jit(solution)/shard_map/ppermute | solution.py:287
  38.7 2.6 %shard_map.108 = (f32[1024,128]{1,0:T(8,128)S(1)}, bf16[64,128]{1,0:T(8,128)(2,1)S(1)}, bf16[64,128]{1,0:T(8,128)(2,1)S(1)}) custom-call(bf16[9,128,128]{2,1,0:T(8,128)(2,1)S(1)} %copy-done.3, s32[2,3072]{1,0:T(2,128)S(1)} %copy-done.8, bf16[128,3072]{1,0:T(8,128)(2,1)S(1)} %get-tuple-element.79.dm_ref), custom_call_target="tpu_custom_call" | custom-call | flops 2000000000 | bytes 4000000 | tf_op jit(solution)/shard_map/pallas_call | solution.py:269
  41.3 0.0 collective-permute-done.6
  41.4 2.5 %collective-permute-start.7 = (bf16[144,128]{1,0:T(8,128)(2,1)S(1)}, bf16[144,128]{1,0:T(8,128)(2,1)S(1)}, u32[]{:S(2)}, u32[]{:S(2)}) collective-permute-start(bf16[144,128]{1,0:T(8,128)(2,1)S(1)} %get-tuple-element.119), channel_id=1, source_target_pairs={{0,1},{1,0},{2,3},{3,2},{4,5},{5,4},{6,7},{7,6},{8,9},{9,8},{10,11... | collective-permute-start | bytes 110600 | tf_op jit(solution)/shard_map/ppermute | solution.py:287
  43.8 2.6 %collective-permute-start.8 = (bf16[144,128]{1,0:T(8,128)(2,1)S(1)}, bf16[144,128]{1,0:T(8,128)(2,1)S(1)}, u32[]{:S(2)}, u32[]{:S(2)}) collective-permute-start(bf16[144,128]{1,0:T(8,128)(2,1)S(1)} %get-tuple-element.118), channel_id=1, source_target_pairs={{0,2},{1,3},{2,0},{3,1},{4,6},{5,7},{6,4},{7,5},{8,10},{9,11},{10,... | collective-permute-start | bytes 110600 | tf_op jit(solution)/shard_map/ppermute | solution.py:287
  46.5 0.0 collective-permute-start.9
  46.5 2.8 %shard_map.109 = (bf16[256,128]{1,0:T(8,128)(2,1)S(1)}, bf16[256,128]{1,0:T(8,128)(2,1)S(1)}, bf16[256,128]{1,0:T(8,128)(2,1)S(1)}, bf16[256,128]{1,0:T(8,128)(2,1)S(1)}, f32[256,128]{1,0:T(8,128)S(1)}) custom-call(bf16[9,128,128]{2,1,0:T(8,128)(2,1)S(1)} %copy-done.3, s32[2,8192]{1,0:T(2,128)S(1)} %copy-done.7, bf16[128,8192]{1,0:T(8,128)(2,1)S(1)} %get-tuple-element.85.dc_ref), custom_call_target="tpu_custom_call" | custom-call | flops 2000000000 | bytes 4000000 | tf_op jit(solution)/shard_map/pallas_call | solution.py:269
  49.3 0.0 collective-permute-done.7
  49.3 0.0 collective-permute-done.8
  49.3 1.2 %collective-permute-done.9 = bf16[144,128]{1,0:T(8,128)(2,1)S(1)} collective-permute-done((bf16[144,128]{1,0:T(8,128)(2,1)S(1)}, bf16[144,128]{1,0:T(8,128)(2,1)S(1)}, u32[]{:S(2)}, u32[]{:S(2)}) %collective-permute-start.9) | collective-permute-done | bytes 36896 | tf_op jit(solution)/shard_map/ppermute | solution.py:287
  50.5 2.8 %collective-permute-start.11 = (bf16[144,128]{1,0:T(8,128)(2,1)S(1)}, bf16[144,128]{1,0:T(8,128)(2,1)S(1)}, u32[]{:S(2)}, u32[]{:S(2)}) collective-permute-start(bf16[144,128]{1,0:T(8,128)(2,1)S(1)} %add_convert_fusion.4), channel_id=1, source_target_pairs={{0,128},{1,129},{2,130},{3,131},{4,132},{5,133},{6,134},{7,135},{8... | collective-permute-start | bytes 110600 | tf_op jit(solution)/shard_map/ppermute | solution.py:287
  53.3 1.8 %collective-permute-start.12 = (bf16[144,128]{1,0:T(8,128)(2,1)S(1)}, bf16[144,128]{1,0:T(8,128)(2,1)S(1)}, u32[]{:S(2)}, u32[]{:S(2)}) collective-permute-start(bf16[144,128]{1,0:T(8,128)(2,1)S(1)} %add_convert_fusion.4), channel_id=1, source_target_pairs={{0,132},{1,133},{2,134},{3,135},{4,128},{5,129},{6,130},{7,131},{8... | collective-permute-start | bytes 110600 | tf_op jit(solution)/shard_map/ppermute | solution.py:287
  55.1 0.0 collective-permute-start.10
  55.1 1.3 %collective-permute-start.17 = (bf16[512,128]{1,0:T(8,128)(2,1)S(1)}, bf16[512,128]{1,0:T(8,128)(2,1)S(1)}, u32[]{:S(2)}, u32[]{:S(2)}) collective-permute-start(bf16[512,128]{1,0:T(8,128)(2,1)S(1)} %pad_maximum_fusion.2), channel_id=1, source_target_pairs={{0,32},{1,33},{2,34},{3,35},{4,36},{5,37},{6,38},{7,39},{8,40},{9,... | collective-permute-start | bytes 393224 | tf_op jit(solution)/shard_map/ppermute | solution.py:287
  56.4 0.7 collective-permute-start.14
  57.1 0.0 collective-permute-done.11
  57.1 2.0 %collective-permute-start.16 = (bf16[256,128]{1,0:T(8,128)(2,1)S(1)}, bf16[256,128]{1,0:T(8,128)(2,1)S(1)}, u32[]{:S(2)}, u32[]{:S(2)}) collective-permute-start(bf16[256,128]{1,0:T(8,128)(2,1)S(1)} %get-tuple-element.105), channel_id=1, source_target_pairs={{0,8},{1,9},{2,10},{3,11},{4,12},{5,13},{6,14},{7,15},{8,0},{9,1},... | collective-permute-start | bytes 196616 | tf_op jit(solution)/shard_map/ppermute | solution.py:287
  59.1 0.0 collective-permute-done.12
  59.1 1.1 %collective-permute-start.13 = (bf16[144,128]{1,0:T(8,128)(2,1)S(1)}, bf16[144,128]{1,0:T(8,128)(2,1)S(1)}, u32[]{:S(2)}, u32[]{:S(2)}) collective-permute-start(bf16[144,128]{1,0:T(8,128)(2,1)S(1)} %add_convert_fusion.3), channel_id=1, source_target_pairs={{0,16},{1,17},{2,18},{3,19},{4,20},{5,21},{6,22},{7,23},{8,24},{9,... | collective-permute-start | bytes 110600 | tf_op jit(solution)/shard_map/ppermute | solution.py:287
  60.2 2.3 %shard_map.110.part_ref = f32[1024,128]{1,0:T(8,128)S(1)} custom-call(bf16[9,128,128]{2,1,0:T(8,128)(2,1)S(1)} %copy-done.3, s32[2,3072]{1,0:T(2,128)S(1)} %copy-done.8, bf16[128,3072]{1,0:T(8,128)(2,1)S(1)} %get-tuple-element.79.dm_ref, bf16[1024,128]{1,0:T(8,128)(2,1)S(1)} %get-tuple-element.99.dn_ref, bf16[1024,128]{1,0:T(8,128)(2,1)S(1)} %copy-done.6, ...), custom_call_target="tpu_custom_call" | custom-call | flops 2000000000 | bytes 4000000 | tf_op jit(solution)/shard_map/pallas_call | solution.py:269
  62.5 0.0 collective-permute-done.14.in1_ref
  62.5 0.1 collective-permute-done.13
  62.6 1.7 %collective-permute-start.15 = (bf16[144,128]{1,0:T(8,128)(2,1)S(1)}, bf16[144,128]{1,0:T(8,128)(2,1)S(1)}, u32[]{:S(2)}, u32[]{:S(2)}) collective-permute-start(bf16[144,128]{1,0:T(8,128)(2,1)S(1)} %add_convert_fusion.2), channel_id=1, source_target_pairs={{0,32},{1,33},{2,34},{3,35},{4,36},{5,37},{6,38},{7,39},{8,40},{9,... | collective-permute-start | bytes 110600 | tf_op jit(solution)/shard_map/ppermute | solution.py:287
  64.3 0.0 collective-permute-done.16.in0_ref
  64.3 2.1 %collective-permute-done.15 = bf16[144,128]{1,0:T(8,128)(2,1)S(1)} collective-permute-done((bf16[144,128]{1,0:T(8,128)(2,1)S(1)}, bf16[144,128]{1,0:T(8,128)(2,1)S(1)}, u32[]{:S(2)}, u32[]{:S(2)}) %collective-permute-start.15) | collective-permute-done | bytes 36896 | tf_op jit(solution)/shard_map/ppermute | solution.py:287
  66.4 0.0 collective-permute-done.17
  66.4 0.8 collective-permute-start.18
  67.3 5.0 %collective-permute-done.18 = bf16[400,128]{1,0:T(8,128)(2,1)S(1)} collective-permute-done((bf16[400,128]{1,0:T(8,128)(2,1)S(1)}, bf16[400,128]{1,0:T(8,128)(2,1)S(1)}, u32[]{:S(2)}, u32[]{:S(2)}) %collective-permute-start.18) | collective-permute-done | bytes 102432 | tf_op jit(solution)/shard_map/ppermute | solution.py:287
  72.3 0.1 collective-permute-start.19
  72.4 2.1 %collective-permute-start.21 = (bf16[208,128]{1,0:T(8,128)(2,1)S(1)}, bf16[208,128]{1,0:T(8,128)(2,1)S(1)}, u32[]{:S(2)}, u32[]{:S(2)}) collective-permute-start(bf16[208,128]{1,0:T(8,128)(2,1)S(1)} %get-tuple-element.128), channel_id=1, source_target_pairs={{0,3},{1,2},{2,1},{3,0},{4,7},{5,6},{6,5},{7,4},{8,11},{9,10},{10,... | collective-permute-start | bytes 159752 | tf_op jit(solution)/shard_map/ppermute | solution.py:287
  74.5 1.1 %collective-permute-start.20 = (bf16[144,128]{1,0:T(8,128)(2,1)S(1)}, bf16[144,128]{1,0:T(8,128)(2,1)S(1)}, u32[]{:S(2)}, u32[]{:S(2)}) collective-permute-start(bf16[144,128]{1,0:T(8,128)(2,1)S(1)} %add_convert_fusion), channel_id=1, source_target_pairs={{0,2},{1,3},{2,0},{3,1},{4,6},{5,7},{6,4},{7,5},{8,10},{9,11},{10,... | collective-permute-start | bytes 110600 | tf_op jit(solution)/shard_map/ppermute | solution.py:287
  75.6 3.2 %collective-permute-done.20 = bf16[144,128]{1,0:T(8,128)(2,1)S(1)} collective-permute-done((bf16[144,128]{1,0:T(8,128)(2,1)S(1)}, bf16[144,128]{1,0:T(8,128)(2,1)S(1)}, u32[]{:S(2)}, u32[]{:S(2)}) %collective-permute-start.20) | collective-permute-done | bytes 36896 | tf_op jit(solution)/shard_map/ppermute | solution.py:287
  78.8 0.0 collective-permute-done.19
  78.8 0.0 collective-permute-done.21
  78.9 6.2 %collective-permute-start.22 = (bf16[576,128]{1,0:T(8,128)(2,1)S(1)}, bf16[576,128]{1,0:T(8,128)(2,1)S(1)}, u32[]{:S(2)}, u32[]{:S(2)}) collective-permute-start(bf16[576,128]{1,0:T(8,128)(2,1)S(1)} %pad_maximum_fusion.1), channel_id=1, source_target_pairs={{0,8},{1,9},{2,10},{3,11},{4,12},{5,13},{6,14},{7,15},{8,0},{9,1},... | collective-permute-start | bytes 442376 | tf_op jit(solution)/shard_map/ppermute | solution.py:287
  85.1 1.3 %shard_map.111 = f32[1024,128]{1,0:T(8,128)} custom-call(f32[1024,128]{1,0:T(8,128)S(1)} %shard_map.110.part_ref, f32[256,128]{1,0:T(8,128)S(1)} %get-tuple-element.103.own_ref, bf16[256,128]{1,0:T(8,128)(2,1)S(1)} %collective-permute-done.16.in0_ref, bf16[256,128]{1,0:T(8,128)(2,1)S(1)} %collective-permute-done.14.in1_ref, ...), custom_call_target="tpu_custom_call" | custom-call | flops 100000000 | bytes 4000000 | tf_op jit(solution)/shard_map/pallas_call | solution.py:269
  86.4 0.9 pad_maximum_fusion
  (31 shorter events, 0.3 us)
Async XLA Ops:
  0.6 0.7 copy-start
  1.3 0.9 %copy-start.4 = (bf16[1024,128]{1,0:T(8,128)(2,1)S(1)}, bf16[1024,128]{1,0:T(8,128)(2,1)}, u32[]{:S(2)}) copy-start(bf16[1024,128]{1,0:T(8,128)(2,1)} %lat_ref.1) | copy-start | bytes 786436
  2.3 11.2 %copy-start.8 = (s32[2,3072]{1,0:T(2,128)S(1)}, s32[2,3072]{1,0:T(2,128)}, u32[]{:S(2)}) copy-start(s32[2,3072]{1,0:T(2,128)} %edges_ref.9) | copy-start | bytes 73732
  2.7 21.8 %collective-permute-start.1 = (bf16[128,256]{1,0:T(8,128)(2,1)S(1)}, bf16[128,256]{1,0:T(8,128)(2,1)S(1)}, u32[]{:S(2)}, u32[]{:S(2)}) collective-permute-start(bf16[128,256]{1,0:T(8,128)(2,1)S(1)} %get-tuple-element.60.bound_t_ref), channel_id=1, source_target_pairs={{0,8},{1,9},{2,10},{3,11},{4,12},{5,13},{6,14},{7,15},{8,0},{9,1},... | collective-permute-start | bytes 196616 | tf_op jit(solution)/shard_map/ppermute | solution.py:287
  6.0 18.5 %collective-permute-start.2 = (bf16[128,256]{1,0:T(8,128)(2,1)S(1)}, bf16[128,256]{1,0:T(8,128)(2,1)S(1)}, u32[]{:S(2)}, u32[]{:S(2)}) collective-permute-start(bf16[128,256]{1,0:T(8,128)(2,1)S(1)} %get-tuple-element.60.bound_t_ref), channel_id=1, source_target_pairs={{0,16},{1,17},{2,18},{3,19},{4,20},{5,21},{6,22},{7,23},{8,24},{9,... | collective-permute-start | bytes 196616 | tf_op jit(solution)/shard_map/ppermute | solution.py:287
  6.0 18.5 %collective-permute-start.3 = (bf16[128,256]{1,0:T(8,128)(2,1)S(1)}, bf16[128,256]{1,0:T(8,128)(2,1)S(1)}, u32[]{:S(2)}, u32[]{:S(2)}) collective-permute-start(bf16[128,256]{1,0:T(8,128)(2,1)S(1)} %get-tuple-element.60.bound_t_ref), channel_id=1, source_target_pairs={{0,32},{1,33},{2,34},{3,35},{4,36},{5,37},{6,38},{7,39},{8,40},{9,... | collective-permute-start | bytes 196616 | tf_op jit(solution)/shard_map/ppermute | solution.py:287
  9.0 6.5 %collective-permute-start.4 = (bf16[64,128]{1,0:T(8,128)(2,1)S(1)}, bf16[64,128]{1,0:T(8,128)(2,1)S(1)}, u32[]{:S(2)}, u32[]{:S(2)}) collective-permute-start(bf16[64,128]{1,0:T(8,128)(2,1)S(1)} %get-tuple-element.66), channel_id=1, source_target_pairs={{0,1},{1,2},{2,3},{3,4},{4,5},{5,6},{6,7},{8,9},{9,10},{10,11},{11... | collective-permute-start | bytes 49160 | tf_op jit(solution)/shard_map/ppermute | solution.py:298
  12.2 7.8 %collective-permute-start.5 = (bf16[64,128]{1,0:T(8,128)(2,1)S(1)}, bf16[64,128]{1,0:T(8,128)(2,1)S(1)}, u32[]{:S(2)}, u32[]{:S(2)}) collective-permute-start(bf16[64,128]{1,0:T(8,128)(2,1)S(1)} %get-tuple-element.67), channel_id=1, source_target_pairs={{1,0},{2,1},{3,2},{4,3},{5,4},{6,5},{7,6},{9,8},{10,9},{11,10},{12... | collective-permute-start | bytes 49160 | tf_op jit(solution)/shard_map/ppermute | solution.py:298
  13.5 6.5 %copy-start.2 = (bf16[3072,128]{1,0:T(8,128)(2,1)S(1)}, bf16[3072,128]{1,0:T(8,128)(2,1)}, u32[]{:S(2)}) copy-start(bf16[3072,128]{1,0:T(8,128)(2,1)} %feats_ref.3) | copy-start | bytes 2359300
  13.5 6.5 %copy-start.3 = (bf16[9,128,128]{2,1,0:T(8,128)(2,1)S(1)}, bf16[9,128,128]{2,1,0:T(8,128)(2,1)}, u32[]{:S(2)}) copy-start(bf16[9,128,128]{2,1,0:T(8,128)(2,1)} %w_ref.11) | copy-start | bytes 884740
  15.4 13.5 %collective-permute-start = (bf16[128,256]{1,0:T(8,128)(2,1)S(1)}, bf16[128,256]{1,0:T(8,128)(2,1)S(1)}, u32[]{:S(2)}, u32[]{:S(2)}) collective-permute-start(bf16[128,256]{1,0:T(8,128)(2,1)S(1)} %get-tuple-element.60.bound_t_ref), channel_id=1, source_target_pairs={{0,64},{1,65},{2,66},{3,67},{4,68},{5,69},{6,70},{7,71},{8,72},{9,... | collective-permute-start | bytes 196616 | tf_op jit(solution)/shard_map/ppermute | solution.py:287
  19.9 4.6 %copy-start.7 = (s32[2,8192]{1,0:T(2,128)S(1)}, s32[2,8192]{1,0:T(2,128)}, u32[]{:S(2)}) copy-start(s32[2,8192]{1,0:T(2,128)} %contacts_ref.5) | copy-start | bytes 196612
  19.9 4.6 %copy-start.9 = (s32[1,4]{1,0:T(1,128)S(1)}, s32[1,4]{1,0:T(1,128)}, u32[]{:S(2)}) copy-start(s32[1,4]{1,0:T(1,128)} %counts_ref.3) | copy-start | bytes 52
  24.5 4.5 %copy-start.1 = (s32[256]{0:T(256)S(1)}, s32[256]{0:T(256)}, u32[]{:S(2)}) copy-start(s32[256]{0:T(256)} %param.13) | copy-start | bytes 3076
  24.5 4.5 %copy-start.5 = (bf16[1024,128]{1,0:T(8,128)(2,1)S(1)}, bf16[1024,128]{1,0:T(8,128)(2,1)}, u32[]{:S(2)}) copy-start(bf16[1024,128]{1,0:T(8,128)(2,1)} %lat_ref.1) | copy-start | bytes 786436
  24.5 4.5 %copy-start.6 = (bf16[1024,128]{1,0:T(8,128)(2,1)S(1)}, bf16[1024,128]{1,0:T(8,128)(2,1)}, u32[]{:S(2)}) copy-start(bf16[1024,128]{1,0:T(8,128)(2,1)} %cot_ref.3) | copy-start | bytes 786436
  37.4 3.9 %collective-permute-start.6 = (bf16[576,128]{1,0:T(8,128)(2,1)S(1)}, bf16[576,128]{1,0:T(8,128)(2,1)S(1)}, u32[]{:S(2)}, u32[]{:S(2)}) collective-permute-start(bf16[576,128]{1,0:T(8,128)(2,1)S(1)} %get-tuple-element.78), channel_id=1, source_target_pairs={{0,8},{1,9},{2,10},{3,11},{4,12},{5,13},{6,14},{7,15},{8,0},{9,1},... | collective-permute-start | bytes 442376 | tf_op jit(solution)/shard_map/ppermute | solution.py:287
  41.4 7.9 %collective-permute-start.7 = (bf16[144,128]{1,0:T(8,128)(2,1)S(1)}, bf16[144,128]{1,0:T(8,128)(2,1)S(1)}, u32[]{:S(2)}, u32[]{:S(2)}) collective-permute-start(bf16[144,128]{1,0:T(8,128)(2,1)S(1)} %get-tuple-element.119), channel_id=1, source_target_pairs={{0,1},{1,0},{2,3},{3,2},{4,5},{5,4},{6,7},{7,6},{8,9},{9,8},{10,11... | collective-permute-start | bytes 110600 | tf_op jit(solution)/shard_map/ppermute | solution.py:287
  43.8 5.5 %collective-permute-start.8 = (bf16[144,128]{1,0:T(8,128)(2,1)S(1)}, bf16[144,128]{1,0:T(8,128)(2,1)S(1)}, u32[]{:S(2)}, u32[]{:S(2)}) collective-permute-start(bf16[144,128]{1,0:T(8,128)(2,1)S(1)} %get-tuple-element.118), channel_id=1, source_target_pairs={{0,2},{1,3},{2,0},{3,1},{4,6},{5,7},{6,4},{7,5},{8,10},{9,11},{10,... | collective-permute-start | bytes 110600 | tf_op jit(solution)/shard_map/ppermute | solution.py:287
  46.5 4.0 %collective-permute-start.9 = (bf16[144,128]{1,0:T(8,128)(2,1)S(1)}, bf16[144,128]{1,0:T(8,128)(2,1)S(1)}, u32[]{:S(2)}, u32[]{:S(2)}) collective-permute-start(bf16[144,128]{1,0:T(8,128)(2,1)S(1)} %get-tuple-element.117), channel_id=1, source_target_pairs={{0,3},{1,2},{2,1},{3,0},{4,7},{5,6},{6,5},{7,4},{8,11},{9,10},{10,... | collective-permute-start | bytes 110600 | tf_op jit(solution)/shard_map/ppermute | solution.py:287
  50.5 6.6 %collective-permute-start.11 = (bf16[144,128]{1,0:T(8,128)(2,1)S(1)}, bf16[144,128]{1,0:T(8,128)(2,1)S(1)}, u32[]{:S(2)}, u32[]{:S(2)}) collective-permute-start(bf16[144,128]{1,0:T(8,128)(2,1)S(1)} %add_convert_fusion.4), channel_id=1, source_target_pairs={{0,128},{1,129},{2,130},{3,131},{4,132},{5,133},{6,134},{7,135},{8... | collective-permute-start | bytes 110600 | tf_op jit(solution)/shard_map/ppermute | solution.py:287
  53.3 5.7 %collective-permute-start.12 = (bf16[144,128]{1,0:T(8,128)(2,1)S(1)}, bf16[144,128]{1,0:T(8,128)(2,1)S(1)}, u32[]{:S(2)}, u32[]{:S(2)}) collective-permute-start(bf16[144,128]{1,0:T(8,128)(2,1)S(1)} %add_convert_fusion.4), channel_id=1, source_target_pairs={{0,132},{1,133},{2,134},{3,135},{4,128},{5,129},{6,130},{7,131},{8... | collective-permute-start | bytes 110600 | tf_op jit(solution)/shard_map/ppermute | solution.py:287
  55.1 4.0 %collective-permute-start.10 = (bf16[208,128]{1,0:T(8,128)(2,1)S(1)}, bf16[208,128]{1,0:T(8,128)(2,1)S(1)}, u32[]{:S(2)}, u32[]{:S(2)}) collective-permute-start(bf16[208,128]{1,0:T(8,128)(2,1)S(1)} %pad_maximum_fusion.6), channel_id=1, source_target_pairs={{0,4},{1,5},{2,6},{3,7},{4,0},{5,1},{6,2},{7,3},{8,12},{9,13},{10,... | collective-permute-start | bytes 159752 | tf_op jit(solution)/shard_map/ppermute | solution.py:287
  55.1 11.3 %collective-permute-start.17 = (bf16[512,128]{1,0:T(8,128)(2,1)S(1)}, bf16[512,128]{1,0:T(8,128)(2,1)S(1)}, u32[]{:S(2)}, u32[]{:S(2)}) collective-permute-start(bf16[512,128]{1,0:T(8,128)(2,1)S(1)} %pad_maximum_fusion.2), channel_id=1, source_target_pairs={{0,32},{1,33},{2,34},{3,35},{4,36},{5,37},{6,38},{7,39},{8,40},{9,... | collective-permute-start | bytes 393224 | tf_op jit(solution)/shard_map/ppermute | solution.py:287
  56.4 6.1 %collective-permute-start.14 = (bf16[256,128]{1,0:T(8,128)(2,1)S(1)}, bf16[256,128]{1,0:T(8,128)(2,1)S(1)}, u32[]{:S(2)}, u32[]{:S(2)}) collective-permute-start(bf16[256,128]{1,0:T(8,128)(2,1)S(1)} %get-tuple-element.101), channel_id=1, source_target_pairs={{0,16},{1,17},{2,18},{3,19},{4,20},{5,21},{6,22},{7,23},{8,24},{9,... | collective-permute-start | bytes 196616 | tf_op jit(solution)/shard_map/ppermute | solution.py:287
  57.1 7.2 %collective-permute-start.16 = (bf16[256,128]{1,0:T(8,128)(2,1)S(1)}, bf16[256,128]{1,0:T(8,128)(2,1)S(1)}, u32[]{:S(2)}, u32[]{:S(2)}) collective-permute-start(bf16[256,128]{1,0:T(8,128)(2,1)S(1)} %get-tuple-element.105), channel_id=1, source_target_pairs={{0,8},{1,9},{2,10},{3,11},{4,12},{5,13},{6,14},{7,15},{8,0},{9,1},... | collective-permute-start | bytes 196616 | tf_op jit(solution)/shard_map/ppermute | solution.py:287
  59.1 3.5 %collective-permute-start.13 = (bf16[144,128]{1,0:T(8,128)(2,1)S(1)}, bf16[144,128]{1,0:T(8,128)(2,1)S(1)}, u32[]{:S(2)}, u32[]{:S(2)}) collective-permute-start(bf16[144,128]{1,0:T(8,128)(2,1)S(1)} %add_convert_fusion.3), channel_id=1, source_target_pairs={{0,16},{1,17},{2,18},{3,19},{4,20},{5,21},{6,22},{7,23},{8,24},{9,... | collective-permute-start | bytes 110600 | tf_op jit(solution)/shard_map/ppermute | solution.py:287
  62.6 3.8 %collective-permute-start.15 = (bf16[144,128]{1,0:T(8,128)(2,1)S(1)}, bf16[144,128]{1,0:T(8,128)(2,1)S(1)}, u32[]{:S(2)}, u32[]{:S(2)}) collective-permute-start(bf16[144,128]{1,0:T(8,128)(2,1)S(1)} %add_convert_fusion.2), channel_id=1, source_target_pairs={{0,32},{1,33},{2,34},{3,35},{4,36},{5,37},{6,38},{7,39},{8,40},{9,... | collective-permute-start | bytes 110600 | tf_op jit(solution)/shard_map/ppermute | solution.py:287
  66.4 5.8 %collective-permute-start.18 = (bf16[400,128]{1,0:T(8,128)(2,1)S(1)}, bf16[400,128]{1,0:T(8,128)(2,1)S(1)}, u32[]{:S(2)}, u32[]{:S(2)}) collective-permute-start(bf16[400,128]{1,0:T(8,128)(2,1)S(1)} %pad_maximum_fusion.3), channel_id=1, source_target_pairs={{0,96},{1,97},{2,98},{3,99},{4,100},{5,101},{6,102},{7,103},{8,104... | collective-permute-start | bytes 307208 | tf_op jit(solution)/shard_map/ppermute | solution.py:287
  72.3 6.5 %collective-permute-start.19 = (bf16[208,128]{1,0:T(8,128)(2,1)S(1)}, bf16[208,128]{1,0:T(8,128)(2,1)S(1)}, u32[]{:S(2)}, u32[]{:S(2)}) collective-permute-start(bf16[208,128]{1,0:T(8,128)(2,1)S(1)} %get-tuple-element.129), channel_id=1, source_target_pairs={{0,1},{1,0},{2,3},{3,2},{4,5},{5,4},{6,7},{7,6},{8,9},{9,8},{10,11... | collective-permute-start | bytes 159752 | tf_op jit(solution)/shard_map/ppermute | solution.py:287
  72.4 6.4 %collective-permute-start.21 = (bf16[208,128]{1,0:T(8,128)(2,1)S(1)}, bf16[208,128]{1,0:T(8,128)(2,1)S(1)}, u32[]{:S(2)}, u32[]{:S(2)}) collective-permute-start(bf16[208,128]{1,0:T(8,128)(2,1)S(1)} %get-tuple-element.128), channel_id=1, source_target_pairs={{0,3},{1,2},{2,1},{3,0},{4,7},{5,6},{6,5},{7,4},{8,11},{9,10},{10,... | collective-permute-start | bytes 159752 | tf_op jit(solution)/shard_map/ppermute | solution.py:287
  74.5 4.3 %collective-permute-start.20 = (bf16[144,128]{1,0:T(8,128)(2,1)S(1)}, bf16[144,128]{1,0:T(8,128)(2,1)S(1)}, u32[]{:S(2)}, u32[]{:S(2)}) collective-permute-start(bf16[144,128]{1,0:T(8,128)(2,1)S(1)} %add_convert_fusion), channel_id=1, source_target_pairs={{0,2},{1,3},{2,0},{3,1},{4,6},{5,7},{6,4},{7,5},{8,10},{9,11},{10,... | collective-permute-start | bytes 110600 | tf_op jit(solution)/shard_map/ppermute | solution.py:287
  78.9 7.5 %collective-permute-start.22 = (bf16[576,128]{1,0:T(8,128)(2,1)S(1)}, bf16[576,128]{1,0:T(8,128)(2,1)S(1)}, u32[]{:S(2)}, u32[]{:S(2)}) collective-permute-start(bf16[576,128]{1,0:T(8,128)(2,1)S(1)} %pad_maximum_fusion.1), channel_id=1, source_target_pairs={{0,8},{1,9},{2,10},{3,11},{4,12},{5,13},{6,14},{7,15},{8,0},{9,1},... | collective-permute-start | bytes 442376 | tf_op jit(solution)/shard_map/ppermute | solution.py:287

commit v8 on v7

--- a/solution.py
+++ b/solution.py
@@ -399,6 +399,26 @@
         mib=20,
     )
     other = exchanged(sent, mask_core=1)
+    *far_grads, own_grad = call(
+        contact_back_kernel,
+        [((bound_count, width), BF)] * rounds + [((bound_count, width), F32)],
+        [weights, contact_edges, d_contact],
+        flops=2 * 10**9,
+        mib=16,
+    )
+    other, *far_grads = tie(other, *far_grads)
+    block = kept + wide(other)
+    size = block.shape[0] // 4
+    pieces = [
+        lax.dynamic_slice_in_dim(block, (row_y ^ mask) * size, size, 0) for mask in range(4)
+    ]
+    found = [exchanged(pieces[mask].astype(BF), mask_y=mask) for mask in (1, 2, 3)]
+    pair = exchanged(jnp.concatenate(far_grads[2:], axis=0), mask_z=2)
+    in_one = exchanged(far_grads[1], mask_z=1)
+    one, two, three, d_mesh = tie(*found, d_mesh)
+    block = ((pieces[0] + wide(one)) + (wide(two) + wide(three))).astype(BF)
+
+    other = exchanged(block, mask_z=1)
     part, low, high = call(
         send_back_kernel,
         [((rows_dev, width), F32), ((HB, width), BF), ((HB, width), BF)],
@@ -407,33 +427,9 @@
         flops=2 * 10**9,
         mib=16,
     )
-    other, part, low, high, d_contact = tie(other, part, low, high, d_contact)
-    block = kept + wide(other)
-    size = block.shape[0] // 4
-    pieces = [
-        lax.dynamic_slice_in_dim(block, (row_y ^ mask) * size, size, 0) for mask in range(4)
-    ]
-    found = [exchanged(pieces[mask].astype(BF), mask_y=mask) for mask in (1, 2, 3)]
-    *far_grads, own_grad = call(
-        contact_back_kernel,
-        [((bound_count, width), BF)] * rounds + [((bound_count, width), F32)],
-        [weights, contact_edges, d_contact],
-        flops=2 * 10**9,
-        mib=16,
-    )
-    one, two, three, *far_grads = tie(*found, *far_grads)
-    block = ((pieces[0] + wide(one)) + (wide(two) + wide(three))).astype(BF)
-
-    rim = jnp.where(row_y == 0, low, high)
-    one = exchanged(jnp.concatenate([block, rim], axis=0), mask_x=1)
-    two, three = [exchanged(block, mask_x=mask) for mask in (2, 3)]
-    in_one = exchanged(far_grads[1], mask_z=1)
-    pair = exchanged(jnp.concatenate(far_grads[2:], axis=0), mask_z=2)
-    one, two, three, part = tie(one, two, three, part)
-    rim = one[size:]
-    block = ((wide(block) + wide(one[:size])) + (wide(two) + wide(three))).astype(BF)
-
-    other = exchanged(block, mask_z=1)
+    other, part, low, high, in_one = tie(other, part, low, high, in_one)
+    block = (wide(block) + wide(other)).astype(BF)
+    other = exchanged(block, mask_z=2)
     (part,) = call(
         recv_back_kernel,
         [((rows_dev, width), F32)],
@@ -442,16 +438,21 @@
         flops=2 * 10**9,
         mib=16,
     )
-    other, part, in_one = tie(other, part, in_one)
+    other, part, pair = tie(other, part, pair)
     block = (wide(block) + wide(other)).astype(BF)
-    other = exchanged(block, mask_z=2)
+    other = exchanged(block, mask_z=6)
+    in_two = pair[:bound_count]
+    in_three = exchanged(pair[bound_count:], mask_z=6)
     in_zero = exchanged(far_grads[0], mask_core=1)
-    other, in_zero, pair = tie(other, in_zero, pair)
+    other, in_zero = tie(other, in_zero)
     block = (wide(block) + wide(other)).astype(BF)
-    in_two = pair[:bound_count]
-    other = exchanged(jnp.concatenate([block, pair[bound_count:]], axis=0), mask_z=6)
-    in_three = other[size:]
-    block = (wide(block) + wide(other[:size])).astype(BF)
+
+    rim = jnp.where(row_y == 0, low, high)
+    one = exchanged(jnp.concatenate([block, rim], axis=0), mask_x=1)
+    two, three = [exchanged(block, mask_x=mask) for mask in (2, 3)]
+    one, two, three, in_three = tie(one, two, three, in_three)
+    rim = one[size:]
+    block = ((wide(block) + wide(one[:size])) + (wide(two) + wide(three))).astype(BF)
 
     rim = jnp.where(row_y == 1, high, jnp.where(row_y == 2, low, rim))
     three = exchanged(jnp.concatenate([block, rim], axis=0), mask_y=3)

time: 87.4 us -> 88.9 us (1.017)
  starting transfers between devices: 43.3 us -> 48.4 us
  waiting for transfers between devices: 11.6 us -> 7.89 us
    ppermute x21 -> x22, starting transfers between devices: 38.8 us -> 44 us  [exchanged(): return lax.ppermute(block, ('region', 'panel'), route)]
    ppermute x21 -> x22, waiting for transfers between devices: 11.6 us -> 7.89 us  [exchanged(): return lax.ppermute(block, ('region', 'panel'), route)]
  transfers between devices with their start and end apart: 23 -> 24, of which waited for: 5 -> 6; matrix products, arithmetic and copies ran while one was open for 0% -> 0% of each run, Pallas kernels for 23% -> 22%
where the time goes in v8:
time: 88.9 us; the launch traced here: 88.7 us
  starting transfers between devices  48.4 us (54%)
  Pallas kernels  28.6 us (32%)
  waiting for transfers between devices  7.89 us (9%)
  local copies, waits for them, and re-layouts  1.71 us (2%)
  other arithmetic  1.1 us (1%)
  between operations  1.04 us (1%)
    ppermute x22, starting transfers between devices, exchanged(): return lax.ppermute(block, ('region', 'panel'), route)  44 us
    pallas_call x9, Pallas kernels, call(): pl.pallas_call(kernel, out_shape=[jax.ShapeDtypeStruct(shape, kind) for s...  28.6 us
    ppermute x22, waiting for transfers between devices, exchanged(): return lax.ppermute(block, ('region', 'panel'), route)  7.89 us
    ppermute x2, starting transfers between devices, shifted(): return lax.ppermute(array, 'panel', pairs)  4.48 us
  transfers between devices with their start and end apart: 24, of which 6 were waited for; matrix products, arithmetic and copies ran while one was open for 0% of the time, Pallas kernels for 22%

profile of v8, /device:TPU:1, one launch (start us, length us, event | category | flops | bytes accessed | tf_op | source)
XLA Modules:
  0.0 88.7 jit_solution(17498319914039321655)
XLA Ops:
  0.6 0.0 copy-start
  0.6 0.7 copy-done
  1.3 0.9 %copy-done.4 = bf16[1024,128]{1,0:T(8,128)(2,1)S(1)} copy-done((bf16[1024,128]{1,0:T(8,128)(2,1)S(1)}, bf16[1024,128]{1,0:T(8,128)(2,1)}, u32[]{:S(2)}) %copy-start.4) | copy-done | bytes 262168
  2.3 0.4 shard_map.103
  2.7 3.3 %collective-permute-start.1 = (bf16[128,256]{1,0:T(8,128)(2,1)S(1)}, bf16[128,256]{1,0:T(8,128)(2,1)S(1)}, u32[]{:S(2)}, u32[]{:S(2)}) collective-permute-start(bf16[128,256]{1,0:T(8,128)(2,1)S(1)} %get-tuple-element.61.bound_t_ref), channel_id=1, source_target_pairs={{0,8},{1,9},{2,10},{3,11},{4,12},{5,13},{6,14},{7,15},{8,0},{9,1},... | collective-permute-start | bytes 196616 | tf_op jit(solution)/shard_map/ppermute | solution.py:287
  6.0 0.0 collective-permute-start.2
  6.0 2.9 %collective-permute-start.3 = (bf16[128,256]{1,0:T(8,128)(2,1)S(1)}, bf16[128,256]{1,0:T(8,128)(2,1)S(1)}, u32[]{:S(2)}, u32[]{:S(2)}) collective-permute-start(bf16[128,256]{1,0:T(8,128)(2,1)S(1)} %get-tuple-element.61.bound_t_ref), channel_id=1, source_target_pairs={{0,32},{1,33},{2,34},{3,35},{4,36},{5,37},{6,38},{7,39},{8,40},{9,... | collective-permute-start | bytes 196616 | tf_op jit(solution)/shard_map/ppermute | solution.py:287
  9.0 3.2 %collective-permute-start.4 = (bf16[64,128]{1,0:T(8,128)(2,1)S(1)}, bf16[64,128]{1,0:T(8,128)(2,1)S(1)}, u32[]{:S(2)}, u32[]{:S(2)}) collective-permute-start(bf16[64,128]{1,0:T(8,128)(2,1)S(1)} %get-tuple-element.67), channel_id=1, source_target_pairs={{0,1},{1,2},{2,3},{3,4},{4,5},{5,6},{6,7},{8,9},{9,10},{10,11},{11... | collective-permute-start | bytes 49160 | tf_op jit(solution)/shard_map/ppermute | solution.py:298
  12.2 1.3 %collective-permute-start.5 = (bf16[64,128]{1,0:T(8,128)(2,1)S(1)}, bf16[64,128]{1,0:T(8,128)(2,1)S(1)}, u32[]{:S(2)}, u32[]{:S(2)}) collective-permute-start(bf16[64,128]{1,0:T(8,128)(2,1)S(1)} %get-tuple-element.68), channel_id=1, source_target_pairs={{1,0},{2,1},{3,2},{4,3},{5,4},{6,5},{7,6},{9,8},{10,9},{11,10},{12... | collective-permute-start | bytes 49160 | tf_op jit(solution)/shard_map/ppermute | solution.py:298
  13.5 0.0 copy-start.2
  13.5 0.0 copy-start.3
  13.5 1.9 %shard_map.105 = (bf16[128,3072]{1,0:T(8,128)(2,1)S(1)}, bf16[128,3072]{1,0:T(8,128)(2,1)S(1)}) custom-call(bf16[128,1024]{1,0:T(8,128)(2,1)S(1)} %get-tuple-element.60.lat_t_ref, s32[2,3072]{1,0:T(2,128)S(1)} %copy-done.8), custom_call_target="tpu_custom_call" | custom-call | flops 4000000000 | bytes 4000000 | tf_op jit(solution)/shard_map/pallas_call | solution.py:269
  15.4 0.0 collective-permute-done.4.before_ref
  15.4 4.5 %collective-permute-start = (bf16[128,256]{1,0:T(8,128)(2,1)S(1)}, bf16[128,256]{1,0:T(8,128)(2,1)S(1)}, u32[]{:S(2)}, u32[]{:S(2)}) collective-permute-start(bf16[128,256]{1,0:T(8,128)(2,1)S(1)} %get-tuple-element.61.bound_t_ref), channel_id=1, source_target_pairs={{0,64},{1,65},{2,66},{3,67},{4,68},{5,69},{6,70},{7,71},{8,72},{9,... | collective-permute-start | bytes 196616 | tf_op jit(solution)/shard_map/ppermute | solution.py:287
  19.9 0.0 collective-permute-done.5.after_ref
  19.9 0.0 copy-start.7
  19.9 0.0 copy-start.9
  20.0 4.5 %shard_map.106 = (bf16[128,3072]{1,0:T(8,128)(2,1)S(1)}, f32[128,3072]{1,0:T(8,128)S(1)}, bf16[1024,128]{1,0:T(8,128)(2,1)S(1)}) custom-call(bf16[64,128]{1,0:T(8,128)(2,1)S(1)} %collective-permute-done.4.before_ref, bf16[64,128]{1,0:T(8,128)(2,1)S(1)} %collective-permute-done.5.after_ref, bf16[128,3072]{1,0:T(8,128)(2,1)S(1)} %get-tuple-element.72.own_ref, ...), custom_call_target="tpu_custom_call" | custom-call | flops 3000000000 | bytes 4000000 | tf_op jit(solution)/shard_map/pallas_call | solution.py:269
  24.5 0.0 copy-start.1
  24.5 0.0 copy-start.5
  24.5 0.0 copy-start.6
  24.5 0.0 collective-permute-done.1.far0_ref
  24.5 0.0 collective-permute-done.2.far1_ref
  24.5 0.0 collective-permute-done.3.far2_ref
  24.5 4.4 %shard_map.104 = (bf16[256,6144]{1,0:T(8,128)(2,1)S(1)}, f32[128,6144]{1,0:T(8,128)S(1)}, f32[256,128]{1,0:T(8,128)S(1)}) custom-call(s32[1,4]{1,0:T(1,128)S(1)} %copy-done.9, bf16[128,256]{1,0:T(8,128)(2,1)S(1)} %get-tuple-element.61.bound_t_ref, bf16[128,256]{1,0:T(8,128)(2,1)S(1)} %collective-permute-done.1.far0_ref, ...), custom_call_target="tpu_custom_call" | custom-call | flops 3000000000 | bytes 4000000 | tf_op jit(solution)/shard_map/pallas_call | solution.py:269
  28.9 0.0 collective-permute-done.far3_ref
  29.0 8.4 %shard_map.107 = (bf16[1024,128]{1,0:T(8,128)(2,1)}, f32[576,128]{1,0:T(8,128)S(1)}, bf16[576,128]{1,0:T(8,128)(2,1)S(1)}, bf16[128,3072]{1,0:T(8,128)(2,1)S(1)}...) custom-call(s32[1,4]{1,0:T(1,128)S(1)} %copy-done.9, s32[1]{0:T(128)} %bitcast.core_ref, ...), custom_call_target="tpu_custom_call" | custom-call | flops 6000000000 | bytes 4000000 | tf_op jit(solution)/shard_map/pallas_call | solution.py:269
  37.4 1.3 %collective-permute-start.6 = (bf16[576,128]{1,0:T(8,128)(2,1)S(1)}, bf16[576,128]{1,0:T(8,128)(2,1)S(1)}, u32[]{:S(2)}, u32[]{:S(2)}) collective-permute-start(bf16[576,128]{1,0:T(8,128)(2,1)S(1)} %get-tuple-element.79), channel_id=1, source_target_pairs={{0,8},{1,9},{2,10},{3,11},{4,12},{5,13},{6,14},{7,15},{8,0},{9,1},... | collective-permute-start | bytes 442376 | tf_op jit(solution)/shard_map/ppermute | solution.py:287
  38.7 2.8 %shard_map.108 = (bf16[256,128]{1,0:T(8,128)(2,1)S(1)}, bf16[256,128]{1,0:T(8,128)(2,1)S(1)}, bf16[256,128]{1,0:T(8,128)(2,1)S(1)}, bf16[256,128]{1,0:T(8,128)(2,1)S(1)}, f32[256,128]{1,0:T(8,128)S(1)}) custom-call(bf16[9,128,128]{2,1,0:T(8,128)(2,1)S(1)} %copy-done.3, s32[2,8192]{1,0:T(2,128)S(1)} %copy-done.7, bf16[128,8192]{1,0:T(8,128)(2,1)S(1)} %get-tuple-element.80.dc_ref), custom_call_target="tpu_custom_call" | custom-call | flops 2000000000 | bytes 4000000 | tf_op jit(solution)/shard_map/pallas_call | solution.py:269
  41.5 0.0 collective-permute-done.6
  41.5 2.5 %collective-permute-start.7 = (bf16[144,128]{1,0:T(8,128)(2,1)S(1)}, bf16[144,128]{1,0:T(8,128)(2,1)S(1)}, u32[]{:S(2)}, u32[]{:S(2)}) collective-permute-start(bf16[144,128]{1,0:T(8,128)(2,1)S(1)} %get-tuple-element.121), channel_id=1, source_target_pairs={{0,1},{1,0},{2,3},{3,2},{4,5},{5,4},{6,7},{7,6},{8,9},{9,8},{10,11... | collective-permute-start | bytes 110600 | tf_op jit(solution)/shard_map/ppermute | solution.py:287
  44.0 2.6 %collective-permute-start.8 = (bf16[144,128]{1,0:T(8,128)(2,1)S(1)}, bf16[144,128]{1,0:T(8,128)(2,1)S(1)}, u32[]{:S(2)}, u32[]{:S(2)}) collective-permute-start(bf16[144,128]{1,0:T(8,128)(2,1)S(1)} %get-tuple-element.120), channel_id=1, source_target_pairs={{0,2},{1,3},{2,0},{3,1},{4,6},{5,7},{6,4},{7,5},{8,10},{9,11},{10,... | collective-permute-start | bytes 110600 | tf_op jit(solution)/shard_map/ppermute | solution.py:287
  46.6 0.0 collective-permute-start.9
  46.6 1.3 %collective-permute-start.13 = (bf16[512,128]{1,0:T(8,128)(2,1)S(1)}, bf16[512,128]{1,0:T(8,128)(2,1)S(1)}, u32[]{:S(2)}, u32[]{:S(2)}) collective-permute-start(bf16[512,128]{1,0:T(8,128)(2,1)S(1)} %pad_maximum_fusion.2), channel_id=1, source_target_pairs={{0,32},{1,33},{2,34},{3,35},{4,36},{5,37},{6,38},{7,39},{8,40},{9,... | collective-permute-start | bytes 393224 | tf_op jit(solution)/shard_map/ppermute | solution.py:287
  47.9 0.7 collective-permute-start.11
  48.6 0.0 collective-permute-done.7
  48.6 1.1 %collective-permute-start.15 = (bf16[256,128]{1,0:T(8,128)(2,1)S(1)}, bf16[256,128]{1,0:T(8,128)(2,1)S(1)}, u32[]{:S(2)}, u32[]{:S(2)}) collective-permute-start(bf16[256,128]{1,0:T(8,128)(2,1)S(1)} %get-tuple-element.103), channel_id=1, source_target_pairs={{0,8},{1,9},{2,10},{3,11},{4,12},{5,13},{6,14},{7,15},{8,0},{9,1},... | collective-permute-start | bytes 196616 | tf_op jit(solution)/shard_map/ppermute | solution.py:287
  49.8 0.0 collective-permute-done.8
  49.8 0.9 collective-permute-done.9
  50.7 0.8 collective-permute-start.10
  51.5 2.6 %shard_map.109 = (f32[1024,128]{1,0:T(8,128)S(1)}, bf16[64,128]{1,0:T(8,128)(2,1)S(1)}, bf16[64,128]{1,0:T(8,128)(2,1)S(1)}) custom-call(bf16[9,128,128]{2,1,0:T(8,128)(2,1)S(1)} %copy-done.3, s32[2,3072]{1,0:T(2,128)S(1)} %copy-done.8, bf16[128,3072]{1,0:T(8,128)(2,1)S(1)} %get-tuple-element.90.dm_ref), custom_call_target="tpu_custom_call" | custom-call | flops 2000000000 | bytes 4000000 | tf_op jit(solution)/shard_map/pallas_call | solution.py:269
  54.1 0.0 collective-permute-done.11.in1_ref
  54.1 0.0 collective-permute-done.10
  54.2 1.7 %collective-permute-start.12 = (bf16[144,128]{1,0:T(8,128)(2,1)S(1)}, bf16[144,128]{1,0:T(8,128)(2,1)S(1)}, u32[]{:S(2)}, u32[]{:S(2)}) collective-permute-start(bf16[144,128]{1,0:T(8,128)(2,1)S(1)} %add_convert_fusion.3), channel_id=1, source_target_pairs={{0,32},{1,33},{2,34},{3,35},{4,36},{5,37},{6,38},{7,39},{8,40},{9,... | collective-permute-start | bytes 110600 | tf_op jit(solution)/shard_map/ppermute | solution.py:287
  55.9 2.3 %shard_map.110.part_ref = f32[1024,128]{1,0:T(8,128)S(1)} custom-call(bf16[9,128,128]{2,1,0:T(8,128)(2,1)S(1)} %copy-done.3, s32[2,3072]{1,0:T(2,128)S(1)} %copy-done.8, bf16[128,3072]{1,0:T(8,128)(2,1)S(1)} %get-tuple-element.90.dm_ref, bf16[1024,128]{1,0:T(8,128)(2,1)S(1)} %get-tuple-element.96.dn_ref, bf16[1024,128]{1,0:T(8,128)(2,1)S(1)} %copy-done.6, ...), custom_call_target="tpu_custom_call" | custom-call | flops 2000000000 | bytes 4000000 | tf_op jit(solution)/shard_map/pallas_call | solution.py:269
  58.1 0.1 collective-permute-done.12
  58.2 0.0 collective-permute-done.13
  58.2 1.7 %collective-permute-start.14 = (bf16[144,128]{1,0:T(8,128)(2,1)S(1)}, bf16[144,128]{1,0:T(8,128)(2,1)S(1)}, u32[]{:S(2)}, u32[]{:S(2)}) collective-permute-start(bf16[144,128]{1,0:T(8,128)(2,1)S(1)} %add_convert_fusion.2), channel_id=1, source_target_pairs={{0,96},{1,97},{2,98},{3,99},{4,100},{5,101},{6,102},{7,103},{8,104... | collective-permute-start | bytes 110600 | tf_op jit(solution)/shard_map/ppermute | solution.py:287
  60.0 2.0 %collective-permute-start.19 = (bf16[256,128]{1,0:T(8,128)(2,1)S(1)}, bf16[256,128]{1,0:T(8,128)(2,1)S(1)}, u32[]{:S(2)}, u32[]{:S(2)}) collective-permute-start(bf16[256,128]{1,0:T(8,128)(2,1)S(1)} %get-tuple-element.126), channel_id=1, source_target_pairs={{0,96},{1,97},{2,98},{3,99},{4,100},{5,101},{6,102},{7,103},{8,104... | collective-permute-start | bytes 196616 | tf_op jit(solution)/shard_map/ppermute | solution.py:287
  62.0 0.0 collective-permute-done.15.in0_ref
  62.0 1.3 %collective-permute-done.14 = bf16[144,128]{1,0:T(8,128)(2,1)S(1)} collective-permute-done((bf16[144,128]{1,0:T(8,128)(2,1)S(1)}, bf16[144,128]{1,0:T(8,128)(2,1)S(1)}, u32[]{:S(2)}, u32[]{:S(2)}) %collective-permute-start.14) | collective-permute-done | bytes 36896 | tf_op jit(solution)/shard_map/ppermute | solution.py:287
  63.4 3.8 %collective-permute-start.16 = (bf16[208,128]{1,0:T(8,128)(2,1)S(1)}, bf16[208,128]{1,0:T(8,128)(2,1)S(1)}, u32[]{:S(2)}, u32[]{:S(2)}) collective-permute-start(bf16[208,128]{1,0:T(8,128)(2,1)S(1)} %pad_maximum_fusion.5), channel_id=1, source_target_pairs={{0,4},{1,5},{2,6},{3,7},{4,0},{5,1},{6,2},{7,3},{8,12},{9,13},{10,... | collective-permute-start | bytes 159752 | tf_op jit(solution)/shard_map/ppermute | solution.py:287
  67.2 2.4 %collective-permute-start.17 = (bf16[144,128]{1,0:T(8,128)(2,1)S(1)}, bf16[144,128]{1,0:T(8,128)(2,1)S(1)}, u32[]{:S(2)}, u32[]{:S(2)}) collective-permute-start(bf16[144,128]{1,0:T(8,128)(2,1)S(1)} %add_convert_fusion.1), channel_id=1, source_target_pairs={{0,128},{1,129},{2,130},{3,131},{4,132},{5,133},{6,134},{7,135},{8... | collective-permute-start | bytes 110600 | tf_op jit(solution)/shard_map/ppermute | solution.py:287
  69.6 0.0 collective-permute-start.18
  69.6 0.0 collective-permute-done.19.in3_ref
  69.6 1.9 %collective-permute-done.17 = bf16[144,128]{1,0:T(8,128)(2,1)S(1)} collective-permute-done((bf16[144,128]{1,0:T(8,128)(2,1)S(1)}, bf16[144,128]{1,0:T(8,128)(2,1)S(1)}, u32[]{:S(2)}, u32[]{:S(2)}) %collective-permute-start.17) | collective-permute-done | bytes 36896 | tf_op jit(solution)/shard_map/ppermute | solution.py:287
  71.5 2.1 %collective-permute-done.18 = bf16[144,128]{1,0:T(8,128)(2,1)S(1)} collective-permute-done((bf16[144,128]{1,0:T(8,128)(2,1)S(1)}, bf16[144,128]{1,0:T(8,128)(2,1)S(1)}, u32[]{:S(2)}, u32[]{:S(2)}) %collective-permute-start.18) | collective-permute-done | bytes 36896 | tf_op jit(solution)/shard_map/ppermute | solution.py:287
  73.7 0.1 collective-permute-start.20
  73.8 0.5 collective-permute-start.22
  74.3 2.8 %collective-permute-start.21 = (bf16[144,128]{1,0:T(8,128)(2,1)S(1)}, bf16[144,128]{1,0:T(8,128)(2,1)S(1)}, u32[]{:S(2)}, u32[]{:S(2)}) collective-permute-start(bf16[144,128]{1,0:T(8,128)(2,1)S(1)} %add_convert_fusion), channel_id=1, source_target_pairs={{0,2},{1,3},{2,0},{3,1},{4,6},{5,7},{6,4},{7,5},{8,10},{9,11},{10,... | collective-permute-start | bytes 110600 | tf_op jit(solution)/shard_map/ppermute | solution.py:287
  77.0 1.6 %collective-permute-done.21 = bf16[144,128]{1,0:T(8,128)(2,1)S(1)} collective-permute-done((bf16[144,128]{1,0:T(8,128)(2,1)S(1)}, bf16[144,128]{1,0:T(8,128)(2,1)S(1)}, u32[]{:S(2)}, u32[]{:S(2)}) %collective-permute-start.21) | collective-permute-done | bytes 36896 | tf_op jit(solution)/shard_map/ppermute | solution.py:287
  78.6 7.9 %collective-permute-start.23 = (bf16[576,128]{1,0:T(8,128)(2,1)S(1)}, bf16[576,128]{1,0:T(8,128)(2,1)S(1)}, u32[]{:S(2)}, u32[]{:S(2)}) collective-permute-start(bf16[576,128]{1,0:T(8,128)(2,1)S(1)} %pad_maximum_fusion.1), channel_id=1, source_target_pairs={{0,8},{1,9},{2,10},{3,11},{4,12},{5,13},{6,14},{7,15},{8,0},{9,1},... | collective-permute-start | bytes 442376 | tf_op jit(solution)/shard_map/ppermute | solution.py:287
  86.6 1.2 %shard_map.111 = f32[1024,128]{1,0:T(8,128)} custom-call(f32[1024,128]{1,0:T(8,128)S(1)} %shard_map.110.part_ref, f32[256,128]{1,0:T(8,128)S(1)} %get-tuple-element.101.own_ref, bf16[256,128]{1,0:T(8,128)(2,1)S(1)} %collective-permute-done.15.in0_ref, bf16[256,128]{1,0:T(8,128)(2,1)S(1)} %collective-permute-done.11.in1_ref, ...), custom_call_target="tpu_custom_call" | custom-call | flops 100000000 | bytes 4000000 | tf_op jit(solution)/shard_map/pallas_call | solution.py:269
  87.9 0.9 pad_maximum_fusion
  (31 shorter events, 0.3 us)
Async XLA Ops:
  0.6 0.7 copy-start
  1.3 0.9 %copy-start.4 = (bf16[1024,128]{1,0:T(8,128)(2,1)S(1)}, bf16[1024,128]{1,0:T(8,128)(2,1)}, u32[]{:S(2)}) copy-start(bf16[1024,128]{1,0:T(8,128)(2,1)} %lat_ref.1) | copy-start | bytes 786436
  2.3 11.2 %copy-start.8 = (s32[2,3072]{1,0:T(2,128)S(1)}, s32[2,3072]{1,0:T(2,128)}, u32[]{:S(2)}) copy-start(s32[2,3072]{1,0:T(2,128)} %edges_ref.9) | copy-start | bytes 73732
  2.7 21.8 %collective-permute-start.1 = (bf16[128,256]{1,0:T(8,128)(2,1)S(1)}, bf16[128,256]{1,0:T(8,128)(2,1)S(1)}, u32[]{:S(2)}, u32[]{:S(2)}) collective-permute-start(bf16[128,256]{1,0:T(8,128)(2,1)S(1)} %get-tuple-element.61.bound_t_ref), channel_id=1, source_target_pairs={{0,8},{1,9},{2,10},{3,11},{4,12},{5,13},{6,14},{7,15},{8,0},{9,1},... | collective-permute-start | bytes 196616 | tf_op jit(solution)/shard_map/ppermute | solution.py:287
  6.0 18.5 %collective-permute-start.2 = (bf16[128,256]{1,0:T(8,128)(2,1)S(1)}, bf16[128,256]{1,0:T(8,128)(2,1)S(1)}, u32[]{:S(2)}, u32[]{:S(2)}) collective-permute-start(bf16[128,256]{1,0:T(8,128)(2,1)S(1)} %get-tuple-element.61.bound_t_ref), channel_id=1, source_target_pairs={{0,16},{1,17},{2,18},{3,19},{4,20},{5,21},{6,22},{7,23},{8,24},{9,... | collective-permute-start | bytes 196616 | tf_op jit(solution)/shard_map/ppermute | solution.py:287
  6.0 18.5 %collective-permute-start.3 = (bf16[128,256]{1,0:T(8,128)(2,1)S(1)}, bf16[128,256]{1,0:T(8,128)(2,1)S(1)}, u32[]{:S(2)}, u32[]{:S(2)}) collective-permute-start(bf16[128,256]{1,0:T(8,128)(2,1)S(1)} %get-tuple-element.61.bound_t_ref), channel_id=1, source_target_pairs={{0,32},{1,33},{2,34},{3,35},{4,36},{5,37},{6,38},{7,39},{8,40},{9,... | collective-permute-start | bytes 196616 | tf_op jit(solution)/shard_map/ppermute | solution.py:287
  9.0 6.5 %collective-permute-start.4 = (bf16[64,128]{1,0:T(8,128)(2,1)S(1)}, bf16[64,128]{1,0:T(8,128)(2,1)S(1)}, u32[]{:S(2)}, u32[]{:S(2)}) collective-permute-start(bf16[64,128]{1,0:T(8,128)(2,1)S(1)} %get-tuple-element.67), channel_id=1, source_target_pairs={{0,1},{1,2},{2,3},{3,4},{4,5},{5,6},{6,7},{8,9},{9,10},{10,11},{11... | collective-permute-start | bytes 49160 | tf_op jit(solution)/shard_map/ppermute | solution.py:298
  12.2 7.8 %collective-permute-start.5 = (bf16[64,128]{1,0:T(8,128)(2,1)S(1)}, bf16[64,128]{1,0:T(8,128)(2,1)S(1)}, u32[]{:S(2)}, u32[]{:S(2)}) collective-permute-start(bf16[64,128]{1,0:T(8,128)(2,1)S(1)} %get-tuple-element.68), channel_id=1, source_target_pairs={{1,0},{2,1},{3,2},{4,3},{5,4},{6,5},{7,6},{9,8},{10,9},{11,10},{12... | collective-permute-start | bytes 49160 | tf_op jit(solution)/shard_map/ppermute | solution.py:298
  13.5 6.5 %copy-start.2 = (bf16[3072,128]{1,0:T(8,128)(2,1)S(1)}, bf16[3072,128]{1,0:T(8,128)(2,1)}, u32[]{:S(2)}) copy-start(bf16[3072,128]{1,0:T(8,128)(2,1)} %feats_ref.3) | copy-start | bytes 2359300
  13.5 6.5 %copy-start.3 = (bf16[9,128,128]{2,1,0:T(8,128)(2,1)S(1)}, bf16[9,128,128]{2,1,0:T(8,128)(2,1)}, u32[]{:S(2)}) copy-start(bf16[9,128,128]{2,1,0:T(8,128)(2,1)} %w_ref.11) | copy-start | bytes 884740
  15.4 13.5 %collective-permute-start = (bf16[128,256]{1,0:T(8,128)(2,1)S(1)}, bf16[128,256]{1,0:T(8,128)(2,1)S(1)}, u32[]{:S(2)}, u32[]{:S(2)}) collective-permute-start(bf16[128,256]{1,0:T(8,128)(2,1)S(1)} %get-tuple-element.61.bound_t_ref), channel_id=1, source_target_pairs={{0,64},{1,65},{2,66},{3,67},{4,68},{5,69},{6,70},{7,71},{8,72},{9,... | collective-permute-start | bytes 196616 | tf_op jit(solution)/shard_map/ppermute | solution.py:287
  19.9 4.6 %copy-start.7 = (s32[2,8192]{1,0:T(2,128)S(1)}, s32[2,8192]{1,0:T(2,128)}, u32[]{:S(2)}) copy-start(s32[2,8192]{1,0:T(2,128)} %contacts_ref.5) | copy-start | bytes 196612
  19.9 4.6 %copy-start.9 = (s32[1,4]{1,0:T(1,128)S(1)}, s32[1,4]{1,0:T(1,128)}, u32[]{:S(2)}) copy-start(s32[1,4]{1,0:T(1,128)} %counts_ref.3) | copy-start | bytes 52
  24.5 4.5 %copy-start.1 = (s32[256]{0:T(256)S(1)}, s32[256]{0:T(256)}, u32[]{:S(2)}) copy-start(s32[256]{0:T(256)} %param.13) | copy-start | bytes 3076
  24.5 4.5 %copy-start.5 = (bf16[1024,128]{1,0:T(8,128)(2,1)S(1)}, bf16[1024,128]{1,0:T(8,128)(2,1)}, u32[]{:S(2)}) copy-start(bf16[1024,128]{1,0:T(8,128)(2,1)} %lat_ref.1) | copy-start | bytes 786436
  24.5 4.5 %copy-start.6 = (bf16[1024,128]{1,0:T(8,128)(2,1)S(1)}, bf16[1024,128]{1,0:T(8,128)(2,1)}, u32[]{:S(2)}) copy-start(bf16[1024,128]{1,0:T(8,128)(2,1)} %cot_ref.3) | copy-start | bytes 786436
  37.4 4.1 %collective-permute-start.6 = (bf16[576,128]{1,0:T(8,128)(2,1)S(1)}, bf16[576,128]{1,0:T(8,128)(2,1)S(1)}, u32[]{:S(2)}, u32[]{:S(2)}) collective-permute-start(bf16[576,128]{1,0:T(8,128)(2,1)S(1)} %get-tuple-element.79), channel_id=1, source_target_pairs={{0,8},{1,9},{2,10},{3,11},{4,12},{5,13},{6,14},{7,15},{8,0},{9,1},... | collective-permute-start | bytes 442376 | tf_op jit(solution)/shard_map/ppermute | solution.py:287
  41.5 7.1 %collective-permute-start.7 = (bf16[144,128]{1,0:T(8,128)(2,1)S(1)}, bf16[144,128]{1,0:T(8,128)(2,1)S(1)}, u32[]{:S(2)}, u32[]{:S(2)}) collective-permute-start(bf16[144,128]{1,0:T(8,128)(2,1)S(1)} %get-tuple-element.121), channel_id=1, source_target_pairs={{0,1},{1,0},{2,3},{3,2},{4,5},{5,4},{6,7},{7,6},{8,9},{9,8},{10,11... | collective-permute-start | bytes 110600 | tf_op jit(solution)/shard_map/ppermute | solution.py:287
  44.0 5.8 %collective-permute-start.8 = (bf16[144,128]{1,0:T(8,128)(2,1)S(1)}, bf16[144,128]{1,0:T(8,128)(2,1)S(1)}, u32[]{:S(2)}, u32[]{:S(2)}) collective-permute-start(bf16[144,128]{1,0:T(8,128)(2,1)S(1)} %get-tuple-element.120), channel_id=1, source_target_pairs={{0,2},{1,3},{2,0},{3,1},{4,6},{5,7},{6,4},{7,5},{8,10},{9,11},{10,... | collective-permute-start | bytes 110600 | tf_op jit(solution)/shard_map/ppermute | solution.py:287
  46.6 4.0 %collective-permute-start.9 = (bf16[144,128]{1,0:T(8,128)(2,1)S(1)}, bf16[144,128]{1,0:T(8,128)(2,1)S(1)}, u32[]{:S(2)}, u32[]{:S(2)}) collective-permute-start(bf16[144,128]{1,0:T(8,128)(2,1)S(1)} %get-tuple-element.119), channel_id=1, source_target_pairs={{0,3},{1,2},{2,1},{3,0},{4,7},{5,6},{6,5},{7,4},{8,11},{9,10},{10,... | collective-permute-start | bytes 110600 | tf_op jit(solution)/shard_map/ppermute | solution.py:287
  46.6 11.6 %collective-permute-start.13 = (bf16[512,128]{1,0:T(8,128)(2,1)S(1)}, bf16[512,128]{1,0:T(8,128)(2,1)S(1)}, u32[]{:S(2)}, u32[]{:S(2)}) collective-permute-start(bf16[512,128]{1,0:T(8,128)(2,1)S(1)} %pad_maximum_fusion.2), channel_id=1, source_target_pairs={{0,32},{1,33},{2,34},{3,35},{4,36},{5,37},{6,38},{7,39},{8,40},{9,... | collective-permute-start | bytes 393224 | tf_op jit(solution)/shard_map/ppermute | solution.py:287
  47.9 6.2 %collective-permute-start.11 = (bf16[256,128]{1,0:T(8,128)(2,1)S(1)}, bf16[256,128]{1,0:T(8,128)(2,1)S(1)}, u32[]{:S(2)}, u32[]{:S(2)}) collective-permute-start(bf16[256,128]{1,0:T(8,128)(2,1)S(1)} %get-tuple-element.94), channel_id=1, source_target_pairs={{0,16},{1,17},{2,18},{3,19},{4,20},{5,21},{6,22},{7,23},{8,24},{9,... | collective-permute-start | bytes 196616 | tf_op jit(solution)/shard_map/ppermute | solution.py:287
  48.6 13.4 %collective-permute-start.15 = (bf16[256,128]{1,0:T(8,128)(2,1)S(1)}, bf16[256,128]{1,0:T(8,128)(2,1)S(1)}, u32[]{:S(2)}, u32[]{:S(2)}) collective-permute-start(bf16[256,128]{1,0:T(8,128)(2,1)S(1)} %get-tuple-element.103), channel_id=1, source_target_pairs={{0,8},{1,9},{2,10},{3,11},{4,12},{5,13},{6,14},{7,15},{8,0},{9,1},... | collective-permute-start | bytes 196616 | tf_op jit(solution)/shard_map/ppermute | solution.py:287
  50.7 3.5 %collective-permute-start.10 = (bf16[144,128]{1,0:T(8,128)(2,1)S(1)}, bf16[144,128]{1,0:T(8,128)(2,1)S(1)}, u32[]{:S(2)}, u32[]{:S(2)}) collective-permute-start(bf16[144,128]{1,0:T(8,128)(2,1)S(1)} %add_convert_fusion.4), channel_id=1, source_target_pairs={{0,16},{1,17},{2,18},{3,19},{4,20},{5,21},{6,22},{7,23},{8,24},{9,... | collective-permute-start | bytes 110600 | tf_op jit(solution)/shard_map/ppermute | solution.py:287
  54.2 4.1 %collective-permute-start.12 = (bf16[144,128]{1,0:T(8,128)(2,1)S(1)}, bf16[144,128]{1,0:T(8,128)(2,1)S(1)}, u32[]{:S(2)}, u32[]{:S(2)}) collective-permute-start(bf16[144,128]{1,0:T(8,128)(2,1)S(1)} %add_convert_fusion.3), channel_id=1, source_target_pairs={{0,32},{1,33},{2,34},{3,35},{4,36},{5,37},{6,38},{7,39},{8,40},{9,... | collective-permute-start | bytes 110600 | tf_op jit(solution)/shard_map/ppermute | solution.py:287
  58.2 5.1 %collective-permute-start.14 = (bf16[144,128]{1,0:T(8,128)(2,1)S(1)}, bf16[144,128]{1,0:T(8,128)(2,1)S(1)}, u32[]{:S(2)}, u32[]{:S(2)}) collective-permute-start(bf16[144,128]{1,0:T(8,128)(2,1)S(1)} %add_convert_fusion.2), channel_id=1, source_target_pairs={{0,96},{1,97},{2,98},{3,99},{4,100},{5,101},{6,102},{7,103},{8,104... | collective-permute-start | bytes 110600 | tf_op jit(solution)/shard_map/ppermute | solution.py:287
  60.0 9.7 %collective-permute-start.19 = (bf16[256,128]{1,0:T(8,128)(2,1)S(1)}, bf16[256,128]{1,0:T(8,128)(2,1)S(1)}, u32[]{:S(2)}, u32[]{:S(2)}) collective-permute-start(bf16[256,128]{1,0:T(8,128)(2,1)S(1)} %get-tuple-element.126), channel_id=1, source_target_pairs={{0,96},{1,97},{2,98},{3,99},{4,100},{5,101},{6,102},{7,103},{8,104... | collective-permute-start | bytes 196616 | tf_op jit(solution)/shard_map/ppermute | solution.py:287
  63.4 10.2 %collective-permute-start.16 = (bf16[208,128]{1,0:T(8,128)(2,1)S(1)}, bf16[208,128]{1,0:T(8,128)(2,1)S(1)}, u32[]{:S(2)}, u32[]{:S(2)}) collective-permute-start(bf16[208,128]{1,0:T(8,128)(2,1)S(1)} %pad_maximum_fusion.5), channel_id=1, source_target_pairs={{0,4},{1,5},{2,6},{3,7},{4,0},{5,1},{6,2},{7,3},{8,12},{9,13},{10,... | collective-permute-start | bytes 159752 | tf_op jit(solution)/shard_map/ppermute | solution.py:287
  67.2 4.4 %collective-permute-start.17 = (bf16[144,128]{1,0:T(8,128)(2,1)S(1)}, bf16[144,128]{1,0:T(8,128)(2,1)S(1)}, u32[]{:S(2)}, u32[]{:S(2)}) collective-permute-start(bf16[144,128]{1,0:T(8,128)(2,1)S(1)} %add_convert_fusion.1), channel_id=1, source_target_pairs={{0,128},{1,129},{2,130},{3,131},{4,132},{5,133},{6,134},{7,135},{8... | collective-permute-start | bytes 110600 | tf_op jit(solution)/shard_map/ppermute | solution.py:287
  69.6 4.0 %collective-permute-start.18 = (bf16[144,128]{1,0:T(8,128)(2,1)S(1)}, bf16[144,128]{1,0:T(8,128)(2,1)S(1)}, u32[]{:S(2)}, u32[]{:S(2)}) collective-permute-start(bf16[144,128]{1,0:T(8,128)(2,1)S(1)} %add_convert_fusion.1), channel_id=1, source_target_pairs={{0,132},{1,133},{2,134},{3,135},{4,128},{5,129},{6,130},{7,131},{8... | collective-permute-start | bytes 110600 | tf_op jit(solution)/shard_map/ppermute | solution.py:287
  73.7 4.9 %collective-permute-start.20 = (bf16[208,128]{1,0:T(8,128)(2,1)S(1)}, bf16[208,128]{1,0:T(8,128)(2,1)S(1)}, u32[]{:S(2)}, u32[]{:S(2)}) collective-permute-start(bf16[208,128]{1,0:T(8,128)(2,1)S(1)} %get-tuple-element.131), channel_id=1, source_target_pairs={{0,1},{1,0},{2,3},{3,2},{4,5},{5,4},{6,7},{7,6},{8,9},{9,8},{10,11... | collective-permute-start | bytes 159752 | tf_op jit(solution)/shard_map/ppermute | solution.py:287
  73.8 4.8 %collective-permute-start.22 = (bf16[208,128]{1,0:T(8,128)(2,1)S(1)}, bf16[208,128]{1,0:T(8,128)(2,1)S(1)}, u32[]{:S(2)}, u32[]{:S(2)}) collective-permute-start(bf16[208,128]{1,0:T(8,128)(2,1)S(1)} %get-tuple-element.130), channel_id=1, source_target_pairs={{0,3},{1,2},{2,1},{3,0},{4,7},{5,6},{6,5},{7,4},{8,11},{9,10},{10,... | collective-permute-start | bytes 159752 | tf_op jit(solution)/shard_map/ppermute | solution.py:287
  74.3 4.3 %collective-permute-start.21 = (bf16[144,128]{1,0:T(8,128)(2,1)S(1)}, bf16[144,128]{1,0:T(8,128)(2,1)S(1)}, u32[]{:S(2)}, u32[]{:S(2)}) collective-permute-start(bf16[144,128]{1,0:T(8,128)(2,1)S(1)} %add_convert_fusion), channel_id=1, source_target_pairs={{0,2},{1,3},{2,0},{3,1},{4,6},{5,7},{6,4},{7,5},{8,10},{9,11},{10,... | collective-permute-start | bytes 110600 | tf_op jit(solution)/shard_map/ppermute | solution.py:287
  78.6 9.2 %collective-permute-start.23 = (bf16[576,128]{1,0:T(8,128)(2,1)S(1)}, bf16[576,128]{1,0:T(8,128)(2,1)S(1)}, u32[]{:S(2)}, u32[]{:S(2)}) collective-permute-start(bf16[576,128]{1,0:T(8,128)(2,1)S(1)} %pad_maximum_fusion.1), channel_id=1, source_target_pairs={{0,8},{1,9},{2,10},{3,11},{4,12},{5,13},{6,14},{7,15},{8,0},{9,1},... | collective-permute-start | bytes 442376 | tf_op jit(solution)/shard_map/ppermute | solution.py:287

commit v9 on v8

--- a/solution.py
+++ b/solution.py
@@ -142,7 +142,7 @@
 
 
 def main_kernel(
-    counts_ref, core_ref, lat_ref, lat_t_ref, bound_t_ref, far3_ref, both_ref, slope_c_ref,
+    counts_ref, lat_ref, lat_t_ref, bound_t_ref, far3_ref, both_ref, slope_c_ref,
     aggb_ref, send_ref, recv_ref, slope_m_ref, agg_ref, feats_ref, cot_ref, w_ref, edges_ref,
     contacts_ref, bnd_ref,
     new_ref, kept_ref, sent_ref, dm_ref, dc_ref, dn_ref,
@@ -202,11 +202,9 @@
         pair = nt(both, d)
         gw_ref[384:640, :] = pair + gw_ref[384:640, :] if r else pair
 
-    half = gw_ref.shape[0] // 2
-    core = core_ref[0]
-    kept_ref[...] = gw_ref[pl.ds(pl.multiple_of(core * half, 64), half), :] * scale
-    sent = gw_ref[pl.ds(pl.multiple_of((1 - core) * half, 64), half), :] * scale
-    sent_ref[...] = sent.astype(BF)
+    total = gw_ref[...] * scale
+    kept_ref[...] = total
+    sent_ref[...] = total.astype(BF)
 
 
 def contact_back_kernel(
@@ -277,19 +275,16 @@
     )(*args)
 
 
-def exchanged(block, mask_x=0, mask_y=0, mask_z=0, mask_core=0):
+def exchanged(block, mask_x=0, mask_y=0, mask_z=0, mask_core=0, only_core=None):
     route = []
     for region in range(32):
+        if only_core is not None and region % 2 != only_core:
+            continue
         for panel in range(8):
             other_region = region ^ ((mask_x >> 1) << 4 | mask_z << 1 | mask_core)
             other_panel = panel ^ ((mask_x & 1) << 2 | mask_y)
             route.append((region * 8 + panel, other_region * 8 + other_panel))
     return lax.ppermute(block, ("region", "panel"), route)
-
-
-def swapped(block, bit):
-    size = lax.axis_size("region")
-    return lax.ppermute(block, "region", [(i, i ^ (1 << bit)) for i in range(size)])
 
 
 def shifted(array, by):
@@ -309,12 +304,6 @@
     ordered = [jnp.where(high, b, a) for a, b in zip(low_pair, high_pair)]
     ordered += [jnp.where(high, a, b) for a, b in zip(low_pair, high_pair)]
     return jnp.concatenate(ordered, axis=0)
-
-
-def joined(own, other, which):
-    first = jnp.where(which == 0, own, other)
-    second = jnp.where(which == 0, other, own)
-    return jnp.concatenate([first, second], axis=0)
 
 
 def tie(*arrays):
@@ -377,13 +366,13 @@
         functools.partial(main_kernel, scale=scale),
         [
             ((rows_dev, width), BF),
-            ((9 * width // 2, width), F32),
-            ((9 * width // 2, width), BF),
+            ((9 * width, width), F32),
+            ((9 * width, width), BF),
             ((width, edge_count), BF),
             ((width, contact_count), BF),
             ((rows_dev, width), BF),
         ],
-        [contact_counts, core.reshape(1), latents, lat_t, bound_t, fars[3], both, slope_c, aggb]
+        [contact_counts, latents, lat_t, bound_t, fars[3], both, slope_c, aggb]
         + [send_rows, recv_rows, slope, agg]
         + [edge_feats, cotangent, weights, mesh_edges, contact_edges, bnd],
         [
@@ -394,11 +383,12 @@
             ((width, rows_dev), BF),
             ((width, rows_dev), BF),
         ],
-        smem=2,
+        smem=1,
         flops=6 * 10**9,
         mib=20,
     )
-    other = exchanged(sent, mask_core=1)
+    by = functools.partial(exchanged, only_core=1)
+    other = exchanged(sent, mask_core=1, only_core=0)
     *far_grads, own_grad = call(
         contact_back_kernel,
         [((bound_count, width), BF)] * rounds + [((bound_count, width), F32)],
@@ -412,13 +402,13 @@
     pieces = [
         lax.dynamic_slice_in_dim(block, (row_y ^ mask) * size, size, 0) for mask in range(4)
     ]
-    found = [exchanged(pieces[mask].astype(BF), mask_y=mask) for mask in (1, 2, 3)]
+    found = [by(pieces[mask].astype(BF), mask_y=mask) for mask in (1, 2, 3)]
     pair = exchanged(jnp.concatenate(far_grads[2:], axis=0), mask_z=2)
     in_one = exchanged(far_grads[1], mask_z=1)
     one, two, three, d_mesh = tie(*found, d_mesh)
     block = ((pieces[0] + wide(one)) + (wide(two) + wide(three))).astype(BF)
 
-    other = exchanged(block, mask_z=1)
+    other = by(block, mask_z=1)
     part, low, high = call(
         send_back_kernel,
         [((rows_dev, width), F32), ((HB, width), BF), ((HB, width), BF)],
@@ -429,7 +419,9 @@
     )
     other, part, low, high, in_one = tie(other, part, low, high, in_one)
     block = (wide(block) + wide(other)).astype(BF)
-    other = exchanged(block, mask_z=2)
+    other = by(block, mask_z=2)
+    rims = jnp.concatenate([low, high], axis=0)
+    zero_rims = exchanged(rims, mask_core=1, only_core=0)
     (part,) = call(
         recv_back_kernel,
         [((rows_dev, width), F32)],
@@ -438,27 +430,29 @@
         flops=2 * 10**9,
         mib=16,
     )
-    other, part, pair = tie(other, part, pair)
+    other, part, pair, zero_rims = tie(other, part, pair, zero_rims)
     block = (wide(block) + wide(other)).astype(BF)
-    other = exchanged(block, mask_z=6)
+    other = by(block, mask_z=6)
     in_two = pair[:bound_count]
     in_three = exchanged(pair[bound_count:], mask_z=6)
     in_zero = exchanged(far_grads[0], mask_core=1)
     other, in_zero = tie(other, in_zero)
     block = (wide(block) + wide(other)).astype(BF)
 
+    low = jnp.concatenate([zero_rims[:HB], low], axis=0)
+    high = jnp.concatenate([zero_rims[HB:], high], axis=0)
     rim = jnp.where(row_y == 0, low, high)
-    one = exchanged(jnp.concatenate([block, rim], axis=0), mask_x=1)
-    two, three = [exchanged(block, mask_x=mask) for mask in (2, 3)]
+    one = by(jnp.concatenate([block, rim], axis=0), mask_x=1)
+    two, three = [by(block, mask_x=mask) for mask in (2, 3)]
     one, two, three, in_three = tie(one, two, three, in_three)
     rim = one[size:]
     block = ((wide(block) + wide(one[:size])) + (wide(two) + wide(three))).astype(BF)
 
     rim = jnp.where(row_y == 1, high, jnp.where(row_y == 2, low, rim))
-    three = exchanged(jnp.concatenate([block, rim], axis=0), mask_y=3)
+    three = by(jnp.concatenate([block, rim], axis=0), mask_y=3)
     rim = jnp.where(row_y % 2 == 0, high, low)
-    one = exchanged(jnp.concatenate([block, rim], axis=0), mask_y=1)
-    two = exchanged(block, mask_y=2)
+    one = by(jnp.concatenate([block, rim], axis=0), mask_y=1)
+    two = by(block, mask_y=2)
     one, two, three = tie(one, two, three)
     panel = lax.axis_index("panel")
     nothing = jnp.zeros_like(rim)
@@ -466,8 +460,11 @@
     from_prev = jnp.where(panel == 0, nothing, from_prev)
     from_next = jnp.where(row_y % 2 == 0, one[size:], three[size:])
     from_next = jnp.where(panel == lax.axis_size("panel") - 1, nothing, from_next)
+    zero_rims = by(jnp.concatenate([from_prev[:HB], from_next[:HB]], axis=0), mask_core=1)
+    from_prev = jnp.where(core == 1, from_prev[HB:], zero_rims[:HB])
+    from_next = jnp.where(core == 1, from_next[HB:], zero_rims[HB:])
     block = ordered_by_y([block, one[:size], two, three[:size]], row_y)
-    other = exchanged(block, mask_core=1)
+    other = by(block, mask_core=1)
     (grad_rows,) = call(
         last_kernel,
         [((rows_dev, width), F32)],
@@ -475,7 +472,7 @@
         flops=10**8,
         mib=8,
     )
-    block = joined(wide(block), wide(other), core)
+    block = wide(jnp.where(core == 1, block, other))
     return (new_rows, grad_rows, block.reshape(9, width, width))
 
 

time: 88.9 us -> 114 us (1.28)
  starting transfers between devices: 48.4 us -> 60.3 us
  waiting for transfers between devices: 7.89 us -> 17.2 us
  local copies, waits for them, and re-layouts: 1.71 us -> 4.65 us
    ppermute x22 -> x24, starting transfers between devices: 44 us -> 55.8 us  [exchanged(): return lax.ppermute(block, ('region', 'panel'), route)]
    ppermute x22 -> x24, waiting for transfers between devices: 7.89 us -> 17.2 us  [exchanged(): return lax.ppermute(block, ('region', 'panel'), route)]
    unnamed x20 -> x24, local copies, waits for them, and re-layouts: 1.67 us -> 4.59 us
  transfers between devices with their start and end apart: 24 -> 26, of which waited for: 6 -> 6; matrix products, arithmetic and copies ran while one was open for 0% -> 0% of each run, Pallas kernels for 22% -> 17%
where the time goes in v9:
time: 114 us; the launch traced here: 113 us
  starting transfers between devices  60.3 us (53%)
  Pallas kernels  28.5 us (25%)
  waiting for transfers between devices  17.2 us (15%)
  local copies, waits for them, and re-layouts  4.65 us (4%)
  other arithmetic  1.34 us (1%)
  between operations  1.26 us (1%)
    ppermute x24, starting transfers between devices, exchanged(): return lax.ppermute(block, ('region', 'panel'), route)  55.8 us
    pallas_call x9, Pallas kernels, call(): pl.pallas_call(kernel, out_shape=[jax.ShapeDtypeStruct(shape, kind) for s...  28.5 us
    ppermute x24, waiting for transfers between devices, exchanged(): return lax.ppermute(block, ('region', 'panel'), route)  17.2 us
    unnamed x24, local copies, waits for them, and re-layouts  4.59 us
    ppermute x2, starting transfers between devices, shifted(): return lax.ppermute(array, 'panel', pairs)  4.48 us
  transfers between devices with their start and end apart: 26, of which 6 were waited for; matrix products, arithmetic and copies ran while one was open for 0% of the time, Pallas kernels for 17%

profile of v9, /device:TPU:1, one launch (start us, length us, event | category | flops | bytes accessed | tf_op | source)
XLA Modules:
  0.0 113.2 jit_solution(12828431806939514312)
XLA Ops:
  0.6 0.0 copy-start
  0.6 0.7 copy-done
  1.3 0.9 copy-done.4
  2.3 0.4 shard_map.103
  2.7 3.3 %collective-permute-start.1 = (bf16[128,256]{1,0:T(8,128)(2,1)S(1)}, bf16[128,256]{1,0:T(8,128)(2,1)S(1)}, u32[]{:S(2)}, u32[]{:S(2)}) collective-permute-start(bf16[128,256]{1,0:T(8,128)(2,1)S(1)} %get-tuple-element.62.bound_t_ref), channel_id=1, source_target_pairs={{0,8},{1,9},{2,10},{3,11},{4,12},{5,13},{6,14},{7,15},{8,0},{9,1},... | collective-permute-start | bytes 196616 | tf_op jit(solution)/shard_map/ppermute | solution.py:287
  6.0 0.0 collective-permute-start.2
  6.0 2.9 %collective-permute-start.3 = (bf16[128,256]{1,0:T(8,128)(2,1)S(1)}, bf16[128,256]{1,0:T(8,128)(2,1)S(1)}, u32[]{:S(2)}, u32[]{:S(2)}) collective-permute-start(bf16[128,256]{1,0:T(8,128)(2,1)S(1)} %get-tuple-element.62.bound_t_ref), channel_id=1, source_target_pairs={{0,32},{1,33},{2,34},{3,35},{4,36},{5,37},{6,38},{7,39},{8,40},{9,... | collective-permute-start | bytes 196616 | tf_op jit(solution)/shard_map/ppermute | solution.py:287
  9.0 3.2 %collective-permute-start.4 = (bf16[64,128]{1,0:T(8,128)(2,1)S(1)}, bf16[64,128]{1,0:T(8,128)(2,1)S(1)}, u32[]{:S(2)}, u32[]{:S(2)}) collective-permute-start(bf16[64,128]{1,0:T(8,128)(2,1)S(1)} %get-tuple-element.68), channel_id=1, source_target_pairs={{0,1},{1,2},{2,3},{3,4},{4,5},{5,6},{6,7},{8,9},{9,10},{10,11},{11... | collective-permute-start | bytes 49160 | tf_op jit(solution)/shard_map/ppermute | solution.py:293
  12.2 1.3 %collective-permute-start.5 = (bf16[64,128]{1,0:T(8,128)(2,1)S(1)}, bf16[64,128]{1,0:T(8,128)(2,1)S(1)}, u32[]{:S(2)}, u32[]{:S(2)}) collective-permute-start(bf16[64,128]{1,0:T(8,128)(2,1)S(1)} %get-tuple-element.69), channel_id=1, source_target_pairs={{1,0},{2,1},{3,2},{4,3},{5,4},{6,5},{7,6},{9,8},{10,9},{11,10},{12... | collective-permute-start | bytes 49160 | tf_op jit(solution)/shard_map/ppermute | solution.py:293
  13.5 0.0 copy-start.2
  13.5 0.0 copy-start.3
  13.5 1.9 %shard_map.105 = (bf16[128,3072]{1,0:T(8,128)(2,1)S(1)}, bf16[128,3072]{1,0:T(8,128)(2,1)S(1)}) custom-call(bf16[128,1024]{1,0:T(8,128)(2,1)S(1)} %get-tuple-element.61.lat_t_ref, s32[2,3072]{1,0:T(2,128)S(1)} %copy-done.8), custom_call_target="tpu_custom_call" | custom-call | flops 4000000000 | bytes 4000000 | tf_op jit(solution)/shard_map/pallas_call | solution.py:267
  15.4 0.0 collective-permute-done.4.before_ref
  15.4 4.5 %collective-permute-start = (bf16[128,256]{1,0:T(8,128)(2,1)S(1)}, bf16[128,256]{1,0:T(8,128)(2,1)S(1)}, u32[]{:S(2)}, u32[]{:S(2)}) collective-permute-start(bf16[128,256]{1,0:T(8,128)(2,1)S(1)} %get-tuple-element.62.bound_t_ref), channel_id=1, source_target_pairs={{0,64},{1,65},{2,66},{3,67},{4,68},{5,69},{6,70},{7,71},{8,72},{9,... | collective-permute-start | bytes 196616 | tf_op jit(solution)/shard_map/ppermute | solution.py:287
  19.9 0.0 copy-start.7
  19.9 0.0 copy-start.9
  19.9 4.5 %shard_map.106 = (bf16[128,3072]{1,0:T(8,128)(2,1)S(1)}, f32[128,3072]{1,0:T(8,128)S(1)}, bf16[1024,128]{1,0:T(8,128)(2,1)S(1)}) custom-call(bf16[64,128]{1,0:T(8,128)(2,1)S(1)} %collective-permute-done.4.before_ref, bf16[64,128]{1,0:T(8,128)(2,1)S(1)} %collective-permute-done.5.after_ref, bf16[128,3072]{1,0:T(8,128)(2,1)S(1)} %get-tuple-element.73.own_ref, ...), custom_call_target="tpu_custom_call" | custom-call | flops 3000000000 | bytes 4000000 | tf_op jit(solution)/shard_map/pallas_call | solution.py:267
  24.4 0.0 copy-start.1
  24.4 0.0 copy-start.5
  24.4 0.0 copy-start.6
  24.5 0.0 collective-permute-done.2.far1_ref
  24.5 0.0 collective-permute-done.3.far2_ref
  24.5 4.4 %shard_map.104 = (bf16[256,6144]{1,0:T(8,128)(2,1)S(1)}, f32[128,6144]{1,0:T(8,128)S(1)}, f32[256,128]{1,0:T(8,128)S(1)}) custom-call(s32[1,4]{1,0:T(1,128)S(1)} %copy-done.9, bf16[128,256]{1,0:T(8,128)(2,1)S(1)} %get-tuple-element.62.bound_t_ref, bf16[128,256]{1,0:T(8,128)(2,1)S(1)} %collective-permute-done.1.far0_ref, ...), custom_call_target="tpu_custom_call" | custom-call | flops 3000000000 | bytes 4000000 | tf_op jit(solution)/shard_map/pallas_call | solution.py:267
  28.9 0.0 collective-permute-done.far3_ref
  28.9 8.3 %shard_map.107 = (bf16[1024,128]{1,0:T(8,128)(2,1)}, f32[1152,128]{1,0:T(8,128)S(1)}, bf16[1152,128]{1,0:T(8,128)(2,1)S(1)}, bf16[128,3072]{1,0:T(8,128)(2,1)S(1...) custom-call(s32[1,4]{1,0:T(1,128)S(1)} %copy-done.9, bf16[1024,128]{1,0:T(8,128)(2,1)S(1)} %copy-done.5, ...), custom_call_target="tpu_custom_call" | custom-call | flops 6000000000 | bytes 4000000 | tf_op jit(solution)/shard_map/pallas_call | solution.py:267
  37.3 1.3 %copy-done.10 = bf16[128,8192]{1,0:T(8,128)(2,1)} copy-done((bf16[128,8192]{1,0:T(8,128)(2,1)}, bf16[128,8192]{1,0:T(8,128)(2,1)S(1)}, u32[]{:S(2)}) %copy-start.10) | copy-done | bytes 2097176
  38.6 1.3 %collective-permute-start.6 = (bf16[1152,128]{1,0:T(8,128)(2,1)S(1)}, bf16[1152,128]{1,0:T(8,128)(2,1)S(1)}, u32[]{:S(2)}, u32[]{:S(2)}) collective-permute-start(bf16[1152,128]{1,0:T(8,128)(2,1)S(1)} %get-tuple-element.80), channel_id=1, source_target_pairs={{0,8},{1,9},{2,10},{3,11},{4,12},{5,13},{6,14},{7,15},{16,24},{17,... | collective-permute-start | bytes 884744 | tf_op jit(solution)/shard_map/ppermute | solution.py:287
  39.9 1.6 %copy-done.11 = bf16[128,8192]{1,0:T(8,128)(2,1)S(1)} copy-done((bf16[128,8192]{1,0:T(8,128)(2,1)S(1)}, bf16[128,8192]{1,0:T(8,128)(2,1)}, u32[]{:S(2)}) %copy-start.11) | copy-done | bytes 2097176
  41.5 2.8 %shard_map.108 = (bf16[256,128]{1,0:T(8,128)(2,1)S(1)}, bf16[256,128]{1,0:T(8,128)(2,1)S(1)}, bf16[256,128]{1,0:T(8,128)(2,1)S(1)}, bf16[256,128]{1,0:T(8,128)(2,1)S(1)}, f32[256,128]{1,0:T(8,128)S(1)}) custom-call(bf16[9,128,128]{2,1,0:T(8,128)(2,1)S(1)} %copy-done.3, s32[2,8192]{1,0:T(2,128)S(1)} %copy-done.7, bf16[128,8192]{1,0:T(8,128)(2,1)S(1)} %copy-done.11), custom_call_target="tpu_custom_call" | custom-call | flops 2000000000 | bytes 4000000 | tf_op jit(solution)/shard_map/pallas_call | solution.py:267
  44.3 0.1 convert_add_fusion
  44.5 4.0 %collective-permute-start.7 = (bf16[288,128]{1,0:T(8,128)(2,1)S(1)}, bf16[288,128]{1,0:T(8,128)(2,1)S(1)}, u32[]{:S(2)}, u32[]{:S(2)}) collective-permute-start(bf16[288,128]{1,0:T(8,128)(2,1)S(1)} %get-tuple-element.121), channel_id=1, source_target_pairs={{8,9},{9,8},{10,11},{11,10},{12,13},{13,12},{14,15},{15,14},{24,25... | collective-permute-start | bytes 221192 | tf_op jit(solution)/shard_map/ppermute | solution.py:287
  48.5 4.5 %collective-permute-start.8 = (bf16[288,128]{1,0:T(8,128)(2,1)S(1)}, bf16[288,128]{1,0:T(8,128)(2,1)S(1)}, u32[]{:S(2)}, u32[]{:S(2)}) collective-permute-start(bf16[288,128]{1,0:T(8,128)(2,1)S(1)} %get-tuple-element.120), channel_id=1, source_target_pairs={{8,10},{9,11},{10,8},{11,9},{12,14},{13,15},{14,12},{15,13},{24,26... | collective-permute-start | bytes 221192 | tf_op jit(solution)/shard_map/ppermute | solution.py:287
  53.0 1.9 %collective-permute-start.9 = (bf16[288,128]{1,0:T(8,128)(2,1)S(1)}, bf16[288,128]{1,0:T(8,128)(2,1)S(1)}, u32[]{:S(2)}, u32[]{:S(2)}) collective-permute-start(bf16[288,128]{1,0:T(8,128)(2,1)S(1)} %get-tuple-element.119), channel_id=1, source_target_pairs={{8,11},{9,10},{10,9},{11,8},{12,15},{13,14},{14,13},{15,12},{24,27... | collective-permute-start | bytes 221192 | tf_op jit(solution)/shard_map/ppermute | solution.py:287
  54.9 0.8 collective-permute-start.11
  55.8 1.3 %collective-permute-start.13 = (bf16[512,128]{1,0:T(8,128)(2,1)S(1)}, bf16[512,128]{1,0:T(8,128)(2,1)S(1)}, u32[]{:S(2)}, u32[]{:S(2)}) collective-permute-start(bf16[512,128]{1,0:T(8,128)(2,1)S(1)} %pad_maximum_fusion.1), channel_id=1, source_target_pairs={{0,32},{1,33},{2,34},{3,35},{4,36},{5,37},{6,38},{7,39},{8,40},{9,... | collective-permute-start | bytes 393224 | tf_op jit(solution)/shard_map/ppermute | solution.py:287
  57.0 0.0 collective-permute-done.8
  57.0 2.3 %collective-permute-done.9 = bf16[288,128]{1,0:T(8,128)(2,1)S(1)} collective-permute-done((bf16[288,128]{1,0:T(8,128)(2,1)S(1)}, bf16[288,128]{1,0:T(8,128)(2,1)S(1)}, u32[]{:S(2)}, u32[]{:S(2)}) %collective-permute-start.9) | collective-permute-done | bytes 73760 | tf_op jit(solution)/shard_map/ppermute | solution.py:287
  59.4 2.6 %collective-permute-start.10 = (bf16[288,128]{1,0:T(8,128)(2,1)S(1)}, bf16[288,128]{1,0:T(8,128)(2,1)S(1)}, u32[]{:S(2)}, u32[]{:S(2)}) collective-permute-start(bf16[288,128]{1,0:T(8,128)(2,1)S(1)} %add_convert_fusion.4), channel_id=1, source_target_pairs={{8,24},{9,25},{10,26},{11,27},{12,28},{13,29},{14,30},{15,31},{24,... | collective-permute-start | bytes 221192 | tf_op jit(solution)/shard_map/ppermute | solution.py:287
  62.0 2.6 %shard_map.109 = (f32[1024,128]{1,0:T(8,128)S(1)}, bf16[64,128]{1,0:T(8,128)(2,1)S(1)}, bf16[64,128]{1,0:T(8,128)(2,1)S(1)}) custom-call(bf16[9,128,128]{2,1,0:T(8,128)(2,1)S(1)} %copy-done.3, s32[2,3072]{1,0:T(2,128)S(1)} %copy-done.8, bf16[128,3072]{1,0:T(8,128)(2,1)S(1)} %get-tuple-element.91.dm_ref), custom_call_target="tpu_custom_call" | custom-call | flops 2000000000 | bytes 4000000 | tf_op jit(solution)/shard_map/pallas_call | solution.py:267
  64.7 0.0 collective-permute-done.10
  64.7 1.3 %collective-permute-start.14 = (bf16[128,128]{1,0:T(8,128)(2,1)S(1)}, bf16[128,128]{1,0:T(8,128)(2,1)S(1)}, u32[]{:S(2)}, u32[]{:S(2)}) collective-permute-start(bf16[128,128]{1,0:T(8,128)(2,1)S(1)} %pad_maximum_fusion.6), channel_id=1, source_target_pairs={{0,8},{1,9},{2,10},{3,11},{4,12},{5,13},{6,14},{7,15},{16,24},{17,... | collective-permute-start | bytes 98312 | tf_op jit(solution)/shard_map/ppermute | solution.py:287
  66.0 3.1 %collective-permute-start.12 = (bf16[288,128]{1,0:T(8,128)(2,1)S(1)}, bf16[288,128]{1,0:T(8,128)(2,1)S(1)}, u32[]{:S(2)}, u32[]{:S(2)}) collective-permute-start(bf16[288,128]{1,0:T(8,128)(2,1)S(1)} %add_convert_fusion.3), channel_id=1, source_target_pairs={{8,40},{9,41},{10,42},{11,43},{12,44},{13,45},{14,46},{15,47},{24,... | collective-permute-start | bytes 221192 | tf_op jit(solution)/shard_map/ppermute | solution.py:287
  69.1 2.3 %shard_map.110.part_ref = f32[1024,128]{1,0:T(8,128)S(1)} custom-call(bf16[9,128,128]{2,1,0:T(8,128)(2,1)S(1)} %copy-done.3, s32[2,3072]{1,0:T(2,128)S(1)} %copy-done.8, bf16[128,3072]{1,0:T(8,128)(2,1)S(1)} %get-tuple-element.91.dm_ref, bf16[1024,128]{1,0:T(8,128)(2,1)S(1)} %get-tuple-element.97.dn_ref, bf16[1024,128]{1,0:T(8,128)(2,1)S(1)} %copy-done.6, ...), custom_call_target="tpu_custom_call" | custom-call | flops 2000000000 | bytes 4000000 | tf_op jit(solution)/shard_map/pallas_call | solution.py:267
  71.4 0.0 collective-permute-done.14
  71.4 1.4 %collective-permute-done.12 = bf16[288,128]{1,0:T(8,128)(2,1)S(1)} collective-permute-done((bf16[288,128]{1,0:T(8,128)(2,1)S(1)}, bf16[288,128]{1,0:T(8,128)(2,1)S(1)}, u32[]{:S(2)}, u32[]{:S(2)}) %collective-permute-start.12) | collective-permute-done | bytes 73760 | tf_op jit(solution)/shard_map/ppermute | solution.py:287
  72.8 2.2 %collective-permute-start.15 = (bf16[288,128]{1,0:T(8,128)(2,1)S(1)}, bf16[288,128]{1,0:T(8,128)(2,1)S(1)}, u32[]{:S(2)}, u32[]{:S(2)}) collective-permute-start(bf16[288,128]{1,0:T(8,128)(2,1)S(1)} %add_convert_fusion.2), channel_id=1, source_target_pairs={{8,104},{9,105},{10,106},{11,107},{12,108},{13,109},{14,110},{15,1... | collective-permute-start | bytes 221192 | tf_op jit(solution)/shard_map/ppermute | solution.py:287
  75.0 5.0 %collective-permute-done.15 = bf16[288,128]{1,0:T(8,128)(2,1)S(1)} collective-permute-done((bf16[288,128]{1,0:T(8,128)(2,1)S(1)}, bf16[288,128]{1,0:T(8,128)(2,1)S(1)}, u32[]{:S(2)}, u32[]{:S(2)}) %collective-permute-start.15) | collective-permute-done | bytes 73760 | tf_op jit(solution)/shard_map/ppermute | solution.py:287
  80.1 4.7 %collective-permute-start.18 = (bf16[288,128]{1,0:T(8,128)(2,1)S(1)}, bf16[288,128]{1,0:T(8,128)(2,1)S(1)}, u32[]{:S(2)}, u32[]{:S(2)}) collective-permute-start(bf16[288,128]{1,0:T(8,128)(2,1)S(1)} %add_convert_fusion.1), channel_id=1, source_target_pairs={{8,136},{9,137},{10,138},{11,139},{12,140},{13,141},{14,142},{15,1... | collective-permute-start | bytes 221192 | tf_op jit(solution)/shard_map/ppermute | solution.py:287
  84.7 2.9 %collective-permute-start.19 = (bf16[288,128]{1,0:T(8,128)(2,1)S(1)}, bf16[288,128]{1,0:T(8,128)(2,1)S(1)}, u32[]{:S(2)}, u32[]{:S(2)}) collective-permute-start(bf16[288,128]{1,0:T(8,128)(2,1)S(1)} %add_convert_fusion.1), channel_id=1, source_target_pairs={{8,140},{9,141},{10,142},{11,143},{12,136},{13,137},{14,138},{15,1... | collective-permute-start | bytes 221192 | tf_op jit(solution)/shard_map/ppermute | solution.py:287
  87.6 1.9 %collective-permute-start.17 = (bf16[416,128]{1,0:T(8,128)(2,1)S(1)}, bf16[416,128]{1,0:T(8,128)(2,1)S(1)}, u32[]{:S(2)}, u32[]{:S(2)}) collective-permute-start(bf16[416,128]{1,0:T(8,128)(2,1)S(1)} %pad_maximum_fusion.4), channel_id=1, source_target_pairs={{8,12},{9,13},{10,14},{11,15},{12,8},{13,9},{14,10},{15,11},{24,28... | collective-permute-start | bytes 319496 | tf_op jit(solution)/shard_map/ppermute | solution.py:287
  89.6 1.0 collective-permute-start.20
  90.6 4.3 %collective-permute-done.20.in3_ref = bf16[256,128]{1,0:T(8,128)(2,1)S(1)} collective-permute-done((bf16[256,128]{1,0:T(8,128)(2,1)S(1)}, bf16[256,128]{1,0:T(8,128)(2,1)S(1)}, u32[]{:S(2)}, u32[]{:S(2)}) %collective-permute-start.20) | collective-permute-done | bytes 65568 | tf_op jit(solution)/shard_map/ppermute | solution.py:287
  95.0 1.9 %collective-permute-start.21 = (bf16[416,128]{1,0:T(8,128)(2,1)S(1)}, bf16[416,128]{1,0:T(8,128)(2,1)S(1)}, u32[]{:S(2)}, u32[]{:S(2)}) collective-permute-start(bf16[416,128]{1,0:T(8,128)(2,1)S(1)} %get-tuple-element.131), channel_id=1, source_target_pairs={{8,9},{9,8},{10,11},{11,10},{12,13},{13,12},{14,15},{15,14},{24,25... | collective-permute-start | bytes 319496 | tf_op jit(solution)/shard_map/ppermute | solution.py:287
  97.0 3.8 %collective-permute-start.23 = (bf16[416,128]{1,0:T(8,128)(2,1)S(1)}, bf16[416,128]{1,0:T(8,128)(2,1)S(1)}, u32[]{:S(2)}, u32[]{:S(2)}) collective-permute-start(bf16[416,128]{1,0:T(8,128)(2,1)S(1)} %get-tuple-element.130), channel_id=1, source_target_pairs={{8,11},{9,10},{10,9},{11,8},{12,15},{13,14},{14,13},{15,12},{24,27... | collective-permute-start | bytes 319496 | tf_op jit(solution)/shard_map/ppermute | solution.py:287
  100.8 3.2 %collective-permute-start.22 = (bf16[288,128]{1,0:T(8,128)(2,1)S(1)}, bf16[288,128]{1,0:T(8,128)(2,1)S(1)}, u32[]{:S(2)}, u32[]{:S(2)}) collective-permute-start(bf16[288,128]{1,0:T(8,128)(2,1)S(1)} %add_convert_fusion), channel_id=1, source_target_pairs={{8,10},{9,11},{10,8},{11,9},{12,14},{13,15},{14,12},{15,13},{24,26... | collective-permute-start | bytes 221192 | tf_op jit(solution)/shard_map/ppermute | solution.py:287
  104.1 3.4 %collective-permute-done.22 = bf16[288,128]{1,0:T(8,128)(2,1)S(1)} collective-permute-done((bf16[288,128]{1,0:T(8,128)(2,1)S(1)}, bf16[288,128]{1,0:T(8,128)(2,1)S(1)}, u32[]{:S(2)}, u32[]{:S(2)}) %collective-permute-start.22) | collective-permute-done | bytes 73760 | tf_op jit(solution)/shard_map/ppermute | solution.py:287
  107.4 0.0 collective-permute-done.21
  107.4 0.0 collective-permute-done.23
  107.5 1.3 %collective-permute-start.25 = (bf16[1152,128]{1,0:T(8,128)(2,1)S(1)}, bf16[1152,128]{1,0:T(8,128)(2,1)S(1)}, u32[]{:S(2)}, u32[]{:S(2)}) collective-permute-start(bf16[1152,128]{1,0:T(8,128)(2,1)S(1)} %pad_maximum_fusion), channel_id=1, source_target_pairs={{8,0},{9,1},{10,2},{11,3},{12,4},{13,5},{14,6},{15,7},{24,16},{25,... | collective-permute-start | bytes 884744 | tf_op jit(solution)/shard_map/ppermute | solution.py:287
  108.9 1.3 %collective-permute-start.24 = (bf16[128,128]{1,0:T(8,128)(2,1)S(1)}, bf16[128,128]{1,0:T(8,128)(2,1)S(1)}, u32[]{:S(2)}, u32[]{:S(2)}) collective-permute-start(bf16[128,128]{1,0:T(8,128)(2,1)S(1)} %pad_maximum_fusion.8), channel_id=1, source_target_pairs={{8,0},{9,1},{10,2},{11,3},{12,4},{13,5},{14,6},{15,7},{24,16},{25,... | collective-permute-start | bytes 98312 | tf_op jit(solution)/shard_map/ppermute | solution.py:287
  110.2 0.8 collective-permute-done.24
  111.0 1.2 %shard_map.111 = f32[1024,128]{1,0:T(8,128)} custom-call(f32[1024,128]{1,0:T(8,128)S(1)} %shard_map.110.part_ref, f32[256,128]{1,0:T(8,128)S(1)} %get-tuple-element.104.own_ref, bf16[256,128]{1,0:T(8,128)(2,1)S(1)} %collective-permute-done.16.in0_ref, bf16[256,128]{1,0:T(8,128)(2,1)S(1)} %collective-permute-done.11.in1_ref, ...), custom_call_target="tpu_custom_call" | custom-call | flops 100000000 | bytes 4000000 | tf_op jit(solution)/shard_map/pallas_call | solution.py:267
  112.3 0.1 broadcast_select_fusion
  112.4 0.9 convert.1
  (45 shorter events, 0.4 us)
Async XLA Ops:
  0.6 0.7 copy-start
  1.3 0.9 copy-start.4
  2.3 11.2 %copy-start.8 = (s32[2,3072]{1,0:T(2,128)S(1)}, s32[2,3072]{1,0:T(2,128)}, u32[]{:S(2)}) copy-start(s32[2,3072]{1,0:T(2,128)} %edges_ref.9) | copy-start | bytes 73732
  2.7 21.7 %collective-permute-start.1 = (bf16[128,256]{1,0:T(8,128)(2,1)S(1)}, bf16[128,256]{1,0:T(8,128)(2,1)S(1)}, u32[]{:S(2)}, u32[]{:S(2)}) collective-permute-start(bf16[128,256]{1,0:T(8,128)(2,1)S(1)} %get-tuple-element.62.bound_t_ref), channel_id=1, source_target_pairs={{0,8},{1,9},{2,10},{3,11},{4,12},{5,13},{6,14},{7,15},{8,0},{9,1},... | collective-permute-start | bytes 196616 | tf_op jit(solution)/shard_map/ppermute | solution.py:287
  6.0 18.4 %collective-permute-start.2 = (bf16[128,256]{1,0:T(8,128)(2,1)S(1)}, bf16[128,256]{1,0:T(8,128)(2,1)S(1)}, u32[]{:S(2)}, u32[]{:S(2)}) collective-permute-start(bf16[128,256]{1,0:T(8,128)(2,1)S(1)} %get-tuple-element.62.bound_t_ref), channel_id=1, source_target_pairs={{0,16},{1,17},{2,18},{3,19},{4,20},{5,21},{6,22},{7,23},{8,24},{9,... | collective-permute-start | bytes 196616 | tf_op jit(solution)/shard_map/ppermute | solution.py:287
  6.0 18.4 %collective-permute-start.3 = (bf16[128,256]{1,0:T(8,128)(2,1)S(1)}, bf16[128,256]{1,0:T(8,128)(2,1)S(1)}, u32[]{:S(2)}, u32[]{:S(2)}) collective-permute-start(bf16[128,256]{1,0:T(8,128)(2,1)S(1)} %get-tuple-element.62.bound_t_ref), channel_id=1, source_target_pairs={{0,32},{1,33},{2,34},{3,35},{4,36},{5,37},{6,38},{7,39},{8,40},{9,... | collective-permute-start | bytes 196616 | tf_op jit(solution)/shard_map/ppermute | solution.py:287
  9.0 6.4 %collective-permute-start.4 = (bf16[64,128]{1,0:T(8,128)(2,1)S(1)}, bf16[64,128]{1,0:T(8,128)(2,1)S(1)}, u32[]{:S(2)}, u32[]{:S(2)}) collective-permute-start(bf16[64,128]{1,0:T(8,128)(2,1)S(1)} %get-tuple-element.68), channel_id=1, source_target_pairs={{0,1},{1,2},{2,3},{3,4},{4,5},{5,6},{6,7},{8,9},{9,10},{10,11},{11... | collective-permute-start | bytes 49160 | tf_op jit(solution)/shard_map/ppermute | solution.py:293
  12.2 7.7 %collective-permute-start.5 = (bf16[64,128]{1,0:T(8,128)(2,1)S(1)}, bf16[64,128]{1,0:T(8,128)(2,1)S(1)}, u32[]{:S(2)}, u32[]{:S(2)}) collective-permute-start(bf16[64,128]{1,0:T(8,128)(2,1)S(1)} %get-tuple-element.69), channel_id=1, source_target_pairs={{1,0},{2,1},{3,2},{4,3},{5,4},{6,5},{7,6},{9,8},{10,9},{11,10},{12... | collective-permute-start | bytes 49160 | tf_op jit(solution)/shard_map/ppermute | solution.py:293
  13.5 6.4 %copy-start.2 = (bf16[3072,128]{1,0:T(8,128)(2,1)S(1)}, bf16[3072,128]{1,0:T(8,128)(2,1)}, u32[]{:S(2)}) copy-start(bf16[3072,128]{1,0:T(8,128)(2,1)} %feats_ref.3) | copy-start | bytes 2359300
  13.5 6.4 %copy-start.3 = (bf16[9,128,128]{2,1,0:T(8,128)(2,1)S(1)}, bf16[9,128,128]{2,1,0:T(8,128)(2,1)}, u32[]{:S(2)}) copy-start(bf16[9,128,128]{2,1,0:T(8,128)(2,1)} %w_ref.11) | copy-start | bytes 884740
  15.4 13.5 %collective-permute-start = (bf16[128,256]{1,0:T(8,128)(2,1)S(1)}, bf16[128,256]{1,0:T(8,128)(2,1)S(1)}, u32[]{:S(2)}, u32[]{:S(2)}) collective-permute-start(bf16[128,256]{1,0:T(8,128)(2,1)S(1)} %get-tuple-element.62.bound_t_ref), channel_id=1, source_target_pairs={{0,64},{1,65},{2,66},{3,67},{4,68},{5,69},{6,70},{7,71},{8,72},{9,... | collective-permute-start | bytes 196616 | tf_op jit(solution)/shard_map/ppermute | solution.py:287
  19.9 4.6 %copy-start.7 = (s32[2,8192]{1,0:T(2,128)S(1)}, s32[2,8192]{1,0:T(2,128)}, u32[]{:S(2)}) copy-start(s32[2,8192]{1,0:T(2,128)} %contacts_ref.5) | copy-start | bytes 196612
  19.9 4.6 %copy-start.9 = (s32[1,4]{1,0:T(1,128)S(1)}, s32[1,4]{1,0:T(1,128)}, u32[]{:S(2)}) copy-start(s32[1,4]{1,0:T(1,128)} %counts_ref.3) | copy-start | bytes 52
  24.4 4.5 %copy-start.1 = (s32[256]{0:T(256)S(1)}, s32[256]{0:T(256)}, u32[]{:S(2)}) copy-start(s32[256]{0:T(256)} %param.13) | copy-start | bytes 3076
  24.4 4.5 %copy-start.5 = (bf16[1024,128]{1,0:T(8,128)(2,1)S(1)}, bf16[1024,128]{1,0:T(8,128)(2,1)}, u32[]{:S(2)}) copy-start(bf16[1024,128]{1,0:T(8,128)(2,1)} %lat_ref.1) | copy-start | bytes 786436
  24.4 4.5 %copy-start.6 = (bf16[1024,128]{1,0:T(8,128)(2,1)S(1)}, bf16[1024,128]{1,0:T(8,128)(2,1)}, u32[]{:S(2)}) copy-start(bf16[1024,128]{1,0:T(8,128)(2,1)} %cot_ref.3) | copy-start | bytes 786436
  37.3 1.3 %copy-start.10 = (bf16[128,8192]{1,0:T(8,128)(2,1)}, bf16[128,8192]{1,0:T(8,128)(2,1)S(1)}, u32[]{:S(2)}) copy-start(bf16[128,8192]{1,0:T(8,128)(2,1)S(1)} %get-tuple-element.81.dc_ref) | copy-start | bytes 6291460
  38.6 5.7 %collective-permute-start.6 = (bf16[1152,128]{1,0:T(8,128)(2,1)S(1)}, bf16[1152,128]{1,0:T(8,128)(2,1)S(1)}, u32[]{:S(2)}, u32[]{:S(2)}) collective-permute-start(bf16[1152,128]{1,0:T(8,128)(2,1)S(1)} %get-tuple-element.80), channel_id=1, source_target_pairs={{0,8},{1,9},{2,10},{3,11},{4,12},{5,13},{6,14},{7,15},{16,24},{17,... | collective-permute-start | bytes 884744 | tf_op jit(solution)/shard_map/ppermute | solution.py:287
  39.9 1.6 %copy-start.11 = (bf16[128,8192]{1,0:T(8,128)(2,1)S(1)}, bf16[128,8192]{1,0:T(8,128)(2,1)}, u32[]{:S(2)}) copy-start(bf16[128,8192]{1,0:T(8,128)(2,1)} %copy-done.10) | copy-start | bytes 6291460
  44.5 12.6 %collective-permute-start.7 = (bf16[288,128]{1,0:T(8,128)(2,1)S(1)}, bf16[288,128]{1,0:T(8,128)(2,1)S(1)}, u32[]{:S(2)}, u32[]{:S(2)}) collective-permute-start(bf16[288,128]{1,0:T(8,128)(2,1)S(1)} %get-tuple-element.121), channel_id=1, source_target_pairs={{8,9},{9,8},{10,11},{11,10},{12,13},{13,12},{14,15},{15,14},{24,25... | collective-permute-start | bytes 221192 | tf_op jit(solution)/shard_map/ppermute | solution.py:287
  48.5 8.6 %collective-permute-start.8 = (bf16[288,128]{1,0:T(8,128)(2,1)S(1)}, bf16[288,128]{1,0:T(8,128)(2,1)S(1)}, u32[]{:S(2)}, u32[]{:S(2)}) collective-permute-start(bf16[288,128]{1,0:T(8,128)(2,1)S(1)} %get-tuple-element.120), channel_id=1, source_target_pairs={{8,10},{9,11},{10,8},{11,9},{12,14},{13,15},{14,12},{15,13},{24,26... | collective-permute-start | bytes 221192 | tf_op jit(solution)/shard_map/ppermute | solution.py:287
  53.0 6.3 %collective-permute-start.9 = (bf16[288,128]{1,0:T(8,128)(2,1)S(1)}, bf16[288,128]{1,0:T(8,128)(2,1)S(1)}, u32[]{:S(2)}, u32[]{:S(2)}) collective-permute-start(bf16[288,128]{1,0:T(8,128)(2,1)S(1)} %get-tuple-element.119), channel_id=1, source_target_pairs={{8,11},{9,10},{10,9},{11,8},{12,15},{13,14},{14,13},{15,12},{24,27... | collective-permute-start | bytes 221192 | tf_op jit(solution)/shard_map/ppermute | solution.py:287
  54.9 9.7 %collective-permute-start.11 = (bf16[256,128]{1,0:T(8,128)(2,1)S(1)}, bf16[256,128]{1,0:T(8,128)(2,1)S(1)}, u32[]{:S(2)}, u32[]{:S(2)}) collective-permute-start(bf16[256,128]{1,0:T(8,128)(2,1)S(1)} %get-tuple-element.95), channel_id=1, source_target_pairs={{0,16},{1,17},{2,18},{3,19},{4,20},{5,21},{6,22},{7,23},{8,24},{9,... | collective-permute-start | bytes 196616 | tf_op jit(solution)/shard_map/ppermute | solution.py:287
  55.8 15.6 %collective-permute-start.13 = (bf16[512,128]{1,0:T(8,128)(2,1)S(1)}, bf16[512,128]{1,0:T(8,128)(2,1)S(1)}, u32[]{:S(2)}, u32[]{:S(2)}) collective-permute-start(bf16[512,128]{1,0:T(8,128)(2,1)S(1)} %pad_maximum_fusion.1), channel_id=1, source_target_pairs={{0,32},{1,33},{2,34},{3,35},{4,36},{5,37},{6,38},{7,39},{8,40},{9,... | collective-permute-start | bytes 393224 | tf_op jit(solution)/shard_map/ppermute | solution.py:287
  57.0 18.0 %collective-permute-start.16 = (bf16[256,128]{1,0:T(8,128)(2,1)S(1)}, bf16[256,128]{1,0:T(8,128)(2,1)S(1)}, u32[]{:S(2)}, u32[]{:S(2)}) collective-permute-start(bf16[256,128]{1,0:T(8,128)(2,1)S(1)} %get-tuple-element.106), channel_id=1, source_target_pairs={{0,8},{1,9},{2,10},{3,11},{4,12},{5,13},{6,14},{7,15},{8,0},{9,1},... | collective-permute-start | bytes 196616 | tf_op jit(solution)/shard_map/ppermute | solution.py:287
  59.4 5.3 %collective-permute-start.10 = (bf16[288,128]{1,0:T(8,128)(2,1)S(1)}, bf16[288,128]{1,0:T(8,128)(2,1)S(1)}, u32[]{:S(2)}, u32[]{:S(2)}) collective-permute-start(bf16[288,128]{1,0:T(8,128)(2,1)S(1)} %add_convert_fusion.4), channel_id=1, source_target_pairs={{8,24},{9,25},{10,26},{11,27},{12,28},{13,29},{14,30},{15,31},{24,... | collective-permute-start | bytes 221192 | tf_op jit(solution)/shard_map/ppermute | solution.py:287
  64.7 6.7 %collective-permute-start.14 = (bf16[128,128]{1,0:T(8,128)(2,1)S(1)}, bf16[128,128]{1,0:T(8,128)(2,1)S(1)}, u32[]{:S(2)}, u32[]{:S(2)}) collective-permute-start(bf16[128,128]{1,0:T(8,128)(2,1)S(1)} %pad_maximum_fusion.6), channel_id=1, source_target_pairs={{0,8},{1,9},{2,10},{3,11},{4,12},{5,13},{6,14},{7,15},{16,24},{17,... | collective-permute-start | bytes 98312 | tf_op jit(solution)/shard_map/ppermute | solution.py:287
  66.0 6.8 %collective-permute-start.12 = (bf16[288,128]{1,0:T(8,128)(2,1)S(1)}, bf16[288,128]{1,0:T(8,128)(2,1)S(1)}, u32[]{:S(2)}, u32[]{:S(2)}) collective-permute-start(bf16[288,128]{1,0:T(8,128)(2,1)S(1)} %add_convert_fusion.3), channel_id=1, source_target_pairs={{8,40},{9,41},{10,42},{11,43},{12,44},{13,45},{14,46},{15,47},{24,... | collective-permute-start | bytes 221192 | tf_op jit(solution)/shard_map/ppermute | solution.py:287
  72.8 7.2 %collective-permute-start.15 = (bf16[288,128]{1,0:T(8,128)(2,1)S(1)}, bf16[288,128]{1,0:T(8,128)(2,1)S(1)}, u32[]{:S(2)}, u32[]{:S(2)}) collective-permute-start(bf16[288,128]{1,0:T(8,128)(2,1)S(1)} %add_convert_fusion.2), channel_id=1, source_target_pairs={{8,104},{9,105},{10,106},{11,107},{12,108},{13,109},{14,110},{15,1... | collective-permute-start | bytes 221192 | tf_op jit(solution)/shard_map/ppermute | solution.py:287
  80.1 14.9 %collective-permute-start.18 = (bf16[288,128]{1,0:T(8,128)(2,1)S(1)}, bf16[288,128]{1,0:T(8,128)(2,1)S(1)}, u32[]{:S(2)}, u32[]{:S(2)}) collective-permute-start(bf16[288,128]{1,0:T(8,128)(2,1)S(1)} %add_convert_fusion.1), channel_id=1, source_target_pairs={{8,136},{9,137},{10,138},{11,139},{12,140},{13,141},{14,142},{15,1... | collective-permute-start | bytes 221192 | tf_op jit(solution)/shard_map/ppermute | solution.py:287
  84.7 10.2 %collective-permute-start.19 = (bf16[288,128]{1,0:T(8,128)(2,1)S(1)}, bf16[288,128]{1,0:T(8,128)(2,1)S(1)}, u32[]{:S(2)}, u32[]{:S(2)}) collective-permute-start(bf16[288,128]{1,0:T(8,128)(2,1)S(1)} %add_convert_fusion.1), channel_id=1, source_target_pairs={{8,140},{9,141},{10,142},{11,143},{12,136},{13,137},{14,138},{15,1... | collective-permute-start | bytes 221192 | tf_op jit(solution)/shard_map/ppermute | solution.py:287
  87.6 7.3 %collective-permute-start.17 = (bf16[416,128]{1,0:T(8,128)(2,1)S(1)}, bf16[416,128]{1,0:T(8,128)(2,1)S(1)}, u32[]{:S(2)}, u32[]{:S(2)}) collective-permute-start(bf16[416,128]{1,0:T(8,128)(2,1)S(1)} %pad_maximum_fusion.4), channel_id=1, source_target_pairs={{8,12},{9,13},{10,14},{11,15},{12,8},{13,9},{14,10},{15,11},{24,28... | collective-permute-start | bytes 319496 | tf_op jit(solution)/shard_map/ppermute | solution.py:287
  89.6 5.3 %collective-permute-start.20 = (bf16[256,128]{1,0:T(8,128)(2,1)S(1)}, bf16[256,128]{1,0:T(8,128)(2,1)S(1)}, u32[]{:S(2)}, u32[]{:S(2)}) collective-permute-start(bf16[256,128]{1,0:T(8,128)(2,1)S(1)} %get-tuple-element.128), channel_id=1, source_target_pairs={{0,96},{1,97},{2,98},{3,99},{4,100},{5,101},{6,102},{7,103},{8,104... | collective-permute-start | bytes 196616 | tf_op jit(solution)/shard_map/ppermute | solution.py:287
  95.0 12.4 %collective-permute-start.21 = (bf16[416,128]{1,0:T(8,128)(2,1)S(1)}, bf16[416,128]{1,0:T(8,128)(2,1)S(1)}, u32[]{:S(2)}, u32[]{:S(2)}) collective-permute-start(bf16[416,128]{1,0:T(8,128)(2,1)S(1)} %get-tuple-element.131), channel_id=1, source_target_pairs={{8,9},{9,8},{10,11},{11,10},{12,13},{13,12},{14,15},{15,14},{24,25... | collective-permute-start | bytes 319496 | tf_op jit(solution)/shard_map/ppermute | solution.py:287
  97.0 10.5 %collective-permute-start.23 = (bf16[416,128]{1,0:T(8,128)(2,1)S(1)}, bf16[416,128]{1,0:T(8,128)(2,1)S(1)}, u32[]{:S(2)}, u32[]{:S(2)}) collective-permute-start(bf16[416,128]{1,0:T(8,128)(2,1)S(1)} %get-tuple-element.130), channel_id=1, source_target_pairs={{8,11},{9,10},{10,9},{11,8},{12,15},{13,14},{14,13},{15,12},{24,27... | collective-permute-start | bytes 319496 | tf_op jit(solution)/shard_map/ppermute | solution.py:287
  100.8 6.6 %collective-permute-start.22 = (bf16[288,128]{1,0:T(8,128)(2,1)S(1)}, bf16[288,128]{1,0:T(8,128)(2,1)S(1)}, u32[]{:S(2)}, u32[]{:S(2)}) collective-permute-start(bf16[288,128]{1,0:T(8,128)(2,1)S(1)} %add_convert_fusion), channel_id=1, source_target_pairs={{8,10},{9,11},{10,8},{11,9},{12,14},{13,15},{14,12},{15,13},{24,26... | collective-permute-start | bytes 221192 | tf_op jit(solution)/shard_map/ppermute | solution.py:287
  107.5 4.8 %collective-permute-start.25 = (bf16[1152,128]{1,0:T(8,128)(2,1)S(1)}, bf16[1152,128]{1,0:T(8,128)(2,1)S(1)}, u32[]{:S(2)}, u32[]{:S(2)}) collective-permute-start(bf16[1152,128]{1,0:T(8,128)(2,1)S(1)} %pad_maximum_fusion), channel_id=1, source_target_pairs={{8,0},{9,1},{10,2},{11,3},{12,4},{13,5},{14,6},{15,7},{24,16},{25,... | collective-permute-start | bytes 884744 | tf_op jit(solution)/shard_map/ppermute | solution.py:287
  108.9 2.1 %collective-permute-start.24 = (bf16[128,128]{1,0:T(8,128)(2,1)S(1)}, bf16[128,128]{1,0:T(8,128)(2,1)S(1)}, u32[]{:S(2)}, u32[]{:S(2)}) collective-permute-start(bf16[128,128]{1,0:T(8,128)(2,1)S(1)} %pad_maximum_fusion.8), channel_id=1, source_target_pairs={{8,0},{9,1},{10,2},{11,3},{12,4},{13,5},{14,6},{15,7},{24,16},{25,... | collective-permute-start | bytes 98312 | tf_op jit(solution)/shard_map/ppermute | solution.py:287

commit v10 on v7

--- a/solution.py
+++ b/solution.py
@@ -287,15 +287,11 @@
     return lax.ppermute(block, ("region", "panel"), route)
 
 
-def swapped(block, bit):
-    size = lax.axis_size("region")
-    return lax.ppermute(block, "region", [(i, i ^ (1 << bit)) for i in range(size)])
-
-
 def shifted(array, by):
-    length = lax.axis_size("panel")
-    pairs = [(i, i + by) for i in range(length) if 0 <= i + by < length]
-    return lax.ppermute(array, "panel", pairs)
+    size = lax.axis_size("panel")
+    array = lax.ppermute(array, "panel", [(i, (i + by) % size) for i in range(size)])
+    end = 0 if by > 0 else size - 1
+    return jnp.where(lax.axis_index("panel") == end, jnp.zeros_like(array), array)
 
 
 def wide(block):
@@ -346,7 +342,7 @@
     before = shifted(high_rows, 1)
     after = shifted(low_rows, -1)
     fars = [exchanged(bound_t, mask_core=1)]
-    fars += [exchanged(bound_t, mask_z=mask) for mask in (1, 2, 4)]
+    fars += [exchanged(bound_t, mask_z=mask) for mask in (1, 2)]
     own_rows, recv_rows = call(
         gather_kernel,
         [((width, edge_count), BF), ((width, edge_count), BF)],
@@ -363,6 +359,8 @@
         flops=3 * 10**9,
         mib=16,
     )
+    far_two, send_rows = tie(fars[2], send_rows)
+    fars.append(exchanged(far_two, mask_z=6))
     first = (rounds - 1) * contact_count // rounds
     both, slope_c, aggb = call(
         contact_kernel,

time: 87.4 us -> 85.8 us (0.982)
  starting transfers between devices: 43.3 us -> 42.4 us
    ppermute x21, waiting for transfers between devices: 11.6 us -> 8.41 us  [exchanged(): return lax.ppermute(block, ('region', 'panel'), route)]
    ppermute x2, waiting for transfers between devices: 0.01 us -> 2.71 us  [shifted(): lax.ppermute(array, 'panel', [(i, (i + by) % size) for i in range(size)])]
where the time goes in v10:
time: 85.8 us; the launch traced here: 85.7 us
  starting transfers between devices  42.4 us (49%)
  Pallas kernels  28.3 us (33%)
  waiting for transfers between devices  11.1 us (13%)
  local copies, waits for them, and re-layouts  1.71 us (2%)
  other arithmetic  1.12 us (1%)
  between operations  1.04 us (1%)
    ppermute x21, starting transfers between devices, exchanged(): return lax.ppermute(block, ('region', 'panel'), route)  38.7 us
    pallas_call x9, Pallas kernels, call(): pl.pallas_call(kernel, out_shape=[jax.ShapeDtypeStruct(shape, kind) for s...  28.3 us
    ppermute x21, waiting for transfers between devices, exchanged(): return lax.ppermute(block, ('region', 'panel'), route)  8.41 us
    ppermute x2, starting transfers between devices, shifted(): lax.ppermute(array, 'panel', [(i, (i + by) % size) for i in range(size)])  3.66 us
    ppermute x2, waiting for transfers between devices, shifted(): lax.ppermute(array, 'panel', [(i, (i + by) % size) for i in range(size)])  2.71 us
  transfers between devices with their start and end apart: 23, of which 5 were waited for; matrix products, arithmetic and copies ran while one was open for 0% of the time, Pallas kernels for 23%

profile of v10, /device:TPU:1, one launch (start us, length us, event | category | flops | bytes accessed | tf_op | source)
XLA Modules:
  0.0 85.7 jit_solution(16254573885906803047)
XLA Ops:
  0.6 0.0 copy-start
  0.6 0.7 copy-done
  1.3 0.9 %copy-done.4 = bf16[1024,128]{1,0:T(8,128)(2,1)S(1)} copy-done((bf16[1024,128]{1,0:T(8,128)(2,1)S(1)}, bf16[1024,128]{1,0:T(8,128)(2,1)}, u32[]{:S(2)}) %copy-start.4) | copy-done | bytes 262168
  2.3 0.4 shard_map.103
  2.7 3.9 %collective-permute-start = (bf16[128,256]{1,0:T(8,128)(2,1)S(1)}, bf16[128,256]{1,0:T(8,128)(2,1)S(1)}, u32[]{:S(2)}, u32[]{:S(2)}) collective-permute-start(bf16[128,256]{1,0:T(8,128)(2,1)S(1)} %get-tuple-element.62.bound_t_ref), channel_id=1, source_target_pairs={{0,32},{1,33},{2,34},{3,35},{4,36},{5,37},{6,38},{7,39},{8,40},{9,... | collective-permute-start | bytes 196616 | tf_op jit(solution)/shard_map/ppermute | solution.py:287
  6.6 1.0 %collective-permute-start.4 = (bf16[128,256]{1,0:T(8,128)(2,1)S(1)}, bf16[128,256]{1,0:T(8,128)(2,1)S(1)}, u32[]{:S(2)}, u32[]{:S(2)}) collective-permute-start(bf16[128,256]{1,0:T(8,128)(2,1)S(1)} %get-tuple-element.62.bound_t_ref), channel_id=1, source_target_pairs={{0,8},{1,9},{2,10},{3,11},{4,12},{5,13},{6,14},{7,15},{8,0},{9,1},... | collective-permute-start | bytes 196616 | tf_op jit(solution)/shard_map/ppermute | solution.py:287
  7.6 1.6 %collective-permute-start.5 = (bf16[128,256]{1,0:T(8,128)(2,1)S(1)}, bf16[128,256]{1,0:T(8,128)(2,1)S(1)}, u32[]{:S(2)}, u32[]{:S(2)}) collective-permute-start(bf16[128,256]{1,0:T(8,128)(2,1)S(1)} %get-tuple-element.62.bound_t_ref), channel_id=1, source_target_pairs={{0,16},{1,17},{2,18},{3,19},{4,20},{5,21},{6,22},{7,23},{8,24},{9,... | collective-permute-start | bytes 196616 | tf_op jit(solution)/shard_map/ppermute | solution.py:287
  9.2 3.7 %collective-permute-start.2 = (bf16[64,128]{1,0:T(8,128)(2,1)S(1)}, bf16[64,128]{1,0:T(8,128)(2,1)S(1)}, u32[]{:S(2)}, u32[]{:S(2)}) collective-permute-start(bf16[64,128]{1,0:T(8,128)(2,1)S(1)} %get-tuple-element.64), channel_id=1, source_target_pairs={{0,7},{1,0},{2,1},{3,2},{4,3},{5,4},{6,5},{7,6},{8,15},{9,8},{10,9... | collective-permute-start | bytes 49160 | tf_op jit(solution)/shard_map/ppermute | solution.py:292
  12.9 0.0 collective-permute-start.1
  12.9 1.9 %shard_map.104 = (bf16[128,3072]{1,0:T(8,128)(2,1)S(1)}, bf16[128,3072]{1,0:T(8,128)(2,1)S(1)}) custom-call(bf16[128,1024]{1,0:T(8,128)(2,1)S(1)} %get-tuple-element.61.lat_t_ref, s32[2,3072]{1,0:T(2,128)S(1)} %copy-done.8), custom_call_target="tpu_custom_call" | custom-call | flops 4000000000 | bytes 4000000 | tf_op jit(solution)/shard_map/pallas_call | solution.py:269
  14.8 0.0 collective-permute-done.2
  14.9 2.7 %collective-permute-done.1 = bf16[64,128]{1,0:T(8,128)(2,1)S(1)} collective-permute-done((bf16[64,128]{1,0:T(8,128)(2,1)S(1)}, bf16[64,128]{1,0:T(8,128)(2,1)S(1)}, u32[]{:S(2)}, u32[]{:S(2)}) %collective-permute-start.1) | collective-permute-done | bytes 16416 | tf_op jit(solution)/shard_map/ppermute | solution.py:292
  17.6 0.0 copy-start.7
  17.6 0.0 copy-start.9
  17.6 4.5 %shard_map.105 = (bf16[128,3072]{1,0:T(8,128)(2,1)S(1)}, f32[128,3072]{1,0:T(8,128)S(1)}, bf16[1024,128]{1,0:T(8,128)(2,1)S(1)}) custom-call(bf16[64,128]{1,0:T(8,128)(2,1)S(1)} %broadcast_select_fusion.11.before_ref, bf16[64,128]{1,0:T(8,128)(2,1)S(1)} %broadcast_select_fusion.10.after_ref, bf16[128,3072]{1,0:T(8,128)(2,1)S(1)} %get-tuple-element.68.own_ref, ...), custom_call_target="tpu_custom_call" | custom-call | flops 3000000000 | bytes 4000000 | tf_op jit(solution)/shard_map/pallas_call | solution.py:269
  22.1 0.0 collective-permute-done.far2_ref
  22.1 0.0 copy-start.1
  22.1 0.0 copy-start.5
  22.2 0.0 copy-start.6
  22.2 3.6 %collective-permute-start.3 = (bf16[128,256]{1,0:T(8,128)(2,1)S(1)}, bf16[128,256]{1,0:T(8,128)(2,1)S(1)}, u32[]{:S(2)}, u32[]{:S(2)}) collective-permute-start(bf16[128,256]{1,0:T(8,128)(2,1)S(1)} %collective-permute-done.far2_ref), channel_id=1, source_target_pairs={{0,96},{1,97},{2,98},{3,99},{4,100},{5,101},{6,102},{7,103},{8,104... | collective-permute-start | bytes 196616 | tf_op jit(solution)/shard_map/ppermute | solution.py:287
  25.7 0.0 collective-permute-done.4.far0_ref
  25.7 0.0 collective-permute-done.5.far1_ref
  25.8 4.4 %shard_map.106 = (bf16[256,6144]{1,0:T(8,128)(2,1)S(1)}, f32[128,6144]{1,0:T(8,128)S(1)}, f32[256,128]{1,0:T(8,128)S(1)}) custom-call(s32[1,4]{1,0:T(1,128)S(1)} %copy-done.9, bf16[128,256]{1,0:T(8,128)(2,1)S(1)} %get-tuple-element.62.bound_t_ref, bf16[128,256]{1,0:T(8,128)(2,1)S(1)} %collective-permute-done.4.far0_ref, ...), custom_call_target="tpu_custom_call" | custom-call | flops 3000000000 | bytes 4000000 | tf_op jit(solution)/shard_map/pallas_call | solution.py:269
  30.2 0.0 collective-permute-done.3.far3_ref
  30.2 8.1 %shard_map.107 = (bf16[1024,128]{1,0:T(8,128)(2,1)}, f32[576,128]{1,0:T(8,128)S(1)}, bf16[576,128]{1,0:T(8,128)(2,1)S(1)}, bf16[128,3072]{1,0:T(8,128)(2,1)S(1)}...) custom-call(s32[1,4]{1,0:T(1,128)S(1)} %copy-done.9, s32[1]{0:T(128)} %bitcast.core_ref, ...), custom_call_target="tpu_custom_call" | custom-call | flops 6000000000 | bytes 4000000 | tf_op jit(solution)/shard_map/pallas_call | solution.py:269
  38.3 2.3 %collective-permute-start.6 = (bf16[576,128]{1,0:T(8,128)(2,1)S(1)}, bf16[576,128]{1,0:T(8,128)(2,1)S(1)}, u32[]{:S(2)}, u32[]{:S(2)}) collective-permute-start(bf16[576,128]{1,0:T(8,128)(2,1)S(1)} %get-tuple-element.82), channel_id=1, source_target_pairs={{0,8},{1,9},{2,10},{3,11},{4,12},{5,13},{6,14},{7,15},{8,0},{9,1},... | collective-permute-start | bytes 442376 | tf_op jit(solution)/shard_map/ppermute | solution.py:287
  40.6 2.6 %shard_map.108 = (f32[1024,128]{1,0:T(8,128)S(1)}, bf16[64,128]{1,0:T(8,128)(2,1)S(1)}, bf16[64,128]{1,0:T(8,128)(2,1)S(1)}) custom-call(bf16[9,128,128]{2,1,0:T(8,128)(2,1)S(1)} %copy-done.3, s32[2,3072]{1,0:T(2,128)S(1)} %copy-done.8, bf16[128,3072]{1,0:T(8,128)(2,1)S(1)} %get-tuple-element.83.dm_ref), custom_call_target="tpu_custom_call" | custom-call | flops 2000000000 | bytes 4000000 | tf_op jit(solution)/shard_map/pallas_call | solution.py:269
  43.3 0.0 collective-permute-done.6
  43.4 0.1 collective-permute-start.7
  43.5 0.3 collective-permute-start.8
  43.7 3.6 %collective-permute-start.9 = (bf16[144,128]{1,0:T(8,128)(2,1)S(1)}, bf16[144,128]{1,0:T(8,128)(2,1)S(1)}, u32[]{:S(2)}, u32[]{:S(2)}) collective-permute-start(bf16[144,128]{1,0:T(8,128)(2,1)S(1)} %get-tuple-element.121), channel_id=1, source_target_pairs={{0,3},{1,2},{2,1},{3,0},{4,7},{5,6},{6,5},{7,4},{8,11},{9,10},{10,... | collective-permute-start | bytes 110600 | tf_op jit(solution)/shard_map/ppermute | solution.py:287
  47.3 2.8 %shard_map.109 = (bf16[256,128]{1,0:T(8,128)(2,1)S(1)}, bf16[256,128]{1,0:T(8,128)(2,1)S(1)}, bf16[256,128]{1,0:T(8,128)(2,1)S(1)}, bf16[256,128]{1,0:T(8,128)(2,1)S(1)}, f32[256,128]{1,0:T(8,128)S(1)}) custom-call(bf16[9,128,128]{2,1,0:T(8,128)(2,1)S(1)} %copy-done.3, s32[2,8192]{1,0:T(2,128)S(1)} %copy-done.7, bf16[128,8192]{1,0:T(8,128)(2,1)S(1)} %get-tuple-element.89.dc_ref), custom_call_target="tpu_custom_call" | custom-call | flops 2000000000 | bytes 4000000 | tf_op jit(solution)/shard_map/pallas_call | solution.py:269
  50.1 0.0 collective-permute-done.7
  50.1 0.0 collective-permute-done.8
  50.1 0.0 collective-permute-done.9
  50.2 2.5 %collective-permute-start.11 = (bf16[144,128]{1,0:T(8,128)(2,1)S(1)}, bf16[144,128]{1,0:T(8,128)(2,1)S(1)}, u32[]{:S(2)}, u32[]{:S(2)}) collective-permute-start(bf16[144,128]{1,0:T(8,128)(2,1)S(1)} %add_convert_fusion.4), channel_id=1, source_target_pairs={{0,128},{1,129},{2,130},{3,131},{4,132},{5,133},{6,134},{7,135},{8... | collective-permute-start | bytes 110600 | tf_op jit(solution)/shard_map/ppermute | solution.py:287
  52.7 0.2 collective-permute-start.12
  52.9 0.0 collective-permute-start.10
  53.0 1.3 %collective-permute-start.17 = (bf16[512,128]{1,0:T(8,128)(2,1)S(1)}, bf16[512,128]{1,0:T(8,128)(2,1)S(1)}, u32[]{:S(2)}, u32[]{:S(2)}) collective-permute-start(bf16[512,128]{1,0:T(8,128)(2,1)S(1)} %pad_maximum_fusion.2), channel_id=1, source_target_pairs={{0,32},{1,33},{2,34},{3,35},{4,36},{5,37},{6,38},{7,39},{8,40},{9,... | collective-permute-start | bytes 393224 | tf_op jit(solution)/shard_map/ppermute | solution.py:287
  54.2 0.7 collective-permute-start.14
  55.0 0.0 collective-permute-done.11
  55.0 2.2 %collective-permute-start.16 = (bf16[256,128]{1,0:T(8,128)(2,1)S(1)}, bf16[256,128]{1,0:T(8,128)(2,1)S(1)}, u32[]{:S(2)}, u32[]{:S(2)}) collective-permute-start(bf16[256,128]{1,0:T(8,128)(2,1)S(1)} %get-tuple-element.109), channel_id=1, source_target_pairs={{0,8},{1,9},{2,10},{3,11},{4,12},{5,13},{6,14},{7,15},{8,0},{9,1},... | collective-permute-start | bytes 196616 | tf_op jit(solution)/shard_map/ppermute | solution.py:287
  57.2 0.0 collective-permute-done.12
  57.2 0.0 collective-permute-done.10
  57.2 0.8 collective-permute-start.13
  58.1 2.3 %shard_map.110.part_ref = f32[1024,128]{1,0:T(8,128)S(1)} custom-call(bf16[9,128,128]{2,1,0:T(8,128)(2,1)S(1)} %copy-done.3, s32[2,3072]{1,0:T(2,128)S(1)} %copy-done.8, bf16[128,3072]{1,0:T(8,128)(2,1)S(1)} %get-tuple-element.83.dm_ref, bf16[1024,128]{1,0:T(8,128)(2,1)S(1)} %get-tuple-element.103.dn_ref, bf16[1024,128]{1,0:T(8,128)(2,1)S(1)} %copy-done.6, ...), custom_call_target="tpu_custom_call" | custom-call | flops 2000000000 | bytes 4000000 | tf_op jit(solution)/shard_map/pallas_call | solution.py:269
  60.3 0.0 collective-permute-done.14.in1_ref
  60.3 0.1 collective-permute-done.13
  60.5 2.0 %collective-permute-start.15 = (bf16[144,128]{1,0:T(8,128)(2,1)S(1)}, bf16[144,128]{1,0:T(8,128)(2,1)S(1)}, u32[]{:S(2)}, u32[]{:S(2)}) collective-permute-start(bf16[144,128]{1,0:T(8,128)(2,1)S(1)} %add_convert_fusion.2), channel_id=1, source_target_pairs={{0,32},{1,33},{2,34},{3,35},{4,36},{5,37},{6,38},{7,39},{8,40},{9,... | collective-permute-start | bytes 110600 | tf_op jit(solution)/shard_map/ppermute | solution.py:287
  62.4 0.0 collective-permute-done.16.in0_ref
  62.4 2.1 %collective-permute-done.15 = bf16[144,128]{1,0:T(8,128)(2,1)S(1)} collective-permute-done((bf16[144,128]{1,0:T(8,128)(2,1)S(1)}, bf16[144,128]{1,0:T(8,128)(2,1)S(1)}, u32[]{:S(2)}, u32[]{:S(2)}) %collective-permute-start.15) | collective-permute-done | bytes 36896 | tf_op jit(solution)/shard_map/ppermute | solution.py:287
  64.5 0.0 collective-permute-done.17
  64.6 2.8 %collective-permute-start.18 = (bf16[400,128]{1,0:T(8,128)(2,1)S(1)}, bf16[400,128]{1,0:T(8,128)(2,1)S(1)}, u32[]{:S(2)}, u32[]{:S(2)}) collective-permute-start(bf16[400,128]{1,0:T(8,128)(2,1)S(1)} %pad_maximum_fusion.3), channel_id=1, source_target_pairs={{0,96},{1,97},{2,98},{3,99},{4,100},{5,101},{6,102},{7,103},{8,104... | collective-permute-start | bytes 307208 | tf_op jit(solution)/shard_map/ppermute | solution.py:287
  67.5 3.0 %collective-permute-done.18 = bf16[400,128]{1,0:T(8,128)(2,1)S(1)} collective-permute-done((bf16[400,128]{1,0:T(8,128)(2,1)S(1)}, bf16[400,128]{1,0:T(8,128)(2,1)S(1)}, u32[]{:S(2)}, u32[]{:S(2)}) %collective-permute-start.18) | collective-permute-done | bytes 102432 | tf_op jit(solution)/shard_map/ppermute | solution.py:287
  70.4 0.1 collective-permute-start.19
  70.5 2.1 %collective-permute-start.21 = (bf16[208,128]{1,0:T(8,128)(2,1)S(1)}, bf16[208,128]{1,0:T(8,128)(2,1)S(1)}, u32[]{:S(2)}, u32[]{:S(2)}) collective-permute-start(bf16[208,128]{1,0:T(8,128)(2,1)S(1)} %get-tuple-element.132), channel_id=1, source_target_pairs={{0,3},{1,2},{2,1},{3,0},{4,7},{5,6},{6,5},{7,4},{8,11},{9,10},{10,... | collective-permute-start | bytes 159752 | tf_op jit(solution)/shard_map/ppermute | solution.py:287
  72.7 1.1 %collective-permute-start.20 = (bf16[144,128]{1,0:T(8,128)(2,1)S(1)}, bf16[144,128]{1,0:T(8,128)(2,1)S(1)}, u32[]{:S(2)}, u32[]{:S(2)}) collective-permute-start(bf16[144,128]{1,0:T(8,128)(2,1)S(1)} %add_convert_fusion), channel_id=1, source_target_pairs={{0,2},{1,3},{2,0},{3,1},{4,6},{5,7},{6,4},{7,5},{8,10},{9,11},{10,... | collective-permute-start | bytes 110600 | tf_op jit(solution)/shard_map/ppermute | solution.py:287
  73.8 3.2 %collective-permute-done.20 = bf16[144,128]{1,0:T(8,128)(2,1)S(1)} collective-permute-done((bf16[144,128]{1,0:T(8,128)(2,1)S(1)}, bf16[144,128]{1,0:T(8,128)(2,1)S(1)}, u32[]{:S(2)}, u32[]{:S(2)}) %collective-permute-start.20) | collective-permute-done | bytes 36896 | tf_op jit(solution)/shard_map/ppermute | solution.py:287
  77.0 0.0 collective-permute-done.19
  77.0 0.0 collective-permute-done.21
  77.0 6.5 %collective-permute-start.22 = (bf16[576,128]{1,0:T(8,128)(2,1)S(1)}, bf16[576,128]{1,0:T(8,128)(2,1)S(1)}, u32[]{:S(2)}, u32[]{:S(2)}) collective-permute-start(bf16[576,128]{1,0:T(8,128)(2,1)S(1)} %pad_maximum_fusion.1), channel_id=1, source_target_pairs={{0,8},{1,9},{2,10},{3,11},{4,12},{5,13},{6,14},{7,15},{8,0},{9,1},... | collective-permute-start | bytes 442376 | tf_op jit(solution)/shard_map/ppermute | solution.py:287
  83.5 1.3 %shard_map.111 = f32[1024,128]{1,0:T(8,128)} custom-call(f32[1024,128]{1,0:T(8,128)S(1)} %shard_map.110.part_ref, f32[256,128]{1,0:T(8,128)S(1)} %get-tuple-element.107.own_ref, bf16[256,128]{1,0:T(8,128)(2,1)S(1)} %collective-permute-done.16.in0_ref, bf16[256,128]{1,0:T(8,128)(2,1)S(1)} %collective-permute-done.14.in1_ref, ...), custom_call_target="tpu_custom_call" | custom-call | flops 100000000 | bytes 4000000 | tf_op jit(solution)/shard_map/pallas_call | solution.py:269
  84.7 0.0 collective-permute-done.22
  84.8 0.9 pad_maximum_fusion
  (33 shorter events, 0.3 us)
Async XLA Ops:
  0.6 0.7 copy-start
  1.3 0.9 %copy-start.4 = (bf16[1024,128]{1,0:T(8,128)(2,1)S(1)}, bf16[1024,128]{1,0:T(8,128)(2,1)}, u32[]{:S(2)}) copy-start(bf16[1024,128]{1,0:T(8,128)(2,1)} %lat_ref.1) | copy-start | bytes 786436
  2.3 10.6 %copy-start.8 = (s32[2,3072]{1,0:T(2,128)S(1)}, s32[2,3072]{1,0:T(2,128)}, u32[]{:S(2)}) copy-start(s32[2,3072]{1,0:T(2,128)} %edges_ref.9) | copy-start | bytes 73732
  2.7 19.4 %collective-permute-start = (bf16[128,256]{1,0:T(8,128)(2,1)S(1)}, bf16[128,256]{1,0:T(8,128)(2,1)S(1)}, u32[]{:S(2)}, u32[]{:S(2)}) collective-permute-start(bf16[128,256]{1,0:T(8,128)(2,1)S(1)} %get-tuple-element.62.bound_t_ref), channel_id=1, source_target_pairs={{0,32},{1,33},{2,34},{3,35},{4,36},{5,37},{6,38},{7,39},{8,40},{9,... | collective-permute-start | bytes 196616 | tf_op jit(solution)/shard_map/ppermute | solution.py:287
  6.6 19.1 %collective-permute-start.4 = (bf16[128,256]{1,0:T(8,128)(2,1)S(1)}, bf16[128,256]{1,0:T(8,128)(2,1)S(1)}, u32[]{:S(2)}, u32[]{:S(2)}) collective-permute-start(bf16[128,256]{1,0:T(8,128)(2,1)S(1)} %get-tuple-element.62.bound_t_ref), channel_id=1, source_target_pairs={{0,8},{1,9},{2,10},{3,11},{4,12},{5,13},{6,14},{7,15},{8,0},{9,1},... | collective-permute-start | bytes 196616 | tf_op jit(solution)/shard_map/ppermute | solution.py:287
  7.6 18.2 %collective-permute-start.5 = (bf16[128,256]{1,0:T(8,128)(2,1)S(1)}, bf16[128,256]{1,0:T(8,128)(2,1)S(1)}, u32[]{:S(2)}, u32[]{:S(2)}) collective-permute-start(bf16[128,256]{1,0:T(8,128)(2,1)S(1)} %get-tuple-element.62.bound_t_ref), channel_id=1, source_target_pairs={{0,16},{1,17},{2,18},{3,19},{4,20},{5,21},{6,22},{7,23},{8,24},{9,... | collective-permute-start | bytes 196616 | tf_op jit(solution)/shard_map/ppermute | solution.py:287
  9.2 5.6 %collective-permute-start.2 = (bf16[64,128]{1,0:T(8,128)(2,1)S(1)}, bf16[64,128]{1,0:T(8,128)(2,1)S(1)}, u32[]{:S(2)}, u32[]{:S(2)}) collective-permute-start(bf16[64,128]{1,0:T(8,128)(2,1)S(1)} %get-tuple-element.64), channel_id=1, source_target_pairs={{0,7},{1,0},{2,1},{3,2},{4,3},{5,4},{6,5},{7,6},{8,15},{9,8},{10,9... | collective-permute-start | bytes 49160 | tf_op jit(solution)/shard_map/ppermute | solution.py:292
  12.9 4.7 %collective-permute-start.1 = (bf16[64,128]{1,0:T(8,128)(2,1)S(1)}, bf16[64,128]{1,0:T(8,128)(2,1)S(1)}, u32[]{:S(2)}, u32[]{:S(2)}) collective-permute-start(bf16[64,128]{1,0:T(8,128)(2,1)S(1)} %get-tuple-element.63), channel_id=1, source_target_pairs={{0,1},{1,2},{2,3},{3,4},{4,5},{5,6},{6,7},{7,0},{8,9},{9,10},{10,1... | collective-permute-start | bytes 49160 | tf_op jit(solution)/shard_map/ppermute | solution.py:292
  12.9 4.7 %copy-start.2 = (bf16[3072,128]{1,0:T(8,128)(2,1)S(1)}, bf16[3072,128]{1,0:T(8,128)(2,1)}, u32[]{:S(2)}) copy-start(bf16[3072,128]{1,0:T(8,128)(2,1)} %feats_ref.3) | copy-start | bytes 2359300
  12.9 4.7 %copy-start.3 = (bf16[9,128,128]{2,1,0:T(8,128)(2,1)S(1)}, bf16[9,128,128]{2,1,0:T(8,128)(2,1)}, u32[]{:S(2)}) copy-start(bf16[9,128,128]{2,1,0:T(8,128)(2,1)} %w_ref.11) | copy-start | bytes 884740
  17.6 8.1 %copy-start.7 = (s32[2,8192]{1,0:T(2,128)S(1)}, s32[2,8192]{1,0:T(2,128)}, u32[]{:S(2)}) copy-start(s32[2,8192]{1,0:T(2,128)} %contacts_ref.5) | copy-start | bytes 196612
  17.6 8.1 %copy-start.9 = (s32[1,4]{1,0:T(1,128)S(1)}, s32[1,4]{1,0:T(1,128)}, u32[]{:S(2)}) copy-start(s32[1,4]{1,0:T(1,128)} %counts_ref.3) | copy-start | bytes 52
  22.1 8.1 %copy-start.1 = (s32[256]{0:T(256)S(1)}, s32[256]{0:T(256)}, u32[]{:S(2)}) copy-start(s32[256]{0:T(256)} %param.13) | copy-start | bytes 3076
  22.1 8.1 %copy-start.5 = (bf16[1024,128]{1,0:T(8,128)(2,1)S(1)}, bf16[1024,128]{1,0:T(8,128)(2,1)}, u32[]{:S(2)}) copy-start(bf16[1024,128]{1,0:T(8,128)(2,1)} %lat_ref.1) | copy-start | bytes 786436
  22.2 8.0 %copy-start.6 = (bf16[1024,128]{1,0:T(8,128)(2,1)S(1)}, bf16[1024,128]{1,0:T(8,128)(2,1)}, u32[]{:S(2)}) copy-start(bf16[1024,128]{1,0:T(8,128)(2,1)} %cot_ref.3) | copy-start | bytes 786436
  22.2 8.0 %collective-permute-start.3 = (bf16[128,256]{1,0:T(8,128)(2,1)S(1)}, bf16[128,256]{1,0:T(8,128)(2,1)S(1)}, u32[]{:S(2)}, u32[]{:S(2)}) collective-permute-start(bf16[128,256]{1,0:T(8,128)(2,1)S(1)} %collective-permute-done.far2_ref), channel_id=1, source_target_pairs={{0,96},{1,97},{2,98},{3,99},{4,100},{5,101},{6,102},{7,103},{8,104... | collective-permute-start | bytes 196616 | tf_op jit(solution)/shard_map/ppermute | solution.py:287
  38.3 4.9 %collective-permute-start.6 = (bf16[576,128]{1,0:T(8,128)(2,1)S(1)}, bf16[576,128]{1,0:T(8,128)(2,1)S(1)}, u32[]{:S(2)}, u32[]{:S(2)}) collective-permute-start(bf16[576,128]{1,0:T(8,128)(2,1)S(1)} %get-tuple-element.82), channel_id=1, source_target_pairs={{0,8},{1,9},{2,10},{3,11},{4,12},{5,13},{6,14},{7,15},{8,0},{9,1},... | collective-permute-start | bytes 442376 | tf_op jit(solution)/shard_map/ppermute | solution.py:287
  43.4 6.8 %collective-permute-start.7 = (bf16[144,128]{1,0:T(8,128)(2,1)S(1)}, bf16[144,128]{1,0:T(8,128)(2,1)S(1)}, u32[]{:S(2)}, u32[]{:S(2)}) collective-permute-start(bf16[144,128]{1,0:T(8,128)(2,1)S(1)} %get-tuple-element.123), channel_id=1, source_target_pairs={{0,1},{1,0},{2,3},{3,2},{4,5},{5,4},{6,7},{7,6},{8,9},{9,8},{10,11... | collective-permute-start | bytes 110600 | tf_op jit(solution)/shard_map/ppermute | solution.py:287
  43.5 6.7 %collective-permute-start.8 = (bf16[144,128]{1,0:T(8,128)(2,1)S(1)}, bf16[144,128]{1,0:T(8,128)(2,1)S(1)}, u32[]{:S(2)}, u32[]{:S(2)}) collective-permute-start(bf16[144,128]{1,0:T(8,128)(2,1)S(1)} %get-tuple-element.122), channel_id=1, source_target_pairs={{0,2},{1,3},{2,0},{3,1},{4,6},{5,7},{6,4},{7,5},{8,10},{9,11},{10,... | collective-permute-start | bytes 110600 | tf_op jit(solution)/shard_map/ppermute | solution.py:287
  43.7 6.4 %collective-permute-start.9 = (bf16[144,128]{1,0:T(8,128)(2,1)S(1)}, bf16[144,128]{1,0:T(8,128)(2,1)S(1)}, u32[]{:S(2)}, u32[]{:S(2)}) collective-permute-start(bf16[144,128]{1,0:T(8,128)(2,1)S(1)} %get-tuple-element.121), channel_id=1, source_target_pairs={{0,3},{1,2},{2,1},{3,0},{4,7},{5,6},{6,5},{7,4},{8,11},{9,10},{10,... | collective-permute-start | bytes 110600 | tf_op jit(solution)/shard_map/ppermute | solution.py:287
  50.2 4.8 %collective-permute-start.11 = (bf16[144,128]{1,0:T(8,128)(2,1)S(1)}, bf16[144,128]{1,0:T(8,128)(2,1)S(1)}, u32[]{:S(2)}, u32[]{:S(2)}) collective-permute-start(bf16[144,128]{1,0:T(8,128)(2,1)S(1)} %add_convert_fusion.4), channel_id=1, source_target_pairs={{0,128},{1,129},{2,130},{3,131},{4,132},{5,133},{6,134},{7,135},{8... | collective-permute-start | bytes 110600 | tf_op jit(solution)/shard_map/ppermute | solution.py:287
  52.7 4.5 %collective-permute-start.12 = (bf16[144,128]{1,0:T(8,128)(2,1)S(1)}, bf16[144,128]{1,0:T(8,128)(2,1)S(1)}, u32[]{:S(2)}, u32[]{:S(2)}) collective-permute-start(bf16[144,128]{1,0:T(8,128)(2,1)S(1)} %add_convert_fusion.4), channel_id=1, source_target_pairs={{0,132},{1,133},{2,134},{3,135},{4,128},{5,129},{6,130},{7,131},{8... | collective-permute-start | bytes 110600 | tf_op jit(solution)/shard_map/ppermute | solution.py:287
  52.9 4.3 %collective-permute-start.10 = (bf16[208,128]{1,0:T(8,128)(2,1)S(1)}, bf16[208,128]{1,0:T(8,128)(2,1)S(1)}, u32[]{:S(2)}, u32[]{:S(2)}) collective-permute-start(bf16[208,128]{1,0:T(8,128)(2,1)S(1)} %pad_maximum_fusion.6), channel_id=1, source_target_pairs={{0,4},{1,5},{2,6},{3,7},{4,0},{5,1},{6,2},{7,3},{8,12},{9,13},{10,... | collective-permute-start | bytes 159752 | tf_op jit(solution)/shard_map/ppermute | solution.py:287
  53.0 11.6 %collective-permute-start.17 = (bf16[512,128]{1,0:T(8,128)(2,1)S(1)}, bf16[512,128]{1,0:T(8,128)(2,1)S(1)}, u32[]{:S(2)}, u32[]{:S(2)}) collective-permute-start(bf16[512,128]{1,0:T(8,128)(2,1)S(1)} %pad_maximum_fusion.2), channel_id=1, source_target_pairs={{0,32},{1,33},{2,34},{3,35},{4,36},{5,37},{6,38},{7,39},{8,40},{9,... | collective-permute-start | bytes 393224 | tf_op jit(solution)/shard_map/ppermute | solution.py:287
  54.2 6.1 %collective-permute-start.14 = (bf16[256,128]{1,0:T(8,128)(2,1)S(1)}, bf16[256,128]{1,0:T(8,128)(2,1)S(1)}, u32[]{:S(2)}, u32[]{:S(2)}) collective-permute-start(bf16[256,128]{1,0:T(8,128)(2,1)S(1)} %get-tuple-element.105), channel_id=1, source_target_pairs={{0,16},{1,17},{2,18},{3,19},{4,20},{5,21},{6,22},{7,23},{8,24},{9,... | collective-permute-start | bytes 196616 | tf_op jit(solution)/shard_map/ppermute | solution.py:287
  55.0 7.5 %collective-permute-start.16 = (bf16[256,128]{1,0:T(8,128)(2,1)S(1)}, bf16[256,128]{1,0:T(8,128)(2,1)S(1)}, u32[]{:S(2)}, u32[]{:S(2)}) collective-permute-start(bf16[256,128]{1,0:T(8,128)(2,1)S(1)} %get-tuple-element.109), channel_id=1, source_target_pairs={{0,8},{1,9},{2,10},{3,11},{4,12},{5,13},{6,14},{7,15},{8,0},{9,1},... | collective-permute-start | bytes 196616 | tf_op jit(solution)/shard_map/ppermute | solution.py:287
  57.2 3.2 %collective-permute-start.13 = (bf16[144,128]{1,0:T(8,128)(2,1)S(1)}, bf16[144,128]{1,0:T(8,128)(2,1)S(1)}, u32[]{:S(2)}, u32[]{:S(2)}) collective-permute-start(bf16[144,128]{1,0:T(8,128)(2,1)S(1)} %add_convert_fusion.3), channel_id=1, source_target_pairs={{0,16},{1,17},{2,18},{3,19},{4,20},{5,21},{6,22},{7,23},{8,24},{9,... | collective-permute-start | bytes 110600 | tf_op jit(solution)/shard_map/ppermute | solution.py:287
  60.5 4.1 %collective-permute-start.15 = (bf16[144,128]{1,0:T(8,128)(2,1)S(1)}, bf16[144,128]{1,0:T(8,128)(2,1)S(1)}, u32[]{:S(2)}, u32[]{:S(2)}) collective-permute-start(bf16[144,128]{1,0:T(8,128)(2,1)S(1)} %add_convert_fusion.2), channel_id=1, source_target_pairs={{0,32},{1,33},{2,34},{3,35},{4,36},{5,37},{6,38},{7,39},{8,40},{9,... | collective-permute-start | bytes 110600 | tf_op jit(solution)/shard_map/ppermute | solution.py:287
  64.6 5.8 %collective-permute-start.18 = (bf16[400,128]{1,0:T(8,128)(2,1)S(1)}, bf16[400,128]{1,0:T(8,128)(2,1)S(1)}, u32[]{:S(2)}, u32[]{:S(2)}) collective-permute-start(bf16[400,128]{1,0:T(8,128)(2,1)S(1)} %pad_maximum_fusion.3), channel_id=1, source_target_pairs={{0,96},{1,97},{2,98},{3,99},{4,100},{5,101},{6,102},{7,103},{8,104... | collective-permute-start | bytes 307208 | tf_op jit(solution)/shard_map/ppermute | solution.py:287
  70.4 6.5 %collective-permute-start.19 = (bf16[208,128]{1,0:T(8,128)(2,1)S(1)}, bf16[208,128]{1,0:T(8,128)(2,1)S(1)}, u32[]{:S(2)}, u32[]{:S(2)}) collective-permute-start(bf16[208,128]{1,0:T(8,128)(2,1)S(1)} %get-tuple-element.133), channel_id=1, source_target_pairs={{0,1},{1,0},{2,3},{3,2},{4,5},{5,4},{6,7},{7,6},{8,9},{9,8},{10,11... | collective-permute-start | bytes 159752 | tf_op jit(solution)/shard_map/ppermute | solution.py:287
  70.5 6.4 %collective-permute-start.21 = (bf16[208,128]{1,0:T(8,128)(2,1)S(1)}, bf16[208,128]{1,0:T(8,128)(2,1)S(1)}, u32[]{:S(2)}, u32[]{:S(2)}) collective-permute-start(bf16[208,128]{1,0:T(8,128)(2,1)S(1)} %get-tuple-element.132), channel_id=1, source_target_pairs={{0,3},{1,2},{2,1},{3,0},{4,7},{5,6},{6,5},{7,4},{8,11},{9,10},{10,... | collective-permute-start | bytes 159752 | tf_op jit(solution)/shard_map/ppermute | solution.py:287
  72.7 4.3 %collective-permute-start.20 = (bf16[144,128]{1,0:T(8,128)(2,1)S(1)}, bf16[144,128]{1,0:T(8,128)(2,1)S(1)}, u32[]{:S(2)}, u32[]{:S(2)}) collective-permute-start(bf16[144,128]{1,0:T(8,128)(2,1)S(1)} %add_convert_fusion), channel_id=1, source_target_pairs={{0,2},{1,3},{2,0},{3,1},{4,6},{5,7},{6,4},{7,5},{8,10},{9,11},{10,... | collective-permute-start | bytes 110600 | tf_op jit(solution)/shard_map/ppermute | solution.py:287
  77.0 7.7 %collective-permute-start.22 = (bf16[576,128]{1,0:T(8,128)(2,1)S(1)}, bf16[576,128]{1,0:T(8,128)(2,1)S(1)}, u32[]{:S(2)}, u32[]{:S(2)}) collective-permute-start(bf16[576,128]{1,0:T(8,128)(2,1)S(1)} %pad_maximum_fusion.1), channel_id=1, source_target_pairs={{0,8},{1,9},{2,10},{3,11},{4,12},{5,13},{6,14},{7,15},{8,0},{9,1},... | collective-permute-start | bytes 442376 | tf_op jit(solution)/shard_map/ppermute | solution.py:287

commit v11 on v10

--- a/solution.py
+++ b/solution.py
@@ -411,7 +411,7 @@
     pieces = [
         lax.dynamic_slice_in_dim(block, (row_y ^ mask) * size, size, 0) for mask in range(4)
     ]
-    found = [exchanged(pieces[mask].astype(BF), mask_y=mask) for mask in (1, 2, 3)]
+    two, one, three = [exchanged(pieces[mask].astype(BF), mask_y=mask) for mask in (2, 1, 3)]
     *far_grads, own_grad = call(
         contact_back_kernel,
         [((bound_count, width), BF)] * rounds + [((bound_count, width), F32)],
@@ -419,12 +419,13 @@
         flops=2 * 10**9,
         mib=16,
     )
-    one, two, three, *far_grads = tie(*found, *far_grads)
+    two, one, three, *far_grads = tie(two, one, three, *far_grads)
     block = ((pieces[0] + wide(one)) + (wide(two) + wide(three))).astype(BF)
 
     rim = jnp.where(row_y == 0, low, high)
+    two = exchanged(block, mask_x=2)
     one = exchanged(jnp.concatenate([block, rim], axis=0), mask_x=1)
-    two, three = [exchanged(block, mask_x=mask) for mask in (2, 3)]
+    three = exchanged(block, mask_x=3)
     in_one = exchanged(far_grads[1], mask_z=1)
     pair = exchanged(jnp.concatenate(far_grads[2:], axis=0), mask_z=2)
     one, two, three, part = tie(one, two, three, part)
@@ -447,23 +448,23 @@
     other, in_zero, pair = tie(other, in_zero, pair)
     block = (wide(block) + wide(other)).astype(BF)
     in_two = pair[:bound_count]
-    other = exchanged(jnp.concatenate([block, pair[bound_count:]], axis=0), mask_z=6)
-    in_three = other[size:]
-    block = (wide(block) + wide(other[:size])).astype(BF)
+    other = exchanged(block, mask_z=6)
+    in_three = exchanged(pair[bound_count:], mask_z=6)
+    block = (wide(block) + wide(other)).astype(BF)
 
     rim = jnp.where(row_y == 1, high, jnp.where(row_y == 2, low, rim))
+    near = jnp.where(row_y % 2 == 0, high, low)
+    two = exchanged(jnp.concatenate([block, near, near[:16]], axis=0), mask_y=2)
+    one = exchanged(jnp.concatenate([block, near], axis=0), mask_y=1)
     three = exchanged(jnp.concatenate([block, rim], axis=0), mask_y=3)
-    rim = jnp.where(row_y % 2 == 0, high, low)
-    one = exchanged(jnp.concatenate([block, rim], axis=0), mask_y=1)
-    two = exchanged(block, mask_y=2)
-    one, two, three = tie(one, two, three)
+    two, one, three, in_three = tie(two, one, three, in_three)
     panel = lax.axis_index("panel")
     nothing = jnp.zeros_like(rim)
     from_prev = jnp.where(row_y % 2 == 0, three[size:], one[size:])
     from_prev = jnp.where(panel == 0, nothing, from_prev)
     from_next = jnp.where(row_y % 2 == 0, one[size:], three[size:])
     from_next = jnp.where(panel == lax.axis_size("panel") - 1, nothing, from_next)
-    block = ordered_by_y([block, one[:size], two, three[:size]], row_y)
+    block = ordered_by_y([block, one[:size], two[:size], three[:size]], row_y)
     other = exchanged(block, mask_core=1)
     (grad_rows,) = call(
         last_kernel,

time: 85.8 us -> 85.1 us (level)
  waiting for transfers between devices: 11.1 us -> 10.1 us
    ppermute x21 -> x22, waiting for transfers between devices: 8.41 us -> 7.43 us  [exchanged(): return lax.ppermute(block, ('region', 'panel'), route)]
    ppermute x21 -> x22, starting transfers between devices: 38.7 us -> 39 us  [exchanged(): return lax.ppermute(block, ('region', 'panel'), route)]
  transfers between devices with their start and end apart: 23 -> 24, of which waited for: 5 -> 6; matrix products, arithmetic and copies ran while one was open for 0% -> 0% of each run, Pallas kernels for 23% -> 23%
where the time goes in v11:
time: 85.1 us; the launch traced here: 84.9 us
  starting transfers between devices  42.6 us (50%)
  Pallas kernels  28.3 us (33%)
  waiting for transfers between devices  10.1 us (12%)
  local copies, waits for them, and re-layouts  1.71 us (2%)
  other arithmetic  1.12 us (1%)
  between operations  1.05 us (1%)
    ppermute x22, starting transfers between devices, exchanged(): return lax.ppermute(block, ('region', 'panel'), route)  39 us
    pallas_call x9, Pallas kernels, call(): pl.pallas_call(kernel, out_shape=[jax.ShapeDtypeStruct(shape, kind) for s...  28.3 us
    ppermute x22, waiting for transfers between devices, exchanged(): return lax.ppermute(block, ('region', 'panel'), route)  7.43 us
    ppermute x2, starting transfers between devices, shifted(): lax.ppermute(array, 'panel', [(i, (i + by) % size) for i in range(size)])  3.66 us
    ppermute x2, waiting for transfers between devices, shifted(): lax.ppermute(array, 'panel', [(i, (i + by) % size) for i in range(size)])  2.69 us
  transfers between devices with their start and end apart: 24, of which 6 were waited for; matrix products, arithmetic and copies ran while one was open for 0% of the time, Pallas kernels for 23%

profile of v11, /device:TPU:1, one launch (start us, length us, event | category | flops | bytes accessed | tf_op | source)
XLA Modules:
  0.0 84.9 jit_solution(4986769090547465937)
XLA Ops:
  0.6 0.0 copy-start
  0.6 0.7 copy-done
  1.3 0.9 %copy-done.4 = bf16[1024,128]{1,0:T(8,128)(2,1)S(1)} copy-done((bf16[1024,128]{1,0:T(8,128)(2,1)S(1)}, bf16[1024,128]{1,0:T(8,128)(2,1)}, u32[]{:S(2)}) %copy-start.4) | copy-done | bytes 262168
  2.3 0.4 shard_map.103
  2.7 3.9 %collective-permute-start = (bf16[128,256]{1,0:T(8,128)(2,1)S(1)}, bf16[128,256]{1,0:T(8,128)(2,1)S(1)}, u32[]{:S(2)}, u32[]{:S(2)}) collective-permute-start(bf16[128,256]{1,0:T(8,128)(2,1)S(1)} %get-tuple-element.63.bound_t_ref), channel_id=1, source_target_pairs={{0,32},{1,33},{2,34},{3,35},{4,36},{5,37},{6,38},{7,39},{8,40},{9,... | collective-permute-start | bytes 196616 | tf_op jit(solution)/shard_map/ppermute | solution.py:287
  6.6 1.0 %collective-permute-start.4 = (bf16[128,256]{1,0:T(8,128)(2,1)S(1)}, bf16[128,256]{1,0:T(8,128)(2,1)S(1)}, u32[]{:S(2)}, u32[]{:S(2)}) collective-permute-start(bf16[128,256]{1,0:T(8,128)(2,1)S(1)} %get-tuple-element.63.bound_t_ref), channel_id=1, source_target_pairs={{0,8},{1,9},{2,10},{3,11},{4,12},{5,13},{6,14},{7,15},{8,0},{9,1},... | collective-permute-start | bytes 196616 | tf_op jit(solution)/shard_map/ppermute | solution.py:287
  7.6 1.6 %collective-permute-start.5 = (bf16[128,256]{1,0:T(8,128)(2,1)S(1)}, bf16[128,256]{1,0:T(8,128)(2,1)S(1)}, u32[]{:S(2)}, u32[]{:S(2)}) collective-permute-start(bf16[128,256]{1,0:T(8,128)(2,1)S(1)} %get-tuple-element.63.bound_t_ref), channel_id=1, source_target_pairs={{0,16},{1,17},{2,18},{3,19},{4,20},{5,21},{6,22},{7,23},{8,24},{9,... | collective-permute-start | bytes 196616 | tf_op jit(solution)/shard_map/ppermute | solution.py:287
  9.2 3.7 %collective-permute-start.2 = (bf16[64,128]{1,0:T(8,128)(2,1)S(1)}, bf16[64,128]{1,0:T(8,128)(2,1)S(1)}, u32[]{:S(2)}, u32[]{:S(2)}) collective-permute-start(bf16[64,128]{1,0:T(8,128)(2,1)S(1)} %get-tuple-element.65), channel_id=1, source_target_pairs={{0,7},{1,0},{2,1},{3,2},{4,3},{5,4},{6,5},{7,6},{8,15},{9,8},{10,9... | collective-permute-start | bytes 49160 | tf_op jit(solution)/shard_map/ppermute | solution.py:292
  12.9 0.0 collective-permute-start.1
  12.9 1.9 %shard_map.104 = (bf16[128,3072]{1,0:T(8,128)(2,1)S(1)}, bf16[128,3072]{1,0:T(8,128)(2,1)S(1)}) custom-call(bf16[128,1024]{1,0:T(8,128)(2,1)S(1)} %get-tuple-element.62.lat_t_ref, s32[2,3072]{1,0:T(2,128)S(1)} %copy-done.8), custom_call_target="tpu_custom_call" | custom-call | flops 4000000000 | bytes 4000000 | tf_op jit(solution)/shard_map/pallas_call | solution.py:269
  14.9 0.0 collective-permute-done.2
  14.9 2.7 %collective-permute-done.1 = bf16[64,128]{1,0:T(8,128)(2,1)S(1)} collective-permute-done((bf16[64,128]{1,0:T(8,128)(2,1)S(1)}, bf16[64,128]{1,0:T(8,128)(2,1)S(1)}, u32[]{:S(2)}, u32[]{:S(2)}) %collective-permute-start.1) | collective-permute-done | bytes 16416 | tf_op jit(solution)/shard_map/ppermute | solution.py:292
  17.6 0.0 copy-start.7
  17.6 0.0 copy-start.9
  17.6 4.5 %shard_map.105 = (bf16[128,3072]{1,0:T(8,128)(2,1)S(1)}, f32[128,3072]{1,0:T(8,128)S(1)}, bf16[1024,128]{1,0:T(8,128)(2,1)S(1)}) custom-call(bf16[64,128]{1,0:T(8,128)(2,1)S(1)} %broadcast_select_fusion.11.before_ref, bf16[64,128]{1,0:T(8,128)(2,1)S(1)} %broadcast_select_fusion.10.after_ref, bf16[128,3072]{1,0:T(8,128)(2,1)S(1)} %get-tuple-element.69.own_ref, ...), custom_call_target="tpu_custom_call" | custom-call | flops 3000000000 | bytes 4000000 | tf_op jit(solution)/shard_map/pallas_call | solution.py:269
  22.1 0.0 collective-permute-done.far2_ref
  22.1 0.0 copy-start.1
  22.1 0.0 copy-start.5
  22.2 0.0 copy-start.6
  22.2 3.6 %collective-permute-start.3 = (bf16[128,256]{1,0:T(8,128)(2,1)S(1)}, bf16[128,256]{1,0:T(8,128)(2,1)S(1)}, u32[]{:S(2)}, u32[]{:S(2)}) collective-permute-start(bf16[128,256]{1,0:T(8,128)(2,1)S(1)} %collective-permute-done.far2_ref), channel_id=1, source_target_pairs={{0,96},{1,97},{2,98},{3,99},{4,100},{5,101},{6,102},{7,103},{8,104... | collective-permute-start | bytes 196616 | tf_op jit(solution)/shard_map/ppermute | solution.py:287
  25.7 0.0 collective-permute-done.4.far0_ref
  25.7 0.0 collective-permute-done.5.far1_ref
  25.8 4.4 %shard_map.106 = (bf16[256,6144]{1,0:T(8,128)(2,1)S(1)}, f32[128,6144]{1,0:T(8,128)S(1)}, f32[256,128]{1,0:T(8,128)S(1)}) custom-call(s32[1,4]{1,0:T(1,128)S(1)} %copy-done.9, bf16[128,256]{1,0:T(8,128)(2,1)S(1)} %get-tuple-element.63.bound_t_ref, bf16[128,256]{1,0:T(8,128)(2,1)S(1)} %collective-permute-done.4.far0_ref, ...), custom_call_target="tpu_custom_call" | custom-call | flops 3000000000 | bytes 4000000 | tf_op jit(solution)/shard_map/pallas_call | solution.py:269
  30.2 0.0 collective-permute-done.3.far3_ref
  30.2 8.1 %shard_map.107 = (bf16[1024,128]{1,0:T(8,128)(2,1)}, f32[576,128]{1,0:T(8,128)S(1)}, bf16[576,128]{1,0:T(8,128)(2,1)S(1)}, bf16[128,3072]{1,0:T(8,128)(2,1)S(1)}...) custom-call(s32[1,4]{1,0:T(1,128)S(1)} %copy-done.9, s32[1]{0:T(128)} %bitcast.core_ref, ...), custom_call_target="tpu_custom_call" | custom-call | flops 6000000000 | bytes 4000000 | tf_op jit(solution)/shard_map/pallas_call | solution.py:269
  38.3 2.3 %collective-permute-start.6 = (bf16[576,128]{1,0:T(8,128)(2,1)S(1)}, bf16[576,128]{1,0:T(8,128)(2,1)S(1)}, u32[]{:S(2)}, u32[]{:S(2)}) collective-permute-start(bf16[576,128]{1,0:T(8,128)(2,1)S(1)} %get-tuple-element.83), channel_id=1, source_target_pairs={{0,8},{1,9},{2,10},{3,11},{4,12},{5,13},{6,14},{7,15},{8,0},{9,1},... | collective-permute-start | bytes 442376 | tf_op jit(solution)/shard_map/ppermute | solution.py:287
  40.6 2.6 %shard_map.108 = (f32[1024,128]{1,0:T(8,128)S(1)}, bf16[64,128]{1,0:T(8,128)(2,1)S(1)}, bf16[64,128]{1,0:T(8,128)(2,1)S(1)}) custom-call(bf16[9,128,128]{2,1,0:T(8,128)(2,1)S(1)} %copy-done.3, s32[2,3072]{1,0:T(2,128)S(1)} %copy-done.8, bf16[128,3072]{1,0:T(8,128)(2,1)S(1)} %get-tuple-element.84.dm_ref), custom_call_target="tpu_custom_call" | custom-call | flops 2000000000 | bytes 4000000 | tf_op jit(solution)/shard_map/pallas_call | solution.py:269
  43.3 0.0 collective-permute-done.6
  43.4 0.1 collective-permute-start.7
  43.5 0.1 collective-permute-start.8
  43.6 3.1 %collective-permute-start.9 = (bf16[144,128]{1,0:T(8,128)(2,1)S(1)}, bf16[144,128]{1,0:T(8,128)(2,1)S(1)}, u32[]{:S(2)}, u32[]{:S(2)}) collective-permute-start(bf16[144,128]{1,0:T(8,128)(2,1)S(1)} %get-tuple-element.123), channel_id=1, source_target_pairs={{0,3},{1,2},{2,1},{3,0},{4,7},{5,6},{6,5},{7,4},{8,11},{9,10},{10,... | collective-permute-start | bytes 110600 | tf_op jit(solution)/shard_map/ppermute | solution.py:287
  46.7 2.8 %shard_map.109 = (bf16[256,128]{1,0:T(8,128)(2,1)S(1)}, bf16[256,128]{1,0:T(8,128)(2,1)S(1)}, bf16[256,128]{1,0:T(8,128)(2,1)S(1)}, bf16[256,128]{1,0:T(8,128)(2,1)S(1)}, f32[256,128]{1,0:T(8,128)S(1)}) custom-call(bf16[9,128,128]{2,1,0:T(8,128)(2,1)S(1)} %copy-done.3, s32[2,8192]{1,0:T(2,128)S(1)} %copy-done.7, bf16[128,8192]{1,0:T(8,128)(2,1)S(1)} %get-tuple-element.90.dc_ref), custom_call_target="tpu_custom_call" | custom-call | flops 2000000000 | bytes 4000000 | tf_op jit(solution)/shard_map/pallas_call | solution.py:269
  49.5 0.0 collective-permute-done.7
  49.5 0.0 collective-permute-done.8
  49.5 0.0 collective-permute-done.9
  49.6 2.5 %collective-permute-start.11 = (bf16[144,128]{1,0:T(8,128)(2,1)S(1)}, bf16[144,128]{1,0:T(8,128)(2,1)S(1)}, u32[]{:S(2)}, u32[]{:S(2)}) collective-permute-start(bf16[144,128]{1,0:T(8,128)(2,1)S(1)} %add_convert_fusion.4), channel_id=1, source_target_pairs={{0,128},{1,129},{2,130},{3,131},{4,132},{5,133},{6,134},{7,135},{8... | collective-permute-start | bytes 110600 | tf_op jit(solution)/shard_map/ppermute | solution.py:287
  52.1 0.2 collective-permute-start.12
  52.3 0.0 collective-permute-start.10
  52.3 1.3 %collective-permute-start.17 = (bf16[512,128]{1,0:T(8,128)(2,1)S(1)}, bf16[512,128]{1,0:T(8,128)(2,1)S(1)}, u32[]{:S(2)}, u32[]{:S(2)}) collective-permute-start(bf16[512,128]{1,0:T(8,128)(2,1)S(1)} %pad_maximum_fusion.2), channel_id=1, source_target_pairs={{0,32},{1,33},{2,34},{3,35},{4,36},{5,37},{6,38},{7,39},{8,40},{9,... | collective-permute-start | bytes 393224 | tf_op jit(solution)/shard_map/ppermute | solution.py:287
  53.6 0.7 collective-permute-start.14
  54.3 0.0 collective-permute-done.11
  54.4 2.2 %collective-permute-start.16 = (bf16[256,128]{1,0:T(8,128)(2,1)S(1)}, bf16[256,128]{1,0:T(8,128)(2,1)S(1)}, u32[]{:S(2)}, u32[]{:S(2)}) collective-permute-start(bf16[256,128]{1,0:T(8,128)(2,1)S(1)} %get-tuple-element.110), channel_id=1, source_target_pairs={{0,8},{1,9},{2,10},{3,11},{4,12},{5,13},{6,14},{7,15},{8,0},{9,1},... | collective-permute-start | bytes 196616 | tf_op jit(solution)/shard_map/ppermute | solution.py:287
  56.6 0.0 collective-permute-done.12
  56.6 0.0 collective-permute-done.10
  56.6 0.8 collective-permute-start.13
  57.5 2.3 %shard_map.110.part_ref = f32[1024,128]{1,0:T(8,128)S(1)} custom-call(bf16[9,128,128]{2,1,0:T(8,128)(2,1)S(1)} %copy-done.3, s32[2,3072]{1,0:T(2,128)S(1)} %copy-done.8, bf16[128,3072]{1,0:T(8,128)(2,1)S(1)} %get-tuple-element.84.dm_ref, bf16[1024,128]{1,0:T(8,128)(2,1)S(1)} %get-tuple-element.104.dn_ref, bf16[1024,128]{1,0:T(8,128)(2,1)S(1)} %copy-done.6, ...), custom_call_target="tpu_custom_call" | custom-call | flops 2000000000 | bytes 4000000 | tf_op jit(solution)/shard_map/pallas_call | solution.py:269
  59.7 0.1 collective-permute-done.13
  59.9 1.7 %collective-permute-start.15 = (bf16[144,128]{1,0:T(8,128)(2,1)S(1)}, bf16[144,128]{1,0:T(8,128)(2,1)S(1)}, u32[]{:S(2)}, u32[]{:S(2)}) collective-permute-start(bf16[144,128]{1,0:T(8,128)(2,1)S(1)} %add_convert_fusion.2), channel_id=1, source_target_pairs={{0,32},{1,33},{2,34},{3,35},{4,36},{5,37},{6,38},{7,39},{8,40},{9,... | collective-permute-start | bytes 110600 | tf_op jit(solution)/shard_map/ppermute | solution.py:287
  61.6 0.0 collective-permute-done.16.in0_ref
  61.6 2.1 %collective-permute-done.15 = bf16[144,128]{1,0:T(8,128)(2,1)S(1)} collective-permute-done((bf16[144,128]{1,0:T(8,128)(2,1)S(1)}, bf16[144,128]{1,0:T(8,128)(2,1)S(1)}, u32[]{:S(2)}, u32[]{:S(2)}) %collective-permute-start.15) | collective-permute-done | bytes 36896 | tf_op jit(solution)/shard_map/ppermute | solution.py:287
  63.7 0.0 collective-permute-done.17
  63.7 3.1 %collective-permute-start.18 = (bf16[144,128]{1,0:T(8,128)(2,1)S(1)}, bf16[144,128]{1,0:T(8,128)(2,1)S(1)}, u32[]{:S(2)}, u32[]{:S(2)}) collective-permute-start(bf16[144,128]{1,0:T(8,128)(2,1)S(1)} %add_convert_fusion.1), channel_id=1, source_target_pairs={{0,96},{1,97},{2,98},{3,99},{4,100},{5,101},{6,102},{7,103},{8,104... | collective-permute-start | bytes 110600 | tf_op jit(solution)/shard_map/ppermute | solution.py:287
  66.8 0.9 %collective-permute-start.22 = (bf16[256,128]{1,0:T(8,128)(2,1)S(1)}, bf16[256,128]{1,0:T(8,128)(2,1)S(1)}, u32[]{:S(2)}, u32[]{:S(2)}) collective-permute-start(bf16[256,128]{1,0:T(8,128)(2,1)S(1)} %get-tuple-element.130), channel_id=1, source_target_pairs={{0,96},{1,97},{2,98},{3,99},{4,100},{5,101},{6,102},{7,103},{8,104... | collective-permute-start | bytes 196616 | tf_op jit(solution)/shard_map/ppermute | solution.py:287
  67.7 1.3 %collective-permute-done.18 = bf16[144,128]{1,0:T(8,128)(2,1)S(1)} collective-permute-done((bf16[144,128]{1,0:T(8,128)(2,1)S(1)}, bf16[144,128]{1,0:T(8,128)(2,1)S(1)}, u32[]{:S(2)}, u32[]{:S(2)}) %collective-permute-start.18) | collective-permute-done | bytes 36896 | tf_op jit(solution)/shard_map/ppermute | solution.py:287
  69.1 0.3 collective-permute-start.19
  69.5 2.4 %collective-permute-start.20 = (bf16[208,128]{1,0:T(8,128)(2,1)S(1)}, bf16[208,128]{1,0:T(8,128)(2,1)S(1)}, u32[]{:S(2)}, u32[]{:S(2)}) collective-permute-start(bf16[208,128]{1,0:T(8,128)(2,1)S(1)} %get-tuple-element.135), channel_id=1, source_target_pairs={{0,1},{1,0},{2,3},{3,2},{4,5},{5,4},{6,7},{7,6},{8,9},{9,8},{10,11... | collective-permute-start | bytes 159752 | tf_op jit(solution)/shard_map/ppermute | solution.py:287
  71.9 0.6 collective-permute-start.21
  72.5 0.0 collective-permute-done.22.in3_ref
  72.5 1.4 %collective-permute-done.20 = bf16[208,128]{1,0:T(8,128)(2,1)S(1)} collective-permute-done((bf16[208,128]{1,0:T(8,128)(2,1)S(1)}, bf16[208,128]{1,0:T(8,128)(2,1)S(1)}, u32[]{:S(2)}, u32[]{:S(2)}) %collective-permute-start.20) | collective-permute-done | bytes 53280 | tf_op jit(solution)/shard_map/ppermute | solution.py:287
  73.9 2.5 %collective-permute-done.21 = bf16[208,128]{1,0:T(8,128)(2,1)S(1)} collective-permute-done((bf16[208,128]{1,0:T(8,128)(2,1)S(1)}, bf16[208,128]{1,0:T(8,128)(2,1)S(1)}, u32[]{:S(2)}, u32[]{:S(2)}) %collective-permute-start.21) | collective-permute-done | bytes 53280 | tf_op jit(solution)/shard_map/ppermute | solution.py:287
  76.4 6.3 %collective-permute-start.23 = (bf16[576,128]{1,0:T(8,128)(2,1)S(1)}, bf16[576,128]{1,0:T(8,128)(2,1)S(1)}, u32[]{:S(2)}, u32[]{:S(2)}) collective-permute-start(bf16[576,128]{1,0:T(8,128)(2,1)S(1)} %pad_maximum_fusion.1), channel_id=1, source_target_pairs={{0,8},{1,9},{2,10},{3,11},{4,12},{5,13},{6,14},{7,15},{8,0},{9,1},... | collective-permute-start | bytes 442376 | tf_op jit(solution)/shard_map/ppermute | solution.py:287
  82.8 1.3 %shard_map.111 = f32[1024,128]{1,0:T(8,128)} custom-call(f32[1024,128]{1,0:T(8,128)S(1)} %shard_map.110.part_ref, f32[256,128]{1,0:T(8,128)S(1)} %get-tuple-element.108.own_ref, bf16[256,128]{1,0:T(8,128)(2,1)S(1)} %collective-permute-done.16.in0_ref, bf16[256,128]{1,0:T(8,128)(2,1)S(1)} %collective-permute-done.14.in1_ref, ...), custom_call_target="tpu_custom_call" | custom-call | flops 100000000 | bytes 4000000 | tf_op jit(solution)/shard_map/pallas_call | solution.py:269
  84.0 0.0 collective-permute-done.23
  84.1 0.9 %pad_maximum_fusion = f32[1152,128]{1,0:T(8,128)} fusion(f32[576,128]{1,0:T(8,128)S(1)} %get-tuple-element.122, f32[576,128]{1,0:T(8,128)S(1)} %get-tuple-element.121), kind=kLoop, calls=%fused_computation | loop fusion | flops 147456 | bytes 1179648 | tf_op jit(solution)/shard_map/concatenate | solution.py:313
  (35 shorter events, 0.3 us)
Async XLA Ops:
  0.6 0.7 copy-start
  1.3 0.9 %copy-start.4 = (bf16[1024,128]{1,0:T(8,128)(2,1)S(1)}, bf16[1024,128]{1,0:T(8,128)(2,1)}, u32[]{:S(2)}) copy-start(bf16[1024,128]{1,0:T(8,128)(2,1)} %lat_ref.1) | copy-start | bytes 786436
  2.3 10.6 %copy-start.8 = (s32[2,3072]{1,0:T(2,128)S(1)}, s32[2,3072]{1,0:T(2,128)}, u32[]{:S(2)}) copy-start(s32[2,3072]{1,0:T(2,128)} %edges_ref.9) | copy-start | bytes 73732
  2.7 19.4 %collective-permute-start = (bf16[128,256]{1,0:T(8,128)(2,1)S(1)}, bf16[128,256]{1,0:T(8,128)(2,1)S(1)}, u32[]{:S(2)}, u32[]{:S(2)}) collective-permute-start(bf16[128,256]{1,0:T(8,128)(2,1)S(1)} %get-tuple-element.63.bound_t_ref), channel_id=1, source_target_pairs={{0,32},{1,33},{2,34},{3,35},{4,36},{5,37},{6,38},{7,39},{8,40},{9,... | collective-permute-start | bytes 196616 | tf_op jit(solution)/shard_map/ppermute | solution.py:287
  6.6 19.1 %collective-permute-start.4 = (bf16[128,256]{1,0:T(8,128)(2,1)S(1)}, bf16[128,256]{1,0:T(8,128)(2,1)S(1)}, u32[]{:S(2)}, u32[]{:S(2)}) collective-permute-start(bf16[128,256]{1,0:T(8,128)(2,1)S(1)} %get-tuple-element.63.bound_t_ref), channel_id=1, source_target_pairs={{0,8},{1,9},{2,10},{3,11},{4,12},{5,13},{6,14},{7,15},{8,0},{9,1},... | collective-permute-start | bytes 196616 | tf_op jit(solution)/shard_map/ppermute | solution.py:287
  7.6 18.2 %collective-permute-start.5 = (bf16[128,256]{1,0:T(8,128)(2,1)S(1)}, bf16[128,256]{1,0:T(8,128)(2,1)S(1)}, u32[]{:S(2)}, u32[]{:S(2)}) collective-permute-start(bf16[128,256]{1,0:T(8,128)(2,1)S(1)} %get-tuple-element.63.bound_t_ref), channel_id=1, source_target_pairs={{0,16},{1,17},{2,18},{3,19},{4,20},{5,21},{6,22},{7,23},{8,24},{9,... | collective-permute-start | bytes 196616 | tf_op jit(solution)/shard_map/ppermute | solution.py:287
  9.2 5.7 %collective-permute-start.2 = (bf16[64,128]{1,0:T(8,128)(2,1)S(1)}, bf16[64,128]{1,0:T(8,128)(2,1)S(1)}, u32[]{:S(2)}, u32[]{:S(2)}) collective-permute-start(bf16[64,128]{1,0:T(8,128)(2,1)S(1)} %get-tuple-element.65), channel_id=1, source_target_pairs={{0,7},{1,0},{2,1},{3,2},{4,3},{5,4},{6,5},{7,6},{8,15},{9,8},{10,9... | collective-permute-start | bytes 49160 | tf_op jit(solution)/shard_map/ppermute | solution.py:292
  12.9 4.7 %collective-permute-start.1 = (bf16[64,128]{1,0:T(8,128)(2,1)S(1)}, bf16[64,128]{1,0:T(8,128)(2,1)S(1)}, u32[]{:S(2)}, u32[]{:S(2)}) collective-permute-start(bf16[64,128]{1,0:T(8,128)(2,1)S(1)} %get-tuple-element.64), channel_id=1, source_target_pairs={{0,1},{1,2},{2,3},{3,4},{4,5},{5,6},{6,7},{7,0},{8,9},{9,10},{10,1... | collective-permute-start | bytes 49160 | tf_op jit(solution)/shard_map/ppermute | solution.py:292
  12.9 4.7 %copy-start.2 = (bf16[3072,128]{1,0:T(8,128)(2,1)S(1)}, bf16[3072,128]{1,0:T(8,128)(2,1)}, u32[]{:S(2)}) copy-start(bf16[3072,128]{1,0:T(8,128)(2,1)} %feats_ref.3) | copy-start | bytes 2359300
  12.9 4.7 %copy-start.3 = (bf16[9,128,128]{2,1,0:T(8,128)(2,1)S(1)}, bf16[9,128,128]{2,1,0:T(8,128)(2,1)}, u32[]{:S(2)}) copy-start(bf16[9,128,128]{2,1,0:T(8,128)(2,1)} %w_ref.11) | copy-start | bytes 884740
  17.6 8.1 %copy-start.7 = (s32[2,8192]{1,0:T(2,128)S(1)}, s32[2,8192]{1,0:T(2,128)}, u32[]{:S(2)}) copy-start(s32[2,8192]{1,0:T(2,128)} %contacts_ref.5) | copy-start | bytes 196612
  17.6 8.1 %copy-start.9 = (s32[1,4]{1,0:T(1,128)S(1)}, s32[1,4]{1,0:T(1,128)}, u32[]{:S(2)}) copy-start(s32[1,4]{1,0:T(1,128)} %counts_ref.3) | copy-start | bytes 52
  22.1 8.0 %copy-start.1 = (s32[256]{0:T(256)S(1)}, s32[256]{0:T(256)}, u32[]{:S(2)}) copy-start(s32[256]{0:T(256)} %param.13) | copy-start | bytes 3076
  22.1 8.0 %copy-start.5 = (bf16[1024,128]{1,0:T(8,128)(2,1)S(1)}, bf16[1024,128]{1,0:T(8,128)(2,1)}, u32[]{:S(2)}) copy-start(bf16[1024,128]{1,0:T(8,128)(2,1)} %lat_ref.1) | copy-start | bytes 786436
  22.2 8.0 %copy-start.6 = (bf16[1024,128]{1,0:T(8,128)(2,1)S(1)}, bf16[1024,128]{1,0:T(8,128)(2,1)}, u32[]{:S(2)}) copy-start(bf16[1024,128]{1,0:T(8,128)(2,1)} %cot_ref.3) | copy-start | bytes 786436
  22.2 8.0 %collective-permute-start.3 = (bf16[128,256]{1,0:T(8,128)(2,1)S(1)}, bf16[128,256]{1,0:T(8,128)(2,1)S(1)}, u32[]{:S(2)}, u32[]{:S(2)}) collective-permute-start(bf16[128,256]{1,0:T(8,128)(2,1)S(1)} %collective-permute-done.far2_ref), channel_id=1, source_target_pairs={{0,96},{1,97},{2,98},{3,99},{4,100},{5,101},{6,102},{7,103},{8,104... | collective-permute-start | bytes 196616 | tf_op jit(solution)/shard_map/ppermute | solution.py:287
  38.3 4.9 %collective-permute-start.6 = (bf16[576,128]{1,0:T(8,128)(2,1)S(1)}, bf16[576,128]{1,0:T(8,128)(2,1)S(1)}, u32[]{:S(2)}, u32[]{:S(2)}) collective-permute-start(bf16[576,128]{1,0:T(8,128)(2,1)S(1)} %get-tuple-element.83), channel_id=1, source_target_pairs={{0,8},{1,9},{2,10},{3,11},{4,12},{5,13},{6,14},{7,15},{8,0},{9,1},... | collective-permute-start | bytes 442376 | tf_op jit(solution)/shard_map/ppermute | solution.py:287
  43.4 6.2 %collective-permute-start.7 = (bf16[144,128]{1,0:T(8,128)(2,1)S(1)}, bf16[144,128]{1,0:T(8,128)(2,1)S(1)}, u32[]{:S(2)}, u32[]{:S(2)}) collective-permute-start(bf16[144,128]{1,0:T(8,128)(2,1)S(1)} %get-tuple-element.125), channel_id=1, source_target_pairs={{0,2},{1,3},{2,0},{3,1},{4,6},{5,7},{6,4},{7,5},{8,10},{9,11},{10,... | collective-permute-start | bytes 110600 | tf_op jit(solution)/shard_map/ppermute | solution.py:287
  43.5 6.1 %collective-permute-start.8 = (bf16[144,128]{1,0:T(8,128)(2,1)S(1)}, bf16[144,128]{1,0:T(8,128)(2,1)S(1)}, u32[]{:S(2)}, u32[]{:S(2)}) collective-permute-start(bf16[144,128]{1,0:T(8,128)(2,1)S(1)} %get-tuple-element.124), channel_id=1, source_target_pairs={{0,1},{1,0},{2,3},{3,2},{4,5},{5,4},{6,7},{7,6},{8,9},{9,8},{10,11... | collective-permute-start | bytes 110600 | tf_op jit(solution)/shard_map/ppermute | solution.py:287
  43.6 6.0 %collective-permute-start.9 = (bf16[144,128]{1,0:T(8,128)(2,1)S(1)}, bf16[144,128]{1,0:T(8,128)(2,1)S(1)}, u32[]{:S(2)}, u32[]{:S(2)}) collective-permute-start(bf16[144,128]{1,0:T(8,128)(2,1)S(1)} %get-tuple-element.123), channel_id=1, source_target_pairs={{0,3},{1,2},{2,1},{3,0},{4,7},{5,6},{6,5},{7,4},{8,11},{9,10},{10,... | collective-permute-start | bytes 110600 | tf_op jit(solution)/shard_map/ppermute | solution.py:287
  49.6 4.8 %collective-permute-start.11 = (bf16[144,128]{1,0:T(8,128)(2,1)S(1)}, bf16[144,128]{1,0:T(8,128)(2,1)S(1)}, u32[]{:S(2)}, u32[]{:S(2)}) collective-permute-start(bf16[144,128]{1,0:T(8,128)(2,1)S(1)} %add_convert_fusion.4), channel_id=1, source_target_pairs={{0,128},{1,129},{2,130},{3,131},{4,132},{5,133},{6,134},{7,135},{8... | collective-permute-start | bytes 110600 | tf_op jit(solution)/shard_map/ppermute | solution.py:287
  52.1 4.5 %collective-permute-start.12 = (bf16[144,128]{1,0:T(8,128)(2,1)S(1)}, bf16[144,128]{1,0:T(8,128)(2,1)S(1)}, u32[]{:S(2)}, u32[]{:S(2)}) collective-permute-start(bf16[144,128]{1,0:T(8,128)(2,1)S(1)} %add_convert_fusion.4), channel_id=1, source_target_pairs={{0,132},{1,133},{2,134},{3,135},{4,128},{5,129},{6,130},{7,131},{8... | collective-permute-start | bytes 110600 | tf_op jit(solution)/shard_map/ppermute | solution.py:287
  52.3 4.3 %collective-permute-start.10 = (bf16[208,128]{1,0:T(8,128)(2,1)S(1)}, bf16[208,128]{1,0:T(8,128)(2,1)S(1)}, u32[]{:S(2)}, u32[]{:S(2)}) collective-permute-start(bf16[208,128]{1,0:T(8,128)(2,1)S(1)} %pad_maximum_fusion.6), channel_id=1, source_target_pairs={{0,4},{1,5},{2,6},{3,7},{4,0},{5,1},{6,2},{7,3},{8,12},{9,13},{10,... | collective-permute-start | bytes 159752 | tf_op jit(solution)/shard_map/ppermute | solution.py:287
  52.3 11.3 %collective-permute-start.17 = (bf16[512,128]{1,0:T(8,128)(2,1)S(1)}, bf16[512,128]{1,0:T(8,128)(2,1)S(1)}, u32[]{:S(2)}, u32[]{:S(2)}) collective-permute-start(bf16[512,128]{1,0:T(8,128)(2,1)S(1)} %pad_maximum_fusion.2), channel_id=1, source_target_pairs={{0,32},{1,33},{2,34},{3,35},{4,36},{5,37},{6,38},{7,39},{8,40},{9,... | collective-permute-start | bytes 393224 | tf_op jit(solution)/shard_map/ppermute | solution.py:287
  53.6 6.1 %collective-permute-start.14 = (bf16[256,128]{1,0:T(8,128)(2,1)S(1)}, bf16[256,128]{1,0:T(8,128)(2,1)S(1)}, u32[]{:S(2)}, u32[]{:S(2)}) collective-permute-start(bf16[256,128]{1,0:T(8,128)(2,1)S(1)} %get-tuple-element.106), channel_id=1, source_target_pairs={{0,16},{1,17},{2,18},{3,19},{4,20},{5,21},{6,22},{7,23},{8,24},{9,... | collective-permute-start | bytes 196616 | tf_op jit(solution)/shard_map/ppermute | solution.py:287
  54.4 7.2 %collective-permute-start.16 = (bf16[256,128]{1,0:T(8,128)(2,1)S(1)}, bf16[256,128]{1,0:T(8,128)(2,1)S(1)}, u32[]{:S(2)}, u32[]{:S(2)}) collective-permute-start(bf16[256,128]{1,0:T(8,128)(2,1)S(1)} %get-tuple-element.110), channel_id=1, source_target_pairs={{0,8},{1,9},{2,10},{3,11},{4,12},{5,13},{6,14},{7,15},{8,0},{9,1},... | collective-permute-start | bytes 196616 | tf_op jit(solution)/shard_map/ppermute | solution.py:287
  56.6 3.2 %collective-permute-start.13 = (bf16[144,128]{1,0:T(8,128)(2,1)S(1)}, bf16[144,128]{1,0:T(8,128)(2,1)S(1)}, u32[]{:S(2)}, u32[]{:S(2)}) collective-permute-start(bf16[144,128]{1,0:T(8,128)(2,1)S(1)} %add_convert_fusion.3), channel_id=1, source_target_pairs={{0,16},{1,17},{2,18},{3,19},{4,20},{5,21},{6,22},{7,23},{8,24},{9,... | collective-permute-start | bytes 110600 | tf_op jit(solution)/shard_map/ppermute | solution.py:287
  59.9 3.8 %collective-permute-start.15 = (bf16[144,128]{1,0:T(8,128)(2,1)S(1)}, bf16[144,128]{1,0:T(8,128)(2,1)S(1)}, u32[]{:S(2)}, u32[]{:S(2)}) collective-permute-start(bf16[144,128]{1,0:T(8,128)(2,1)S(1)} %add_convert_fusion.2), channel_id=1, source_target_pairs={{0,32},{1,33},{2,34},{3,35},{4,36},{5,37},{6,38},{7,39},{8,40},{9,... | collective-permute-start | bytes 110600 | tf_op jit(solution)/shard_map/ppermute | solution.py:287
  63.7 5.4 %collective-permute-start.18 = (bf16[144,128]{1,0:T(8,128)(2,1)S(1)}, bf16[144,128]{1,0:T(8,128)(2,1)S(1)}, u32[]{:S(2)}, u32[]{:S(2)}) collective-permute-start(bf16[144,128]{1,0:T(8,128)(2,1)S(1)} %add_convert_fusion.1), channel_id=1, source_target_pairs={{0,96},{1,97},{2,98},{3,99},{4,100},{5,101},{6,102},{7,103},{8,104... | collective-permute-start | bytes 110600 | tf_op jit(solution)/shard_map/ppermute | solution.py:287
  66.8 5.7 %collective-permute-start.22 = (bf16[256,128]{1,0:T(8,128)(2,1)S(1)}, bf16[256,128]{1,0:T(8,128)(2,1)S(1)}, u32[]{:S(2)}, u32[]{:S(2)}) collective-permute-start(bf16[256,128]{1,0:T(8,128)(2,1)S(1)} %get-tuple-element.130), channel_id=1, source_target_pairs={{0,96},{1,97},{2,98},{3,99},{4,100},{5,101},{6,102},{7,103},{8,104... | collective-permute-start | bytes 196616 | tf_op jit(solution)/shard_map/ppermute | solution.py:287
  69.1 7.3 %collective-permute-start.19 = (bf16[224,128]{1,0:T(8,128)(2,1)S(1)}, bf16[224,128]{1,0:T(8,128)(2,1)S(1)}, u32[]{:S(2)}, u32[]{:S(2)}) collective-permute-start(bf16[224,128]{1,0:T(8,128)(2,1)S(1)} %pad_maximum_fusion.3), channel_id=1, source_target_pairs={{0,2},{1,3},{2,0},{3,1},{4,6},{5,7},{6,4},{7,5},{8,10},{9,11},{10,... | collective-permute-start | bytes 172040 | tf_op jit(solution)/shard_map/ppermute | solution.py:287
  69.5 4.5 %collective-permute-start.20 = (bf16[208,128]{1,0:T(8,128)(2,1)S(1)}, bf16[208,128]{1,0:T(8,128)(2,1)S(1)}, u32[]{:S(2)}, u32[]{:S(2)}) collective-permute-start(bf16[208,128]{1,0:T(8,128)(2,1)S(1)} %get-tuple-element.135), channel_id=1, source_target_pairs={{0,1},{1,0},{2,3},{3,2},{4,5},{5,4},{6,7},{7,6},{8,9},{9,8},{10,11... | collective-permute-start | bytes 159752 | tf_op jit(solution)/shard_map/ppermute | solution.py:287
  71.9 4.5 %collective-permute-start.21 = (bf16[208,128]{1,0:T(8,128)(2,1)S(1)}, bf16[208,128]{1,0:T(8,128)(2,1)S(1)}, u32[]{:S(2)}, u32[]{:S(2)}) collective-permute-start(bf16[208,128]{1,0:T(8,128)(2,1)S(1)} %get-tuple-element.134), channel_id=1, source_target_pairs={{0,3},{1,2},{2,1},{3,0},{4,7},{5,6},{6,5},{7,4},{8,11},{9,10},{10,... | collective-permute-start | bytes 159752 | tf_op jit(solution)/shard_map/ppermute | solution.py:287
  76.4 7.6 %collective-permute-start.23 = (bf16[576,128]{1,0:T(8,128)(2,1)S(1)}, bf16[576,128]{1,0:T(8,128)(2,1)S(1)}, u32[]{:S(2)}, u32[]{:S(2)}) collective-permute-start(bf16[576,128]{1,0:T(8,128)(2,1)S(1)} %pad_maximum_fusion.1), channel_id=1, source_target_pairs={{0,8},{1,9},{2,10},{3,11},{4,12},{5,13},{6,14},{7,15},{8,0},{9,1},... | collective-permute-start | bytes 442376 | tf_op jit(solution)/shard_map/ppermute | solution.py:287

commit v12 on v11

--- a/solution.py
+++ b/solution.py
@@ -426,7 +426,6 @@
     two = exchanged(block, mask_x=2)
     one = exchanged(jnp.concatenate([block, rim], axis=0), mask_x=1)
     three = exchanged(block, mask_x=3)
-    in_one = exchanged(far_grads[1], mask_z=1)
     pair = exchanged(jnp.concatenate(far_grads[2:], axis=0), mask_z=2)
     one, two, three, part = tie(one, two, three, part)
     rim = one[size:]
@@ -441,15 +440,17 @@
         flops=2 * 10**9,
         mib=16,
     )
-    other, part, in_one = tie(other, part, in_one)
+    other, part, far_one = tie(other, part, far_grads[1])
     block = (wide(block) + wide(other)).astype(BF)
     other = exchanged(block, mask_z=2)
+    in_one = exchanged(far_one, mask_z=1)
     in_zero = exchanged(far_grads[0], mask_core=1)
     other, in_zero, pair = tie(other, in_zero, pair)
     block = (wide(block) + wide(other)).astype(BF)
     in_two = pair[:bound_count]
     other = exchanged(block, mask_z=6)
     in_three = exchanged(pair[bound_count:], mask_z=6)
+    other, in_one = tie(other, in_one)
     block = (wide(block) + wide(other)).astype(BF)
 
     rim = jnp.where(row_y == 1, high, jnp.where(row_y == 2, low, rim))

time: 85.1 us -> 85.1 us (level)
  transfers between devices with their start and end apart: 24 -> 24, of which waited for: 6 -> 7; matrix products, arithmetic and copies ran while one was open for 0% -> 0% of each run, Pallas kernels for 23% -> 23%
where the time goes in v12:
time: 85.1 us; the launch traced here: 84.9 us
  starting transfers between devices  43.1 us (51%)
  Pallas kernels  28.3 us (33%)
  waiting for transfers between devices  9.66 us (11%)
  local copies, waits for them, and re-layouts  1.71 us (2%)
  other arithmetic  1.12 us (1%)
  between operations  1.04 us (1%)
    ppermute x22, starting transfers between devices, exchanged(): return lax.ppermute(block, ('region', 'panel'), route)  39.4 us
    pallas_call x9, Pallas kernels, call(): pl.pallas_call(kernel, out_shape=[jax.ShapeDtypeStruct(shape, kind) for s...  28.3 us
    ppermute x22, waiting for transfers between devices, exchanged(): return lax.ppermute(block, ('region', 'panel'), route)  6.97 us
    ppermute x2, starting transfers between devices, shifted(): lax.ppermute(array, 'panel', [(i, (i + by) % size) for i in range(size)])  3.66 us
    ppermute x2, waiting for transfers between devices, shifted(): lax.ppermute(array, 'panel', [(i, (i + by) % size) for i in range(size)])  2.69 us
  transfers between devices with their start and end apart: 24, of which 7 were waited for; matrix products, arithmetic and copies ran while one was open for 0% of the time, Pallas kernels for 23%

profile of v12, /device:TPU:1, one launch (start us, length us, event | category | flops | bytes accessed | tf_op | source)
XLA Modules:
  0.0 84.9 jit_solution(2671959149587169525)
XLA Ops:
  0.6 0.0 copy-start
  0.6 0.7 copy-done
  1.3 0.9 %copy-done.4 = bf16[1024,128]{1,0:T(8,128)(2,1)S(1)} copy-done((bf16[1024,128]{1,0:T(8,128)(2,1)S(1)}, bf16[1024,128]{1,0:T(8,128)(2,1)}, u32[]{:S(2)}) %copy-start.4) | copy-done | bytes 262168
  2.3 0.4 shard_map.103
  2.7 3.9 %collective-permute-start = (bf16[128,256]{1,0:T(8,128)(2,1)S(1)}, bf16[128,256]{1,0:T(8,128)(2,1)S(1)}, u32[]{:S(2)}, u32[]{:S(2)}) collective-permute-start(bf16[128,256]{1,0:T(8,128)(2,1)S(1)} %get-tuple-element.65.bound_t_ref), channel_id=1, source_target_pairs={{0,32},{1,33},{2,34},{3,35},{4,36},{5,37},{6,38},{7,39},{8,40},{9,... | collective-permute-start | bytes 196616 | tf_op jit(solution)/shard_map/ppermute | solution.py:287
  6.6 1.0 %collective-permute-start.4 = (bf16[128,256]{1,0:T(8,128)(2,1)S(1)}, bf16[128,256]{1,0:T(8,128)(2,1)S(1)}, u32[]{:S(2)}, u32[]{:S(2)}) collective-permute-start(bf16[128,256]{1,0:T(8,128)(2,1)S(1)} %get-tuple-element.65.bound_t_ref), channel_id=1, source_target_pairs={{0,8},{1,9},{2,10},{3,11},{4,12},{5,13},{6,14},{7,15},{8,0},{9,1},... | collective-permute-start | bytes 196616 | tf_op jit(solution)/shard_map/ppermute | solution.py:287
  7.6 1.6 %collective-permute-start.5 = (bf16[128,256]{1,0:T(8,128)(2,1)S(1)}, bf16[128,256]{1,0:T(8,128)(2,1)S(1)}, u32[]{:S(2)}, u32[]{:S(2)}) collective-permute-start(bf16[128,256]{1,0:T(8,128)(2,1)S(1)} %get-tuple-element.65.bound_t_ref), channel_id=1, source_target_pairs={{0,16},{1,17},{2,18},{3,19},{4,20},{5,21},{6,22},{7,23},{8,24},{9,... | collective-permute-start | bytes 196616 | tf_op jit(solution)/shard_map/ppermute | solution.py:287
  9.2 3.7 %collective-permute-start.2 = (bf16[64,128]{1,0:T(8,128)(2,1)S(1)}, bf16[64,128]{1,0:T(8,128)(2,1)S(1)}, u32[]{:S(2)}, u32[]{:S(2)}) collective-permute-start(bf16[64,128]{1,0:T(8,128)(2,1)S(1)} %get-tuple-element.67), channel_id=1, source_target_pairs={{0,7},{1,0},{2,1},{3,2},{4,3},{5,4},{6,5},{7,6},{8,15},{9,8},{10,9... | collective-permute-start | bytes 49160 | tf_op jit(solution)/shard_map/ppermute | solution.py:292
  12.9 0.0 collective-permute-start.1
  12.9 1.9 %shard_map.104 = (bf16[128,3072]{1,0:T(8,128)(2,1)S(1)}, bf16[128,3072]{1,0:T(8,128)(2,1)S(1)}) custom-call(bf16[128,1024]{1,0:T(8,128)(2,1)S(1)} %get-tuple-element.64.lat_t_ref, s32[2,3072]{1,0:T(2,128)S(1)} %copy-done.8), custom_call_target="tpu_custom_call" | custom-call | flops 4000000000 | bytes 4000000 | tf_op jit(solution)/shard_map/pallas_call | solution.py:269
  14.9 0.0 collective-permute-done.2
  14.9 2.7 %collective-permute-done.1 = bf16[64,128]{1,0:T(8,128)(2,1)S(1)} collective-permute-done((bf16[64,128]{1,0:T(8,128)(2,1)S(1)}, bf16[64,128]{1,0:T(8,128)(2,1)S(1)}, u32[]{:S(2)}, u32[]{:S(2)}) %collective-permute-start.1) | collective-permute-done | bytes 16416 | tf_op jit(solution)/shard_map/ppermute | solution.py:292
  17.6 0.0 copy-start.7
  17.6 0.0 copy-start.9
  17.6 4.5 %shard_map.105 = (bf16[128,3072]{1,0:T(8,128)(2,1)S(1)}, f32[128,3072]{1,0:T(8,128)S(1)}, bf16[1024,128]{1,0:T(8,128)(2,1)S(1)}) custom-call(bf16[64,128]{1,0:T(8,128)(2,1)S(1)} %broadcast_select_fusion.11.before_ref, bf16[64,128]{1,0:T(8,128)(2,1)S(1)} %broadcast_select_fusion.10.after_ref, bf16[128,3072]{1,0:T(8,128)(2,1)S(1)} %get-tuple-element.71.own_ref, ...), custom_call_target="tpu_custom_call" | custom-call | flops 3000000000 | bytes 4000000 | tf_op jit(solution)/shard_map/pallas_call | solution.py:269
  22.1 0.0 collective-permute-done.far2_ref
  22.1 0.0 copy-start.1
  22.1 0.0 copy-start.5
  22.2 0.0 copy-start.6
  22.2 3.6 %collective-permute-start.3 = (bf16[128,256]{1,0:T(8,128)(2,1)S(1)}, bf16[128,256]{1,0:T(8,128)(2,1)S(1)}, u32[]{:S(2)}, u32[]{:S(2)}) collective-permute-start(bf16[128,256]{1,0:T(8,128)(2,1)S(1)} %collective-permute-done.far2_ref), channel_id=1, source_target_pairs={{0,96},{1,97},{2,98},{3,99},{4,100},{5,101},{6,102},{7,103},{8,104... | collective-permute-start | bytes 196616 | tf_op jit(solution)/shard_map/ppermute | solution.py:287
  25.7 0.0 collective-permute-done.4.far0_ref
  25.7 0.0 collective-permute-done.5.far1_ref
  25.8 4.4 %shard_map.106 = (bf16[256,6144]{1,0:T(8,128)(2,1)S(1)}, f32[128,6144]{1,0:T(8,128)S(1)}, f32[256,128]{1,0:T(8,128)S(1)}) custom-call(s32[1,4]{1,0:T(1,128)S(1)} %copy-done.9, bf16[128,256]{1,0:T(8,128)(2,1)S(1)} %get-tuple-element.65.bound_t_ref, bf16[128,256]{1,0:T(8,128)(2,1)S(1)} %collective-permute-done.4.far0_ref, ...), custom_call_target="tpu_custom_call" | custom-call | flops 3000000000 | bytes 4000000 | tf_op jit(solution)/shard_map/pallas_call | solution.py:269
  30.2 0.0 collective-permute-done.3.far3_ref
  30.2 8.1 %shard_map.107 = (bf16[1024,128]{1,0:T(8,128)(2,1)}, f32[576,128]{1,0:T(8,128)S(1)}, bf16[576,128]{1,0:T(8,128)(2,1)S(1)}, bf16[128,3072]{1,0:T(8,128)(2,1)S(1)}...) custom-call(s32[1,4]{1,0:T(1,128)S(1)} %copy-done.9, s32[1]{0:T(128)} %bitcast.core_ref, ...), custom_call_target="tpu_custom_call" | custom-call | flops 6000000000 | bytes 4000000 | tf_op jit(solution)/shard_map/pallas_call | solution.py:269
  38.3 2.3 %collective-permute-start.6 = (bf16[576,128]{1,0:T(8,128)(2,1)S(1)}, bf16[576,128]{1,0:T(8,128)(2,1)S(1)}, u32[]{:S(2)}, u32[]{:S(2)}) collective-permute-start(bf16[576,128]{1,0:T(8,128)(2,1)S(1)} %get-tuple-element.85), channel_id=1, source_target_pairs={{0,8},{1,9},{2,10},{3,11},{4,12},{5,13},{6,14},{7,15},{8,0},{9,1},... | collective-permute-start | bytes 442376 | tf_op jit(solution)/shard_map/ppermute | solution.py:287
  40.6 2.6 %shard_map.108 = (f32[1024,128]{1,0:T(8,128)S(1)}, bf16[64,128]{1,0:T(8,128)(2,1)S(1)}, bf16[64,128]{1,0:T(8,128)(2,1)S(1)}) custom-call(bf16[9,128,128]{2,1,0:T(8,128)(2,1)S(1)} %copy-done.3, s32[2,3072]{1,0:T(2,128)S(1)} %copy-done.8, bf16[128,3072]{1,0:T(8,128)(2,1)S(1)} %get-tuple-element.86.dm_ref), custom_call_target="tpu_custom_call" | custom-call | flops 2000000000 | bytes 4000000 | tf_op jit(solution)/shard_map/pallas_call | solution.py:269
  43.3 0.0 collective-permute-done.6
  43.4 0.1 collective-permute-start.7
  43.5 0.1 collective-permute-start.8
  43.6 3.1 %collective-permute-start.9 = (bf16[144,128]{1,0:T(8,128)(2,1)S(1)}, bf16[144,128]{1,0:T(8,128)(2,1)S(1)}, u32[]{:S(2)}, u32[]{:S(2)}) collective-permute-start(bf16[144,128]{1,0:T(8,128)(2,1)S(1)} %get-tuple-element.127), channel_id=1, source_target_pairs={{0,3},{1,2},{2,1},{3,0},{4,7},{5,6},{6,5},{7,4},{8,11},{9,10},{10,... | collective-permute-start | bytes 110600 | tf_op jit(solution)/shard_map/ppermute | solution.py:287
  46.7 2.8 %shard_map.109 = (bf16[256,128]{1,0:T(8,128)(2,1)S(1)}, bf16[256,128]{1,0:T(8,128)(2,1)S(1)}, bf16[256,128]{1,0:T(8,128)(2,1)S(1)}, bf16[256,128]{1,0:T(8,128)(2,1)S(1)}, f32[256,128]{1,0:T(8,128)S(1)}) custom-call(bf16[9,128,128]{2,1,0:T(8,128)(2,1)S(1)} %copy-done.3, s32[2,8192]{1,0:T(2,128)S(1)} %copy-done.7, bf16[128,8192]{1,0:T(8,128)(2,1)S(1)} %get-tuple-element.92.dc_ref), custom_call_target="tpu_custom_call" | custom-call | flops 2000000000 | bytes 4000000 | tf_op jit(solution)/shard_map/pallas_call | solution.py:269
  49.5 0.0 collective-permute-done.7
  49.5 0.0 collective-permute-done.8
  49.5 0.0 collective-permute-done.9
  49.6 2.5 %collective-permute-start.11 = (bf16[144,128]{1,0:T(8,128)(2,1)S(1)}, bf16[144,128]{1,0:T(8,128)(2,1)S(1)}, u32[]{:S(2)}, u32[]{:S(2)}) collective-permute-start(bf16[144,128]{1,0:T(8,128)(2,1)S(1)} %add_convert_fusion.4), channel_id=1, source_target_pairs={{0,128},{1,129},{2,130},{3,131},{4,132},{5,133},{6,134},{7,135},{8... | collective-permute-start | bytes 110600 | tf_op jit(solution)/shard_map/ppermute | solution.py:287
  52.1 0.2 collective-permute-start.12
  52.3 0.0 collective-permute-start.10
  52.3 1.3 %collective-permute-start.16 = (bf16[512,128]{1,0:T(8,128)(2,1)S(1)}, bf16[512,128]{1,0:T(8,128)(2,1)S(1)}, u32[]{:S(2)}, u32[]{:S(2)}) collective-permute-start(bf16[512,128]{1,0:T(8,128)(2,1)S(1)} %pad_maximum_fusion.2), channel_id=1, source_target_pairs={{0,32},{1,33},{2,34},{3,35},{4,36},{5,37},{6,38},{7,39},{8,40},{9,... | collective-permute-start | bytes 393224 | tf_op jit(solution)/shard_map/ppermute | solution.py:287
  53.6 2.0 %collective-permute-start.15 = (bf16[256,128]{1,0:T(8,128)(2,1)S(1)}, bf16[256,128]{1,0:T(8,128)(2,1)S(1)}, u32[]{:S(2)}, u32[]{:S(2)}) collective-permute-start(bf16[256,128]{1,0:T(8,128)(2,1)S(1)} %get-tuple-element.112), channel_id=1, source_target_pairs={{0,8},{1,9},{2,10},{3,11},{4,12},{5,13},{6,14},{7,15},{8,0},{9,1},... | collective-permute-start | bytes 196616 | tf_op jit(solution)/shard_map/ppermute | solution.py:287
  55.6 0.0 collective-permute-done.11
  55.6 0.5 collective-permute-done.12
  56.2 0.8 collective-permute-start.13
  57.0 2.3 %shard_map.110.part_ref = f32[1024,128]{1,0:T(8,128)S(1)} custom-call(bf16[9,128,128]{2,1,0:T(8,128)(2,1)S(1)} %copy-done.3, s32[2,3072]{1,0:T(2,128)S(1)} %copy-done.8, bf16[128,3072]{1,0:T(8,128)(2,1)S(1)} %get-tuple-element.86.dm_ref, bf16[1024,128]{1,0:T(8,128)(2,1)S(1)} %get-tuple-element.106.dn_ref, bf16[1024,128]{1,0:T(8,128)(2,1)S(1)} %copy-done.6, ...), custom_call_target="tpu_custom_call" | custom-call | flops 2000000000 | bytes 4000000 | tf_op jit(solution)/shard_map/pallas_call | solution.py:269
  59.3 0.1 collective-permute-done.13
  59.4 1.5 %collective-permute-start.14 = (bf16[144,128]{1,0:T(8,128)(2,1)S(1)}, bf16[144,128]{1,0:T(8,128)(2,1)S(1)}, u32[]{:S(2)}, u32[]{:S(2)}) collective-permute-start(bf16[144,128]{1,0:T(8,128)(2,1)S(1)} %add_convert_fusion.2), channel_id=1, source_target_pairs={{0,32},{1,33},{2,34},{3,35},{4,36},{5,37},{6,38},{7,39},{8,40},{9,... | collective-permute-start | bytes 110600 | tf_op jit(solution)/shard_map/ppermute | solution.py:287
  60.9 0.6 collective-permute-start.18
  61.5 0.0 collective-permute-done.15.in0_ref
  61.5 1.7 %collective-permute-done.14 = bf16[144,128]{1,0:T(8,128)(2,1)S(1)} collective-permute-done((bf16[144,128]{1,0:T(8,128)(2,1)S(1)}, bf16[144,128]{1,0:T(8,128)(2,1)S(1)}, u32[]{:S(2)}, u32[]{:S(2)}) %collective-permute-start.14) | collective-permute-done | bytes 36896 | tf_op jit(solution)/shard_map/ppermute | solution.py:287
  63.2 0.0 collective-permute-done.16
  63.2 2.9 %collective-permute-start.17 = (bf16[144,128]{1,0:T(8,128)(2,1)S(1)}, bf16[144,128]{1,0:T(8,128)(2,1)S(1)}, u32[]{:S(2)}, u32[]{:S(2)}) collective-permute-start(bf16[144,128]{1,0:T(8,128)(2,1)S(1)} %add_convert_fusion.1), channel_id=1, source_target_pairs={{0,96},{1,97},{2,98},{3,99},{4,100},{5,101},{6,102},{7,103},{8,104... | collective-permute-start | bytes 110600 | tf_op jit(solution)/shard_map/ppermute | solution.py:287
  66.1 1.1 %collective-permute-start.22 = (bf16[256,128]{1,0:T(8,128)(2,1)S(1)}, bf16[256,128]{1,0:T(8,128)(2,1)S(1)}, u32[]{:S(2)}, u32[]{:S(2)}) collective-permute-start(bf16[256,128]{1,0:T(8,128)(2,1)S(1)} %get-tuple-element.134), channel_id=1, source_target_pairs={{0,96},{1,97},{2,98},{3,99},{4,100},{5,101},{6,102},{7,103},{8,104... | collective-permute-start | bytes 196616 | tf_op jit(solution)/shard_map/ppermute | solution.py:287
  67.2 1.3 %collective-permute-done.17 = bf16[144,128]{1,0:T(8,128)(2,1)S(1)} collective-permute-done((bf16[144,128]{1,0:T(8,128)(2,1)S(1)}, bf16[144,128]{1,0:T(8,128)(2,1)S(1)}, u32[]{:S(2)}, u32[]{:S(2)}) %collective-permute-start.17) | collective-permute-done | bytes 36896 | tf_op jit(solution)/shard_map/ppermute | solution.py:287
  68.6 0.2 collective-permute-start.19
  68.8 2.3 %collective-permute-start.20 = (bf16[208,128]{1,0:T(8,128)(2,1)S(1)}, bf16[208,128]{1,0:T(8,128)(2,1)S(1)}, u32[]{:S(2)}, u32[]{:S(2)}) collective-permute-start(bf16[208,128]{1,0:T(8,128)(2,1)S(1)} %get-tuple-element.139), channel_id=1, source_target_pairs={{0,1},{1,0},{2,3},{3,2},{4,5},{5,4},{6,7},{7,6},{8,9},{9,8},{10,11... | collective-permute-start | bytes 159752 | tf_op jit(solution)/shard_map/ppermute | solution.py:287
  71.1 0.9 %collective-permute-start.21 = (bf16[208,128]{1,0:T(8,128)(2,1)S(1)}, bf16[208,128]{1,0:T(8,128)(2,1)S(1)}, u32[]{:S(2)}, u32[]{:S(2)}) collective-permute-start(bf16[208,128]{1,0:T(8,128)(2,1)S(1)} %get-tuple-element.138), channel_id=1, source_target_pairs={{0,3},{1,2},{2,1},{3,0},{4,7},{5,6},{6,5},{7,4},{8,11},{9,10},{10,... | collective-permute-start | bytes 159752 | tf_op jit(solution)/shard_map/ppermute | solution.py:287
  72.0 0.0 collective-permute-done.22.in3_ref
  72.0 1.4 %collective-permute-done.20 = bf16[208,128]{1,0:T(8,128)(2,1)S(1)} collective-permute-done((bf16[208,128]{1,0:T(8,128)(2,1)S(1)}, bf16[208,128]{1,0:T(8,128)(2,1)S(1)}, u32[]{:S(2)}, u32[]{:S(2)}) %collective-permute-start.20) | collective-permute-done | bytes 53280 | tf_op jit(solution)/shard_map/ppermute | solution.py:287
  73.4 1.9 %collective-permute-done.21 = bf16[208,128]{1,0:T(8,128)(2,1)S(1)} collective-permute-done((bf16[208,128]{1,0:T(8,128)(2,1)S(1)}, bf16[208,128]{1,0:T(8,128)(2,1)S(1)}, u32[]{:S(2)}, u32[]{:S(2)}) %collective-permute-start.21) | collective-permute-done | bytes 53280 | tf_op jit(solution)/shard_map/ppermute | solution.py:287
  75.3 0.0 collective-permute-done.19
  75.3 7.4 %collective-permute-start.23 = (bf16[576,128]{1,0:T(8,128)(2,1)S(1)}, bf16[576,128]{1,0:T(8,128)(2,1)S(1)}, u32[]{:S(2)}, u32[]{:S(2)}) collective-permute-start(bf16[576,128]{1,0:T(8,128)(2,1)S(1)} %pad_maximum_fusion.1), channel_id=1, source_target_pairs={{0,8},{1,9},{2,10},{3,11},{4,12},{5,13},{6,14},{7,15},{8,0},{9,1},... | collective-permute-start | bytes 442376 | tf_op jit(solution)/shard_map/ppermute | solution.py:287
  82.8 1.2 %shard_map.111 = f32[1024,128]{1,0:T(8,128)} custom-call(f32[1024,128]{1,0:T(8,128)S(1)} %shard_map.110.part_ref, f32[256,128]{1,0:T(8,128)S(1)} %get-tuple-element.110.own_ref, bf16[256,128]{1,0:T(8,128)(2,1)S(1)} %collective-permute-done.15.in0_ref, bf16[256,128]{1,0:T(8,128)(2,1)S(1)} %collective-permute-done.18.in1_ref, ...), custom_call_target="tpu_custom_call" | custom-call | flops 100000000 | bytes 4000000 | tf_op jit(solution)/shard_map/pallas_call | solution.py:269
  84.0 0.0 collective-permute-done.23
  84.1 0.9 %pad_maximum_fusion = f32[1152,128]{1,0:T(8,128)} fusion(f32[576,128]{1,0:T(8,128)S(1)} %get-tuple-element.126, f32[576,128]{1,0:T(8,128)S(1)} %get-tuple-element.125), kind=kLoop, calls=%fused_computation | loop fusion | flops 147456 | bytes 1179648 | tf_op jit(solution)/shard_map/concatenate | solution.py:313
  (35 shorter events, 0.3 us)
Async XLA Ops:
  0.6 0.7 copy-start
  1.3 0.9 %copy-start.4 = (bf16[1024,128]{1,0:T(8,128)(2,1)S(1)}, bf16[1024,128]{1,0:T(8,128)(2,1)}, u32[]{:S(2)}) copy-start(bf16[1024,128]{1,0:T(8,128)(2,1)} %lat_ref.1) | copy-start | bytes 786436
  2.3 10.6 %copy-start.8 = (s32[2,3072]{1,0:T(2,128)S(1)}, s32[2,3072]{1,0:T(2,128)}, u32[]{:S(2)}) copy-start(s32[2,3072]{1,0:T(2,128)} %edges_ref.9) | copy-start | bytes 73732
  2.7 19.4 %collective-permute-start = (bf16[128,256]{1,0:T(8,128)(2,1)S(1)}, bf16[128,256]{1,0:T(8,128)(2,1)S(1)}, u32[]{:S(2)}, u32[]{:S(2)}) collective-permute-start(bf16[128,256]{1,0:T(8,128)(2,1)S(1)} %get-tuple-element.65.bound_t_ref), channel_id=1, source_target_pairs={{0,32},{1,33},{2,34},{3,35},{4,36},{5,37},{6,38},{7,39},{8,40},{9,... | collective-permute-start | bytes 196616 | tf_op jit(solution)/shard_map/ppermute | solution.py:287
  6.6 19.1 %collective-permute-start.4 = (bf16[128,256]{1,0:T(8,128)(2,1)S(1)}, bf16[128,256]{1,0:T(8,128)(2,1)S(1)}, u32[]{:S(2)}, u32[]{:S(2)}) collective-permute-start(bf16[128,256]{1,0:T(8,128)(2,1)S(1)} %get-tuple-element.65.bound_t_ref), channel_id=1, source_target_pairs={{0,8},{1,9},{2,10},{3,11},{4,12},{5,13},{6,14},{7,15},{8,0},{9,1},... | collective-permute-start | bytes 196616 | tf_op jit(solution)/shard_map/ppermute | solution.py:287
  7.6 18.2 %collective-permute-start.5 = (bf16[128,256]{1,0:T(8,128)(2,1)S(1)}, bf16[128,256]{1,0:T(8,128)(2,1)S(1)}, u32[]{:S(2)}, u32[]{:S(2)}) collective-permute-start(bf16[128,256]{1,0:T(8,128)(2,1)S(1)} %get-tuple-element.65.bound_t_ref), channel_id=1, source_target_pairs={{0,16},{1,17},{2,18},{3,19},{4,20},{5,21},{6,22},{7,23},{8,24},{9,... | collective-permute-start | bytes 196616 | tf_op jit(solution)/shard_map/ppermute | solution.py:287
  9.2 5.7 %collective-permute-start.2 = (bf16[64,128]{1,0:T(8,128)(2,1)S(1)}, bf16[64,128]{1,0:T(8,128)(2,1)S(1)}, u32[]{:S(2)}, u32[]{:S(2)}) collective-permute-start(bf16[64,128]{1,0:T(8,128)(2,1)S(1)} %get-tuple-element.67), channel_id=1, source_target_pairs={{0,7},{1,0},{2,1},{3,2},{4,3},{5,4},{6,5},{7,6},{8,15},{9,8},{10,9... | collective-permute-start | bytes 49160 | tf_op jit(solution)/shard_map/ppermute | solution.py:292
  12.9 4.7 %collective-permute-start.1 = (bf16[64,128]{1,0:T(8,128)(2,1)S(1)}, bf16[64,128]{1,0:T(8,128)(2,1)S(1)}, u32[]{:S(2)}, u32[]{:S(2)}) collective-permute-start(bf16[64,128]{1,0:T(8,128)(2,1)S(1)} %get-tuple-element.66), channel_id=1, source_target_pairs={{0,1},{1,2},{2,3},{3,4},{4,5},{5,6},{6,7},{7,0},{8,9},{9,10},{10,1... | collective-permute-start | bytes 49160 | tf_op jit(solution)/shard_map/ppermute | solution.py:292
  12.9 4.7 %copy-start.2 = (bf16[3072,128]{1,0:T(8,128)(2,1)S(1)}, bf16[3072,128]{1,0:T(8,128)(2,1)}, u32[]{:S(2)}) copy-start(bf16[3072,128]{1,0:T(8,128)(2,1)} %feats_ref.3) | copy-start | bytes 2359300
  12.9 4.7 %copy-start.3 = (bf16[9,128,128]{2,1,0:T(8,128)(2,1)S(1)}, bf16[9,128,128]{2,1,0:T(8,128)(2,1)}, u32[]{:S(2)}) copy-start(bf16[9,128,128]{2,1,0:T(8,128)(2,1)} %w_ref.11) | copy-start | bytes 884740
  17.6 8.1 %copy-start.7 = (s32[2,8192]{1,0:T(2,128)S(1)}, s32[2,8192]{1,0:T(2,128)}, u32[]{:S(2)}) copy-start(s32[2,8192]{1,0:T(2,128)} %contacts_ref.5) | copy-start | bytes 196612
  17.6 8.1 %copy-start.9 = (s32[1,4]{1,0:T(1,128)S(1)}, s32[1,4]{1,0:T(1,128)}, u32[]{:S(2)}) copy-start(s32[1,4]{1,0:T(1,128)} %counts_ref.3) | copy-start | bytes 52
  22.1 8.0 %copy-start.1 = (s32[256]{0:T(256)S(1)}, s32[256]{0:T(256)}, u32[]{:S(2)}) copy-start(s32[256]{0:T(256)} %param.13) | copy-start | bytes 3076
  22.1 8.0 %copy-start.5 = (bf16[1024,128]{1,0:T(8,128)(2,1)S(1)}, bf16[1024,128]{1,0:T(8,128)(2,1)}, u32[]{:S(2)}) copy-start(bf16[1024,128]{1,0:T(8,128)(2,1)} %lat_ref.1) | copy-start | bytes 786436
  22.2 8.0 %copy-start.6 = (bf16[1024,128]{1,0:T(8,128)(2,1)S(1)}, bf16[1024,128]{1,0:T(8,128)(2,1)}, u32[]{:S(2)}) copy-start(bf16[1024,128]{1,0:T(8,128)(2,1)} %cot_ref.3) | copy-start | bytes 786436
  22.2 8.0 %collective-permute-start.3 = (bf16[128,256]{1,0:T(8,128)(2,1)S(1)}, bf16[128,256]{1,0:T(8,128)(2,1)S(1)}, u32[]{:S(2)}, u32[]{:S(2)}) collective-permute-start(bf16[128,256]{1,0:T(8,128)(2,1)S(1)} %collective-permute-done.far2_ref), channel_id=1, source_target_pairs={{0,96},{1,97},{2,98},{3,99},{4,100},{5,101},{6,102},{7,103},{8,104... | collective-permute-start | bytes 196616 | tf_op jit(solution)/shard_map/ppermute | solution.py:287
  38.3 4.9 %collective-permute-start.6 = (bf16[576,128]{1,0:T(8,128)(2,1)S(1)}, bf16[576,128]{1,0:T(8,128)(2,1)S(1)}, u32[]{:S(2)}, u32[]{:S(2)}) collective-permute-start(bf16[576,128]{1,0:T(8,128)(2,1)S(1)} %get-tuple-element.85), channel_id=1, source_target_pairs={{0,8},{1,9},{2,10},{3,11},{4,12},{5,13},{6,14},{7,15},{8,0},{9,1},... | collective-permute-start | bytes 442376 | tf_op jit(solution)/shard_map/ppermute | solution.py:287
  43.4 6.2 %collective-permute-start.7 = (bf16[144,128]{1,0:T(8,128)(2,1)S(1)}, bf16[144,128]{1,0:T(8,128)(2,1)S(1)}, u32[]{:S(2)}, u32[]{:S(2)}) collective-permute-start(bf16[144,128]{1,0:T(8,128)(2,1)S(1)} %get-tuple-element.129), channel_id=1, source_target_pairs={{0,2},{1,3},{2,0},{3,1},{4,6},{5,7},{6,4},{7,5},{8,10},{9,11},{10,... | collective-permute-start | bytes 110600 | tf_op jit(solution)/shard_map/ppermute | solution.py:287
  43.5 6.1 %collective-permute-start.8 = (bf16[144,128]{1,0:T(8,128)(2,1)S(1)}, bf16[144,128]{1,0:T(8,128)(2,1)S(1)}, u32[]{:S(2)}, u32[]{:S(2)}) collective-permute-start(bf16[144,128]{1,0:T(8,128)(2,1)S(1)} %get-tuple-element.128), channel_id=1, source_target_pairs={{0,1},{1,0},{2,3},{3,2},{4,5},{5,4},{6,7},{7,6},{8,9},{9,8},{10,11... | collective-permute-start | bytes 110600 | tf_op jit(solution)/shard_map/ppermute | solution.py:287
  43.6 6.0 %collective-permute-start.9 = (bf16[144,128]{1,0:T(8,128)(2,1)S(1)}, bf16[144,128]{1,0:T(8,128)(2,1)S(1)}, u32[]{:S(2)}, u32[]{:S(2)}) collective-permute-start(bf16[144,128]{1,0:T(8,128)(2,1)S(1)} %get-tuple-element.127), channel_id=1, source_target_pairs={{0,3},{1,2},{2,1},{3,0},{4,7},{5,6},{6,5},{7,4},{8,11},{9,10},{10,... | collective-permute-start | bytes 110600 | tf_op jit(solution)/shard_map/ppermute | solution.py:287
  49.6 6.0 %collective-permute-start.11 = (bf16[144,128]{1,0:T(8,128)(2,1)S(1)}, bf16[144,128]{1,0:T(8,128)(2,1)S(1)}, u32[]{:S(2)}, u32[]{:S(2)}) collective-permute-start(bf16[144,128]{1,0:T(8,128)(2,1)S(1)} %add_convert_fusion.4), channel_id=1, source_target_pairs={{0,128},{1,129},{2,130},{3,131},{4,132},{5,133},{6,134},{7,135},{8... | collective-permute-start | bytes 110600 | tf_op jit(solution)/shard_map/ppermute | solution.py:287
  52.1 4.0 %collective-permute-start.12 = (bf16[144,128]{1,0:T(8,128)(2,1)S(1)}, bf16[144,128]{1,0:T(8,128)(2,1)S(1)}, u32[]{:S(2)}, u32[]{:S(2)}) collective-permute-start(bf16[144,128]{1,0:T(8,128)(2,1)S(1)} %add_convert_fusion.4), channel_id=1, source_target_pairs={{0,132},{1,133},{2,134},{3,135},{4,128},{5,129},{6,130},{7,131},{8... | collective-permute-start | bytes 110600 | tf_op jit(solution)/shard_map/ppermute | solution.py:287
  52.3 3.8 %collective-permute-start.10 = (bf16[208,128]{1,0:T(8,128)(2,1)S(1)}, bf16[208,128]{1,0:T(8,128)(2,1)S(1)}, u32[]{:S(2)}, u32[]{:S(2)}) collective-permute-start(bf16[208,128]{1,0:T(8,128)(2,1)S(1)} %pad_maximum_fusion.6), channel_id=1, source_target_pairs={{0,4},{1,5},{2,6},{3,7},{4,0},{5,1},{6,2},{7,3},{8,12},{9,13},{10,... | collective-permute-start | bytes 159752 | tf_op jit(solution)/shard_map/ppermute | solution.py:287
  52.3 10.8 %collective-permute-start.16 = (bf16[512,128]{1,0:T(8,128)(2,1)S(1)}, bf16[512,128]{1,0:T(8,128)(2,1)S(1)}, u32[]{:S(2)}, u32[]{:S(2)}) collective-permute-start(bf16[512,128]{1,0:T(8,128)(2,1)S(1)} %pad_maximum_fusion.2), channel_id=1, source_target_pairs={{0,32},{1,33},{2,34},{3,35},{4,36},{5,37},{6,38},{7,39},{8,40},{9,... | collective-permute-start | bytes 393224 | tf_op jit(solution)/shard_map/ppermute | solution.py:287
  53.6 7.9 %collective-permute-start.15 = (bf16[256,128]{1,0:T(8,128)(2,1)S(1)}, bf16[256,128]{1,0:T(8,128)(2,1)S(1)}, u32[]{:S(2)}, u32[]{:S(2)}) collective-permute-start(bf16[256,128]{1,0:T(8,128)(2,1)S(1)} %get-tuple-element.112), channel_id=1, source_target_pairs={{0,8},{1,9},{2,10},{3,11},{4,12},{5,13},{6,14},{7,15},{8,0},{9,1},... | collective-permute-start | bytes 196616 | tf_op jit(solution)/shard_map/ppermute | solution.py:287
  56.2 3.2 %collective-permute-start.13 = (bf16[144,128]{1,0:T(8,128)(2,1)S(1)}, bf16[144,128]{1,0:T(8,128)(2,1)S(1)}, u32[]{:S(2)}, u32[]{:S(2)}) collective-permute-start(bf16[144,128]{1,0:T(8,128)(2,1)S(1)} %add_convert_fusion.3), channel_id=1, source_target_pairs={{0,16},{1,17},{2,18},{3,19},{4,20},{5,21},{6,22},{7,23},{8,24},{9,... | collective-permute-start | bytes 110600 | tf_op jit(solution)/shard_map/ppermute | solution.py:287
  59.4 3.8 %collective-permute-start.14 = (bf16[144,128]{1,0:T(8,128)(2,1)S(1)}, bf16[144,128]{1,0:T(8,128)(2,1)S(1)}, u32[]{:S(2)}, u32[]{:S(2)}) collective-permute-start(bf16[144,128]{1,0:T(8,128)(2,1)S(1)} %add_convert_fusion.2), channel_id=1, source_target_pairs={{0,32},{1,33},{2,34},{3,35},{4,36},{5,37},{6,38},{7,39},{8,40},{9,... | collective-permute-start | bytes 110600 | tf_op jit(solution)/shard_map/ppermute | solution.py:287
  60.9 6.3 %collective-permute-start.18 = (bf16[256,128]{1,0:T(8,128)(2,1)S(1)}, bf16[256,128]{1,0:T(8,128)(2,1)S(1)}, u32[]{:S(2)}, u32[]{:S(2)}) collective-permute-start(bf16[256,128]{1,0:T(8,128)(2,1)S(1)} %get-tuple-element.117), channel_id=1, source_target_pairs={{0,16},{1,17},{2,18},{3,19},{4,20},{5,21},{6,22},{7,23},{8,24},{9,... | collective-permute-start | bytes 196616 | tf_op jit(solution)/shard_map/ppermute | solution.py:287
  63.2 5.4 %collective-permute-start.17 = (bf16[144,128]{1,0:T(8,128)(2,1)S(1)}, bf16[144,128]{1,0:T(8,128)(2,1)S(1)}, u32[]{:S(2)}, u32[]{:S(2)}) collective-permute-start(bf16[144,128]{1,0:T(8,128)(2,1)S(1)} %add_convert_fusion.1), channel_id=1, source_target_pairs={{0,96},{1,97},{2,98},{3,99},{4,100},{5,101},{6,102},{7,103},{8,104... | collective-permute-start | bytes 110600 | tf_op jit(solution)/shard_map/ppermute | solution.py:287
  66.1 5.9 %collective-permute-start.22 = (bf16[256,128]{1,0:T(8,128)(2,1)S(1)}, bf16[256,128]{1,0:T(8,128)(2,1)S(1)}, u32[]{:S(2)}, u32[]{:S(2)}) collective-permute-start(bf16[256,128]{1,0:T(8,128)(2,1)S(1)} %get-tuple-element.134), channel_id=1, source_target_pairs={{0,96},{1,97},{2,98},{3,99},{4,100},{5,101},{6,102},{7,103},{8,104... | collective-permute-start | bytes 196616 | tf_op jit(solution)/shard_map/ppermute | solution.py:287
  68.6 6.7 %collective-permute-start.19 = (bf16[224,128]{1,0:T(8,128)(2,1)S(1)}, bf16[224,128]{1,0:T(8,128)(2,1)S(1)}, u32[]{:S(2)}, u32[]{:S(2)}) collective-permute-start(bf16[224,128]{1,0:T(8,128)(2,1)S(1)} %pad_maximum_fusion.3), channel_id=1, source_target_pairs={{0,2},{1,3},{2,0},{3,1},{4,6},{5,7},{6,4},{7,5},{8,10},{9,11},{10,... | collective-permute-start | bytes 172040 | tf_op jit(solution)/shard_map/ppermute | solution.py:287
  68.8 4.6 %collective-permute-start.20 = (bf16[208,128]{1,0:T(8,128)(2,1)S(1)}, bf16[208,128]{1,0:T(8,128)(2,1)S(1)}, u32[]{:S(2)}, u32[]{:S(2)}) collective-permute-start(bf16[208,128]{1,0:T(8,128)(2,1)S(1)} %get-tuple-element.139), channel_id=1, source_target_pairs={{0,1},{1,0},{2,3},{3,2},{4,5},{5,4},{6,7},{7,6},{8,9},{9,8},{10,11... | collective-permute-start | bytes 159752 | tf_op jit(solution)/shard_map/ppermute | solution.py:287
  71.1 4.2 %collective-permute-start.21 = (bf16[208,128]{1,0:T(8,128)(2,1)S(1)}, bf16[208,128]{1,0:T(8,128)(2,1)S(1)}, u32[]{:S(2)}, u32[]{:S(2)}) collective-permute-start(bf16[208,128]{1,0:T(8,128)(2,1)S(1)} %get-tuple-element.138), channel_id=1, source_target_pairs={{0,3},{1,2},{2,1},{3,0},{4,7},{5,6},{6,5},{7,4},{8,11},{9,10},{10,... | collective-permute-start | bytes 159752 | tf_op jit(solution)/shard_map/ppermute | solution.py:287
  75.3 8.7 %collective-permute-start.23 = (bf16[576,128]{1,0:T(8,128)(2,1)S(1)}, bf16[576,128]{1,0:T(8,128)(2,1)S(1)}, u32[]{:S(2)}, u32[]{:S(2)}) collective-permute-start(bf16[576,128]{1,0:T(8,128)(2,1)S(1)} %pad_maximum_fusion.1), channel_id=1, source_target_pairs={{0,8},{1,9},{2,10},{3,11},{4,12},{5,13},{6,14},{7,15},{8,0},{9,1},... | collective-permute-start | bytes 442376 | tf_op jit(solution)/shard_map/ppermute | solution.py:287
